TPU v7x, 512 devices: a whole 4x8x8 slice. The times are simulated.
512 devices in a mesh: dp: 64 (over x, z, core), fsdp: 8 (over y).
Axes of the slice: x: 4, y: 8, z: 8, core: 2. Of those that a mesh axis runs over, the one named last changes fastest.
Arguments:
- queries: bfloat16 [8, 8192, 4096], P('fsdp', 'dp'), may hold values from -180 to 180
- key_rows: bfloat16 [8, 8192, 512], P('fsdp', 'dp'), may hold values from -8 to 8
- out_grad: bfloat16 [8, 8192, 4096], P('fsdp', 'dp'), may hold values from -6 to 6
- inputs: bfloat16 [8, 8192, 4096], P('fsdp', 'dp'), may hold values from -6 to 6
- w_value: bfloat16 [4096, 512], P('fsdp'), may hold values from -0.09375 to 0.09375
- doc_pos: int32 [8, 8192], P('fsdp', 'dp'), may hold values from 0 to 384, as said below
Outputs:
- key_grad: bfloat16 [8, 8192, 512], P('fsdp', 'dp')
- weight_grad: bfloat16 [4096, 512], P('fsdp')
Inputs may be any that keep to these rules, and one draw needn't show every extreme that they name: `doc_pos`: documents are contiguous runs 0, 1, 2, ... within a sequence, each of at most 385 tokens; every sequence starts a document at its first token, and in every sequence one document has exactly 385 tokens.
All inputs are finite; a program needn't handle non-finite values.
Results may differ from a plain program's by a relative error of at most 0.02.
Values may be sent and summed in bfloat16 or wider, within the bound.
No kernel may reach another device: no remote copies, remote signals or barrier semaphores. Data moves between devices by JAX's collectives and lax.ppermute only.
A program may use at most 64 MiB of HBM per device.

v0:
```python
import math

import jax
import jax.numpy as jnp
from jax import lax
from jax.sharding import PartitionSpec as P

KEY_HEADS = 4
GROUP_WIDTH = 8
HEAD_SIZE = 128
SPAN = 3


masked_value = -1e30


def from_behind(block, axis, distance):
    devices = range(lax.axis_size(axis))
    route = [(i - distance, i) for i in devices if i - distance in devices]
    return lax.ppermute(block, axis, route)


def attend(query_row_block, key_span_rows, value_span_rows, gradient_rows, position):
    count_of_rows = query_row_block.shape[0]
    span_length = key_span_rows.shape[0]
    score_scale = 1.0 / math.sqrt(HEAD_SIZE)
    offset = (SPAN * count_of_rows + jnp.arange(count_of_rows, dtype=jnp.int32))[
        :, None
    ] - jnp.arange(span_length, dtype=jnp.int32)[None, :]
    allowed = (offset >= 0) & (offset <= position[:, None])
    query_head_matrix = query_row_block.reshape(
        count_of_rows, KEY_HEADS, GROUP_WIDTH, HEAD_SIZE
    ).transpose(1, 2, 0, 3)
    gradient_heads = gradient_rows.reshape(
        count_of_rows, KEY_HEADS, GROUP_WIDTH, HEAD_SIZE
    ).transpose(1, 2, 0, 3)
    key_head_matrix = key_span_rows.reshape(span_length, KEY_HEADS, HEAD_SIZE).transpose(1, 0, 2)
    value_head_matrix = value_span_rows.reshape(span_length, KEY_HEADS, HEAD_SIZE).transpose(
        1, 0, 2
    )

    def one_head(operands):
        query_head, grad_head, key_head, value_head = operands
        scores = (
            jnp.einsum("gtd,wd->gtw", query_head, key_head, preferred_element_type=jnp.float32)
            * score_scale
        )
        scores = jnp.where(allowed[None], scores, masked_value)
        row_max = jnp.max(scores, axis=-1, keepdims=True)
        exp_scores = jnp.exp(scores - row_max)
        attn_weights = exp_scores / jnp.sum(exp_scores, axis=-1, keepdims=True)
        weights_low = attn_weights.astype(jnp.bfloat16)
        output = jnp.einsum(
            "gtw,wd->gtd", weights_low, value_head, preferred_element_type=jnp.float32
        )
        row_delta = jnp.sum(grad_head.astype(jnp.float32) * output, axis=-1, keepdims=True)
        prob_grad = jnp.einsum(
            "gtd,wd->gtw", grad_head, value_head, preferred_element_type=jnp.float32
        )
        score_grad = attn_weights * (prob_grad - row_delta)
        score_low = score_grad.astype(jnp.bfloat16)
        value_portion = jnp.einsum(
            "gtw,gtd->wd", weights_low, grad_head, preferred_element_type=jnp.float32
        )
        key_portion = (
            jnp.einsum("gtw,gtd->wd", score_low, query_head, preferred_element_type=jnp.float32)
            * score_scale
        )
        return (key_portion, value_portion)

    key_portion, value_portion = lax.map(
        one_head, (query_head_matrix, gradient_heads, key_head_matrix, value_head_matrix)
    )
    key_portion = key_portion.transpose(1, 0, 2).reshape(span_length, KEY_HEADS * HEAD_SIZE)
    value_portion = value_portion.transpose(1, 0, 2).reshape(span_length, KEY_HEADS * HEAD_SIZE)
    return (key_portion, value_portion)


def per_device(queries, key_rows, out_grad, inputs, w_value, doc_pos):
    query_row_block = queries[0]
    key_local = key_rows[0]
    gradient_rows = out_grad[0]
    input_rows = inputs[0]
    position = doc_pos[0]
    count_of_rows = query_row_block.shape[0]
    key_width = key_local.shape[1]
    fsdp_size = lax.axis_size("fsdp")
    columns = input_rows
    value_sum = jnp.dot(
        columns,
        lax.all_gather(w_value, "fsdp", axis=0, tiled=True),
        preferred_element_type=jnp.float32,
    )
    value_local = value_sum.astype(jnp.bfloat16)
    key_parts = [key_local]
    value_parts = [value_local]
    for distance in range(1, SPAN + 1):
        earlier_key, earlier_value = from_behind((key_local, value_local), "dp", distance)
        key_parts.insert(0, earlier_key)
        value_parts.insert(0, earlier_value)
    key_span_rows = jnp.concatenate(key_parts, axis=0)
    value_span_rows = jnp.concatenate(value_parts, axis=0)
    key_portion, value_portion = attend(
        query_row_block, key_span_rows, value_span_rows, gradient_rows, position
    )
    blocks = SPAN + 1
    key_blocks = key_portion.reshape(blocks, count_of_rows, key_width)
    value_blocks = value_portion.reshape(blocks, count_of_rows, key_width)
    key_own = key_blocks[SPAN]
    value_own = value_blocks[SPAN]
    for distance in range(1, SPAN + 1):
        later_key, later_value = (
            from_behind(key_blocks[SPAN - distance].astype(jnp.bfloat16), "dp", -distance).astype(
                jnp.float32
            ),
            from_behind(value_blocks[SPAN - distance].astype(jnp.bfloat16), "dp", -distance).astype(
                jnp.float32
            ),
        )
        key_own = key_own + later_key
        value_own = value_own + later_value
    key_grad = key_own.astype(jnp.bfloat16)
    value_low = value_own.astype(jnp.bfloat16)
    columns = input_rows
    product = lax.dot_general(
        columns, value_low, (((0,), (0,)), ((), ())), preferred_element_type=jnp.float32
    )
    partial_grad = lax.psum_scatter(
        lax.optimization_barrier(product.astype(jnp.bfloat16))
        .astype(jnp.float32)
        .astype(jnp.bfloat16),
        "fsdp",
        scatter_dimension=0,
        tiled=True,
    ).astype(jnp.float32)
    total_grad = lax.psum(partial_grad, "dp")
    token_total = fsdp_size * lax.axis_size("dp") * count_of_rows
    weight_grad = (total_grad * (1.0 / math.sqrt(token_total))).astype(jnp.bfloat16)
    return (key_grad[None], weight_grad)


def solution(mesh):
    return jax.shard_map(
        per_device,
        mesh=mesh,
        in_specs=(
            P("fsdp", "dp", None),
            P("fsdp", "dp", None),
            P("fsdp", "dp", None),
            P("fsdp", "dp", None),
            P("fsdp", None),
            P("fsdp", "dp"),
        ),
        out_specs=(P("fsdp", "dp", None), P("fsdp", None)),
        check_vma=False,
    )
```

profile of v0, /device:TPU:1, one launch (start us, length us, event | category | flops | bytes accessed | tf_op | source)
XLA Modules:
  0.0 485.4 jit_solution(3578665116282493027)
XLA Ops:
  9.0 8.0 %collective-permute-start = (bf16[128,512]{0,1:T(8,128)(2,1)S(1)}, bf16[128,512]{0,1:T(8,128)(2,1)}, u32[]{:S(2)}, u32[]{:S(2)}) collective-permute-start(bf16[128,512]{0,1:T(8,128)(2,1)S(1)} %bitcast.186), channel_id=1, source_target_pairs={{0,24},{8,32},{16,40},{24,48},{32,56},{40,64},{48,72},{56,80},{64,... | collective-permute-start | bytes 393224 | tf_op jit(solution)/shard_map/ppermute | solution.py:20
  17.0 4.0 collective-permute-start.1
  22.9 49.8 %all-gather.2.cloned.1.call-done = bf16[4096,512]{1,0:T(8,128)(2,1)} async-done(((bf16[512,512]{1,0:T(8,128)(2,1)}), bf16[4096,512]{1,0:T(8,128)(2,1)}) %all-gather.2.cloned.1.call-update) | async-done | bytes 4194320 | tf_op jit(solution)/shard_map/all_gather | solution.py:91
  72.8 2.9 convolution_convert_fusion.1
  75.7 5.7 %collective-permute-start.3 = (bf16[128,512]{1,0:T(8,128)(2,1)S(1)}, bf16[128,512]{1,0:T(8,128)(2,1)}, u32[]{:S(2)}, u32[]{:S(2)}) collective-permute-start(bf16[128,512]{1,0:T(8,128)(2,1)S(1)} %convolution_convert_fusion.1), channel_id=1, source_target_pairs={{0,24},{8,32},{16,40},{24,48},{32,56},{40,64},{48,72},{56,80},{64,... | collective-permute-start | bytes 393224 | tf_op jit(solution)/shard_map/ppermute | solution.py:20
  81.4 3.3 collective-permute-start.4
  89.8 1.9 bitcast_bitcast_fusion
  91.7 55.7 %while.13 = (s32[]{:T(128)}, f32[4,512,128]{2,1,0:T(8,128)}, f32[4,512,128]{1,2,0:T(8,128)}, bf16[4,8,128,128]{2,3,1,0:T(8,128)(2,1)}, bf16[4,512,128]{1,2,0:T(8...) while((s32[]{:T(128)}, f32[4,512,128]{2,1,0:T(8,128)}, ...), condition=%wide.region_4.5_spmd.clone, body=%wide.region_0.4_spmd.clone.sunk | while | flops 949684736 | bytes 8552041 | solution.py:71
  91.8 3.2 fusion.123
  95.2 3.1 fusion.124
  98.3 3.6 fusion.125
  101.9 3.7 fusion.126
  105.8 3.2 fusion.123
  109.1 3.1 fusion.124
  112.3 3.6 fusion.125
  115.8 3.7 fusion.126
  119.7 3.2 fusion.123
  123.1 3.1 fusion.124
  126.2 3.6 fusion.125
  129.8 3.7 fusion.126
  133.6 3.2 fusion.123
  137.0 3.1 fusion.124
  140.1 3.6 fusion.125
  143.7 3.7 fusion.126
  151.4 3.0 collective-permute-start.9
  156.2 5.8 %collective-permute-done.11 = bf16[128,512]{0,1:T(8,128)(2,1)S(1)} collective-permute-done((bf16[128,512]{0,1:T(8,128)(2,1)S(1)}, bf16[128,512]{0,1:T(8,128)(2,1)S(1)}, u32[]{:S(2)}, u32[]{:S(2)}) %collective-permute-start.11) | collective-permute-done | bytes 131104 | tf_op jit(solution)/shard_map/ppermute | solution.py:20
  162.2 3.2 fusion.73
  166.7 1.9 collective-permute-start.6
  173.0 3.0 collective-permute-done.7
  176.0 5.0 %collective-permute-done.8 = bf16[128,512]{1,0:T(8,128)(2,1)S(1)} collective-permute-done((bf16[128,512]{1,0:T(8,128)(2,1)S(1)}, bf16[128,512]{1,0:T(8,128)(2,1)S(1)}, u32[]{:S(2)}, u32[]{:S(2)}) %collective-permute-start.8) | collective-permute-done | bytes 131104 | tf_op jit(solution)/shard_map/ppermute | solution.py:20
  181.7 39.9 %reduce-scatter.2.cloned.1.call-done = bf16[512,512]{0,1:T(8,128)(2,1)} async-done(((bf16[4096,512]{0,1:T(8,128)(2,1)}), bf16[512,512]{0,1:T(8,128)(2,1)}) %reduce-scatter.2.cloned.1.call-update) | async-done | bytes 524304 | tf_op jit(solution)/shard_map/reduce_scatter | solution.py:128
  221.6 255.8 %all-reduce.1 = f32[512,512]{0,1:T(8,128)S(1)} all-reduce(bf16[512,512]{0,1:T(8,128)(2,1)} %reduce-scatter.2.cloned.1.call-done), channel_id=1, replica_groups=mesh['dp'=64,'fsdp'=8] {'dp'}, use_global_device_ids=true, to_apply=%region_6.7 | all-reduce | flops 262144 | bytes 1572864 | tf_op jit(solution)/shard_map/psum | solution.py:136
  (60 shorter events, 23.4 us)
Async XLA Ops:
  7.2 65.6 %copy-start = (bf16[1,128,4096]{2,1,0:T(8,128)(2,1)S(1)}, bf16[1,128,4096]{2,1,0:T(8,128)(2,1)}, u32[]{:S(2)}) copy-start(bf16[1,128,4096]{2,1,0:T(8,128)(2,1)} %param.11) | copy-start | bytes 3145732
  7.2 65.6 %all-gather.2.cloned.1.call-start = ((), (), s32[]{:S(2)}) async-start(), calls=%async_computation.1 | async-start | bytes 4718592 | tf_op jit(solution)/shard_map/all_gather | solution.py:91
  7.9 213.7 %reduce-scatter.2.cloned.1.call-start = ((), (), s32[]{:S(2)}) async-start(), calls=%async_computation.2 | async-start | bytes 4718592 | tf_op jit(solution)/shard_map/reduce_scatter | solution.py:128
  9.0 77.6 %copy-start.2 = (bf16[1,128,4096]{2,1,0:T(8,128)(2,1)S(1)}, bf16[1,128,4096]{2,1,0:T(8,128)(2,1)}, u32[]{:S(2)}) copy-start(bf16[1,128,4096]{2,1,0:T(8,128)(2,1)} %param.8) | copy-start | bytes 3145732
  9.0 75.7 %collective-permute-start = (bf16[128,512]{0,1:T(8,128)(2,1)S(1)}, bf16[128,512]{0,1:T(8,128)(2,1)}, u32[]{:S(2)}, u32[]{:S(2)}) collective-permute-start(bf16[128,512]{0,1:T(8,128)(2,1)S(1)} %bitcast.186), channel_id=1, source_target_pairs={{0,24},{8,32},{16,40},{24,48},{32,56},{40,64},{48,72},{56,80},{64,... | collective-permute-start | bytes 393224 | tf_op jit(solution)/shard_map/ppermute | solution.py:20
  17.0 71.6 %collective-permute-start.1 = (bf16[128,512]{0,1:T(8,128)(2,1)S(1)}, bf16[128,512]{0,1:T(8,128)(2,1)}, u32[]{:S(2)}, u32[]{:S(2)}) collective-permute-start(bf16[128,512]{0,1:T(8,128)(2,1)S(1)} %bitcast.187), channel_id=1, source_target_pairs={{0,16},{8,24},{16,32},{24,40},{32,48},{40,56},{48,64},{56,72},{64,... | collective-permute-start | bytes 393224 | tf_op jit(solution)/shard_map/ppermute | solution.py:20
  21.0 67.6 %collective-permute-start.2 = (bf16[128,512]{0,1:T(8,128)(2,1)S(1)}, bf16[128,512]{0,1:T(8,128)(2,1)}, u32[]{:S(2)}, u32[]{:S(2)}) collective-permute-start(bf16[128,512]{0,1:T(8,128)(2,1)S(1)} %bitcast.188), channel_id=1, source_target_pairs={{0,8},{8,16},{16,24},{24,32},{32,40},{40,48},{48,56},{56,64},{64,7... | collective-permute-start | bytes 393224 | tf_op jit(solution)/shard_map/ppermute | solution.py:20
  75.7 12.3 %copy-start.3 = (bf16[1,128,4096]{2,1,0:T(8,128)(2,1)S(1)}, bf16[1,128,4096]{2,1,0:T(8,128)(2,1)}, u32[]{:S(2)}) copy-start(bf16[1,128,4096]{2,1,0:T(8,128)(2,1)} %param.10) | copy-start | bytes 3145732
  75.7 14.1 %collective-permute-start.3 = (bf16[128,512]{1,0:T(8,128)(2,1)S(1)}, bf16[128,512]{1,0:T(8,128)(2,1)}, u32[]{:S(2)}, u32[]{:S(2)}) collective-permute-start(bf16[128,512]{1,0:T(8,128)(2,1)S(1)} %convolution_convert_fusion.1), channel_id=1, source_target_pairs={{0,24},{8,32},{16,40},{24,48},{32,56},{40,64},{48,72},{56,80},{64,... | collective-permute-start | bytes 393224 | tf_op jit(solution)/shard_map/ppermute | solution.py:20
  81.4 8.4 %collective-permute-start.4 = (bf16[128,512]{1,0:T(8,128)(2,1)S(1)}, bf16[128,512]{1,0:T(8,128)(2,1)}, u32[]{:S(2)}, u32[]{:S(2)}) collective-permute-start(bf16[128,512]{1,0:T(8,128)(2,1)S(1)} %convolution_convert_fusion.1), channel_id=1, source_target_pairs={{0,16},{8,24},{16,32},{24,40},{32,48},{40,56},{48,64},{56,72},{64,... | collective-permute-start | bytes 393224 | tf_op jit(solution)/shard_map/ppermute | solution.py:20
  84.7 5.1 %collective-permute-start.5 = (bf16[128,512]{1,0:T(8,128)(2,1)S(1)}, bf16[128,512]{1,0:T(8,128)(2,1)}, u32[]{:S(2)}, u32[]{:S(2)}) collective-permute-start(bf16[128,512]{1,0:T(8,128)(2,1)S(1)} %convolution_convert_fusion.1), channel_id=1, source_target_pairs={{0,8},{8,16},{16,24},{24,32},{32,40},{40,48},{48,56},{56,64},{64,7... | collective-permute-start | bytes 393224 | tf_op jit(solution)/shard_map/ppermute | solution.py:20
  87.9 3.7 copy-start.4
  148.8 7.4 %collective-permute-start.10 = (bf16[128,512]{0,1:T(8,128)(2,1)S(1)}, bf16[128,512]{0,1:T(8,128)(2,1)S(1)}, u32[]{:S(2)}, u32[]{:S(2)}) collective-permute-start(bf16[128,512]{0,1:T(8,128)(2,1)S(1)} %bitcast.195), channel_id=1, source_target_pairs={{16,0},{24,8},{32,16},{40,24},{48,32},{56,40},{64,48},{72,56},{80,... | collective-permute-start | bytes 393224 | tf_op jit(solution)/shard_map/ppermute | solution.py:20
  150.1 12.0 %collective-permute-start.11 = (bf16[128,512]{0,1:T(8,128)(2,1)S(1)}, bf16[128,512]{0,1:T(8,128)(2,1)S(1)}, u32[]{:S(2)}, u32[]{:S(2)}) collective-permute-start(bf16[128,512]{0,1:T(8,128)(2,1)S(1)} %bitcast.194), channel_id=1, source_target_pairs={{24,0},{32,8},{40,16},{48,24},{56,32},{64,40},{72,48},{80,56},{88,... | collective-permute-start | bytes 393224 | tf_op jit(solution)/shard_map/ppermute | solution.py:20
  151.4 10.7 %collective-permute-start.9 = (bf16[128,512]{0,1:T(8,128)(2,1)S(1)}, bf16[128,512]{0,1:T(8,128)(2,1)S(1)}, u32[]{:S(2)}, u32[]{:S(2)}) collective-permute-start(bf16[128,512]{0,1:T(8,128)(2,1)S(1)} %bitcast.193), channel_id=1, source_target_pairs={{8,0},{16,8},{24,16},{32,24},{40,32},{48,40},{56,48},{64,56},{72,6... | collective-permute-start | bytes 393224 | tf_op jit(solution)/shard_map/ppermute | solution.py:20
  165.3 1.2 copy-start.1
  166.7 6.3 %collective-permute-start.6 = (bf16[128,512]{1,0:T(8,128)(2,1)S(1)}, bf16[128,512]{1,0:T(8,128)(2,1)S(1)}, u32[]{:S(2)}, u32[]{:S(2)}) collective-permute-start(bf16[128,512]{1,0:T(8,128)(2,1)S(1)} %bitcast.190), channel_id=1, source_target_pairs={{8,0},{16,8},{24,16},{32,24},{40,32},{48,40},{56,48},{64,56},{72,6... | collective-permute-start | bytes 393224 | tf_op jit(solution)/shard_map/ppermute | solution.py:20
  168.7 7.3 %collective-permute-start.7 = (bf16[128,512]{1,0:T(8,128)(2,1)S(1)}, bf16[128,512]{1,0:T(8,128)(2,1)S(1)}, u32[]{:S(2)}, u32[]{:S(2)}) collective-permute-start(bf16[128,512]{1,0:T(8,128)(2,1)S(1)} %bitcast.191), channel_id=1, source_target_pairs={{16,0},{24,8},{32,16},{40,24},{48,32},{56,40},{64,48},{72,56},{80,... | collective-permute-start | bytes 393224 | tf_op jit(solution)/shard_map/ppermute | solution.py:20
  170.0 10.9 %collective-permute-start.8 = (bf16[128,512]{1,0:T(8,128)(2,1)S(1)}, bf16[128,512]{1,0:T(8,128)(2,1)S(1)}, u32[]{:S(2)}, u32[]{:S(2)}) collective-permute-start(bf16[128,512]{1,0:T(8,128)(2,1)S(1)} %bitcast.192), channel_id=1, source_target_pairs={{24,0},{32,8},{40,16},{48,24},{56,32},{64,40},{72,48},{80,56},{88,... | collective-permute-start | bytes 393224 | tf_op jit(solution)/shard_map/ppermute | solution.py:20
Sparse Core Ops, SparseCore 0:
  10.1 62.6 all-gather.1
  165.5 56.0 reduce-scatter.1
where the time goes:
time: 490 us; the launch traced here: 485 us
  blocking collectives  256 us (52%)
  waiting for transfers between devices  107 us (22%)
  matrix products  60.4 us (12%)
  starting transfers between devices  35 us (7%)
  between operations  14.3 us (3%)
  local copies, waits for them, and re-layouts  7.17 us (1%)
  other arithmetic  5.82 us (1%)
    psum x1, blocking collectives, per_device(): total_grad = lax.psum(partial_grad, 'dp')  256 us
    all_gather x1, waiting for transfers between devices, per_device(): lax.all_gather(w_value, 'fsdp', axis=0, tiled=True)  49.8 us
    reduce_scatter x1, waiting for transfers between devices, per_device(): lax.psum_scatter(lax.optimization_barrier(product.astype(jnp.bfloat16)).a...  39.9 us
    ppermute x12, starting transfers between devices, from_behind(): return lax.ppermute(block, axis, route)  34.9 us
    ppermute x12, waiting for transfers between devices, from_behind(): return lax.ppermute(block, axis, route)  16.3 us
    dot_general x4, matrix products, one_head(): jnp.einsum('gtw,gtd->wd', weights_low, grad_head, preferred_element_type=...  14.9 us
    dot_general x4, matrix products, one_head(): jnp.einsum('gtw,gtd->wd', score_low, query_head, preferred_element_type=j...  14.3 us
    sub x4, matrix products, one_head(): exp_scores = jnp.exp(scores - row_max)  12.7 us
  transfers between devices with their start and end apart: 14, of which 7 were waited for; matrix products, arithmetic and copies ran while one was open for 2% of the time, Pallas kernels for 0%

commit v1 on v0

v1 whole, which is shorter than its diff:
```python
import math

import jax
import jax.numpy as jnp
from jax import lax
from jax.experimental import pallas as pl
from jax.experimental.pallas import tpu as pltpu
from jax.sharding import PartitionSpec as P

KEY_HEADS = 4
GROUP_WIDTH = 8
HEAD_SIZE = 128
SPAN = 3
BLOCK = 128
PAIR = 2 * HEAD_SIZE
GROUP_COLUMNS = GROUP_WIDTH * HEAD_SIZE
SPAN_ROWS = (SPAN + 1) * BLOCK

masked_value = -1e30
NT = (((1,), (1,)), ((), ()))


def shift(block, distance):
    devices = range(lax.axis_size("dp"))
    route = [(i, i + distance) for i in devices if i + distance in devices]
    return lax.ppermute(block, "dp", route)


def stacked(ref, pair):
    first = ref[:, pair * PAIR : pair * PAIR + HEAD_SIZE]
    second = ref[:, pair * PAIR + HEAD_SIZE : (pair + 1) * PAIR]
    return jnp.concatenate([first, second], axis=0)


def weights_kernel(
    position_ref, query_ref, grad_ref, k0_ref, k1_ref, k2_ref, k3_ref, weights_ref, v0_ref, v1_ref, v2_ref, v3_ref
):
    keys_down = lax.broadcasted_iota(jnp.int32, (SPAN_ROWS, BLOCK), 0)
    queries_across = lax.broadcasted_iota(jnp.int32, (SPAN_ROWS, BLOCK), 1)
    offset = SPAN * BLOCK + queries_across - keys_down
    allowed = (offset >= 0) & (offset <= position_ref[...])
    mask = jnp.where(allowed, 0.0, masked_value).astype(jnp.bfloat16)
    keys = jnp.concatenate([k0_ref[...], k1_ref[...], k2_ref[...], k3_ref[...]], axis=0)
    keys = jnp.concatenate([keys, mask], axis=1)
    unit = (
        lax.broadcasted_iota(jnp.int32, (PAIR, BLOCK), 0) % BLOCK
        == lax.broadcasted_iota(jnp.int32, (PAIR, BLOCK), 1)
    )
    unit = jnp.where(unit, 1.0, 0.0).astype(jnp.bfloat16)
    score_scale = 1.0 / math.sqrt(HEAD_SIZE)
    total = jnp.zeros((SPAN_ROWS, HEAD_SIZE), jnp.float32)
    for pair in range(GROUP_WIDTH // 2):
        heads = jnp.concatenate([stacked(query_ref, pair), unit], axis=1)
        scores = lax.dot_general(keys, heads, NT, preferred_element_type=jnp.float32)
        top = jnp.max(scores, axis=0, keepdims=True)
        weights = jnp.exp((scores - top) * score_scale)
        weights = weights * (1.0 / jnp.sum(weights, axis=0, keepdims=True))
        low = weights.astype(jnp.bfloat16)
        weights_ref[0, :, pair * PAIR : (pair + 1) * PAIR] = low
        total += jnp.dot(low, stacked(grad_ref, pair), preferred_element_type=jnp.float32)
    for block, out_ref in enumerate((v0_ref, v1_ref, v2_ref, v3_ref)):
        out_ref[...] = total[block * BLOCK : (block + 1) * BLOCK].astype(out_ref.dtype)


def scores_kernel(
    weights_ref, query_ref, grad_ref, v0_ref, v1_ref, v2_ref, v3_ref, k0_ref, k1_ref, k2_ref, k3_ref
):
    values = jnp.concatenate([v0_ref[...], v1_ref[...], v2_ref[...], v3_ref[...]], axis=0)
    total = jnp.zeros((SPAN_ROWS, HEAD_SIZE), jnp.float32)
    for pair in range(GROUP_WIDTH // 2):
        prob_grad = lax.dot_general(
            values, stacked(grad_ref, pair), NT, preferred_element_type=jnp.float32
        )
        weights = weights_ref[0, :, pair * PAIR : (pair + 1) * PAIR].astype(jnp.float32)
        row_delta = jnp.sum(weights * prob_grad, axis=0, keepdims=True)
        low = (weights * (prob_grad - row_delta)).astype(jnp.bfloat16)
        total += jnp.dot(low, stacked(query_ref, pair), preferred_element_type=jnp.float32)
    total = total * (1.0 / math.sqrt(HEAD_SIZE))
    for block, out_ref in enumerate((k0_ref, k1_ref, k2_ref, k3_ref)):
        out_ref[...] = total[block * BLOCK : (block + 1) * BLOCK].astype(out_ref.dtype)


wide = pl.BlockSpec((BLOCK, GROUP_COLUMNS), lambda g: (0, g))
narrow = pl.BlockSpec((BLOCK, HEAD_SIZE), lambda g: (0, g))
held = pl.BlockSpec((1, SPAN_ROWS, GROUP_COLUMNS), lambda g: (g, 0, 0))
gradients = [
    jax.ShapeDtypeStruct((BLOCK, KEY_HEADS * HEAD_SIZE), kind)
    for kind in (jnp.bfloat16, jnp.bfloat16, jnp.bfloat16, jnp.float32)
]
KERNEL_FLOPS = 2 * 2 * SPAN_ROWS * BLOCK * KEY_HEADS * GROUP_COLUMNS
params = pltpu.CompilerParams(vmem_limit_bytes=40 * 1024 * 1024)


def attention_weights(position, queries, grads, keys):
    return pl.pallas_call(
        weights_kernel,
        grid=(KEY_HEADS,),
        in_specs=[pl.BlockSpec((1, BLOCK), lambda g: (0, 0)), wide, wide] + [narrow] * 4,
        out_specs=[held] + [narrow] * 4,
        out_shape=[jax.ShapeDtypeStruct((KEY_HEADS, SPAN_ROWS, GROUP_COLUMNS), jnp.bfloat16)]
        + gradients,
        compiler_params=params,
        cost_estimate=pl.CostEstimate(
            flops=2 * KERNEL_FLOPS, bytes_accessed=8 << 20, transcendentals=SPAN_ROWS * BLOCK * 32
        ),
        name="attention_weights",
    )(position, queries, grads, *keys)


def key_gradient(weights, queries, grads, values):
    return pl.pallas_call(
        scores_kernel,
        grid=(KEY_HEADS,),
        in_specs=[held, wide, wide] + [narrow] * 4,
        out_specs=[narrow] * 4,
        out_shape=gradients,
        compiler_params=params,
        cost_estimate=pl.CostEstimate(
            flops=2 * KERNEL_FLOPS, bytes_accessed=8 << 20, transcendentals=0
        ),
        name="key_gradient",
    )(weights, queries, grads, *values)


def span_of(block):
    return [shift(block, 3), shift(block, 2), shift(block, 1), block]


def owed(parts):
    total = parts[SPAN]
    for distance in (1, 2, 3):
        total = total + shift(parts[SPAN - distance], -distance).astype(jnp.float32)
    return total.astype(jnp.bfloat16)


def sum_over_dp(partial):
    size = lax.axis_size("dp")
    rows, columns = partial.shape
    each = rows // size
    pieces = lax.all_to_all(partial, "dp", 0, 0, tiled=True).reshape(size, each, columns)
    return jnp.sum(pieces.astype(jnp.float32), axis=0)


def per_device(queries, key_rows, out_grad, inputs, w_value, doc_pos):
    queries, keys, grads, rows = queries[0], key_rows[0], out_grad[0], inputs[0]
    key_span = span_of(keys)
    w_whole = lax.all_gather(w_value, "fsdp", axis=0, tiled=True)
    rows_here = lax.all_to_all(rows, "fsdp", 1, 0, tiled=True)
    weights, *value_parts = attention_weights(doc_pos, queries, grads, key_span)
    value_grad = owed(value_parts)
    fsdp_size = lax.axis_size("fsdp")
    copies = jnp.broadcast_to(value_grad[None], (fsdp_size,) + value_grad.shape)
    value_grads = lax.all_to_all(copies, "fsdp", 0, 0, tiled=True).reshape(-1, value_grad.shape[1])

    values = jnp.dot(rows, w_whole, preferred_element_type=jnp.float32).astype(jnp.bfloat16)
    key_parts = key_gradient(weights, queries, grads, span_of(values))
    key_grad = owed(key_parts)

    product = lax.dot_general(
        rows_here, value_grads, (((0,), (0,)), ((), ())), preferred_element_type=jnp.float32
    )
    piece = sum_over_dp(product.astype(jnp.bfloat16))
    dp_size = lax.axis_size("dp")
    token_total = fsdp_size * dp_size * BLOCK
    piece = (piece * (1.0 / math.sqrt(token_total))).astype(jnp.bfloat16)
    copies = jnp.broadcast_to(piece[None], (dp_size,) + piece.shape).reshape(-1, piece.shape[1])
    weight_grad = lax.all_to_all(copies, "dp", 0, 0, tiled=True)
    return (key_grad[None], weight_grad)


def solution(mesh):
    return jax.shard_map(
        per_device,
        mesh=mesh,
        in_specs=(
            P("fsdp", "dp", None),
            P("fsdp", "dp", None),
            P("fsdp", "dp", None),
            P("fsdp", "dp", None),
            P("fsdp", None),
            P("fsdp", "dp"),
        ),
        out_specs=(P("fsdp", "dp", None), P("fsdp", None)),
        check_vma=False,
    )
```

time: 490 us -> 199 us (0.41)
  the two profiles are of different devices: /device:TPU:1 before, /device:TPU:7 now
where the time goes in v1:
time: 199 us
  blocking collectives  71.8 us (36%)
  starting transfers between devices  58.5 us (29%)
  waiting for transfers between devices  28.6 us (14%)
  between operations  14.3 us (7%)
  Pallas kernels  11.4 us (6%)
  local copies, waits for them, and re-layouts  8.22 us (4%)
  matrix products  4.98 us (3%)
    ppermute x12, starting transfers between devices, shift(): return lax.ppermute(block, 'dp', route)  45 us
    all_to_all x1, blocking collectives, per_device(): lax.all_to_all(copies, 'fsdp', 0, 0, tiled=True)  43.7 us
    all_to_all x1, blocking collectives, sum_over_dp(): lax.all_to_all(partial, 'dp', 0, 0, tiled=True).reshape(size, each, columns)  28.1 us
    ppermute x12, waiting for transfers between devices, shift(): return lax.ppermute(block, 'dp', route)  27.9 us
    unnamed x18, local copies, waits for them, and re-layouts  7.31 us
    all_to_all x1, starting transfers between devices, per_device(): rows_here = lax.all_to_all(rows, 'fsdp', 1, 0, tiled=True)  6.82 us
    all_to_all x1, starting transfers between devices, per_device(): weight_grad = lax.all_to_all(copies, 'dp', 0, 0, tiled=True)  6.62 us
    pallas_call x1, Pallas kernels, attention_weights(): pl.pallas_call(weights_kernel, grid=(KEY_HEADS,), in_specs=[pl.BlockSpec(...  6.09 us
  transfers between devices with their start and end apart: 15, of which 8 were waited for; matrix products, arithmetic and copies ran while one was open for 4% of the time, Pallas kernels for 6%

profile of v1, /device:TPU:7, one launch (start us, length us, event | category | flops | bytes accessed | tf_op | source)
XLA Modules:
  0.0 198.7 jit_solution(444222479479602914)
XLA Ops:
  7.9 2.3 %copy.8 = bf16[1,128,4096]{1,2,0:T(8,128)(2,1)} copy(bf16[1,128,4096]{2,1,0:T(8,128)(2,1)} %param.9) | data formatting | bytes 2097152 | tf_op args[3]
  10.3 6.8 %all-to-all-start.1 = ((bf16[128,8,512]{0,2,1:T(8,128)(2,1)}), bf16[128,8,512]{0,2,1:T(8,128)(2,1)S(1)}, u32[]{:S(2)}, u32[]{:S(2)}) async-start(bf16[128,8,512]{0,2,1:T(8,128)(2,1)} %bitcast.5), calls=%async_computation.1 | async-start | bytes 2097152 | tf_op jit(solution)/shard_map/all_to_all | solution.py:148
  17.1 4.8 %collective-permute-start.2 = (bf16[128,512]{1,0:T(8,128)(2,1)S(1)}, bf16[128,512]{1,0:T(8,128)(2,1)S(1)}, u32[]{:S(2)}, u32[]{:S(2)}) collective-permute-start(bf16[128,512]{1,0:T(8,128)(2,1)S(1)} %bitcast.29), channel_id=1, source_target_pairs={{0,8},{8,16},{16,24},{24,32},{32,40},{40,48},{48,56},{56,64},{64,7... | collective-permute-start | bytes 393224 | tf_op jit(solution)/shard_map/ppermute | solution.py:26
  21.9 4.0 %collective-permute-start.1 = (bf16[128,512]{1,0:T(8,128)(2,1)S(1)}, bf16[128,512]{1,0:T(8,128)(2,1)S(1)}, u32[]{:S(2)}, u32[]{:S(2)}) collective-permute-start(bf16[128,512]{1,0:T(8,128)(2,1)S(1)} %bitcast.30), channel_id=1, source_target_pairs={{0,16},{8,24},{16,32},{24,40},{32,48},{40,56},{48,64},{56,72},{64,... | collective-permute-start | bytes 393224 | tf_op jit(solution)/shard_map/ppermute | solution.py:26
  26.0 4.0 %collective-permute-start = (bf16[128,512]{1,0:T(8,128)(2,1)S(1)}, bf16[128,512]{1,0:T(8,128)(2,1)S(1)}, u32[]{:S(2)}, u32[]{:S(2)}) collective-permute-start(bf16[128,512]{1,0:T(8,128)(2,1)S(1)} %bitcast.31), channel_id=1, source_target_pairs={{0,24},{8,32},{16,40},{24,48},{32,56},{40,64},{48,72},{56,80},{64,... | collective-permute-start | bytes 393224 | tf_op jit(solution)/shard_map/ppermute | solution.py:26
  30.0 2.9 %collective-permute-done.1.k1_ref = bf16[128,512]{1,0:T(8,128)(2,1)S(1)} collective-permute-done((bf16[128,512]{1,0:T(8,128)(2,1)S(1)}, bf16[128,512]{1,0:T(8,128)(2,1)S(1)}, u32[]{:S(2)}, u32[]{:S(2)}) %collective-permute-start.1) | collective-permute-done | bytes 131104 | tf_op jit(solution)/shard_map/ppermute | solution.py:26
  32.9 4.6 %collective-permute-done.k0_ref = bf16[128,512]{1,0:T(8,128)(2,1)S(1)} collective-permute-done((bf16[128,512]{1,0:T(8,128)(2,1)S(1)}, bf16[128,512]{1,0:T(8,128)(2,1)S(1)}, u32[]{:S(2)}, u32[]{:S(2)}) %collective-permute-start) | collective-permute-done | bytes 131104 | tf_op jit(solution)/shard_map/ppermute | solution.py:26
  37.5 6.1 %attention_weights.1 = (bf16[4,512,1024]{2,1,0:T(8,128)(2,1)S(1)}, bf16[128,512]{1,0:T(8,128)(2,1)S(1)}, bf16[128,512]{1,0:T(8,128)(2,1)S(1)}, bf16[128,512]{1,0:T(8,128)(2,1)S(1)}, f32[128,512]{1,0:T(8,128)S(1)}) custom-call(s32[1,128]{1,0:T(1,128)S(1)} %copy-done.3, bf16[128,4096]{1,0:T(8,128)(2,1)S(1)} %bitcast.25, bf16[128,4096]{1,0:T(8,128)(2,1)S(1)} %bitcast.27, ...), custom_call_target="tpu_custom_call" | custom-call | flops 2147483648 | bytes 8388608 | tf_op jit(solution)/shard_map/attention_weights/pallas_call | solution.py:95
  43.6 2.0 %copy-done.4 = bf16[4,512,1024]{2,1,0:T(8,128)(2,1)} copy-done((bf16[4,512,1024]{2,1,0:T(8,128)(2,1)}, bf16[4,512,1024]{2,1,0:T(8,128)(2,1)S(1)}, u32[]{:S(2)}) %copy-start.4) | copy-done | bytes 4194328
  45.6 4.2 %collective-permute-start.9 = (bf16[128,512]{1,0:T(8,128)(2,1)S(1)}, bf16[128,512]{1,0:T(8,128)(2,1)S(1)}, u32[]{:S(2)}, u32[]{:S(2)}) collective-permute-start(bf16[128,512]{1,0:T(8,128)(2,1)S(1)} %get-tuple-element.17), channel_id=1, source_target_pairs={{8,0},{16,8},{24,16},{32,24},{40,32},{48,40},{56,48},{64,56},{72,6... | collective-permute-start | bytes 393224 | tf_op jit(solution)/shard_map/ppermute | solution.py:26
  49.8 3.1 %collective-permute-start.10 = (bf16[128,512]{1,0:T(8,128)(2,1)S(1)}, bf16[128,512]{1,0:T(8,128)(2,1)S(1)}, u32[]{:S(2)}, u32[]{:S(2)}) collective-permute-start(bf16[128,512]{1,0:T(8,128)(2,1)S(1)} %get-tuple-element.18), channel_id=1, source_target_pairs={{16,0},{24,8},{32,16},{40,24},{48,32},{56,40},{64,48},{72,56},{80,... | collective-permute-start | bytes 393224 | tf_op jit(solution)/shard_map/ppermute | solution.py:26
  52.9 3.9 %collective-permute-start.11 = (bf16[128,512]{1,0:T(8,128)(2,1)S(1)}, bf16[128,512]{1,0:T(8,128)(2,1)S(1)}, u32[]{:S(2)}, u32[]{:S(2)}) collective-permute-start(bf16[128,512]{1,0:T(8,128)(2,1)S(1)} %get-tuple-element.19), channel_id=1, source_target_pairs={{24,0},{32,8},{40,16},{48,24},{56,32},{64,40},{72,48},{80,56},{88,... | collective-permute-start | bytes 393224 | tf_op jit(solution)/shard_map/ppermute | solution.py:26
  56.9 6.3 %collective-permute-done.11 = bf16[128,512]{1,0:T(8,128)(2,1)S(1)} collective-permute-done((bf16[128,512]{1,0:T(8,128)(2,1)S(1)}, bf16[128,512]{1,0:T(8,128)(2,1)S(1)}, u32[]{:S(2)}, u32[]{:S(2)}) %collective-permute-start.11) | collective-permute-done | bytes 131104 | tf_op jit(solution)/shard_map/ppermute | solution.py:26
  63.3 1.1 copy-done.7
  64.4 43.7 %all_to_all.39 = bf16[8,128,512]{2,1,0:T(8,128)(2,1)S(1)} all-to-all(bf16[8,128,512]{2,1,0:T(8,128)(2,1)S(1)} %broadcast_in_dim.7), channel_id=1, replica_groups=mesh['dp'=64,'fsdp'=8] {'fsdp'}, dimensions={0} | all-to-all | bytes 2097152 | tf_op jit(solution)/shard_map/all_to_all | solution.py:153
  108.1 1.9 fusion.1
  110.1 28.1 %all_to_all.40 = bf16[64,8,512]{2,1,0:T(8,128)(2,1)S(1)} all-to-all(bf16[64,8,512]{2,1,0:T(8,128)(2,1)S(1)} %fusion.1), channel_id=1, replica_groups=mesh['dp'=64,'fsdp'=8] {'dp'}, dimensions={0} | all-to-all | bytes 1048576 | tf_op jit(solution)/shard_map/all_to_all | solution.py:140
  138.3 0.8 broadcast_in_dim.8
  139.1 6.6 %all-to-all-start.3 = ((bf16[64,8,512]{2,1,0:T(8,128)(2,1)}), bf16[64,8,512]{2,1,0:T(8,128)(2,1)}, u32[]{:S(2)}, u32[]{:S(2)}) async-start(bf16[64,8,512]{2,1,0:T(8,128)(2,1)} %broadcast_in_dim.8), calls=%async_computation.3 | async-start | bytes 1048576 | tf_op jit(solution)/shard_map/all_to_all | solution.py:167
  145.8 3.1 %convolution_convert_fusion.v3_ref = bf16[128,512]{1,0:T(8,128)(2,1)S(1)} fusion(bf16[4096,512]{1,0:T(8,128)(2,1)} %all-gather.2.cloned.1.call-done, bf16[1,128,4096]{2,1,0:T(8,128)(2,1)S(1)} %copy-done.6), kind=kOutput, calls=%fused_computation.3 | convolution fusion | flops 536936448 | bytes 5373952 | tf_op jit(solution)/shard_map/dot_general | solution.py:155
  148.8 3.4 %collective-permute-start.5 = (bf16[128,512]{1,0:T(8,128)(2,1)S(1)}, bf16[128,512]{1,0:T(8,128)(2,1)S(1)}, u32[]{:S(2)}, u32[]{:S(2)}) collective-permute-start(bf16[128,512]{1,0:T(8,128)(2,1)S(1)} %convolution_convert_fusion.v3_ref), channel_id=1, source_target_pairs={{0,8},{8,16},{16,24},{24,32},{32,40},{40,48},{48,56},{56,64},{64,7... | collective-permute-start | bytes 393224 | tf_op jit(solution)/shard_map/ppermute | solution.py:26
  152.2 3.1 %collective-permute-start.4 = (bf16[128,512]{1,0:T(8,128)(2,1)S(1)}, bf16[128,512]{1,0:T(8,128)(2,1)S(1)}, u32[]{:S(2)}, u32[]{:S(2)}) collective-permute-start(bf16[128,512]{1,0:T(8,128)(2,1)S(1)} %convolution_convert_fusion.v3_ref), channel_id=1, source_target_pairs={{0,16},{8,24},{16,32},{24,40},{32,48},{40,56},{48,64},{56,72},{64,... | collective-permute-start | bytes 393224 | tf_op jit(solution)/shard_map/ppermute | solution.py:26
  155.3 3.2 %collective-permute-start.3 = (bf16[128,512]{1,0:T(8,128)(2,1)S(1)}, bf16[128,512]{1,0:T(8,128)(2,1)S(1)}, u32[]{:S(2)}, u32[]{:S(2)}) collective-permute-start(bf16[128,512]{1,0:T(8,128)(2,1)S(1)} %convolution_convert_fusion.v3_ref), channel_id=1, source_target_pairs={{0,24},{8,32},{16,40},{24,48},{32,56},{40,64},{48,72},{56,80},{64,... | collective-permute-start | bytes 393224 | tf_op jit(solution)/shard_map/ppermute | solution.py:26
  159.0 6.3 %collective-permute-done.4.v1_ref = bf16[128,512]{1,0:T(8,128)(2,1)S(1)} collective-permute-done((bf16[128,512]{1,0:T(8,128)(2,1)S(1)}, bf16[128,512]{1,0:T(8,128)(2,1)S(1)}, u32[]{:S(2)}, u32[]{:S(2)}) %collective-permute-start.4) | collective-permute-done | bytes 131104 | tf_op jit(solution)/shard_map/ppermute | solution.py:26
  165.4 1.3 collective-permute-done.3.v0_ref
  166.7 5.3 %key_gradient.1 = (bf16[128,512]{1,0:T(8,128)(2,1)S(1)}, bf16[128,512]{1,0:T(8,128)(2,1)S(1)}, bf16[128,512]{1,0:T(8,128)(2,1)S(1)}, f32[128,512]{1,0:T(8,128)S(1)}) custom-call(bf16[4,512,1024]{2,1,0:T(8,128)(2,1)S(1)} %copy-done.5, bf16[128,4096]{1,0:T(8,128)(2,1)S(1)} %bitcast.26, bf16[128,4096]{1,0:T(8,128)(2,1)S(1)} %bitcast.28, ...), custom_call_target="tpu_custom_call" | custom-call | flops 2147483648 | bytes 8388608 | tf_op jit(solution)/shard_map/key_gradient/pallas_call | solution.py:111
  172.0 5.5 %collective-permute-start.6 = (bf16[128,512]{1,0:T(8,128)(2,1)S(1)}, bf16[128,512]{1,0:T(8,128)(2,1)S(1)}, u32[]{:S(2)}, u32[]{:S(2)}) collective-permute-start(bf16[128,512]{1,0:T(8,128)(2,1)S(1)} %get-tuple-element.13), channel_id=1, source_target_pairs={{8,0},{16,8},{24,16},{32,24},{40,32},{48,40},{56,48},{64,56},{72,6... | collective-permute-start | bytes 393224 | tf_op jit(solution)/shard_map/ppermute | solution.py:26
  177.5 1.9 collective-permute-start.7
  179.4 3.9 %collective-permute-start.8 = (bf16[128,512]{1,0:T(8,128)(2,1)S(1)}, bf16[128,512]{1,0:T(8,128)(2,1)S(1)}, u32[]{:S(2)}, u32[]{:S(2)}) collective-permute-start(bf16[128,512]{1,0:T(8,128)(2,1)S(1)} %get-tuple-element.15), channel_id=1, source_target_pairs={{24,0},{32,8},{40,16},{48,24},{56,32},{64,40},{72,48},{80,56},{88,... | collective-permute-start | bytes 393224 | tf_op jit(solution)/shard_map/ppermute | solution.py:26
  183.3 1.2 collective-permute-done.7
  184.5 4.8 %collective-permute-done.8 = bf16[128,512]{1,0:T(8,128)(2,1)S(1)} collective-permute-done((bf16[128,512]{1,0:T(8,128)(2,1)S(1)}, bf16[128,512]{1,0:T(8,128)(2,1)S(1)}, u32[]{:S(2)}, u32[]{:S(2)}) %collective-permute-start.8) | collective-permute-done | bytes 131104 | tf_op jit(solution)/shard_map/ppermute | solution.py:26
  190.0 1.9 copy.10
  (29 shorter events, 2.2 us)
Async XLA Ops:
  7.2 9.9 %copy-start.2 = (bf16[1,128,512]{2,1,0:T(8,128)(2,1)S(1)}, bf16[1,128,512]{2,1,0:T(8,128)(2,1)}, u32[]{:S(2)}) copy-start(bf16[1,128,512]{2,1,0:T(8,128)(2,1)} %param.7) | copy-start | bytes 393220
  7.2 30.3 %copy-start.3 = (s32[1,128]{1,0:T(1,128)S(1)}, s32[1,128]{1,0:T(1,128)}, u32[]{:S(2)}) copy-start(s32[1,128]{1,0:T(1,128)} %position_ref.1) | copy-start | bytes 1540
  7.2 30.3 %copy-start.1 = (bf16[1,128,4096]{2,1,0:T(8,128)(2,1)S(1)}, bf16[1,128,4096]{2,1,0:T(8,128)(2,1)}, u32[]{:S(2)}) copy-start(bf16[1,128,4096]{2,1,0:T(8,128)(2,1)} %param.8) | copy-start | bytes 3145732
  7.2 30.3 %copy-start = (bf16[1,128,4096]{2,1,0:T(8,128)(2,1)S(1)}, bf16[1,128,4096]{2,1,0:T(8,128)(2,1)}, u32[]{:S(2)}) copy-start(bf16[1,128,4096]{2,1,0:T(8,128)(2,1)} %param.6) | copy-start | bytes 3145732
  7.2 138.5 %all-gather.2.cloned.1.call-start = ((), (), s32[]{:S(2)}) async-start(), calls=%async_computation.4 | async-start | bytes 4718592 | tf_op jit(solution)/shard_map/all_gather | solution.py:147
  10.3 53.0 %all-to-all-start.1 = ((bf16[128,8,512]{0,2,1:T(8,128)(2,1)}), bf16[128,8,512]{0,2,1:T(8,128)(2,1)S(1)}, u32[]{:S(2)}, u32[]{:S(2)}) async-start(bf16[128,8,512]{0,2,1:T(8,128)(2,1)} %bitcast.5), calls=%async_computation.1 | async-start | bytes 2097152 | tf_op jit(solution)/shard_map/all_to_all | solution.py:148
  17.1 12.9 %collective-permute-start.2 = (bf16[128,512]{1,0:T(8,128)(2,1)S(1)}, bf16[128,512]{1,0:T(8,128)(2,1)S(1)}, u32[]{:S(2)}, u32[]{:S(2)}) collective-permute-start(bf16[128,512]{1,0:T(8,128)(2,1)S(1)} %bitcast.29), channel_id=1, source_target_pairs={{0,8},{8,16},{16,24},{24,32},{32,40},{40,48},{48,56},{56,64},{64,7... | collective-permute-start | bytes 393224 | tf_op jit(solution)/shard_map/ppermute | solution.py:26
  21.9 10.9 %collective-permute-start.1 = (bf16[128,512]{1,0:T(8,128)(2,1)S(1)}, bf16[128,512]{1,0:T(8,128)(2,1)S(1)}, u32[]{:S(2)}, u32[]{:S(2)}) collective-permute-start(bf16[128,512]{1,0:T(8,128)(2,1)S(1)} %bitcast.30), channel_id=1, source_target_pairs={{0,16},{8,24},{16,32},{24,40},{32,48},{40,56},{48,64},{56,72},{64,... | collective-permute-start | bytes 393224 | tf_op jit(solution)/shard_map/ppermute | solution.py:26
  26.0 11.5 %collective-permute-start = (bf16[128,512]{1,0:T(8,128)(2,1)S(1)}, bf16[128,512]{1,0:T(8,128)(2,1)S(1)}, u32[]{:S(2)}, u32[]{:S(2)}) collective-permute-start(bf16[128,512]{1,0:T(8,128)(2,1)S(1)} %bitcast.31), channel_id=1, source_target_pairs={{0,24},{8,32},{16,40},{24,48},{32,56},{40,64},{48,72},{56,80},{64,... | collective-permute-start | bytes 393224 | tf_op jit(solution)/shard_map/ppermute | solution.py:26
  43.6 2.0 %copy-start.4 = (bf16[4,512,1024]{2,1,0:T(8,128)(2,1)}, bf16[4,512,1024]{2,1,0:T(8,128)(2,1)S(1)}, u32[]{:S(2)}) copy-start(bf16[4,512,1024]{2,1,0:T(8,128)(2,1)S(1)} %get-tuple-element.11.weights_ref) | copy-start | bytes 12582916
  45.6 11.2 %collective-permute-start.9 = (bf16[128,512]{1,0:T(8,128)(2,1)S(1)}, bf16[128,512]{1,0:T(8,128)(2,1)S(1)}, u32[]{:S(2)}, u32[]{:S(2)}) collective-permute-start(bf16[128,512]{1,0:T(8,128)(2,1)S(1)} %get-tuple-element.17), channel_id=1, source_target_pairs={{8,0},{16,8},{24,16},{32,24},{40,32},{48,40},{56,48},{64,56},{72,6... | collective-permute-start | bytes 393224 | tf_op jit(solution)/shard_map/ppermute | solution.py:26
  49.8 7.0 %collective-permute-start.10 = (bf16[128,512]{1,0:T(8,128)(2,1)S(1)}, bf16[128,512]{1,0:T(8,128)(2,1)S(1)}, u32[]{:S(2)}, u32[]{:S(2)}) collective-permute-start(bf16[128,512]{1,0:T(8,128)(2,1)S(1)} %get-tuple-element.18), channel_id=1, source_target_pairs={{16,0},{24,8},{32,16},{40,24},{48,32},{56,40},{64,48},{72,56},{80,... | collective-permute-start | bytes 393224 | tf_op jit(solution)/shard_map/ppermute | solution.py:26
  52.9 10.3 %collective-permute-start.11 = (bf16[128,512]{1,0:T(8,128)(2,1)S(1)}, bf16[128,512]{1,0:T(8,128)(2,1)S(1)}, u32[]{:S(2)}, u32[]{:S(2)}) collective-permute-start(bf16[128,512]{1,0:T(8,128)(2,1)S(1)} %get-tuple-element.19), channel_id=1, source_target_pairs={{24,0},{32,8},{40,16},{48,24},{56,32},{64,40},{72,48},{80,56},{88,... | collective-permute-start | bytes 393224 | tf_op jit(solution)/shard_map/ppermute | solution.py:26
  63.3 1.1 copy-start.7
  64.4 81.3 %copy-start.6 = (bf16[1,128,4096]{2,1,0:T(8,128)(2,1)S(1)}, bf16[1,128,4096]{2,1,0:T(8,128)(2,1)}, u32[]{:S(2)}) copy-start(bf16[1,128,4096]{2,1,0:T(8,128)(2,1)} %param.9) | copy-start | bytes 3145732
  139.1 44.2 %all-to-all-start.3 = ((bf16[64,8,512]{2,1,0:T(8,128)(2,1)}), bf16[64,8,512]{2,1,0:T(8,128)(2,1)}, u32[]{:S(2)}, u32[]{:S(2)}) async-start(bf16[64,8,512]{2,1,0:T(8,128)(2,1)} %broadcast_in_dim.8), calls=%async_computation.3 | async-start | bytes 1048576 | tf_op jit(solution)/shard_map/all_to_all | solution.py:167
  145.8 20.9 %copy-start.5 = (bf16[4,512,1024]{2,1,0:T(8,128)(2,1)S(1)}, bf16[4,512,1024]{2,1,0:T(8,128)(2,1)}, u32[]{:S(2)}) copy-start(bf16[4,512,1024]{2,1,0:T(8,128)(2,1)} %copy-done.4) | copy-start | bytes 12582916
  148.8 10.2 %collective-permute-start.5 = (bf16[128,512]{1,0:T(8,128)(2,1)S(1)}, bf16[128,512]{1,0:T(8,128)(2,1)S(1)}, u32[]{:S(2)}, u32[]{:S(2)}) collective-permute-start(bf16[128,512]{1,0:T(8,128)(2,1)S(1)} %convolution_convert_fusion.v3_ref), channel_id=1, source_target_pairs={{0,8},{8,16},{16,24},{24,32},{32,40},{40,48},{48,56},{56,64},{64,7... | collective-permute-start | bytes 393224 | tf_op jit(solution)/shard_map/ppermute | solution.py:26
  152.2 13.2 %collective-permute-start.4 = (bf16[128,512]{1,0:T(8,128)(2,1)S(1)}, bf16[128,512]{1,0:T(8,128)(2,1)S(1)}, u32[]{:S(2)}, u32[]{:S(2)}) collective-permute-start(bf16[128,512]{1,0:T(8,128)(2,1)S(1)} %convolution_convert_fusion.v3_ref), channel_id=1, source_target_pairs={{0,16},{8,24},{16,32},{24,40},{32,48},{40,56},{48,64},{56,72},{64,... | collective-permute-start | bytes 393224 | tf_op jit(solution)/shard_map/ppermute | solution.py:26
  155.3 11.4 %collective-permute-start.3 = (bf16[128,512]{1,0:T(8,128)(2,1)S(1)}, bf16[128,512]{1,0:T(8,128)(2,1)S(1)}, u32[]{:S(2)}, u32[]{:S(2)}) collective-permute-start(bf16[128,512]{1,0:T(8,128)(2,1)S(1)} %convolution_convert_fusion.v3_ref), channel_id=1, source_target_pairs={{0,24},{8,32},{16,40},{24,48},{32,56},{40,64},{48,72},{56,80},{64,... | collective-permute-start | bytes 393224 | tf_op jit(solution)/shard_map/ppermute | solution.py:26
  172.0 11.3 %collective-permute-start.6 = (bf16[128,512]{1,0:T(8,128)(2,1)S(1)}, bf16[128,512]{1,0:T(8,128)(2,1)S(1)}, u32[]{:S(2)}, u32[]{:S(2)}) collective-permute-start(bf16[128,512]{1,0:T(8,128)(2,1)S(1)} %get-tuple-element.13), channel_id=1, source_target_pairs={{8,0},{16,8},{24,16},{32,24},{40,32},{48,40},{56,48},{64,56},{72,6... | collective-permute-start | bytes 393224 | tf_op jit(solution)/shard_map/ppermute | solution.py:26
  177.5 7.0 %collective-permute-start.7 = (bf16[128,512]{1,0:T(8,128)(2,1)S(1)}, bf16[128,512]{1,0:T(8,128)(2,1)S(1)}, u32[]{:S(2)}, u32[]{:S(2)}) collective-permute-start(bf16[128,512]{1,0:T(8,128)(2,1)S(1)} %get-tuple-element.14), channel_id=1, source_target_pairs={{16,0},{24,8},{32,16},{40,24},{48,32},{56,40},{64,48},{72,56},{80,... | collective-permute-start | bytes 393224 | tf_op jit(solution)/shard_map/ppermute | solution.py:26
  179.4 9.9 %collective-permute-start.8 = (bf16[128,512]{1,0:T(8,128)(2,1)S(1)}, bf16[128,512]{1,0:T(8,128)(2,1)S(1)}, u32[]{:S(2)}, u32[]{:S(2)}) collective-permute-start(bf16[128,512]{1,0:T(8,128)(2,1)S(1)} %get-tuple-element.15), channel_id=1, source_target_pairs={{24,0},{32,8},{40,16},{48,24},{56,32},{64,40},{72,48},{80,56},{88,... | collective-permute-start | bytes 393224 | tf_op jit(solution)/shard_map/ppermute | solution.py:26
Sparse Core Ops, SparseCore 0:
  10.1 91.5 all-gather.1

commit v2 on v1

--- a/solution.py
+++ b/solution.py
@@ -5,7 +5,7 @@
 from jax import lax
 from jax.experimental import pallas as pl
 from jax.experimental.pallas import tpu as pltpu
-from jax.sharding import PartitionSpec as P
+from jax.sharding import Mesh, PartitionSpec as P
 
 KEY_HEADS = 4
 GROUP_WIDTH = 8
@@ -16,14 +16,15 @@
 GROUP_COLUMNS = GROUP_WIDTH * HEAD_SIZE
 SPAN_ROWS = (SPAN + 1) * BLOCK
 
+DP = ("x", "z", "c")
 masked_value = -1e30
 NT = (((1,), (1,)), ((), ()))
 
 
 def shift(block, distance):
-    devices = range(lax.axis_size("dp"))
+    devices = range(lax.axis_size(DP))
     route = [(i, i + distance) for i in devices if i + distance in devices]
-    return lax.ppermute(block, "dp", route)
+    return lax.ppermute(block, DP, route)
 
 
 def stacked(ref, pair):
@@ -133,53 +134,75 @@
     return total.astype(jnp.bfloat16)
 
 
-def sum_over_dp(partial):
-    size = lax.axis_size("dp")
-    rows, columns = partial.shape
-    each = rows // size
-    pieces = lax.all_to_all(partial, "dp", 0, 0, tiled=True).reshape(size, each, columns)
-    return jnp.sum(pieces.astype(jnp.float32), axis=0)
+def exchange_rows(rows):
+    columns = rows.shape[1]
+    quarter = columns // 4
+    copies = [rows[:, x * quarter : (x + 1) * quarter] for x in range(4) for c in range(2)]
+    copies = jnp.concatenate(copies, axis=0)
+    return lax.all_to_all(copies, ("x", "c"), 0, 0, tiled=True)
+
+
+def exchange_value_grad(value_grad):
+    half = value_grad.shape[1] // 2
+    copies = jnp.concatenate([value_grad[:, :half], value_grad[:, half:]] * 4, axis=0)
+    return lax.all_to_all(copies, ("x", "c"), 0, 0, tiled=True)
+
+
+def to_plane(piece):
+    route = []
+    for x in range(4):
+        for z in range(8):
+            for c in range(2):
+                for y in range(8):
+                    source = ((x * 8 + z) * 2 + c) * 8 + y
+                    target = (((y % 4) * 8 + z) * 2 + c) * 8 + 2 * x + y // 4
+                    route.append((source, target))
+    return lax.ppermute(piece, ("x", "z", "c", "y"), route)
+
+
+def whole_shard(piece):
+    rows, columns = piece.shape
+    copies = jnp.broadcast_to(piece[None], (32, rows, columns)).reshape(32 * rows, columns)
+    half = lax.all_to_all(copies, ("x", "z"), 0, 0, tiled=True)
+    other = lax.ppermute(half, "c", [(0, 1), (1, 0)])
+    first = lax.axis_index("c") == 0
+    return jnp.concatenate(
+        [jnp.where(first, half, other), jnp.where(first, other, half)], axis=1
+    )
 
 
 def per_device(queries, key_rows, out_grad, inputs, w_value, doc_pos):
     queries, keys, grads, rows = queries[0], key_rows[0], out_grad[0], inputs[0]
     key_span = span_of(keys)
-    w_whole = lax.all_gather(w_value, "fsdp", axis=0, tiled=True)
-    rows_here = lax.all_to_all(rows, "fsdp", 1, 0, tiled=True)
+    w_whole = lax.all_gather(w_value, "y", axis=0, tiled=True)
+    rows_here = exchange_rows(rows)
     weights, *value_parts = attention_weights(doc_pos, queries, grads, key_span)
-    value_grad = owed(value_parts)
-    fsdp_size = lax.axis_size("fsdp")
-    copies = jnp.broadcast_to(value_grad[None], (fsdp_size,) + value_grad.shape)
-    value_grads = lax.all_to_all(copies, "fsdp", 0, 0, tiled=True).reshape(-1, value_grad.shape[1])
-
+    value_grads = exchange_value_grad(owed(value_parts))
+    product = lax.dot_general(
+        rows_here, value_grads, (((0,), (0,)), ((), ())), preferred_element_type=jnp.float32
+    ).astype(jnp.bfloat16)
+
+    w_whole, product = lax.optimization_barrier((w_whole, product))
+    pieces = lax.all_to_all(product, ("y", "z"), 0, 0, tiled=True)
     values = jnp.dot(rows, w_whole, preferred_element_type=jnp.float32).astype(jnp.bfloat16)
     key_parts = key_gradient(weights, queries, grads, span_of(values))
+    pieces, key_parts = lax.optimization_barrier((pieces, key_parts))
+
     key_grad = owed(key_parts)
-
-    product = lax.dot_general(
-        rows_here, value_grads, (((0,), (0,)), ((), ())), preferred_element_type=jnp.float32
-    )
-    piece = sum_over_dp(product.astype(jnp.bfloat16))
-    dp_size = lax.axis_size("dp")
-    token_total = fsdp_size * dp_size * BLOCK
-    piece = (piece * (1.0 / math.sqrt(token_total))).astype(jnp.bfloat16)
-    copies = jnp.broadcast_to(piece[None], (dp_size,) + piece.shape).reshape(-1, piece.shape[1])
-    weight_grad = lax.all_to_all(copies, "dp", 0, 0, tiled=True)
+    pieces = pieces.reshape(64, -1, pieces.shape[1]).astype(jnp.float32)
+    token_total = lax.axis_size(("x", "z", "c", "y")) * BLOCK
+    piece = (jnp.sum(pieces, axis=0) * (1.0 / math.sqrt(token_total))).astype(jnp.bfloat16)
+    weight_grad = whole_shard(to_plane(piece))
     return (key_grad[None], weight_grad)
 
 
 def solution(mesh):
+    mesh = Mesh(mesh.devices.reshape(4, 8, 2, 8), ("x", "z", "c", "y"))
+    tokens = P("y", DP, None)
     return jax.shard_map(
         per_device,
         mesh=mesh,
-        in_specs=(
-            P("fsdp", "dp", None),
-            P("fsdp", "dp", None),
-            P("fsdp", "dp", None),
-            P("fsdp", "dp", None),
-            P("fsdp", None),
-            P("fsdp", "dp"),
-        ),
-        out_specs=(P("fsdp", "dp", None), P("fsdp", None)),
+        in_specs=(tokens, tokens, tokens, tokens, P("y", None), P("y", DP)),
+        out_specs=(tokens, P("y", None)),
         check_vma=False,
     )

time: 199 us -> 184 us (0.925)
  the two profiles are of different devices: /device:TPU:7 before, /device:TPU:1 now
where the time goes in v2:
time: 184 us; the launch traced here: 181 us
  starting transfers between devices  73.9 us (40%)
  blocking collectives  30.8 us (17%)
  waiting for transfers between devices  28.5 us (15%)
  between operations  14.5 us (8%)
  local copies, waits for them, and re-layouts  13.9 us (8%)
  Pallas kernels  11.4 us (6%)
  matrix products  5.59 us (3%)
  other arithmetic  2.82 us (2%)
    ppermute x12, starting transfers between devices, shift(): return lax.ppermute(block, DP, route)  35.4 us
    all_to_all x1, blocking collectives, exchange_rows(): return lax.all_to_all(copies, ('x', 'c'), 0, 0, tiled=True)  30.8 us
    ppermute x12, waiting for transfers between devices, shift(): return lax.ppermute(block, DP, route)  20.7 us
    all_to_all x1, starting transfers between devices, whole_shard(): half = lax.all_to_all(copies, ('x', 'z'), 0, 0, tiled=True)  14 us
    all_to_all x1, starting transfers between devices, per_device(): pieces = lax.all_to_all(product, ('y', 'z'), 0, 0, tiled=True)  12.2 us
    unnamed x32, local copies, waits for them, and re-layouts  8.5 us
    ppermute x1, starting transfers between devices, whole_shard(): other = lax.ppermute(half, 'c', [(0, 1), (1, 0)])  6.35 us
    pallas_call x1, Pallas kernels, attention_weights(): pl.pallas_call(weights_kernel, grid=(KEY_HEADS,), in_specs=[pl.BlockSpec(...  6.09 us
  transfers between devices with their start and end apart: 18, of which 9 were waited for; matrix products, arithmetic and copies ran while one was open for 9% of the time, Pallas kernels for 6%

profile of v2, /device:TPU:1, one launch (start us, length us, event | category | flops | bytes accessed | tf_op | source)
XLA Modules:
  0.0 181.5 jit_solution(16009033145415430183)
XLA Ops:
  7.9 7.2 %collective-permute-start = (bf16[128,512]{1,0:T(8,128)(2,1)}, bf16[128,512]{1,0:T(8,128)(2,1)S(1)}, u32[]{:S(2)}, u32[]{:S(2)}) collective-permute-start(bf16[128,512]{1,0:T(8,128)(2,1)} %bitcast.30), channel_id=1, source_target_pairs={{0,24},{8,32},{16,40},{24,48},{32,56},{40,64},{48,72},{56,80},{64,... | collective-permute-start | bytes 393224 | tf_op jit(solution)/shard_map/ppermute | solution.py:27
  15.1 4.0 %collective-permute-start.1 = (bf16[128,512]{1,0:T(8,128)(2,1)}, bf16[128,512]{1,0:T(8,128)(2,1)S(1)}, u32[]{:S(2)}, u32[]{:S(2)}) collective-permute-start(bf16[128,512]{1,0:T(8,128)(2,1)} %bitcast.31), channel_id=1, source_target_pairs={{0,16},{8,24},{16,32},{24,40},{32,48},{40,56},{48,64},{56,72},{64,... | collective-permute-start | bytes 393224 | tf_op jit(solution)/shard_map/ppermute | solution.py:27
  19.2 2.2 %collective-permute-start.2 = (bf16[128,512]{1,0:T(8,128)(2,1)}, bf16[128,512]{1,0:T(8,128)(2,1)S(1)}, u32[]{:S(2)}, u32[]{:S(2)}) collective-permute-start(bf16[128,512]{1,0:T(8,128)(2,1)} %bitcast.32), channel_id=1, source_target_pairs={{0,8},{8,16},{16,24},{24,32},{32,40},{40,48},{48,56},{56,64},{64,7... | collective-permute-start | bytes 393224 | tf_op jit(solution)/shard_map/ppermute | solution.py:27
  26.3 6.1 %attention_weights.1 = (bf16[4,512,1024]{2,1,0:T(8,128)(2,1)S(1)}, bf16[128,512]{1,0:T(8,128)(2,1)S(1)}, bf16[128,512]{1,0:T(8,128)(2,1)S(1)}, bf16[128,512]{1,0:T(8,128)(2,1)S(1)}, f32[128,512]{1,0:T(8,128)S(1)}) custom-call(s32[1,128]{1,0:T(1,128)S(1)} %copy-done.3, bf16[128,4096]{1,0:T(8,128)(2,1)S(1)} %bitcast.26, bf16[128,4096]{1,0:T(8,128)(2,1)S(1)} %bitcast.28, ...), custom_call_target="tpu_custom_call" | custom-call | flops 2147483648 | bytes 8388608 | tf_op jit(solution)/shard_map/attention_weights/pallas_call | solution.py:96
  32.4 2.0 %copy-done.4 = bf16[4,512,1024]{2,1,0:T(8,128)(2,1)} copy-done((bf16[4,512,1024]{2,1,0:T(8,128)(2,1)}, bf16[4,512,1024]{2,1,0:T(8,128)(2,1)S(1)}, u32[]{:S(2)}) %copy-start.4) | copy-done | bytes 4194328
  34.4 2.1 %collective-permute-start.3 = (bf16[128,512]{1,0:T(8,128)(2,1)S(1)}, bf16[128,512]{1,0:T(8,128)(2,1)S(1)}, u32[]{:S(2)}, u32[]{:S(2)}) collective-permute-start(bf16[128,512]{1,0:T(8,128)(2,1)S(1)} %get-tuple-element.19), channel_id=1, source_target_pairs={{8,0},{16,8},{24,16},{32,24},{40,32},{48,40},{56,48},{64,56},{72,6... | collective-permute-start | bytes 393224 | tf_op jit(solution)/shard_map/ppermute | solution.py:27
  36.6 1.3 collective-permute-start.4
  37.9 1.3 collective-permute-start.5
  39.2 3.6 %collective-permute-done.3 = bf16[128,512]{1,0:T(8,128)(2,1)S(1)} collective-permute-done((bf16[128,512]{1,0:T(8,128)(2,1)S(1)}, bf16[128,512]{1,0:T(8,128)(2,1)S(1)}, u32[]{:S(2)}, u32[]{:S(2)}) %collective-permute-start.3) | collective-permute-done | bytes 131104 | tf_op jit(solution)/shard_map/ppermute | solution.py:27
  42.8 2.9 %collective-permute-done.4 = bf16[128,512]{1,0:T(8,128)(2,1)S(1)} collective-permute-done((bf16[128,512]{1,0:T(8,128)(2,1)S(1)}, bf16[128,512]{1,0:T(8,128)(2,1)S(1)}, u32[]{:S(2)}, u32[]{:S(2)}) %collective-permute-start.4) | collective-permute-done | bytes 131104 | tf_op jit(solution)/shard_map/ppermute | solution.py:27
  45.7 5.4 %collective-permute-done.5 = bf16[128,512]{1,0:T(8,128)(2,1)S(1)} collective-permute-done((bf16[128,512]{1,0:T(8,128)(2,1)S(1)}, bf16[128,512]{1,0:T(8,128)(2,1)S(1)}, u32[]{:S(2)}, u32[]{:S(2)}) %collective-permute-start.5) | collective-permute-done | bytes 131104 | tf_op jit(solution)/shard_map/ppermute | solution.py:27
  52.1 5.3 %all-to-all-start.1 = ((bf16[8,128,256]{2,1,0:T(8,128)(2,1)}), bf16[8,128,256]{2,1,0:T(8,128)(2,1)}, u32[]{:S(2)}, u32[]{:S(2)}) async-start(bf16[8,128,256]{2,1,0:T(8,128)(2,1)} %bitcast.44), calls=%async_computation.1 | async-start | bytes 1048576 | tf_op jit(solution)/shard_map/all_to_all | solution.py:148
  58.9 4.0 %copy.9 = bf16[8,128,1024]{1,2,0:T(8,128)(2,1)} copy(bf16[8,128,1024]{2,1,0:T(8,128)(2,1)} %bitcast.42) | data formatting | bytes 4194304 | tf_op jit(solution)/shard_map/all_to_all | solution.py:142
  62.8 4.1 %all-to-all-done.1 = bf16[8,128,256]{2,1,0:T(8,128)(2,1)} async-done(((bf16[8,128,256]{2,1,0:T(8,128)(2,1)}), bf16[8,128,256]{2,1,0:T(8,128)(2,1)}, u32[]{:S(2)}, u32[]{:S(2)}) %all-to-all-start.1) | async-done | bytes 524320 | tf_op jit(solution)/shard_map/all_to_all | solution.py:148
  66.9 30.8 %all_to_all.39 = bf16[8,128,1024]{1,2,0:T(8,128)(2,1)S(1)} all-to-all(bf16[8,128,1024]{1,2,0:T(8,128)(2,1)} %copy.9), channel_id=1, replica_groups=mesh['x'=4,'z'=8,'c'=2,'y'=8] {'x','c'}, dimensions={0} | all-to-all | bytes 4194304 | tf_op jit(solution)/shard_map/all_to_all | solution.py:142
  97.8 2.5 %fusion = bf16[1024,256]{1,0:T(8,128)(2,1)} fusion(bf16[8,128,1024]{1,2,0:T(8,128)(2,1)S(1)} %all_to_all.39, bf16[8,128,256]{2,1,0:T(8,128)(2,1)} %all-to-all-done.1), kind=kOutput, calls=%fused_computation.1 | convolution fusion | flops 537133056 | bytes 3145728 | tf_op jit(solution)/shard_map/dot_general | solution.py:181
  100.3 12.2 %all-to-all-start.2 = ((bf16[64,16,256]{2,1,0:T(8,128)(2,1)}), bf16[64,16,256]{2,1,0:T(8,128)(2,1)}, u32[]{:S(2)}, u32[]{:S(2)}) async-start(bf16[64,16,256]{2,1,0:T(8,128)(2,1)} %bitcast.45), calls=%async_computation.2 | async-start | bytes 1048576 | tf_op jit(solution)/shard_map/all_to_all | solution.py:186
  112.5 3.1 %fusion.1.v3_ref = bf16[128,512]{1,0:T(8,128)(2,1)S(1)} fusion(bf16[4096,512]{1,0:T(8,128)(2,1)} %all-gather.2.cloned.1.call-done, bf16[1,128,4096]{2,1,0:T(8,128)(2,1)S(1)} %copy-done.6), kind=kOutput, calls=%fused_computation.3 | convolution fusion | flops 536936448 | bytes 5373952 | tf_op jit(solution)/shard_map/dot_general | solution.py:187
  115.6 5.2 %collective-permute-start.6 = (bf16[128,512]{1,0:T(8,128)(2,1)S(1)}, bf16[128,512]{1,0:T(8,128)(2,1)S(1)}, u32[]{:S(2)}, u32[]{:S(2)}) collective-permute-start(bf16[128,512]{1,0:T(8,128)(2,1)S(1)} %fusion.1.v3_ref), channel_id=1, source_target_pairs={{0,24},{8,32},{16,40},{24,48},{32,56},{40,64},{48,72},{56,80},{64,... | collective-permute-start | bytes 393224 | tf_op jit(solution)/shard_map/ppermute | solution.py:27
  120.8 3.1 %collective-permute-start.7 = (bf16[128,512]{1,0:T(8,128)(2,1)S(1)}, bf16[128,512]{1,0:T(8,128)(2,1)S(1)}, u32[]{:S(2)}, u32[]{:S(2)}) collective-permute-start(bf16[128,512]{1,0:T(8,128)(2,1)S(1)} %fusion.1.v3_ref), channel_id=1, source_target_pairs={{0,16},{8,24},{16,32},{24,40},{32,48},{40,56},{48,64},{56,72},{64,... | collective-permute-start | bytes 393224 | tf_op jit(solution)/shard_map/ppermute | solution.py:27
  123.9 1.9 %collective-permute-start.8 = (bf16[128,512]{1,0:T(8,128)(2,1)S(1)}, bf16[128,512]{1,0:T(8,128)(2,1)S(1)}, u32[]{:S(2)}, u32[]{:S(2)}) collective-permute-start(bf16[128,512]{1,0:T(8,128)(2,1)S(1)} %fusion.1.v3_ref), channel_id=1, source_target_pairs={{0,8},{8,16},{16,24},{24,32},{32,40},{40,48},{48,56},{56,64},{64,7... | collective-permute-start | bytes 393224 | tf_op jit(solution)/shard_map/ppermute | solution.py:27
  125.9 3.8 %collective-permute-done.6.v0_ref = bf16[128,512]{1,0:T(8,128)(2,1)S(1)} collective-permute-done((bf16[128,512]{1,0:T(8,128)(2,1)S(1)}, bf16[128,512]{1,0:T(8,128)(2,1)S(1)}, u32[]{:S(2)}, u32[]{:S(2)}) %collective-permute-start.6) | collective-permute-done | bytes 131104 | tf_op jit(solution)/shard_map/ppermute | solution.py:27
  129.7 3.6 %collective-permute-done.7.v1_ref = bf16[128,512]{1,0:T(8,128)(2,1)S(1)} collective-permute-done((bf16[128,512]{1,0:T(8,128)(2,1)S(1)}, bf16[128,512]{1,0:T(8,128)(2,1)S(1)}, u32[]{:S(2)}, u32[]{:S(2)}) %collective-permute-start.7) | collective-permute-done | bytes 131104 | tf_op jit(solution)/shard_map/ppermute | solution.py:27
  133.2 1.4 collective-permute-done.8.v2_ref
  134.6 5.3 %key_gradient.1 = (bf16[128,512]{1,0:T(8,128)(2,1)S(1)}, bf16[128,512]{1,0:T(8,128)(2,1)S(1)}, bf16[128,512]{1,0:T(8,128)(2,1)S(1)}, f32[128,512]{1,0:T(8,128)S(1)}) custom-call(bf16[4,512,1024]{2,1,0:T(8,128)(2,1)S(1)} %copy-done.5, bf16[128,4096]{1,0:T(8,128)(2,1)S(1)} %bitcast.27, bf16[128,4096]{1,0:T(8,128)(2,1)S(1)} %bitcast.29, ...), custom_call_target="tpu_custom_call" | custom-call | flops 2147483648 | bytes 8388608 | tf_op jit(solution)/shard_map/key_gradient/pallas_call | solution.py:112
  140.0 1.1 convert_reduce_fusion
  142.5 14.0 %all-to-all-start.3 = ((bf16[32,16,256]{2,1,0:T(8,128)(2,1)}), bf16[32,16,256]{2,1,0:T(8,128)(2,1)S(1)}, u32[]{:S(2)}, u32[]{:S(2)}) async-start(bf16[32,16,256]{2,1,0:T(8,128)(2,1)} %broadcast_in_dim.10), calls=%async_computation.3 | async-start | bytes 524288 | tf_op jit(solution)/shard_map/all_to_all | solution.py:166
  156.5 1.3 collective-permute-start.10
  157.8 1.3 collective-permute-start.11
  159.1 4.5 %collective-permute-start.9 = (bf16[128,512]{1,0:T(8,128)(2,1)S(1)}, bf16[128,512]{1,0:T(8,128)(2,1)S(1)}, u32[]{:S(2)}, u32[]{:S(2)}) collective-permute-start(bf16[128,512]{1,0:T(8,128)(2,1)S(1)} %get-tuple-element.30), channel_id=1, source_target_pairs={{8,0},{16,8},{24,16},{32,24},{40,32},{48,40},{56,48},{64,56},{72,6... | collective-permute-start | bytes 393224 | tf_op jit(solution)/shard_map/ppermute | solution.py:27
  163.6 2.6 %all-to-all-done.3 = bf16[32,16,256]{2,1,0:T(8,128)(2,1)S(1)} async-done(((bf16[32,16,256]{2,1,0:T(8,128)(2,1)}), bf16[32,16,256]{2,1,0:T(8,128)(2,1)S(1)}, u32[]{:S(2)}, u32[]{:S(2)}) %all-to-all-start.3) | async-done | bytes 262176 | tf_op jit(solution)/shard_map/all_to_all | solution.py:166
  166.2 6.4 %collective-permute-start.13 = (bf16[512,256]{1,0:T(8,128)(2,1)S(1)}, bf16[512,256]{1,0:T(8,128)(2,1)S(1)}, u32[]{:S(2)}, u32[]{:S(2)}) collective-permute-start(bf16[512,256]{1,0:T(8,128)(2,1)S(1)} %bitcast.43), channel_id=1, source_target_pairs={{0,8},{8,0},{1,9},{9,1},{2,10},{10,2},{3,11},{11,3},{4,12},{12,4},... | collective-permute-start | bytes 786440 | tf_op jit(solution)/shard_map/ppermute | solution.py:167
  (52 shorter events, 11.4 us)
Async XLA Ops:
  7.2 19.1 %copy-start.2 = (bf16[1,128,512]{2,1,0:T(8,128)(2,1)S(1)}, bf16[1,128,512]{2,1,0:T(8,128)(2,1)}, u32[]{:S(2)}) copy-start(bf16[1,128,512]{2,1,0:T(8,128)(2,1)} %param.7) | copy-start | bytes 393220
  7.2 19.1 %copy-start = (bf16[1,128,4096]{2,1,0:T(8,128)(2,1)S(1)}, bf16[1,128,4096]{2,1,0:T(8,128)(2,1)}, u32[]{:S(2)}) copy-start(bf16[1,128,4096]{2,1,0:T(8,128)(2,1)} %param.6) | copy-start | bytes 3145732
  7.2 19.1 %copy-start.1 = (bf16[1,128,4096]{2,1,0:T(8,128)(2,1)S(1)}, bf16[1,128,4096]{2,1,0:T(8,128)(2,1)}, u32[]{:S(2)}) copy-start(bf16[1,128,4096]{2,1,0:T(8,128)(2,1)} %param.8) | copy-start | bytes 3145732
  7.2 19.1 %copy-start.3 = (s32[1,128]{1,0:T(1,128)S(1)}, s32[1,128]{1,0:T(1,128)}, u32[]{:S(2)}) copy-start(s32[1,128]{1,0:T(1,128)} %position_ref.1) | copy-start | bytes 1540
  7.2 93.1 %all-gather.2.cloned.1.call-start = ((), (), s32[]{:S(2)}) async-start(), calls=%async_computation.4 | async-start | bytes 4718592 | tf_op jit(solution)/shard_map/all_gather | solution.py:177
  7.9 18.3 %collective-permute-start = (bf16[128,512]{1,0:T(8,128)(2,1)}, bf16[128,512]{1,0:T(8,128)(2,1)S(1)}, u32[]{:S(2)}, u32[]{:S(2)}) collective-permute-start(bf16[128,512]{1,0:T(8,128)(2,1)} %bitcast.30), channel_id=1, source_target_pairs={{0,24},{8,32},{16,40},{24,48},{32,56},{40,64},{48,72},{56,80},{64,... | collective-permute-start | bytes 393224 | tf_op jit(solution)/shard_map/ppermute | solution.py:27
  15.1 11.1 %collective-permute-start.1 = (bf16[128,512]{1,0:T(8,128)(2,1)}, bf16[128,512]{1,0:T(8,128)(2,1)S(1)}, u32[]{:S(2)}, u32[]{:S(2)}) collective-permute-start(bf16[128,512]{1,0:T(8,128)(2,1)} %bitcast.31), channel_id=1, source_target_pairs={{0,16},{8,24},{16,32},{24,40},{32,48},{40,56},{48,64},{56,72},{64,... | collective-permute-start | bytes 393224 | tf_op jit(solution)/shard_map/ppermute | solution.py:27
  19.2 7.1 %collective-permute-start.2 = (bf16[128,512]{1,0:T(8,128)(2,1)}, bf16[128,512]{1,0:T(8,128)(2,1)S(1)}, u32[]{:S(2)}, u32[]{:S(2)}) collective-permute-start(bf16[128,512]{1,0:T(8,128)(2,1)} %bitcast.32), channel_id=1, source_target_pairs={{0,8},{8,16},{16,24},{24,32},{32,40},{40,48},{48,56},{56,64},{64,7... | collective-permute-start | bytes 393224 | tf_op jit(solution)/shard_map/ppermute | solution.py:27
  26.3 12.9 %copy-start.6 = (bf16[1,128,4096]{2,1,0:T(8,128)(2,1)S(1)}, bf16[1,128,4096]{2,1,0:T(8,128)(2,1)}, u32[]{:S(2)}) copy-start(bf16[1,128,4096]{2,1,0:T(8,128)(2,1)} %param.9) | copy-start | bytes 3145732
  32.4 2.0 %copy-start.4 = (bf16[4,512,1024]{2,1,0:T(8,128)(2,1)}, bf16[4,512,1024]{2,1,0:T(8,128)(2,1)S(1)}, u32[]{:S(2)}) copy-start(bf16[4,512,1024]{2,1,0:T(8,128)(2,1)S(1)} %get-tuple-element.23.weights_ref) | copy-start | bytes 12582916
  34.4 8.4 %collective-permute-start.3 = (bf16[128,512]{1,0:T(8,128)(2,1)S(1)}, bf16[128,512]{1,0:T(8,128)(2,1)S(1)}, u32[]{:S(2)}, u32[]{:S(2)}) collective-permute-start(bf16[128,512]{1,0:T(8,128)(2,1)S(1)} %get-tuple-element.19), channel_id=1, source_target_pairs={{8,0},{16,8},{24,16},{32,24},{40,32},{48,40},{56,48},{64,56},{72,6... | collective-permute-start | bytes 393224 | tf_op jit(solution)/shard_map/ppermute | solution.py:27
  36.6 9.2 %collective-permute-start.4 = (bf16[128,512]{1,0:T(8,128)(2,1)S(1)}, bf16[128,512]{1,0:T(8,128)(2,1)S(1)}, u32[]{:S(2)}, u32[]{:S(2)}) collective-permute-start(bf16[128,512]{1,0:T(8,128)(2,1)S(1)} %get-tuple-element.20), channel_id=1, source_target_pairs={{16,0},{24,8},{32,16},{40,24},{48,32},{56,40},{64,48},{72,56},{80,... | collective-permute-start | bytes 393224 | tf_op jit(solution)/shard_map/ppermute | solution.py:27
  37.9 13.2 %collective-permute-start.5 = (bf16[128,512]{1,0:T(8,128)(2,1)S(1)}, bf16[128,512]{1,0:T(8,128)(2,1)S(1)}, u32[]{:S(2)}, u32[]{:S(2)}) collective-permute-start(bf16[128,512]{1,0:T(8,128)(2,1)S(1)} %get-tuple-element.21), channel_id=1, source_target_pairs={{24,0},{32,8},{40,16},{48,24},{56,32},{64,40},{72,48},{80,56},{88,... | collective-permute-start | bytes 393224 | tf_op jit(solution)/shard_map/ppermute | solution.py:27
  39.2 12.1 %copy-start.7 = (bf16[1024,1024]{1,0:T(8,128)(2,1)}, bf16[1024,1024]{1,0:T(8,128)(2,1)S(1)}, u32[]{:S(2)}) copy-start(bf16[1024,1024]{1,0:T(8,128)(2,1)S(1)} %slice_dynamic-update-slice_fusion.3) | copy-start | bytes 6291460
  51.3 0.8 copy-start.8
  52.1 14.8 %all-to-all-start.1 = ((bf16[8,128,256]{2,1,0:T(8,128)(2,1)}), bf16[8,128,256]{2,1,0:T(8,128)(2,1)}, u32[]{:S(2)}, u32[]{:S(2)}) async-start(bf16[8,128,256]{2,1,0:T(8,128)(2,1)} %bitcast.44), calls=%async_computation.1 | async-start | bytes 1048576 | tf_op jit(solution)/shard_map/all_to_all | solution.py:148
  100.3 39.7 %all-to-all-start.2 = ((bf16[64,16,256]{2,1,0:T(8,128)(2,1)}), bf16[64,16,256]{2,1,0:T(8,128)(2,1)}, u32[]{:S(2)}, u32[]{:S(2)}) async-start(bf16[64,16,256]{2,1,0:T(8,128)(2,1)} %bitcast.45), calls=%async_computation.2 | async-start | bytes 1048576 | tf_op jit(solution)/shard_map/all_to_all | solution.py:186
  112.5 22.1 %copy-start.5 = (bf16[4,512,1024]{2,1,0:T(8,128)(2,1)S(1)}, bf16[4,512,1024]{2,1,0:T(8,128)(2,1)}, u32[]{:S(2)}) copy-start(bf16[4,512,1024]{2,1,0:T(8,128)(2,1)} %copy-done.4) | copy-start | bytes 12582916
  115.6 14.0 %collective-permute-start.6 = (bf16[128,512]{1,0:T(8,128)(2,1)S(1)}, bf16[128,512]{1,0:T(8,128)(2,1)S(1)}, u32[]{:S(2)}, u32[]{:S(2)}) collective-permute-start(bf16[128,512]{1,0:T(8,128)(2,1)S(1)} %fusion.1.v3_ref), channel_id=1, source_target_pairs={{0,24},{8,32},{16,40},{24,48},{32,56},{40,64},{48,72},{56,80},{64,... | collective-permute-start | bytes 393224 | tf_op jit(solution)/shard_map/ppermute | solution.py:27
  120.8 12.4 %collective-permute-start.7 = (bf16[128,512]{1,0:T(8,128)(2,1)S(1)}, bf16[128,512]{1,0:T(8,128)(2,1)S(1)}, u32[]{:S(2)}, u32[]{:S(2)}) collective-permute-start(bf16[128,512]{1,0:T(8,128)(2,1)S(1)} %fusion.1.v3_ref), channel_id=1, source_target_pairs={{0,16},{8,24},{16,32},{24,40},{32,48},{40,56},{48,64},{56,72},{64,... | collective-permute-start | bytes 393224 | tf_op jit(solution)/shard_map/ppermute | solution.py:27
  123.9 10.7 %collective-permute-start.8 = (bf16[128,512]{1,0:T(8,128)(2,1)S(1)}, bf16[128,512]{1,0:T(8,128)(2,1)S(1)}, u32[]{:S(2)}, u32[]{:S(2)}) collective-permute-start(bf16[128,512]{1,0:T(8,128)(2,1)S(1)} %fusion.1.v3_ref), channel_id=1, source_target_pairs={{0,8},{8,16},{16,24},{24,32},{32,40},{40,48},{48,56},{56,64},{64,7... | collective-permute-start | bytes 393224 | tf_op jit(solution)/shard_map/ppermute | solution.py:27
  141.1 0.7 collective-permute-start.12
  142.5 23.7 %all-to-all-start.3 = ((bf16[32,16,256]{2,1,0:T(8,128)(2,1)}), bf16[32,16,256]{2,1,0:T(8,128)(2,1)S(1)}, u32[]{:S(2)}, u32[]{:S(2)}) async-start(bf16[32,16,256]{2,1,0:T(8,128)(2,1)} %broadcast_in_dim.10), calls=%async_computation.3 | async-start | bytes 524288 | tf_op jit(solution)/shard_map/all_to_all | solution.py:166
  156.5 16.1 %collective-permute-start.10 = (bf16[128,512]{1,0:T(8,128)(2,1)S(1)}, bf16[128,512]{1,0:T(8,128)(2,1)S(1)}, u32[]{:S(2)}, u32[]{:S(2)}) collective-permute-start(bf16[128,512]{1,0:T(8,128)(2,1)S(1)} %get-tuple-element.31), channel_id=1, source_target_pairs={{16,0},{24,8},{32,16},{40,24},{48,32},{56,40},{64,48},{72,56},{80,... | collective-permute-start | bytes 393224 | tf_op jit(solution)/shard_map/ppermute | solution.py:27
  157.8 14.8 %collective-permute-start.11 = (bf16[128,512]{1,0:T(8,128)(2,1)S(1)}, bf16[128,512]{1,0:T(8,128)(2,1)S(1)}, u32[]{:S(2)}, u32[]{:S(2)}) collective-permute-start(bf16[128,512]{1,0:T(8,128)(2,1)S(1)} %get-tuple-element.32), channel_id=1, source_target_pairs={{24,0},{32,8},{40,16},{48,24},{56,32},{64,40},{72,48},{80,56},{88,... | collective-permute-start | bytes 393224 | tf_op jit(solution)/shard_map/ppermute | solution.py:27
  159.1 13.5 %collective-permute-start.9 = (bf16[128,512]{1,0:T(8,128)(2,1)S(1)}, bf16[128,512]{1,0:T(8,128)(2,1)S(1)}, u32[]{:S(2)}, u32[]{:S(2)}) collective-permute-start(bf16[128,512]{1,0:T(8,128)(2,1)S(1)} %get-tuple-element.30), channel_id=1, source_target_pairs={{8,0},{16,8},{24,16},{32,24},{40,32},{48,40},{56,48},{64,56},{72,6... | collective-permute-start | bytes 393224 | tf_op jit(solution)/shard_map/ppermute | solution.py:27
  166.2 7.5 %collective-permute-start.13 = (bf16[512,256]{1,0:T(8,128)(2,1)S(1)}, bf16[512,256]{1,0:T(8,128)(2,1)S(1)}, u32[]{:S(2)}, u32[]{:S(2)}) collective-permute-start(bf16[512,256]{1,0:T(8,128)(2,1)S(1)} %bitcast.43), channel_id=1, source_target_pairs={{0,8},{8,0},{1,9},{9,1},{2,10},{10,2},{3,11},{11,3},{4,12},{12,4},... | collective-permute-start | bytes 786440 | tf_op jit(solution)/shard_map/ppermute | solution.py:167
Sparse Core Ops, SparseCore 0:
  10.1 62.6 all-gather.1

commit v3 on v2

--- a/solution.py
+++ b/solution.py
@@ -134,21 +134,115 @@
     return total.astype(jnp.bfloat16)
 
 
+OTHER_CORE = [(0, 1), (1, 0)]
+QUARTER = 1024
+HALF = 256
+
+
+def quarters_kernel(rows_ref, out_ref):
+    out_ref[...] = rows_ref[...]
+
+
+def partial_values_kernel(core_ref, near_ref, far_ref, weight_ref, out_ref):
+    block = pl.program_id(0)
+    for rows_ref, core in ((near_ref, core_ref[0]), (far_ref, 1 - core_ref[0])):
+        values = jnp.dot(rows_ref[...], weight_ref[...], preferred_element_type=jnp.float32)
+        out_ref[pl.ds(pl.multiple_of((2 * block + core) * BLOCK, BLOCK), BLOCK), :] = values.astype(
+            jnp.bfloat16
+        )
+
+
+def pack_kernel(own_ref, one_ref, two_ref, three_ref, values_ref, out_ref):
+    total = own_ref[...] + one_ref[...].astype(jnp.float32)
+    total = total + two_ref[...].astype(jnp.float32) + three_ref[...].astype(jnp.float32)
+    low = total.astype(jnp.bfloat16)
+    for device in range(8):
+        core = device % 2
+        rows = slice(device * BLOCK, (device + 1) * BLOCK)
+        out_ref[rows, :HALF] = low[:, core * HALF : (core + 1) * HALF]
+        out_ref[rows, HALF:] = values_ref[rows, :]
+
+
+def product_kernel(core_ref, near_ref, far_ref, grads_ref, out_ref):
+    total = None
+    for rows_ref, core in ((near_ref, core_ref[0]), (far_ref, 1 - core_ref[0])):
+        grads = [
+            grads_ref[pl.ds(pl.multiple_of((2 * x + core) * BLOCK, BLOCK), BLOCK), :HALF]
+            for x in range(4)
+        ]
+        part = lax.dot_general(
+            rows_ref[...],
+            jnp.concatenate(grads, axis=0),
+            (((0,), (0,)), ((), ())),
+            preferred_element_type=jnp.float32,
+        )
+        total = part if total is None else total + part
+    out_ref[...] = total.astype(jnp.bfloat16)
+
+
 def exchange_rows(rows):
-    columns = rows.shape[1]
-    quarter = columns // 4
-    copies = [rows[:, x * quarter : (x + 1) * quarter] for x in range(4) for c in range(2)]
-    copies = jnp.concatenate(copies, axis=0)
-    return lax.all_to_all(copies, ("x", "c"), 0, 0, tiled=True)
-
-
-def exchange_value_grad(value_grad):
-    half = value_grad.shape[1] // 2
-    copies = jnp.concatenate([value_grad[:, :half], value_grad[:, half:]] * 4, axis=0)
-    return lax.all_to_all(copies, ("x", "c"), 0, 0, tiled=True)
-
-
-def to_plane(piece):
+    quarters = pl.pallas_call(
+        quarters_kernel,
+        grid=(4,),
+        in_specs=[pl.BlockSpec((BLOCK, QUARTER), lambda x: (0, x))],
+        out_specs=pl.BlockSpec((BLOCK, QUARTER), lambda x: (x, 0)),
+        out_shape=jax.ShapeDtypeStruct((4 * BLOCK, QUARTER), jnp.bfloat16),
+        name="quarters",
+    )(rows)
+    near = lax.all_to_all(quarters, "x", 0, 0, tiled=True)
+    return near, lax.ppermute(near, "c", OTHER_CORE)
+
+
+def exchange_projection(w_value):
+    route = [(target, source) for source, target in plane_route()]
+    start = (lax.axis_index("x") * BLOCK, lax.axis_index("c") * HALF)
+    piece = lax.dynamic_slice(w_value, start, (BLOCK, HALF))
+    piece = lax.ppermute(piece, ("x", "z", "c", "y"), route)
+    copies = jnp.broadcast_to(piece[None], (8, BLOCK, HALF)).reshape(8 * BLOCK, HALF)
+    return lax.all_to_all(copies, "y", 0, 0, tiled=True)
+
+
+def partial_values(core, near, far, weight):
+    rows = pl.BlockSpec((BLOCK, QUARTER), lambda x, core: (x, 0))
+    return pl.pallas_call(
+        partial_values_kernel,
+        grid_spec=pltpu.PrefetchScalarGridSpec(
+            num_scalar_prefetch=1,
+            grid=(4,),
+            in_specs=[rows, rows, pl.BlockSpec((QUARTER, HALF), lambda x, core: (0, 0))],
+            out_specs=pl.BlockSpec((8 * BLOCK, HALF), lambda x, core: (0, 0)),
+        ),
+        out_shape=jax.ShapeDtypeStruct((8 * BLOCK, HALF), jnp.bfloat16),
+        name="partial_values",
+    )(core, near, far, weight)
+
+
+def exchange_packed(value_parts, values):
+    received = [shift(value_parts[SPAN - distance], -distance) for distance in (1, 2, 3)]
+    packed = pl.pallas_call(
+        pack_kernel,
+        out_shape=jax.ShapeDtypeStruct((8 * BLOCK, 2 * HALF), jnp.bfloat16),
+        name="pack",
+    )(value_parts[SPAN], *received, values)
+    return lax.all_to_all(packed, ("x", "c"), 0, 0, tiled=True)
+
+
+def group_product(core, near, far, packed):
+    rows = pl.BlockSpec((4 * BLOCK, HALF), lambda part, core: (0, part))
+    return pl.pallas_call(
+        product_kernel,
+        grid_spec=pltpu.PrefetchScalarGridSpec(
+            num_scalar_prefetch=1,
+            grid=(QUARTER // HALF,),
+            in_specs=[rows, rows, pl.BlockSpec((8 * BLOCK, 2 * HALF), lambda part, core: (0, 0))],
+            out_specs=pl.BlockSpec((HALF, HALF), lambda part, core: (part, 0)),
+        ),
+        out_shape=jax.ShapeDtypeStruct((QUARTER, HALF), jnp.bfloat16),
+        name="group_product",
+    )(core, near, far, packed)
+
+
+def plane_route():
     route = []
     for x in range(4):
         for z in range(8):
@@ -157,14 +251,14 @@
                     source = ((x * 8 + z) * 2 + c) * 8 + y
                     target = (((y % 4) * 8 + z) * 2 + c) * 8 + 2 * x + y // 4
                     route.append((source, target))
-    return lax.ppermute(piece, ("x", "z", "c", "y"), route)
+    return route
 
 
 def whole_shard(piece):
     rows, columns = piece.shape
     copies = jnp.broadcast_to(piece[None], (32, rows, columns)).reshape(32 * rows, columns)
     half = lax.all_to_all(copies, ("x", "z"), 0, 0, tiled=True)
-    other = lax.ppermute(half, "c", [(0, 1), (1, 0)])
+    other = lax.ppermute(half, "c", OTHER_CORE)
     first = lax.axis_index("c") == 0
     return jnp.concatenate(
         [jnp.where(first, half, other), jnp.where(first, other, half)], axis=1
@@ -173,26 +267,28 @@
 
 def per_device(queries, key_rows, out_grad, inputs, w_value, doc_pos):
     queries, keys, grads, rows = queries[0], key_rows[0], out_grad[0], inputs[0]
+    core = lax.axis_index("c").astype(jnp.int32).reshape(1)
     key_span = span_of(keys)
-    w_whole = lax.all_gather(w_value, "y", axis=0, tiled=True)
-    rows_here = exchange_rows(rows)
+    near, far = exchange_rows(rows)
+    weight = exchange_projection(w_value)
+    values = partial_values(core, near, far, weight)
     weights, *value_parts = attention_weights(doc_pos, queries, grads, key_span)
-    value_grads = exchange_value_grad(owed(value_parts))
-    product = lax.dot_general(
-        rows_here, value_grads, (((0,), (0,)), ((), ())), preferred_element_type=jnp.float32
-    ).astype(jnp.bfloat16)
-
-    w_whole, product = lax.optimization_barrier((w_whole, product))
+    packed = exchange_packed(value_parts, values)
+    product = group_product(core, near, far, packed)
     pieces = lax.all_to_all(product, ("y", "z"), 0, 0, tiled=True)
-    values = jnp.dot(rows, w_whole, preferred_element_type=jnp.float32).astype(jnp.bfloat16)
-    key_parts = key_gradient(weights, queries, grads, span_of(values))
-    pieces, key_parts = lax.optimization_barrier((pieces, key_parts))
-
+
+    parts = packed.reshape(4, 2, BLOCK, 2 * HALF)[..., HALF:].astype(jnp.float32)
+    values = jnp.sum(parts, axis=0).astype(jnp.bfloat16)
+    values = jnp.concatenate([values[0], values[1]], axis=1)
+    value_span = span_of(values)
+    pieces, value_span = lax.optimization_barrier((pieces, value_span))
+    key_parts = key_gradient(weights, queries, grads, value_span)
     key_grad = owed(key_parts)
-    pieces = pieces.reshape(64, -1, pieces.shape[1]).astype(jnp.float32)
+
+    pieces = pieces.reshape(64, -1, HALF).astype(jnp.float32)
     token_total = lax.axis_size(("x", "z", "c", "y")) * BLOCK
     piece = (jnp.sum(pieces, axis=0) * (1.0 / math.sqrt(token_total))).astype(jnp.bfloat16)
-    weight_grad = whole_shard(to_plane(piece))
+    weight_grad = whole_shard(lax.ppermute(piece, ("x", "z", "c", "y"), plane_route()))
     return (key_grad[None], weight_grad)
 
 

time: 184 us -> 193 us (1.049)
  the two profiles are of different devices: /device:TPU:1 before, /device:TPU:31 now
where the time goes in v3:
time: 193 us; the launch traced here: 192 us
  starting transfers between devices  88.3 us (46%)
  blocking collectives  37.8 us (20%)
  waiting for transfers between devices  26.9 us (14%)
  Pallas kernels  25.9 us (13%)
  local copies, waits for them, and re-layouts  8.73 us (5%)
  other arithmetic  2.84 us (1%)
    ppermute x12, starting transfers between devices, shift(): return lax.ppermute(block, DP, route)  46.4 us
    all_to_all x1, blocking collectives, exchange_packed(): return lax.all_to_all(packed, ('x', 'c'), 0, 0, tiled=True)  20.9 us
    ppermute x12, waiting for transfers between devices, shift(): return lax.ppermute(block, DP, route)  17.8 us
    all_to_all x1, blocking collectives, exchange_rows(): near = lax.all_to_all(quarters, 'x', 0, 0, tiled=True)  16.8 us
    all_to_all x1, starting transfers between devices, per_device(): pieces = lax.all_to_all(product, ('y', 'z'), 0, 0, tiled=True)  10.3 us
    all_to_all x1, starting transfers between devices, exchange_projection(): return lax.all_to_all(copies, 'y', 0, 0, tiled=True)  7.66 us
    ppermute x1, waiting for transfers between devices, per_device(): lax.ppermute(piece, ('x', 'z', 'c', 'y'), plane_route())  6.73 us
    all_to_all x1, starting transfers between devices, whole_shard(): half = lax.all_to_all(copies, ('x', 'z'), 0, 0, tiled=True)  6.47 us
  transfers between devices with their start and end apart: 19, of which 8 were waited for; matrix products, arithmetic and copies ran while one was open for 1% of the time, Pallas kernels for 8%

profile of v3, /device:TPU:31, one launch (start us, length us, event | category | flops | bytes accessed | tf_op | source)
XLA Modules:
  0.0 191.5 jit_solution(2097063253880272838)
XLA Ops:
  0.7 3.5 %quarters.1 = bf16[512,1024]{1,0:T(8,128)(2,1)} custom-call(bf16[128,4096]{1,0:T(8,128)(2,1)} %bitcast.38), custom_call_target="tpu_custom_call" | custom-call | tf_op jit(solution)/shard_map/quarters/pallas_call | solution.py:184
  4.2 16.8 %all_to_all.51 = bf16[4,128,1024]{2,1,0:T(8,128)(2,1)} all-to-all(bf16[4,128,1024]{2,1,0:T(8,128)(2,1)} %bitcast.35), channel_id=1, replica_groups=mesh['x'=4,'z'=8,'c'=2,'y'=8] {'x'}, dimensions={0} | all-to-all | bytes 2097152 | tf_op jit(solution)/shard_map/all_to_all | solution.py:192
  21.0 3.8 %collective-permute-start.3 = (bf16[512,1024]{1,0:T(8,128)(2,1)}, bf16[512,1024]{1,0:T(8,128)(2,1)}, u32[]{:S(2)}, u32[]{:S(2)}) collective-permute-start(bf16[512,1024]{1,0:T(8,128)(2,1)} %bitcast.6.near_ref), channel_id=1, source_target_pairs={{0,8},{8,0},{1,9},{9,1},{2,10},{10,2},{3,11},{11,3},{4,12},{12,4},... | collective-permute-start | bytes 3145736 | tf_op jit(solution)/shard_map/ppermute | solution.py:193
  25.7 6.3 %collective-permute-start.7 = (bf16[128,256]{1,0:T(8,128)(2,1)S(1)}, bf16[128,256]{1,0:T(8,128)(2,1)S(1)}, u32[]{:S(2)}, u32[]{:S(2)}) collective-permute-start(bf16[128,256]{1,0:T(8,128)(2,1)S(1)} %dynamic_slice.3), channel_id=1, source_target_pairs={{0,0},{128,1},{256,2},{384,3},{1,4},{129,5},{257,6},{385,7},{8,8},... | collective-permute-start | bytes 196616 | tf_op jit(solution)/shard_map/ppermute | solution.py:200
  32.0 2.3 %collective-permute-done.7 = bf16[128,256]{1,0:T(8,128)(2,1)S(1)} collective-permute-done((bf16[128,256]{1,0:T(8,128)(2,1)S(1)}, bf16[128,256]{1,0:T(8,128)(2,1)S(1)}, u32[]{:S(2)}, u32[]{:S(2)}) %collective-permute-start.7) | collective-permute-done | bytes 65568 | tf_op jit(solution)/shard_map/ppermute | solution.py:200
  35.2 7.7 %all-to-all-start.1 = ((bf16[8,128,256]{2,1,0:T(8,128)(2,1)}), bf16[8,128,256]{2,1,0:T(8,128)(2,1)S(1)}, u32[]{:S(2)}, u32[]{:S(2)}) async-start(bf16[8,128,256]{2,1,0:T(8,128)(2,1)} %broadcast_in_dim.6), calls=%async_computation.1 | async-start | bytes 1048576 | tf_op jit(solution)/shard_map/all_to_all | solution.py:202
  42.8 7.0 %collective-permute-start = (bf16[128,512]{1,0:T(8,128)(2,1)S(1)}, bf16[128,512]{1,0:T(8,128)(2,1)S(1)}, u32[]{:S(2)}, u32[]{:S(2)}) collective-permute-start(bf16[128,512]{1,0:T(8,128)(2,1)S(1)} %bitcast.28), channel_id=1, source_target_pairs={{0,24},{8,32},{16,40},{24,48},{32,56},{40,64},{48,72},{56,80},{64,... | collective-permute-start | bytes 393224 | tf_op jit(solution)/shard_map/ppermute | solution.py:27
  49.9 4.0 %collective-permute-start.1 = (bf16[128,512]{1,0:T(8,128)(2,1)S(1)}, bf16[128,512]{1,0:T(8,128)(2,1)S(1)}, u32[]{:S(2)}, u32[]{:S(2)}) collective-permute-start(bf16[128,512]{1,0:T(8,128)(2,1)S(1)} %bitcast.29), channel_id=1, source_target_pairs={{0,16},{8,24},{16,32},{24,40},{32,48},{40,56},{48,64},{56,72},{64,... | collective-permute-start | bytes 393224 | tf_op jit(solution)/shard_map/ppermute | solution.py:27
  57.4 2.9 %collective-permute-done.1.k1_ref = bf16[128,512]{1,0:T(8,128)(2,1)S(1)} collective-permute-done((bf16[128,512]{1,0:T(8,128)(2,1)S(1)}, bf16[128,512]{1,0:T(8,128)(2,1)S(1)}, u32[]{:S(2)}, u32[]{:S(2)}) %collective-permute-start.1) | collective-permute-done | bytes 131104 | tf_op jit(solution)/shard_map/ppermute | solution.py:27
  60.3 6.1 %attention_weights.1 = (bf16[4,512,1024]{2,1,0:T(8,128)(2,1)S(1)}, bf16[128,512]{1,0:T(8,128)(2,1)S(1)}, bf16[128,512]{1,0:T(8,128)(2,1)S(1)}, bf16[128,512]{1,0:T(8,128)(2,1)S(1)}, f32[128,512]{1,0:T(8,128)S(1)}) custom-call(s32[1,128]{1,0:T(1,128)S(1)} %copy-done.4, bf16[128,4096]{1,0:T(8,128)(2,1)S(1)} %bitcast.24, bf16[128,4096]{1,0:T(8,128)(2,1)S(1)} %bitcast.26, ...), custom_call_target="tpu_custom_call" | custom-call | flops 2147483648 | bytes 8388608 | tf_op jit(solution)/shard_map/attention_weights/pallas_call | solution.py:96
  67.1 2.0 %copy-done.5 = bf16[4,512,1024]{2,1,0:T(8,128)(2,1)} copy-done((bf16[4,512,1024]{2,1,0:T(8,128)(2,1)}, bf16[4,512,1024]{2,1,0:T(8,128)(2,1)S(1)}, u32[]{:S(2)}) %copy-start.5) | copy-done | bytes 4194328
  69.1 3.8 %collective-permute-start.4 = (bf16[128,512]{1,0:T(8,128)(2,1)S(1)}, bf16[128,512]{1,0:T(8,128)(2,1)S(1)}, u32[]{:S(2)}, u32[]{:S(2)}) collective-permute-start(bf16[128,512]{1,0:T(8,128)(2,1)S(1)} %get-tuple-element.18), channel_id=1, source_target_pairs={{8,0},{16,8},{24,16},{32,24},{40,32},{48,40},{56,48},{64,56},{72,6... | collective-permute-start | bytes 393224 | tf_op jit(solution)/shard_map/ppermute | solution.py:27
  72.9 2.6 %collective-permute-start.5 = (bf16[128,512]{1,0:T(8,128)(2,1)S(1)}, bf16[128,512]{1,0:T(8,128)(2,1)S(1)}, u32[]{:S(2)}, u32[]{:S(2)}) collective-permute-start(bf16[128,512]{1,0:T(8,128)(2,1)S(1)} %get-tuple-element.19), channel_id=1, source_target_pairs={{16,0},{24,8},{32,16},{40,24},{48,32},{56,40},{64,48},{72,56},{80,... | collective-permute-start | bytes 393224 | tf_op jit(solution)/shard_map/ppermute | solution.py:27
  75.5 3.8 %collective-permute-start.6 = (bf16[128,512]{1,0:T(8,128)(2,1)S(1)}, bf16[128,512]{1,0:T(8,128)(2,1)S(1)}, u32[]{:S(2)}, u32[]{:S(2)}) collective-permute-start(bf16[128,512]{1,0:T(8,128)(2,1)S(1)} %get-tuple-element.20), channel_id=1, source_target_pairs={{24,0},{32,8},{40,16},{48,24},{56,32},{64,40},{72,48},{80,56},{88,... | collective-permute-start | bytes 393224 | tf_op jit(solution)/shard_map/ppermute | solution.py:27
  80.1 4.1 %partial_values.1.values_ref = bf16[1024,256]{1,0:T(8,128)(2,1)} custom-call(s32[1]{0:T(128)} %bitcast.3.core_ref, bf16[512,1024]{1,0:T(8,128)(2,1)} %bitcast.6.near_ref, bf16[512,1024]{1,0:T(8,128)(2,1)} %collective-permute-done.3.far_ref, bf16[1024,256]{1,0:T(8,128)(2,1)} %bitcast.36), custom_call_target="tpu_custom_call" | custom-call | tf_op jit(solution)/shard_map/partial_values/pallas_call | solution.py:207
  85.3 2.3 %pack.1 = bf16[1024,512]{1,0:T(8,128)(2,1)} custom-call(f32[128,512]{1,0:T(8,128)} %copy-done, bf16[128,512]{1,0:T(8,128)(2,1)} %copy-done.9, bf16[128,512]{1,0:T(8,128)(2,1)} %copy-done.10, bf16[128,512]{1,0:T(8,128)(2,1)} %copy-done.11, bf16[1024,256]{1,0:T(8,128)(2,1)} %partial_values.1.values_ref), custom_call_target="tpu_custom_call" | custom-call | tf_op jit(solution)/shard_map/pack/pallas_call | solution.py:222
  87.7 20.9 %all_to_all.52 = bf16[8,128,512]{2,1,0:T(8,128)(2,1)} all-to-all(bf16[8,128,512]{2,1,0:T(8,128)(2,1)} %bitcast.34), channel_id=1, replica_groups=mesh['x'=4,'z'=8,'c'=2,'y'=8] {'x','c'}, dimensions={0} | all-to-all | bytes 2097152 | tf_op jit(solution)/shard_map/all_to_all | solution.py:227
  108.6 4.6 %group_product.1 = bf16[1024,256]{1,0:T(8,128)(2,1)} custom-call(s32[1]{0:T(128)} %bitcast.3.core_ref, bf16[512,1024]{1,0:T(8,128)(2,1)} %bitcast.6.near_ref, bf16[512,1024]{1,0:T(8,128)(2,1)} %collective-permute-done.3.far_ref, bf16[1024,512]{1,0:T(8,128)(2,1)} %bitcast.32), custom_call_target="tpu_custom_call" | custom-call | tf_op jit(solution)/shard_map/group_product/pallas_call | solution.py:232
  113.2 10.3 %all-to-all-start.3 = ((bf16[64,16,256]{2,1,0:T(8,128)(2,1)}), bf16[64,16,256]{2,1,0:T(8,128)(2,1)}, u32[]{:S(2)}, u32[]{:S(2)}) async-start(bf16[64,16,256]{2,1,0:T(8,128)(2,1)} %bitcast.37), calls=%async_computation.3 | async-start | bytes 1048576 | tf_op jit(solution)/shard_map/all_to_all | solution.py:278
  123.7 5.5 %collective-permute-start.8 = (bf16[128,512]{1,0:T(8,128)(2,1)S(1)}, bf16[128,512]{1,0:T(8,128)(2,1)S(1)}, u32[]{:S(2)}, u32[]{:S(2)}) collective-permute-start(bf16[128,512]{1,0:T(8,128)(2,1)S(1)} %pad_maximum_fusion.1.v3_ref), channel_id=1, source_target_pairs={{0,24},{8,32},{16,40},{24,48},{32,56},{40,64},{48,72},{56,80},{64,... | collective-permute-start | bytes 393224 | tf_op jit(solution)/shard_map/ppermute | solution.py:27
  129.2 3.1 %collective-permute-start.9 = (bf16[128,512]{1,0:T(8,128)(2,1)S(1)}, bf16[128,512]{1,0:T(8,128)(2,1)S(1)}, u32[]{:S(2)}, u32[]{:S(2)}) collective-permute-start(bf16[128,512]{1,0:T(8,128)(2,1)S(1)} %pad_maximum_fusion.1.v3_ref), channel_id=1, source_target_pairs={{0,16},{8,24},{16,32},{24,40},{32,48},{40,56},{48,64},{56,72},{64,... | collective-permute-start | bytes 393224 | tf_op jit(solution)/shard_map/ppermute | solution.py:27
  132.3 1.9 %collective-permute-start.10 = (bf16[128,512]{1,0:T(8,128)(2,1)S(1)}, bf16[128,512]{1,0:T(8,128)(2,1)S(1)}, u32[]{:S(2)}, u32[]{:S(2)}) collective-permute-start(bf16[128,512]{1,0:T(8,128)(2,1)S(1)} %pad_maximum_fusion.1.v3_ref), channel_id=1, source_target_pairs={{0,8},{8,16},{16,24},{24,32},{32,40},{40,48},{48,56},{56,64},{64,7... | collective-permute-start | bytes 393224 | tf_op jit(solution)/shard_map/ppermute | solution.py:27
  134.2 9.0 %collective-permute-done.8.v0_ref = bf16[128,512]{1,0:T(8,128)(2,1)S(1)} collective-permute-done((bf16[128,512]{1,0:T(8,128)(2,1)S(1)}, bf16[128,512]{1,0:T(8,128)(2,1)S(1)}, u32[]{:S(2)}, u32[]{:S(2)}) %collective-permute-start.8) | collective-permute-done | bytes 131104 | tf_op jit(solution)/shard_map/ppermute | solution.py:27
  143.2 3.1 %collective-permute-done.9.v1_ref = bf16[128,512]{1,0:T(8,128)(2,1)S(1)} collective-permute-done((bf16[128,512]{1,0:T(8,128)(2,1)S(1)}, bf16[128,512]{1,0:T(8,128)(2,1)S(1)}, u32[]{:S(2)}, u32[]{:S(2)}) %collective-permute-start.9) | collective-permute-done | bytes 131104 | tf_op jit(solution)/shard_map/ppermute | solution.py:27
  147.4 4.0 %collective-permute-start.14 = (bf16[16,256]{1,0:T(8,128)(2,1)S(1)}, bf16[16,256]{1,0:T(8,128)(2,1)S(1)}, u32[]{:S(2)}, u32[]{:S(2)}) collective-permute-start(bf16[16,256]{1,0:T(8,128)(2,1)S(1)} %multiply_convert_fusion), channel_id=1, source_target_pairs={{0,0},{1,128},{2,256},{3,384},{4,1},{5,129},{6,257},{7,385},{8,8},... | collective-permute-start | bytes 24584 | tf_op jit(solution)/shard_map/ppermute | solution.py:291
  151.4 6.7 %collective-permute-done.14 = bf16[16,256]{1,0:T(8,128)(2,1)S(1)} collective-permute-done((bf16[16,256]{1,0:T(8,128)(2,1)S(1)}, bf16[16,256]{1,0:T(8,128)(2,1)S(1)}, u32[]{:S(2)}, u32[]{:S(2)}) %collective-permute-start.14) | collective-permute-done | bytes 8224 | tf_op jit(solution)/shard_map/ppermute | solution.py:291
  158.8 6.5 %all-to-all-start.4 = ((bf16[32,16,256]{2,1,0:T(8,128)(2,1)}), bf16[32,16,256]{2,1,0:T(8,128)(2,1)S(1)}, u32[]{:S(2)}, u32[]{:S(2)}) async-start(bf16[32,16,256]{2,1,0:T(8,128)(2,1)} %broadcast_in_dim.8), calls=%async_computation.4 | async-start | bytes 524288 | tf_op jit(solution)/shard_map/all_to_all | solution.py:260
  165.3 2.2 %copy-done.6 = bf16[4,512,1024]{2,1,0:T(8,128)(2,1)S(1)} copy-done((bf16[4,512,1024]{2,1,0:T(8,128)(2,1)S(1)}, bf16[4,512,1024]{2,1,0:T(8,128)(2,1)}, u32[]{:S(2)}) %copy-start.6) | copy-done | bytes 4194328
  167.5 5.3 %key_gradient.1 = (bf16[128,512]{1,0:T(8,128)(2,1)S(1)}, bf16[128,512]{1,0:T(8,128)(2,1)S(1)}, bf16[128,512]{1,0:T(8,128)(2,1)S(1)}, f32[128,512]{1,0:T(8,128)S(1)}) custom-call(bf16[4,512,1024]{2,1,0:T(8,128)(2,1)S(1)} %copy-done.6, bf16[128,4096]{1,0:T(8,128)(2,1)S(1)} %bitcast.25, bf16[128,4096]{1,0:T(8,128)(2,1)S(1)} %bitcast.27, ...), custom_call_target="tpu_custom_call" | custom-call | flops 2147483648 | bytes 8388608 | tf_op jit(solution)/shard_map/key_gradient/pallas_call | solution.py:112
  172.8 7.7 %collective-permute-start.13 = (bf16[128,512]{1,0:T(8,128)(2,1)S(1)}, bf16[128,512]{1,0:T(8,128)(2,1)S(1)}, u32[]{:S(2)}, u32[]{:S(2)}) collective-permute-start(bf16[128,512]{1,0:T(8,128)(2,1)S(1)} %get-tuple-element.28), channel_id=1, source_target_pairs={{24,0},{32,8},{40,16},{48,24},{56,32},{64,40},{72,48},{80,56},{88,... | collective-permute-start | bytes 393224 | tf_op jit(solution)/shard_map/ppermute | solution.py:27
  180.5 3.1 %collective-permute-start.12 = (bf16[128,512]{1,0:T(8,128)(2,1)S(1)}, bf16[128,512]{1,0:T(8,128)(2,1)S(1)}, u32[]{:S(2)}, u32[]{:S(2)}) collective-permute-start(bf16[128,512]{1,0:T(8,128)(2,1)S(1)} %get-tuple-element.27), channel_id=1, source_target_pairs={{16,0},{24,8},{32,16},{40,24},{48,32},{56,40},{64,48},{72,56},{80,... | collective-permute-start | bytes 393224 | tf_op jit(solution)/shard_map/ppermute | solution.py:27
  185.6 3.5 %collective-permute-start.15 = (bf16[512,256]{1,0:T(8,128)(2,1)S(1)}, bf16[512,256]{1,0:T(8,128)(2,1)S(1)}, u32[]{:S(2)}, u32[]{:S(2)}) collective-permute-start(bf16[512,256]{1,0:T(8,128)(2,1)S(1)} %bitcast.39), channel_id=1, source_target_pairs={{0,8},{8,0},{1,9},{9,1},{2,10},{10,2},{3,11},{11,3},{4,12},{12,4},... | collective-permute-start | bytes 786440 | tf_op jit(solution)/shard_map/ppermute | solution.py:261
  (49 shorter events, 14.2 us)
Async XLA Ops:
  0.6 42.2 %copy-start.3 = (bf16[1,128,512]{2,1,0:T(8,128)(2,1)S(1)}, bf16[1,128,512]{2,1,0:T(8,128)(2,1)}, u32[]{:S(2)}) copy-start(bf16[1,128,512]{2,1,0:T(8,128)(2,1)} %param.7) | copy-start | bytes 393220
  0.6 59.7 %copy-start.4 = (s32[1,128]{1,0:T(1,128)S(1)}, s32[1,128]{1,0:T(1,128)}, u32[]{:S(2)}) copy-start(s32[1,128]{1,0:T(1,128)} %position_ref.1) | copy-start | bytes 1540
  0.7 59.6 %copy-start.1 = (bf16[1,128,4096]{2,1,0:T(8,128)(2,1)S(1)}, bf16[1,128,4096]{2,1,0:T(8,128)(2,1)}, u32[]{:S(2)}) copy-start(bf16[1,128,4096]{2,1,0:T(8,128)(2,1)} %param.6) | copy-start | bytes 3145732
  0.7 59.6 %copy-start.2 = (bf16[1,128,4096]{2,1,0:T(8,128)(2,1)S(1)}, bf16[1,128,4096]{2,1,0:T(8,128)(2,1)}, u32[]{:S(2)}) copy-start(bf16[1,128,4096]{2,1,0:T(8,128)(2,1)} %param.8) | copy-start | bytes 3145732
  21.0 58.3 %collective-permute-start.3 = (bf16[512,1024]{1,0:T(8,128)(2,1)}, bf16[512,1024]{1,0:T(8,128)(2,1)}, u32[]{:S(2)}, u32[]{:S(2)}) collective-permute-start(bf16[512,1024]{1,0:T(8,128)(2,1)} %bitcast.6.near_ref), channel_id=1, source_target_pairs={{0,8},{8,0},{1,9},{9,1},{2,10},{10,2},{3,11},{11,3},{4,12},{12,4},... | collective-permute-start | bytes 3145736 | tf_op jit(solution)/shard_map/ppermute | solution.py:193
  25.7 8.6 %collective-permute-start.7 = (bf16[128,256]{1,0:T(8,128)(2,1)S(1)}, bf16[128,256]{1,0:T(8,128)(2,1)S(1)}, u32[]{:S(2)}, u32[]{:S(2)}) collective-permute-start(bf16[128,256]{1,0:T(8,128)(2,1)S(1)} %dynamic_slice.3), channel_id=1, source_target_pairs={{0,0},{128,1},{256,2},{384,3},{1,4},{129,5},{257,6},{385,7},{8,8},... | collective-permute-start | bytes 196616 | tf_op jit(solution)/shard_map/ppermute | solution.py:200
  35.2 44.2 %all-to-all-start.1 = ((bf16[8,128,256]{2,1,0:T(8,128)(2,1)}), bf16[8,128,256]{2,1,0:T(8,128)(2,1)S(1)}, u32[]{:S(2)}, u32[]{:S(2)}) async-start(bf16[8,128,256]{2,1,0:T(8,128)(2,1)} %broadcast_in_dim.6), calls=%async_computation.1 | async-start | bytes 1048576 | tf_op jit(solution)/shard_map/all_to_all | solution.py:202
  42.8 14.5 %collective-permute-start = (bf16[128,512]{1,0:T(8,128)(2,1)S(1)}, bf16[128,512]{1,0:T(8,128)(2,1)S(1)}, u32[]{:S(2)}, u32[]{:S(2)}) collective-permute-start(bf16[128,512]{1,0:T(8,128)(2,1)S(1)} %bitcast.28), channel_id=1, source_target_pairs={{0,24},{8,32},{16,40},{24,48},{32,56},{40,64},{48,72},{56,80},{64,... | collective-permute-start | bytes 393224 | tf_op jit(solution)/shard_map/ppermute | solution.py:27
  49.9 10.4 %collective-permute-start.1 = (bf16[128,512]{1,0:T(8,128)(2,1)S(1)}, bf16[128,512]{1,0:T(8,128)(2,1)S(1)}, u32[]{:S(2)}, u32[]{:S(2)}) collective-permute-start(bf16[128,512]{1,0:T(8,128)(2,1)S(1)} %bitcast.29), channel_id=1, source_target_pairs={{0,16},{8,24},{16,32},{24,40},{32,48},{40,56},{48,64},{56,72},{64,... | collective-permute-start | bytes 393224 | tf_op jit(solution)/shard_map/ppermute | solution.py:27
  53.9 6.4 %collective-permute-start.2 = (bf16[128,512]{1,0:T(8,128)(2,1)S(1)}, bf16[128,512]{1,0:T(8,128)(2,1)S(1)}, u32[]{:S(2)}, u32[]{:S(2)}) collective-permute-start(bf16[128,512]{1,0:T(8,128)(2,1)S(1)} %bitcast.30), channel_id=1, source_target_pairs={{0,8},{8,16},{16,24},{24,32},{32,40},{40,48},{48,56},{56,64},{64,7... | collective-permute-start | bytes 393224 | tf_op jit(solution)/shard_map/ppermute | solution.py:27
  66.4 0.7 copy-start
  67.1 2.0 %copy-start.5 = (bf16[4,512,1024]{2,1,0:T(8,128)(2,1)}, bf16[4,512,1024]{2,1,0:T(8,128)(2,1)S(1)}, u32[]{:S(2)}) copy-start(bf16[4,512,1024]{2,1,0:T(8,128)(2,1)S(1)} %get-tuple-element.16.weights_ref) | copy-start | bytes 12582916
  69.1 15.1 %collective-permute-start.4 = (bf16[128,512]{1,0:T(8,128)(2,1)S(1)}, bf16[128,512]{1,0:T(8,128)(2,1)S(1)}, u32[]{:S(2)}, u32[]{:S(2)}) collective-permute-start(bf16[128,512]{1,0:T(8,128)(2,1)S(1)} %get-tuple-element.18), channel_id=1, source_target_pairs={{8,0},{16,8},{24,16},{32,24},{40,32},{48,40},{56,48},{64,56},{72,6... | collective-permute-start | bytes 393224 | tf_op jit(solution)/shard_map/ppermute | solution.py:27
  72.9 11.3 %collective-permute-start.5 = (bf16[128,512]{1,0:T(8,128)(2,1)S(1)}, bf16[128,512]{1,0:T(8,128)(2,1)S(1)}, u32[]{:S(2)}, u32[]{:S(2)}) collective-permute-start(bf16[128,512]{1,0:T(8,128)(2,1)S(1)} %get-tuple-element.19), channel_id=1, source_target_pairs={{16,0},{24,8},{32,16},{40,24},{48,32},{56,40},{64,48},{72,56},{80,... | collective-permute-start | bytes 393224 | tf_op jit(solution)/shard_map/ppermute | solution.py:27
  75.5 9.2 %collective-permute-start.6 = (bf16[128,512]{1,0:T(8,128)(2,1)S(1)}, bf16[128,512]{1,0:T(8,128)(2,1)S(1)}, u32[]{:S(2)}, u32[]{:S(2)}) collective-permute-start(bf16[128,512]{1,0:T(8,128)(2,1)S(1)} %get-tuple-element.20), channel_id=1, source_target_pairs={{24,0},{32,8},{40,16},{48,24},{56,32},{64,40},{72,48},{80,56},{88,... | collective-permute-start | bytes 393224 | tf_op jit(solution)/shard_map/ppermute | solution.py:27
  79.3 0.8 copy-start.8
  84.2 0.7 copy-start.9
  84.2 0.7 copy-start.10
  84.7 0.6 copy-start.11
  108.6 14.9 %copy-start.7 = (bf16[8,128,512]{2,1,0:T(8,128)(2,1)S(1)}, bf16[8,128,512]{2,1,0:T(8,128)(2,1)}, u32[]{:S(2)}) copy-start(bf16[8,128,512]{2,1,0:T(8,128)(2,1)} %all_to_all.52) | copy-start | bytes 3145732
  113.2 33.1 %all-to-all-start.3 = ((bf16[64,16,256]{2,1,0:T(8,128)(2,1)}), bf16[64,16,256]{2,1,0:T(8,128)(2,1)}, u32[]{:S(2)}, u32[]{:S(2)}) async-start(bf16[64,16,256]{2,1,0:T(8,128)(2,1)} %bitcast.37), calls=%async_computation.3 | async-start | bytes 1048576 | tf_op jit(solution)/shard_map/all_to_all | solution.py:278
  123.7 19.5 %collective-permute-start.8 = (bf16[128,512]{1,0:T(8,128)(2,1)S(1)}, bf16[128,512]{1,0:T(8,128)(2,1)S(1)}, u32[]{:S(2)}, u32[]{:S(2)}) collective-permute-start(bf16[128,512]{1,0:T(8,128)(2,1)S(1)} %pad_maximum_fusion.1.v3_ref), channel_id=1, source_target_pairs={{0,24},{8,32},{16,40},{24,48},{32,56},{40,64},{48,72},{56,80},{64,... | collective-permute-start | bytes 393224 | tf_op jit(solution)/shard_map/ppermute | solution.py:27
  129.2 17.1 %collective-permute-start.9 = (bf16[128,512]{1,0:T(8,128)(2,1)S(1)}, bf16[128,512]{1,0:T(8,128)(2,1)S(1)}, u32[]{:S(2)}, u32[]{:S(2)}) collective-permute-start(bf16[128,512]{1,0:T(8,128)(2,1)S(1)} %pad_maximum_fusion.1.v3_ref), channel_id=1, source_target_pairs={{0,16},{8,24},{16,32},{24,40},{32,48},{40,56},{48,64},{56,72},{64,... | collective-permute-start | bytes 393224 | tf_op jit(solution)/shard_map/ppermute | solution.py:27
  132.3 14.0 %collective-permute-start.10 = (bf16[128,512]{1,0:T(8,128)(2,1)S(1)}, bf16[128,512]{1,0:T(8,128)(2,1)S(1)}, u32[]{:S(2)}, u32[]{:S(2)}) collective-permute-start(bf16[128,512]{1,0:T(8,128)(2,1)S(1)} %pad_maximum_fusion.1.v3_ref), channel_id=1, source_target_pairs={{0,8},{8,16},{16,24},{24,32},{32,40},{40,48},{48,56},{56,64},{64,7... | collective-permute-start | bytes 393224 | tf_op jit(solution)/shard_map/ppermute | solution.py:27
  147.4 10.7 %collective-permute-start.14 = (bf16[16,256]{1,0:T(8,128)(2,1)S(1)}, bf16[16,256]{1,0:T(8,128)(2,1)S(1)}, u32[]{:S(2)}, u32[]{:S(2)}) collective-permute-start(bf16[16,256]{1,0:T(8,128)(2,1)S(1)} %multiply_convert_fusion), channel_id=1, source_target_pairs={{0,0},{1,128},{2,256},{3,384},{4,1},{5,129},{6,257},{7,385},{8,8},... | collective-permute-start | bytes 24584 | tf_op jit(solution)/shard_map/ppermute | solution.py:291
  158.8 26.7 %all-to-all-start.4 = ((bf16[32,16,256]{2,1,0:T(8,128)(2,1)}), bf16[32,16,256]{2,1,0:T(8,128)(2,1)S(1)}, u32[]{:S(2)}, u32[]{:S(2)}) async-start(bf16[32,16,256]{2,1,0:T(8,128)(2,1)} %broadcast_in_dim.8), calls=%async_computation.4 | async-start | bytes 524288 | tf_op jit(solution)/shard_map/all_to_all | solution.py:260
  165.3 2.2 %copy-start.6 = (bf16[4,512,1024]{2,1,0:T(8,128)(2,1)S(1)}, bf16[4,512,1024]{2,1,0:T(8,128)(2,1)}, u32[]{:S(2)}) copy-start(bf16[4,512,1024]{2,1,0:T(8,128)(2,1)} %copy-done.5) | copy-start | bytes 12582916
  172.8 16.2 %collective-permute-start.13 = (bf16[128,512]{1,0:T(8,128)(2,1)S(1)}, bf16[128,512]{1,0:T(8,128)(2,1)S(1)}, u32[]{:S(2)}, u32[]{:S(2)}) collective-permute-start(bf16[128,512]{1,0:T(8,128)(2,1)S(1)} %get-tuple-element.28), channel_id=1, source_target_pairs={{24,0},{32,8},{40,16},{48,24},{56,32},{64,40},{72,48},{80,56},{88,... | collective-permute-start | bytes 393224 | tf_op jit(solution)/shard_map/ppermute | solution.py:27
  180.5 8.5 %collective-permute-start.12 = (bf16[128,512]{1,0:T(8,128)(2,1)S(1)}, bf16[128,512]{1,0:T(8,128)(2,1)S(1)}, u32[]{:S(2)}, u32[]{:S(2)}) collective-permute-start(bf16[128,512]{1,0:T(8,128)(2,1)S(1)} %get-tuple-element.27), channel_id=1, source_target_pairs={{16,0},{24,8},{32,16},{40,24},{48,32},{56,40},{64,48},{72,56},{80,... | collective-permute-start | bytes 393224 | tf_op jit(solution)/shard_map/ppermute | solution.py:27
  183.6 6.3 %collective-permute-start.11 = (bf16[128,512]{1,0:T(8,128)(2,1)S(1)}, bf16[128,512]{1,0:T(8,128)(2,1)S(1)}, u32[]{:S(2)}, u32[]{:S(2)}) collective-permute-start(bf16[128,512]{1,0:T(8,128)(2,1)S(1)} %get-tuple-element.26), channel_id=1, source_target_pairs={{8,0},{16,8},{24,16},{32,24},{40,32},{48,40},{56,48},{64,56},{72,6... | collective-permute-start | bytes 393224 | tf_op jit(solution)/shard_map/ppermute | solution.py:27
  185.6 5.1 %collective-permute-start.15 = (bf16[512,256]{1,0:T(8,128)(2,1)S(1)}, bf16[512,256]{1,0:T(8,128)(2,1)S(1)}, u32[]{:S(2)}, u32[]{:S(2)}) collective-permute-start(bf16[512,256]{1,0:T(8,128)(2,1)S(1)} %bitcast.39), channel_id=1, source_target_pairs={{0,8},{8,0},{1,9},{9,1},{2,10},{10,2},{3,11},{11,3},{4,12},{12,4},... | collective-permute-start | bytes 786440 | tf_op jit(solution)/shard_map/ppermute | solution.py:261

commit v4 on v3

--- a/solution.py
+++ b/solution.py
@@ -89,7 +89,7 @@
     for kind in (jnp.bfloat16, jnp.bfloat16, jnp.bfloat16, jnp.float32)
 ]
 KERNEL_FLOPS = 2 * 2 * SPAN_ROWS * BLOCK * KEY_HEADS * GROUP_COLUMNS
-params = pltpu.CompilerParams(vmem_limit_bytes=40 * 1024 * 1024)
+params = pltpu.CompilerParams(vmem_limit_bytes=16 * 1024 * 1024)
 
 
 def attention_weights(position, queries, grads, keys):
@@ -139,17 +139,28 @@
 HALF = 256
 
 
-def quarters_kernel(rows_ref, out_ref):
-    out_ref[...] = rows_ref[...]
+def quarters_kernel(rows_ref, out_ref, sems):
+    copies = [
+        pltpu.make_async_copy(
+            rows_ref.at[:, pl.ds(x * QUARTER, QUARTER)],
+            out_ref.at[pl.ds(x * BLOCK, BLOCK), :],
+            sems.at[x],
+        )
+        for x in range(4)
+    ]
+    for copy in copies:
+        copy.start()
+    for copy in copies:
+        copy.wait()
 
 
 def partial_values_kernel(core_ref, near_ref, far_ref, weight_ref, out_ref):
-    block = pl.program_id(0)
     for rows_ref, core in ((near_ref, core_ref[0]), (far_ref, 1 - core_ref[0])):
         values = jnp.dot(rows_ref[...], weight_ref[...], preferred_element_type=jnp.float32)
-        out_ref[pl.ds(pl.multiple_of((2 * block + core) * BLOCK, BLOCK), BLOCK), :] = values.astype(
-            jnp.bfloat16
-        )
+        values = values.astype(jnp.bfloat16)
+        for x in range(4):
+            rows = pl.ds(pl.multiple_of((2 * x + core) * BLOCK, BLOCK), BLOCK)
+            out_ref[rows, :] = values[x * BLOCK : (x + 1) * BLOCK]
 
 
 def pack_kernel(own_ref, one_ref, two_ref, three_ref, values_ref, out_ref):
@@ -171,48 +182,51 @@
             for x in range(4)
         ]
         part = lax.dot_general(
+            jnp.concatenate(grads, axis=0),
             rows_ref[...],
-            jnp.concatenate(grads, axis=0),
             (((0,), (0,)), ((), ())),
             preferred_element_type=jnp.float32,
         )
         total = part if total is None else total + part
-    out_ref[...] = total.astype(jnp.bfloat16)
+    out_ref[...] = total.T.astype(jnp.bfloat16)
 
 
 def exchange_rows(rows):
     quarters = pl.pallas_call(
         quarters_kernel,
-        grid=(4,),
-        in_specs=[pl.BlockSpec((BLOCK, QUARTER), lambda x: (0, x))],
-        out_specs=pl.BlockSpec((BLOCK, QUARTER), lambda x: (x, 0)),
+        in_specs=[pl.BlockSpec(memory_space=pl.ANY)],
+        out_specs=pl.BlockSpec(memory_space=pl.ANY),
         out_shape=jax.ShapeDtypeStruct((4 * BLOCK, QUARTER), jnp.bfloat16),
+        scratch_shapes=[pltpu.SemaphoreType.DMA((4,))],
+        compiler_params=params,
         name="quarters",
     )(rows)
-    near = lax.all_to_all(quarters, "x", 0, 0, tiled=True)
-    return near, lax.ppermute(near, "c", OTHER_CORE)
-
-
-def exchange_projection(w_value):
+    return lax.all_to_all(quarters, "x", 0, 0, tiled=True)
+
+
+def projection_piece(w_value):
     route = [(target, source) for source, target in plane_route()]
     start = (lax.axis_index("x") * BLOCK, lax.axis_index("c") * HALF)
     piece = lax.dynamic_slice(w_value, start, (BLOCK, HALF))
-    piece = lax.ppermute(piece, ("x", "z", "c", "y"), route)
+    return lax.ppermute(piece, ("x", "z", "c", "y"), route)
+
+
+def projection_part(piece):
     copies = jnp.broadcast_to(piece[None], (8, BLOCK, HALF)).reshape(8 * BLOCK, HALF)
     return lax.all_to_all(copies, "y", 0, 0, tiled=True)
 
 
+in_smem = pl.BlockSpec(memory_space=pltpu.SMEM)
+in_vmem = pl.BlockSpec(memory_space=pltpu.VMEM)
+
+
 def partial_values(core, near, far, weight):
-    rows = pl.BlockSpec((BLOCK, QUARTER), lambda x, core: (x, 0))
     return pl.pallas_call(
         partial_values_kernel,
-        grid_spec=pltpu.PrefetchScalarGridSpec(
-            num_scalar_prefetch=1,
-            grid=(4,),
-            in_specs=[rows, rows, pl.BlockSpec((QUARTER, HALF), lambda x, core: (0, 0))],
-            out_specs=pl.BlockSpec((8 * BLOCK, HALF), lambda x, core: (0, 0)),
-        ),
+        in_specs=[in_smem, in_vmem, in_vmem, in_vmem],
+        out_specs=in_vmem,
         out_shape=jax.ShapeDtypeStruct((8 * BLOCK, HALF), jnp.bfloat16),
+        compiler_params=params,
         name="partial_values",
     )(core, near, far, weight)
 
@@ -222,22 +236,21 @@
     packed = pl.pallas_call(
         pack_kernel,
         out_shape=jax.ShapeDtypeStruct((8 * BLOCK, 2 * HALF), jnp.bfloat16),
+        compiler_params=params,
         name="pack",
     )(value_parts[SPAN], *received, values)
     return lax.all_to_all(packed, ("x", "c"), 0, 0, tiled=True)
 
 
 def group_product(core, near, far, packed):
-    rows = pl.BlockSpec((4 * BLOCK, HALF), lambda part, core: (0, part))
+    rows = pl.BlockSpec((4 * BLOCK, HALF), lambda part: (0, part))
     return pl.pallas_call(
         product_kernel,
-        grid_spec=pltpu.PrefetchScalarGridSpec(
-            num_scalar_prefetch=1,
-            grid=(QUARTER // HALF,),
-            in_specs=[rows, rows, pl.BlockSpec((8 * BLOCK, 2 * HALF), lambda part, core: (0, 0))],
-            out_specs=pl.BlockSpec((HALF, HALF), lambda part, core: (part, 0)),
-        ),
+        grid=(QUARTER // HALF,),
+        in_specs=[in_smem, rows, rows, pl.BlockSpec((8 * BLOCK, 2 * HALF), lambda part: (0, 0))],
+        out_specs=pl.BlockSpec((HALF, HALF), lambda part: (part, 0)),
         out_shape=jax.ShapeDtypeStruct((QUARTER, HALF), jnp.bfloat16),
+        compiler_params=params,
         name="group_product",
     )(core, near, far, packed)
 
@@ -269,10 +282,13 @@
     queries, keys, grads, rows = queries[0], key_rows[0], out_grad[0], inputs[0]
     core = lax.axis_index("c").astype(jnp.int32).reshape(1)
     key_span = span_of(keys)
-    near, far = exchange_rows(rows)
-    weight = exchange_projection(w_value)
-    values = partial_values(core, near, far, weight)
+    near = exchange_rows(rows)
+    weight = projection_piece(w_value)
     weights, *value_parts = attention_weights(doc_pos, queries, grads, key_span)
+    near, weight, value_parts = lax.optimization_barrier((near, weight, value_parts))
+
+    far = lax.ppermute(near, "c", OTHER_CORE)
+    values = partial_values(core, near, far, projection_part(weight))
     packed = exchange_packed(value_parts, values)
     product = group_product(core, near, far, packed)
     pieces = lax.all_to_all(product, ("y", "z"), 0, 0, tiled=True)
@@ -283,12 +299,14 @@
     value_span = span_of(values)
     pieces, value_span = lax.optimization_barrier((pieces, value_span))
     key_parts = key_gradient(weights, queries, grads, value_span)
-    key_grad = owed(key_parts)
 
     pieces = pieces.reshape(64, -1, HALF).astype(jnp.float32)
     token_total = lax.axis_size(("x", "z", "c", "y")) * BLOCK
     piece = (jnp.sum(pieces, axis=0) * (1.0 / math.sqrt(token_total))).astype(jnp.bfloat16)
-    weight_grad = whole_shard(lax.ppermute(piece, ("x", "z", "c", "y"), plane_route()))
+    piece = lax.ppermute(piece, ("x", "z", "c", "y"), plane_route())
+    piece, key_parts = lax.optimization_barrier((piece, key_parts))
+    weight_grad = whole_shard(piece)
+    key_grad = owed(key_parts)
     return (key_grad[None], weight_grad)
 
 

time: 193 us -> 164 us (0.85)
  the two profiles are of different devices: /device:TPU:31 before, /device:TPU:1 now
where the time goes in v4:
time: 164 us; the launch traced here: 163 us
  starting transfers between devices  75.5 us (46%)
  waiting for transfers between devices  35.5 us (22%)
  blocking collectives  21.1 us (13%)
  Pallas kernels  15.9 us (10%)
  local copies, waits for them, and re-layouts  12.3 us (8%)
  other arithmetic  1.79 us (1%)
    ppermute x12, starting transfers between devices, shift(): return lax.ppermute(block, DP, route)  32.2 us
    all_to_all x1, blocking collectives, exchange_packed(): return lax.all_to_all(packed, ('x', 'c'), 0, 0, tiled=True)  21.1 us
    ppermute x12, waiting for transfers between devices, shift(): return lax.ppermute(block, DP, route)  16.1 us
    all_to_all x1, starting transfers between devices, whole_shard(): half = lax.all_to_all(copies, ('x', 'z'), 0, 0, tiled=True)  14 us
    all_to_all x1, waiting for transfers between devices, projection_part(): return lax.all_to_all(copies, 'y', 0, 0, tiled=True)  13.2 us
    all_to_all x1, starting transfers between devices, projection_part(): return lax.all_to_all(copies, 'y', 0, 0, tiled=True)  10.7 us
    unnamed x20, local copies, waits for them, and re-layouts  9.84 us
    all_to_all x1, starting transfers between devices, per_device(): pieces = lax.all_to_all(product, ('y', 'z'), 0, 0, tiled=True)  6.98 us
  transfers between devices with their start and end apart: 20, of which 7 were waited for; matrix products, arithmetic and copies ran while one was open for 2% of the time, Pallas kernels for 8%

profile of v4, /device:TPU:1, one launch (start us, length us, event | category | flops | bytes accessed | tf_op | source)
XLA Modules:
  0.0 163.1 jit_solution(728690497408607202)
XLA Ops:
  2.9 4.9 %all-to-all-start = ((bf16[4,128,1024]{2,1,0:T(8,128)(2,1)}), bf16[4,128,1024]{2,1,0:T(8,128)(2,1)S(1)}, u32[]{:S(2)}, u32[]{:S(2)}) async-start(bf16[4,128,1024]{2,1,0:T(8,128)(2,1)} %bitcast.2), calls=%async_computation | async-start | bytes 2097152 | tf_op jit(solution)/shard_map/all_to_all | solution.py:204
  7.8 6.6 %collective-permute-start.1 = (bf16[128,512]{1,0:T(8,128)(2,1)S(1)}, bf16[128,512]{1,0:T(8,128)(2,1)S(1)}, u32[]{:S(2)}, u32[]{:S(2)}) collective-permute-start(bf16[128,512]{1,0:T(8,128)(2,1)S(1)} %bitcast.37), channel_id=1, source_target_pairs={{0,24},{8,32},{16,40},{24,48},{32,56},{40,64},{48,72},{56,80},{64,... | collective-permute-start | bytes 393224 | tf_op jit(solution)/shard_map/ppermute | solution.py:27
  14.4 4.0 %collective-permute-start.2 = (bf16[128,512]{1,0:T(8,128)(2,1)S(1)}, bf16[128,512]{1,0:T(8,128)(2,1)S(1)}, u32[]{:S(2)}, u32[]{:S(2)}) collective-permute-start(bf16[128,512]{1,0:T(8,128)(2,1)S(1)} %bitcast.38), channel_id=1, source_target_pairs={{0,16},{8,24},{16,32},{24,40},{32,48},{40,56},{48,64},{56,72},{64,... | collective-permute-start | bytes 393224 | tf_op jit(solution)/shard_map/ppermute | solution.py:27
  18.4 1.9 %collective-permute-start.3 = (bf16[128,512]{1,0:T(8,128)(2,1)S(1)}, bf16[128,512]{1,0:T(8,128)(2,1)S(1)}, u32[]{:S(2)}, u32[]{:S(2)}) collective-permute-start(bf16[128,512]{1,0:T(8,128)(2,1)S(1)} %bitcast.39), channel_id=1, source_target_pairs={{0,8},{8,16},{16,24},{24,32},{32,40},{40,48},{48,56},{56,64},{64,7... | collective-permute-start | bytes 393224 | tf_op jit(solution)/shard_map/ppermute | solution.py:27
  21.9 1.4 collective-permute-done.3.k2_ref
  23.4 1.2 copy-done.4
  24.6 6.7 %attention_weights.1 = (bf16[4,512,1024]{2,1,0:T(8,128)(2,1)S(1)}, bf16[128,512]{1,0:T(8,128)(2,1)S(1)}, bf16[128,512]{1,0:T(8,128)(2,1)S(1)}, bf16[128,512]{1,0:T(8,128)(2,1)}, f32[128,512]{1,0:T(8,128)S(1)}) custom-call(s32[1,128]{1,0:T(1,128)S(1)} %copy-done.7, bf16[128,4096]{1,0:T(8,128)(2,1)S(1)} %bitcast.33, bf16[128,4096]{1,0:T(8,128)(2,1)S(1)} %bitcast.35, ...), custom_call_target="tpu_custom_call" | custom-call | flops 2147483648 | bytes 8388608 | tf_op jit(solution)/shard_map/attention_weights/pallas_call | solution.py:96
  31.3 2.0 %copy-done.8 = bf16[4,512,1024]{2,1,0:T(8,128)(2,1)} copy-done((bf16[4,512,1024]{2,1,0:T(8,128)(2,1)}, bf16[4,512,1024]{2,1,0:T(8,128)(2,1)S(1)}, u32[]{:S(2)}) %copy-start.8) | copy-done | bytes 4194328
  33.2 1.9 %collective-permute-start.4 = (bf16[512,1024]{1,0:T(8,128)(2,1)S(1)}, bf16[512,1024]{1,0:T(8,128)(2,1)S(1)}, u32[]{:S(2)}, u32[]{:S(2)}) collective-permute-start(bf16[512,1024]{1,0:T(8,128)(2,1)S(1)} %bitcast.24), channel_id=1, source_target_pairs={{0,8},{8,0},{1,9},{9,1},{2,10},{10,2},{3,11},{11,3},{4,12},{12,4},... | collective-permute-start | bytes 3145736 | tf_op jit(solution)/shard_map/ppermute | solution.py:290
  36.0 10.7 %all-to-all-start.1 = ((bf16[8,128,256]{2,1,0:T(8,128)(2,1)}), bf16[8,128,256]{2,1,0:T(8,128)(2,1)S(1)}, u32[]{:S(2)}, u32[]{:S(2)}) async-start(bf16[8,128,256]{2,1,0:T(8,128)(2,1)} %broadcast_in_dim.6), calls=%async_computation.1 | async-start | bytes 1048576 | tf_op jit(solution)/shard_map/all_to_all | solution.py:216
  46.7 2.2 %collective-permute-start.5 = (bf16[128,512]{1,0:T(8,128)(2,1)}, bf16[128,512]{1,0:T(8,128)(2,1)S(1)}, u32[]{:S(2)}, u32[]{:S(2)}) collective-permute-start(bf16[128,512]{1,0:T(8,128)(2,1)} %get-tuple-element.33), channel_id=1, source_target_pairs={{8,0},{16,8},{24,16},{32,24},{40,32},{48,40},{56,48},{64,56},{72,6... | collective-permute-start | bytes 393224 | tf_op jit(solution)/shard_map/ppermute | solution.py:27
  48.9 1.3 collective-permute-start.6
  50.2 1.3 collective-permute-start.7
  51.5 13.2 %all-to-all-done.1 = bf16[8,128,256]{2,1,0:T(8,128)(2,1)S(1)} async-done(((bf16[8,128,256]{2,1,0:T(8,128)(2,1)}), bf16[8,128,256]{2,1,0:T(8,128)(2,1)S(1)}, u32[]{:S(2)}, u32[]{:S(2)}) %all-to-all-start.1) | async-done | bytes 524320 | tf_op jit(solution)/shard_map/all_to_all | solution.py:216
  65.5 21.1 %all_to_all.52 = bf16[8,128,512]{2,1,0:T(8,128)(2,1)S(1)} all-to-all(bf16[8,128,512]{2,1,0:T(8,128)(2,1)S(1)} %bitcast.29), channel_id=1, replica_groups=mesh['x'=4,'z'=8,'c'=2,'y'=8] {'x','c'}, dimensions={0} | all-to-all | bytes 2097152 | tf_op jit(solution)/shard_map/all_to_all | solution.py:242
  86.7 2.0 %group_product.1 = bf16[1024,256]{1,0:T(8,128)(2,1)S(1)} custom-call(s32[1]{0:T(128)} %bitcast.core_ref, bf16[512,1024]{1,0:T(8,128)(2,1)S(1)} %bitcast.26, bf16[512,1024]{1,0:T(8,128)(2,1)S(1)} %collective-permute-done.4.far_ref, bf16[1024,512]{1,0:T(8,128)(2,1)S(1)} %bitcast.27), custom_call_target="tpu_custom_call" | custom-call | tf_op jit(solution)/shard_map/group_product/pallas_call | solution.py:247
  89.5 7.0 %all-to-all-start.3 = ((bf16[64,16,256]{2,1,0:T(8,128)(2,1)}), bf16[64,16,256]{2,1,0:T(8,128)(2,1)S(1)}, u32[]{:S(2)}, u32[]{:S(2)}) async-start(bf16[64,16,256]{2,1,0:T(8,128)(2,1)} %bitcast.30), calls=%async_computation.3 | async-start | bytes 1048576 | tf_op jit(solution)/shard_map/all_to_all | solution.py:294
  96.6 4.4 %collective-permute-start.10 = (bf16[128,512]{1,0:T(8,128)(2,1)S(1)}, bf16[128,512]{1,0:T(8,128)(2,1)S(1)}, u32[]{:S(2)}, u32[]{:S(2)}) collective-permute-start(bf16[128,512]{1,0:T(8,128)(2,1)S(1)} %pad_maximum_fusion.1.v3_ref), channel_id=1, source_target_pairs={{0,8},{8,16},{16,24},{24,32},{32,40},{40,48},{48,56},{56,64},{64,7... | collective-permute-start | bytes 393224 | tf_op jit(solution)/shard_map/ppermute | solution.py:27
  101.0 2.8 %collective-permute-start.8 = (bf16[128,512]{1,0:T(8,128)(2,1)S(1)}, bf16[128,512]{1,0:T(8,128)(2,1)S(1)}, u32[]{:S(2)}, u32[]{:S(2)}) collective-permute-start(bf16[128,512]{1,0:T(8,128)(2,1)S(1)} %pad_maximum_fusion.1.v3_ref), channel_id=1, source_target_pairs={{0,24},{8,32},{16,40},{24,48},{32,56},{40,64},{48,72},{56,80},{64,... | collective-permute-start | bytes 393224 | tf_op jit(solution)/shard_map/ppermute | solution.py:27
  103.9 3.1 %collective-permute-start.9 = (bf16[128,512]{1,0:T(8,128)(2,1)S(1)}, bf16[128,512]{1,0:T(8,128)(2,1)S(1)}, u32[]{:S(2)}, u32[]{:S(2)}) collective-permute-start(bf16[128,512]{1,0:T(8,128)(2,1)S(1)} %pad_maximum_fusion.1.v3_ref), channel_id=1, source_target_pairs={{0,16},{8,24},{16,32},{24,40},{32,48},{40,56},{48,64},{56,72},{64,... | collective-permute-start | bytes 393224 | tf_op jit(solution)/shard_map/ppermute | solution.py:27
  107.0 5.4 %collective-permute-done.10.v2_ref = bf16[128,512]{1,0:T(8,128)(2,1)S(1)} collective-permute-done((bf16[128,512]{1,0:T(8,128)(2,1)S(1)}, bf16[128,512]{1,0:T(8,128)(2,1)S(1)}, u32[]{:S(2)}, u32[]{:S(2)}) %collective-permute-start.10) | collective-permute-done | bytes 131104 | tf_op jit(solution)/shard_map/ppermute | solution.py:27
  112.3 4.0 %collective-permute-done.8.v0_ref = bf16[128,512]{1,0:T(8,128)(2,1)S(1)} collective-permute-done((bf16[128,512]{1,0:T(8,128)(2,1)S(1)}, bf16[128,512]{1,0:T(8,128)(2,1)S(1)}, u32[]{:S(2)}, u32[]{:S(2)}) %collective-permute-start.8) | collective-permute-done | bytes 131104 | tf_op jit(solution)/shard_map/ppermute | solution.py:27
  116.4 2.4 %collective-permute-done.9.v1_ref = bf16[128,512]{1,0:T(8,128)(2,1)S(1)} collective-permute-done((bf16[128,512]{1,0:T(8,128)(2,1)S(1)}, bf16[128,512]{1,0:T(8,128)(2,1)S(1)}, u32[]{:S(2)}, u32[]{:S(2)}) %collective-permute-start.9) | collective-permute-done | bytes 131104 | tf_op jit(solution)/shard_map/ppermute | solution.py:27
  122.0 2.2 %copy-done.9 = bf16[4,512,1024]{2,1,0:T(8,128)(2,1)S(1)} copy-done((bf16[4,512,1024]{2,1,0:T(8,128)(2,1)S(1)}, bf16[4,512,1024]{2,1,0:T(8,128)(2,1)}, u32[]{:S(2)}) %copy-start.9) | copy-done | bytes 4194328
  124.2 5.3 %key_gradient.1 = (bf16[128,512]{1,0:T(8,128)(2,1)S(1)}, bf16[128,512]{1,0:T(8,128)(2,1)S(1)}, bf16[128,512]{1,0:T(8,128)(2,1)S(1)}, f32[128,512]{1,0:T(8,128)S(1)}) custom-call(bf16[4,512,1024]{2,1,0:T(8,128)(2,1)S(1)} %copy-done.9, bf16[128,4096]{1,0:T(8,128)(2,1)S(1)} %bitcast.34, bf16[128,4096]{1,0:T(8,128)(2,1)S(1)} %bitcast.36, ...), custom_call_target="tpu_custom_call" | custom-call | flops 2147483648 | bytes 8388608 | tf_op jit(solution)/shard_map/key_gradient/pallas_call | solution.py:112
  130.2 14.0 %all-to-all-start.4 = ((bf16[32,16,256]{2,1,0:T(8,128)(2,1)}), bf16[32,16,256]{2,1,0:T(8,128)(2,1)S(1)}, u32[]{:S(2)}, u32[]{:S(2)}) async-start(bf16[32,16,256]{2,1,0:T(8,128)(2,1)} %broadcast_in_dim.8), calls=%async_computation.4 | async-start | bytes 524288 | tf_op jit(solution)/shard_map/all_to_all | solution.py:273
  144.2 1.9 %collective-permute-start.12 = (bf16[128,512]{1,0:T(8,128)(2,1)S(1)}, bf16[128,512]{1,0:T(8,128)(2,1)S(1)}, u32[]{:S(2)}, u32[]{:S(2)}) collective-permute-start(bf16[128,512]{1,0:T(8,128)(2,1)S(1)} %get-tuple-element.48), channel_id=1, source_target_pairs={{8,0},{16,8},{24,16},{32,24},{40,32},{48,40},{56,48},{64,56},{72,6... | collective-permute-start | bytes 393224 | tf_op jit(solution)/shard_map/ppermute | solution.py:27
  146.2 1.3 collective-permute-start.13
  147.5 1.3 collective-permute-start.14
  148.8 6.2 %all-to-all-done.4 = bf16[32,16,256]{2,1,0:T(8,128)(2,1)S(1)} async-done(((bf16[32,16,256]{2,1,0:T(8,128)(2,1)}), bf16[32,16,256]{2,1,0:T(8,128)(2,1)S(1)}, u32[]{:S(2)}, u32[]{:S(2)}) %all-to-all-start.4) | async-done | bytes 262176 | tf_op jit(solution)/shard_map/all_to_all | solution.py:273
  155.0 3.6 %collective-permute-start.15 = (bf16[512,256]{1,0:T(8,128)(2,1)S(1)}, bf16[512,256]{1,0:T(8,128)(2,1)S(1)}, u32[]{:S(2)}, u32[]{:S(2)}) collective-permute-start(bf16[512,256]{1,0:T(8,128)(2,1)S(1)} %bitcast.41), channel_id=1, source_target_pairs={{0,8},{8,0},{1,9},{9,1},{2,10},{10,2},{3,11},{11,3},{4,12},{12,4},... | collective-permute-start | bytes 786440 | tf_op jit(solution)/shard_map/ppermute | solution.py:274
  158.6 2.9 %collective-permute-done.14 = bf16[128,512]{1,0:T(8,128)(2,1)S(1)} collective-permute-done((bf16[128,512]{1,0:T(8,128)(2,1)S(1)}, bf16[128,512]{1,0:T(8,128)(2,1)S(1)}, u32[]{:S(2)}, u32[]{:S(2)}) %collective-permute-start.14) | collective-permute-done | bytes 131104 | tf_op jit(solution)/shard_map/ppermute | solution.py:27
  (46 shorter events, 11.9 us)
Async XLA Ops:
  0.6 22.7 %copy-start.7 = (s32[1,128]{1,0:T(1,128)S(1)}, s32[1,128]{1,0:T(1,128)}, u32[]{:S(2)}) copy-start(s32[1,128]{1,0:T(1,128)} %position_ref.1) | copy-start | bytes 1540
  0.6 1.2 copy-start.1
  1.9 5.9 %copy-start.6 = (bf16[1,128,512]{2,1,0:T(8,128)(2,1)S(1)}, bf16[1,128,512]{2,1,0:T(8,128)(2,1)}, u32[]{:S(2)}) copy-start(bf16[1,128,512]{2,1,0:T(8,128)(2,1)} %param.7) | copy-start | bytes 393220
  1.9 21.5 %copy-start.2 = (bf16[1,128,4096]{2,1,0:T(8,128)(2,1)S(1)}, bf16[1,128,4096]{2,1,0:T(8,128)(2,1)}, u32[]{:S(2)}) copy-start(bf16[1,128,4096]{2,1,0:T(8,128)(2,1)} %param.6) | copy-start | bytes 3145732
  2.9 30.3 %all-to-all-start = ((bf16[4,128,1024]{2,1,0:T(8,128)(2,1)}), bf16[4,128,1024]{2,1,0:T(8,128)(2,1)S(1)}, u32[]{:S(2)}, u32[]{:S(2)}) async-start(bf16[4,128,1024]{2,1,0:T(8,128)(2,1)} %bitcast.2), calls=%async_computation | async-start | bytes 2097152 | tf_op jit(solution)/shard_map/all_to_all | solution.py:204
  7.8 14.1 %collective-permute-start.1 = (bf16[128,512]{1,0:T(8,128)(2,1)S(1)}, bf16[128,512]{1,0:T(8,128)(2,1)S(1)}, u32[]{:S(2)}, u32[]{:S(2)}) collective-permute-start(bf16[128,512]{1,0:T(8,128)(2,1)S(1)} %bitcast.37), channel_id=1, source_target_pairs={{0,24},{8,32},{16,40},{24,48},{32,56},{40,64},{48,72},{56,80},{64,... | collective-permute-start | bytes 393224 | tf_op jit(solution)/shard_map/ppermute | solution.py:27
  14.4 7.5 %collective-permute-start.2 = (bf16[128,512]{1,0:T(8,128)(2,1)S(1)}, bf16[128,512]{1,0:T(8,128)(2,1)S(1)}, u32[]{:S(2)}, u32[]{:S(2)}) collective-permute-start(bf16[128,512]{1,0:T(8,128)(2,1)S(1)} %bitcast.38), channel_id=1, source_target_pairs={{0,16},{8,24},{16,32},{24,40},{32,48},{40,56},{48,64},{56,72},{64,... | collective-permute-start | bytes 393224 | tf_op jit(solution)/shard_map/ppermute | solution.py:27
  18.4 4.9 %collective-permute-start.3 = (bf16[128,512]{1,0:T(8,128)(2,1)S(1)}, bf16[128,512]{1,0:T(8,128)(2,1)S(1)}, u32[]{:S(2)}, u32[]{:S(2)}) collective-permute-start(bf16[128,512]{1,0:T(8,128)(2,1)S(1)} %bitcast.39), channel_id=1, source_target_pairs={{0,8},{8,16},{16,24},{24,32},{32,40},{40,48},{48,56},{56,64},{64,7... | collective-permute-start | bytes 393224 | tf_op jit(solution)/shard_map/ppermute | solution.py:27
  21.2 12.0 %collective-permute-start = (bf16[128,256]{1,0:T(8,128)(2,1)S(1)}, bf16[128,256]{1,0:T(8,128)(2,1)S(1)}, u32[]{:S(2)}, u32[]{:S(2)}) collective-permute-start(bf16[128,256]{1,0:T(8,128)(2,1)S(1)} %dynamic_slice.3), channel_id=1, source_target_pairs={{0,0},{128,1},{256,2},{384,3},{1,4},{129,5},{257,6},{385,7},{8,8},... | collective-permute-start | bytes 196616 | tf_op jit(solution)/shard_map/ppermute | solution.py:211
  23.4 1.2 copy-start.4
  31.3 2.0 %copy-start.8 = (bf16[4,512,1024]{2,1,0:T(8,128)(2,1)}, bf16[4,512,1024]{2,1,0:T(8,128)(2,1)S(1)}, u32[]{:S(2)}) copy-start(bf16[4,512,1024]{2,1,0:T(8,128)(2,1)S(1)} %get-tuple-element.38.weights_ref) | copy-start | bytes 12582916
  33.2 31.4 %collective-permute-start.4 = (bf16[512,1024]{1,0:T(8,128)(2,1)S(1)}, bf16[512,1024]{1,0:T(8,128)(2,1)S(1)}, u32[]{:S(2)}, u32[]{:S(2)}) collective-permute-start(bf16[512,1024]{1,0:T(8,128)(2,1)S(1)} %bitcast.24), channel_id=1, source_target_pairs={{0,8},{8,0},{1,9},{9,1},{2,10},{10,2},{3,11},{11,3},{4,12},{12,4},... | collective-permute-start | bytes 3145736 | tf_op jit(solution)/shard_map/ppermute | solution.py:290
  36.0 28.7 %all-to-all-start.1 = ((bf16[8,128,256]{2,1,0:T(8,128)(2,1)}), bf16[8,128,256]{2,1,0:T(8,128)(2,1)S(1)}, u32[]{:S(2)}, u32[]{:S(2)}) async-start(bf16[8,128,256]{2,1,0:T(8,128)(2,1)} %broadcast_in_dim.6), calls=%async_computation.1 | async-start | bytes 1048576 | tf_op jit(solution)/shard_map/all_to_all | solution.py:216
  46.7 18.8 %collective-permute-start.5 = (bf16[128,512]{1,0:T(8,128)(2,1)}, bf16[128,512]{1,0:T(8,128)(2,1)S(1)}, u32[]{:S(2)}, u32[]{:S(2)}) collective-permute-start(bf16[128,512]{1,0:T(8,128)(2,1)} %get-tuple-element.33), channel_id=1, source_target_pairs={{8,0},{16,8},{24,16},{32,24},{40,32},{48,40},{56,48},{64,56},{72,6... | collective-permute-start | bytes 393224 | tf_op jit(solution)/shard_map/ppermute | solution.py:27
  48.9 16.6 %collective-permute-start.6 = (bf16[128,512]{1,0:T(8,128)(2,1)S(1)}, bf16[128,512]{1,0:T(8,128)(2,1)S(1)}, u32[]{:S(2)}, u32[]{:S(2)}) collective-permute-start(bf16[128,512]{1,0:T(8,128)(2,1)S(1)} %get-tuple-element.34), channel_id=1, source_target_pairs={{16,0},{24,8},{32,16},{40,24},{48,32},{56,40},{64,48},{72,56},{80,... | collective-permute-start | bytes 393224 | tf_op jit(solution)/shard_map/ppermute | solution.py:27
  50.2 15.3 %collective-permute-start.7 = (bf16[128,512]{1,0:T(8,128)(2,1)S(1)}, bf16[128,512]{1,0:T(8,128)(2,1)S(1)}, u32[]{:S(2)}, u32[]{:S(2)}) collective-permute-start(bf16[128,512]{1,0:T(8,128)(2,1)S(1)} %get-tuple-element.35), channel_id=1, source_target_pairs={{24,0},{32,8},{40,16},{48,24},{56,32},{64,40},{72,48},{80,56},{88,... | collective-permute-start | bytes 393224 | tf_op jit(solution)/shard_map/ppermute | solution.py:27
  88.7 0.8 copy-start
  89.5 29.2 %all-to-all-start.3 = ((bf16[64,16,256]{2,1,0:T(8,128)(2,1)}), bf16[64,16,256]{2,1,0:T(8,128)(2,1)S(1)}, u32[]{:S(2)}, u32[]{:S(2)}) async-start(bf16[64,16,256]{2,1,0:T(8,128)(2,1)} %bitcast.30), calls=%async_computation.3 | async-start | bytes 1048576 | tf_op jit(solution)/shard_map/all_to_all | solution.py:294
  96.6 15.7 %collective-permute-start.10 = (bf16[128,512]{1,0:T(8,128)(2,1)S(1)}, bf16[128,512]{1,0:T(8,128)(2,1)S(1)}, u32[]{:S(2)}, u32[]{:S(2)}) collective-permute-start(bf16[128,512]{1,0:T(8,128)(2,1)S(1)} %pad_maximum_fusion.1.v3_ref), channel_id=1, source_target_pairs={{0,8},{8,16},{16,24},{24,32},{32,40},{40,48},{48,56},{56,64},{64,7... | collective-permute-start | bytes 393224 | tf_op jit(solution)/shard_map/ppermute | solution.py:27
  101.0 15.3 %collective-permute-start.8 = (bf16[128,512]{1,0:T(8,128)(2,1)S(1)}, bf16[128,512]{1,0:T(8,128)(2,1)S(1)}, u32[]{:S(2)}, u32[]{:S(2)}) collective-permute-start(bf16[128,512]{1,0:T(8,128)(2,1)S(1)} %pad_maximum_fusion.1.v3_ref), channel_id=1, source_target_pairs={{0,24},{8,32},{16,40},{24,48},{32,56},{40,64},{48,72},{56,80},{64,... | collective-permute-start | bytes 393224 | tf_op jit(solution)/shard_map/ppermute | solution.py:27
  103.9 14.9 %collective-permute-start.9 = (bf16[128,512]{1,0:T(8,128)(2,1)S(1)}, bf16[128,512]{1,0:T(8,128)(2,1)S(1)}, u32[]{:S(2)}, u32[]{:S(2)}) collective-permute-start(bf16[128,512]{1,0:T(8,128)(2,1)S(1)} %pad_maximum_fusion.1.v3_ref), channel_id=1, source_target_pairs={{0,16},{8,24},{16,32},{24,40},{32,48},{40,56},{48,64},{56,72},{64,... | collective-permute-start | bytes 393224 | tf_op jit(solution)/shard_map/ppermute | solution.py:27
  118.8 10.6 %collective-permute-start.11 = (bf16[16,256]{1,0:T(8,128)(2,1)S(1)}, bf16[16,256]{1,0:T(8,128)(2,1)S(1)}, u32[]{:S(2)}, u32[]{:S(2)}) collective-permute-start(bf16[16,256]{1,0:T(8,128)(2,1)S(1)} %multiply_convert_fusion), channel_id=1, source_target_pairs={{0,0},{1,128},{2,256},{3,384},{4,1},{5,129},{6,257},{7,385},{8,8},... | collective-permute-start | bytes 24584 | tf_op jit(solution)/shard_map/ppermute | solution.py:306
  119.5 1.2 copy-start.3
  120.7 1.2 copy-start.5
  122.0 2.2 %copy-start.9 = (bf16[4,512,1024]{2,1,0:T(8,128)(2,1)S(1)}, bf16[4,512,1024]{2,1,0:T(8,128)(2,1)}, u32[]{:S(2)}) copy-start(bf16[4,512,1024]{2,1,0:T(8,128)(2,1)} %copy-done.8) | copy-start | bytes 12582916
  130.2 24.7 %all-to-all-start.4 = ((bf16[32,16,256]{2,1,0:T(8,128)(2,1)}), bf16[32,16,256]{2,1,0:T(8,128)(2,1)S(1)}, u32[]{:S(2)}, u32[]{:S(2)}) async-start(bf16[32,16,256]{2,1,0:T(8,128)(2,1)} %broadcast_in_dim.8), calls=%async_computation.4 | async-start | bytes 524288 | tf_op jit(solution)/shard_map/all_to_all | solution.py:273
  144.2 14.3 %collective-permute-start.12 = (bf16[128,512]{1,0:T(8,128)(2,1)S(1)}, bf16[128,512]{1,0:T(8,128)(2,1)S(1)}, u32[]{:S(2)}, u32[]{:S(2)}) collective-permute-start(bf16[128,512]{1,0:T(8,128)(2,1)S(1)} %get-tuple-element.48), channel_id=1, source_target_pairs={{8,0},{16,8},{24,16},{32,24},{40,32},{48,40},{56,48},{64,56},{72,6... | collective-permute-start | bytes 393224 | tf_op jit(solution)/shard_map/ppermute | solution.py:27
  146.2 12.4 %collective-permute-start.13 = (bf16[128,512]{1,0:T(8,128)(2,1)S(1)}, bf16[128,512]{1,0:T(8,128)(2,1)S(1)}, u32[]{:S(2)}, u32[]{:S(2)}) collective-permute-start(bf16[128,512]{1,0:T(8,128)(2,1)S(1)} %get-tuple-element.49), channel_id=1, source_target_pairs={{16,0},{24,8},{32,16},{40,24},{48,32},{56,40},{64,48},{72,56},{80,... | collective-permute-start | bytes 393224 | tf_op jit(solution)/shard_map/ppermute | solution.py:27
  147.5 14.0 %collective-permute-start.14 = (bf16[128,512]{1,0:T(8,128)(2,1)S(1)}, bf16[128,512]{1,0:T(8,128)(2,1)S(1)}, u32[]{:S(2)}, u32[]{:S(2)}) collective-permute-start(bf16[128,512]{1,0:T(8,128)(2,1)S(1)} %get-tuple-element.50), channel_id=1, source_target_pairs={{24,0},{32,8},{40,16},{48,24},{56,32},{64,40},{72,48},{80,56},{88,... | collective-permute-start | bytes 393224 | tf_op jit(solution)/shard_map/ppermute | solution.py:27
  155.0 7.2 %collective-permute-start.15 = (bf16[512,256]{1,0:T(8,128)(2,1)S(1)}, bf16[512,256]{1,0:T(8,128)(2,1)S(1)}, u32[]{:S(2)}, u32[]{:S(2)}) collective-permute-start(bf16[512,256]{1,0:T(8,128)(2,1)S(1)} %bitcast.41), channel_id=1, source_target_pairs={{0,8},{8,0},{1,9},{9,1},{2,10},{10,2},{3,11},{11,3},{4,12},{12,4},... | collective-permute-start | bytes 786440 | tf_op jit(solution)/shard_map/ppermute | solution.py:274

commit v5 on v4

--- a/solution.py
+++ b/solution.py
@@ -17,14 +17,45 @@
 SPAN_ROWS = (SPAN + 1) * BLOCK
 
 DP = ("x", "z", "c")
+OTHER_CORE = [(0, 1), (1, 0)]
+QUARTER = 1024
+HALF = 256
 masked_value = -1e30
 NT = (((1,), (1,)), ((), ()))
 
 
-def shift(block, distance):
+def shift(block, distance, parities=(0, 1)):
     devices = range(lax.axis_size(DP))
-    route = [(i, i + distance) for i in devices if i + distance in devices]
+    route = [(i, i + distance) for i in devices if i + distance in devices and i % 2 in parities]
     return lax.ppermute(block, DP, route)
+
+
+def swap(block):
+    return lax.ppermute(block, "c", OTHER_CORE)
+
+
+def from_earlier(block):
+    two = shift(block, 2)
+    three = shift(block, 3, (1,))
+    one = shift(block, 1, (0,))
+    return one, two, three, swap(two)
+
+
+def to_earlier(parts, even):
+    third, second, first, _ = parts
+    from_three = shift(third, -3, (0,))
+    across = swap(first)
+    across_third = shift(third, -1, (1,))
+    joined = second.astype(jnp.float32) + jnp.where(even, across_third, across).astype(jnp.float32)
+    from_two = shift(joined.astype(jnp.bfloat16), -2)
+    return from_two, across, from_three
+
+
+def span_rows(core_ref, own_ref, one_ref, two_ref, three_ref, swapped_ref):
+    even = core_ref[0] == 0
+    third = jnp.where(even, three_ref[...], swapped_ref[...])
+    first = jnp.where(even, swapped_ref[...], one_ref[...])
+    return jnp.concatenate([third, two_ref[...], first, own_ref[...]], axis=0)
 
 
 def stacked(ref, pair):
@@ -33,16 +64,14 @@
     return jnp.concatenate([first, second], axis=0)
 
 
-def weights_kernel(
-    position_ref, query_ref, grad_ref, k0_ref, k1_ref, k2_ref, k3_ref, weights_ref, v0_ref, v1_ref, v2_ref, v3_ref
-):
+def weights_kernel(core_ref, position_ref, query_ref, grad_ref, *refs):
     keys_down = lax.broadcasted_iota(jnp.int32, (SPAN_ROWS, BLOCK), 0)
     queries_across = lax.broadcasted_iota(jnp.int32, (SPAN_ROWS, BLOCK), 1)
     offset = SPAN * BLOCK + queries_across - keys_down
     allowed = (offset >= 0) & (offset <= position_ref[...])
     mask = jnp.where(allowed, 0.0, masked_value).astype(jnp.bfloat16)
-    keys = jnp.concatenate([k0_ref[...], k1_ref[...], k2_ref[...], k3_ref[...]], axis=0)
-    keys = jnp.concatenate([keys, mask], axis=1)
+    key_refs, weights_ref, out_refs = refs[:5], refs[5], refs[6:]
+    keys = jnp.concatenate([span_rows(core_ref, *key_refs), mask], axis=1)
     unit = (
         lax.broadcasted_iota(jnp.int32, (PAIR, BLOCK), 0) % BLOCK
         == lax.broadcasted_iota(jnp.int32, (PAIR, BLOCK), 1)
@@ -59,14 +88,13 @@
         low = weights.astype(jnp.bfloat16)
         weights_ref[0, :, pair * PAIR : (pair + 1) * PAIR] = low
         total += jnp.dot(low, stacked(grad_ref, pair), preferred_element_type=jnp.float32)
-    for block, out_ref in enumerate((v0_ref, v1_ref, v2_ref, v3_ref)):
+    for block, out_ref in enumerate(out_refs):
         out_ref[...] = total[block * BLOCK : (block + 1) * BLOCK].astype(out_ref.dtype)
 
 
-def scores_kernel(
-    weights_ref, query_ref, grad_ref, v0_ref, v1_ref, v2_ref, v3_ref, k0_ref, k1_ref, k2_ref, k3_ref
-):
-    values = jnp.concatenate([v0_ref[...], v1_ref[...], v2_ref[...], v3_ref[...]], axis=0)
+def scores_kernel(core_ref, weights_ref, query_ref, grad_ref, *refs):
+    value_refs, out_refs = refs[:5], refs[5:]
+    values = span_rows(core_ref, *value_refs)
     total = jnp.zeros((SPAN_ROWS, HEAD_SIZE), jnp.float32)
     for pair in range(GROUP_WIDTH // 2):
         prob_grad = lax.dot_general(
@@ -77,10 +105,12 @@
         low = (weights * (prob_grad - row_delta)).astype(jnp.bfloat16)
         total += jnp.dot(low, stacked(query_ref, pair), preferred_element_type=jnp.float32)
     total = total * (1.0 / math.sqrt(HEAD_SIZE))
-    for block, out_ref in enumerate((k0_ref, k1_ref, k2_ref, k3_ref)):
+    for block, out_ref in enumerate(out_refs):
         out_ref[...] = total[block * BLOCK : (block + 1) * BLOCK].astype(out_ref.dtype)
 
 
+in_smem = pl.BlockSpec(memory_space=pltpu.SMEM)
+in_vmem = pl.BlockSpec(memory_space=pltpu.VMEM)
 wide = pl.BlockSpec((BLOCK, GROUP_COLUMNS), lambda g: (0, g))
 narrow = pl.BlockSpec((BLOCK, HEAD_SIZE), lambda g: (0, g))
 held = pl.BlockSpec((1, SPAN_ROWS, GROUP_COLUMNS), lambda g: (g, 0, 0))
@@ -92,27 +122,30 @@
 params = pltpu.CompilerParams(vmem_limit_bytes=16 * 1024 * 1024)
 
 
-def attention_weights(position, queries, grads, keys):
+def in_hbm(array):
+    return pltpu.with_memory_space_constraint(array, pltpu.HBM)
+
+
+def attention_weights(core, position, queries, grads, keys):
     return pl.pallas_call(
         weights_kernel,
         grid=(KEY_HEADS,),
-        in_specs=[pl.BlockSpec((1, BLOCK), lambda g: (0, 0)), wide, wide] + [narrow] * 4,
+        in_specs=[in_smem, pl.BlockSpec((1, BLOCK), lambda g: (0, 0)), wide, wide] + [narrow] * 5,
         out_specs=[held] + [narrow] * 4,
-        out_shape=[jax.ShapeDtypeStruct((KEY_HEADS, SPAN_ROWS, GROUP_COLUMNS), jnp.bfloat16)]
-        + gradients,
+        out_shape=[pltpu.HBM((KEY_HEADS, SPAN_ROWS, GROUP_COLUMNS), jnp.bfloat16)] + gradients,
         compiler_params=params,
         cost_estimate=pl.CostEstimate(
             flops=2 * KERNEL_FLOPS, bytes_accessed=8 << 20, transcendentals=SPAN_ROWS * BLOCK * 32
         ),
         name="attention_weights",
-    )(position, queries, grads, *keys)
-
-
-def key_gradient(weights, queries, grads, values):
+    )(core, position, in_hbm(queries), in_hbm(grads), *keys)
+
+
+def key_gradient(core, weights, queries, grads, values):
     return pl.pallas_call(
         scores_kernel,
         grid=(KEY_HEADS,),
-        in_specs=[held, wide, wide] + [narrow] * 4,
+        in_specs=[in_smem, held, wide, wide] + [narrow] * 5,
         out_specs=[narrow] * 4,
         out_shape=gradients,
         compiler_params=params,
@@ -120,23 +153,7 @@
             flops=2 * KERNEL_FLOPS, bytes_accessed=8 << 20, transcendentals=0
         ),
         name="key_gradient",
-    )(weights, queries, grads, *values)
-
-
-def span_of(block):
-    return [shift(block, 3), shift(block, 2), shift(block, 1), block]
-
-
-def owed(parts):
-    total = parts[SPAN]
-    for distance in (1, 2, 3):
-        total = total + shift(parts[SPAN - distance], -distance).astype(jnp.float32)
-    return total.astype(jnp.bfloat16)
-
-
-OTHER_CORE = [(0, 1), (1, 0)]
-QUARTER = 1024
-HALF = 256
+    )(core, in_hbm(weights), in_hbm(queries), in_hbm(grads), *values)
 
 
 def quarters_kernel(rows_ref, out_ref, sems):
@@ -163,9 +180,9 @@
             out_ref[rows, :] = values[x * BLOCK : (x + 1) * BLOCK]
 
 
-def pack_kernel(own_ref, one_ref, two_ref, three_ref, values_ref, out_ref):
-    total = own_ref[...] + one_ref[...].astype(jnp.float32)
-    total = total + two_ref[...].astype(jnp.float32) + three_ref[...].astype(jnp.float32)
+def pack_kernel(core_ref, own_ref, two_ref, across_ref, three_ref, values_ref, out_ref):
+    last = jnp.where(core_ref[0] == 0, across_ref[...], three_ref[...])
+    total = own_ref[...] + two_ref[...].astype(jnp.float32) + last.astype(jnp.float32)
     low = total.astype(jnp.bfloat16)
     for device in range(8):
         core = device % 2
@@ -200,7 +217,7 @@
         scratch_shapes=[pltpu.SemaphoreType.DMA((4,))],
         compiler_params=params,
         name="quarters",
-    )(rows)
+    )(in_hbm(rows))
     return lax.all_to_all(quarters, "x", 0, 0, tiled=True)
 
 
@@ -214,10 +231,6 @@
 def projection_part(piece):
     copies = jnp.broadcast_to(piece[None], (8, BLOCK, HALF)).reshape(8 * BLOCK, HALF)
     return lax.all_to_all(copies, "y", 0, 0, tiled=True)
-
-
-in_smem = pl.BlockSpec(memory_space=pltpu.SMEM)
-in_vmem = pl.BlockSpec(memory_space=pltpu.VMEM)
 
 
 def partial_values(core, near, far, weight):
@@ -231,14 +244,15 @@
     )(core, near, far, weight)
 
 
-def exchange_packed(value_parts, values):
-    received = [shift(value_parts[SPAN - distance], -distance) for distance in (1, 2, 3)]
+def exchange_packed(core, own, received, values):
     packed = pl.pallas_call(
         pack_kernel,
+        in_specs=[in_smem] + [in_vmem] * 5,
+        out_specs=in_vmem,
         out_shape=jax.ShapeDtypeStruct((8 * BLOCK, 2 * HALF), jnp.bfloat16),
         compiler_params=params,
         name="pack",
-    )(value_parts[SPAN], *received, values)
+    )(core, own, *received, values)
     return lax.all_to_all(packed, ("x", "c"), 0, 0, tiled=True)
 
 
@@ -271,7 +285,7 @@
     rows, columns = piece.shape
     copies = jnp.broadcast_to(piece[None], (32, rows, columns)).reshape(32 * rows, columns)
     half = lax.all_to_all(copies, ("x", "z"), 0, 0, tiled=True)
-    other = lax.ppermute(half, "c", OTHER_CORE)
+    other = swap(half)
     first = lax.axis_index("c") == 0
     return jnp.concatenate(
         [jnp.where(first, half, other), jnp.where(first, other, half)], axis=1
@@ -281,24 +295,26 @@
 def per_device(queries, key_rows, out_grad, inputs, w_value, doc_pos):
     queries, keys, grads, rows = queries[0], key_rows[0], out_grad[0], inputs[0]
     core = lax.axis_index("c").astype(jnp.int32).reshape(1)
-    key_span = span_of(keys)
+    even = core[0] == 0
+    key_blocks = from_earlier(keys)
     near = exchange_rows(rows)
     weight = projection_piece(w_value)
-    weights, *value_parts = attention_weights(doc_pos, queries, grads, key_span)
+    weights, *value_parts = attention_weights(core, doc_pos, queries, grads, (keys,) + key_blocks)
     near, weight, value_parts = lax.optimization_barrier((near, weight, value_parts))
 
-    far = lax.ppermute(near, "c", OTHER_CORE)
+    received = to_earlier(value_parts, even)
+    far = swap(near)
     values = partial_values(core, near, far, projection_part(weight))
-    packed = exchange_packed(value_parts, values)
+    packed = exchange_packed(core, value_parts[SPAN], received, values)
     product = group_product(core, near, far, packed)
     pieces = lax.all_to_all(product, ("y", "z"), 0, 0, tiled=True)
 
     parts = packed.reshape(4, 2, BLOCK, 2 * HALF)[..., HALF:].astype(jnp.float32)
     values = jnp.sum(parts, axis=0).astype(jnp.bfloat16)
     values = jnp.concatenate([values[0], values[1]], axis=1)
-    value_span = span_of(values)
-    pieces, value_span = lax.optimization_barrier((pieces, value_span))
-    key_parts = key_gradient(weights, queries, grads, value_span)
+    value_blocks = from_earlier(values)
+    pieces, value_blocks = lax.optimization_barrier((pieces, value_blocks))
+    key_parts = key_gradient(core, weights, queries, grads, (values,) + value_blocks)
 
     pieces = pieces.reshape(64, -1, HALF).astype(jnp.float32)
     token_total = lax.axis_size(("x", "z", "c", "y")) * BLOCK
@@ -306,8 +322,10 @@
     piece = lax.ppermute(piece, ("x", "z", "c", "y"), plane_route())
     piece, key_parts = lax.optimization_barrier((piece, key_parts))
     weight_grad = whole_shard(piece)
-    key_grad = owed(key_parts)
-    return (key_grad[None], weight_grad)
+    two, across, three = to_earlier(key_parts, even)
+    key_grad = key_parts[SPAN] + two.astype(jnp.float32)
+    key_grad = key_grad + jnp.where(even, across, three).astype(jnp.float32)
+    return (key_grad.astype(jnp.bfloat16)[None], weight_grad)
 
 
 def solution(mesh):

time: 164 us -> 190 us (1.16)
  Pallas kernels: 15.9 us -> 50 us
  starting transfers between devices: 75.5 us -> 101 us
  waiting for transfers between devices: 35.5 us -> 13.9 us
  local copies, waits for them, and re-layouts: 12.3 us -> 3.21 us
  blocking collectives: 21.1 us -> 18 us
    pallas_call x1, Pallas kernels: 1.05 us -> 32.9 us  [exchange_rows(): pl.pallas_call(quarters_kernel, in_specs=[pl.BlockSpec(memory_space=pl.AN...]
    ppermute x2 -> x6, starting transfers between devices: 5.52 us -> 24.5 us  [swap(): return lax.ppermute(block, 'c', OTHER_CORE)]
    ppermute x12, waiting for transfers between devices: 16.1 us -> 0.03 us  [shift(): return lax.ppermute(block, DP, route)]
    unnamed x20 -> x6, local copies, waits for them, and re-layouts: 9.84 us -> 0.8 us
    all_to_all x1, starting transfers between devices: 10.7 us -> 15.7 us  [projection_part(): return lax.all_to_all(copies, 'y', 0, 0, tiled=True)]
    all_to_all x1, waiting for transfers between devices: 6.19 us -> 2.23 us  [whole_shard(): half = lax.all_to_all(copies, ('x', 'z'), 0, 0, tiled=True)]
    all_to_all x1, blocking collectives: 21.1 us -> 18 us  [exchange_packed(): return lax.all_to_all(packed, ('x', 'c'), 0, 0, tiled=True)]
    all_to_all x1, waiting for transfers between devices: 13.2 us -> 10.3 us  [projection_part(): return lax.all_to_all(copies, 'y', 0, 0, tiled=True)]
  transfers between devices with their start and end apart: 20 -> 24, of which waited for: 7 -> 4; matrix products, arithmetic and copies ran while one was open for 2% -> 1% of each run, Pallas kernels for 8% -> 8%
where the time goes in v5:
time: 190 us; the launch traced here: 189 us
  starting transfers between devices  101 us (53%)
  Pallas kernels  50 us (26%)
  blocking collectives  18 us (9%)
  waiting for transfers between devices  13.9 us (7%)
  local copies, waits for them, and re-layouts  3.21 us (2%)
  other arithmetic  1.91 us (1%)
    pallas_call x1, Pallas kernels, exchange_rows(): pl.pallas_call(quarters_kernel, in_specs=[pl.BlockSpec(memory_space=pl.AN...  32.9 us
    ppermute x12, starting transfers between devices, shift(): return lax.ppermute(block, DP, route)  31.8 us
    ppermute x6, starting transfers between devices, swap(): return lax.ppermute(block, 'c', OTHER_CORE)  24.5 us
    all_to_all x1, blocking collectives, exchange_packed(): return lax.all_to_all(packed, ('x', 'c'), 0, 0, tiled=True)  18 us
    all_to_all x1, starting transfers between devices, projection_part(): return lax.all_to_all(copies, 'y', 0, 0, tiled=True)  15.7 us
    all_to_all x1, starting transfers between devices, whole_shard(): half = lax.all_to_all(copies, ('x', 'z'), 0, 0, tiled=True)  14.6 us
    all_to_all x1, waiting for transfers between devices, projection_part(): return lax.all_to_all(copies, 'y', 0, 0, tiled=True)  10.3 us
    all_to_all x1, starting transfers between devices, per_device(): pieces = lax.all_to_all(product, ('y', 'z'), 0, 0, tiled=True)  7.75 us
  transfers between devices with their start and end apart: 24, of which 4 were waited for; matrix products, arithmetic and copies ran while one was open for 1% of the time, Pallas kernels for 8%

profile of v5, /device:TPU:1, one launch (start us, length us, event | category | flops | bytes accessed | tf_op | source)
XLA Modules:
  0.0 188.6 jit_solution(15760059316250678343)
XLA Ops:
  0.7 32.9 %quarters.1 = bf16[512,1024]{1,0:T(8,128)(2,1)} custom-call(bf16[128,4096]{1,0:T(8,128)(2,1)} %bitcast.36), custom_call_target="tpu_custom_call" | custom-call | tf_op jit(solution)/shard_map/quarters/pallas_call | solution.py:212
  33.6 4.9 %all-to-all-start = ((bf16[4,128,1024]{2,1,0:T(8,128)(2,1)}), bf16[4,128,1024]{2,1,0:T(8,128)(2,1)S(1)}, u32[]{:S(2)}, u32[]{:S(2)}) async-start(bf16[4,128,1024]{2,1,0:T(8,128)(2,1)} %bitcast.2), calls=%async_computation | async-start | bytes 2097152 | tf_op jit(solution)/shard_map/all_to_all | solution.py:221
  38.4 4.0 %collective-permute-start.2 = (bf16[128,512]{1,0:T(8,128)(2,1)S(1)}, bf16[128,512]{1,0:T(8,128)(2,1)S(1)}, u32[]{:S(2)}, u32[]{:S(2)}) collective-permute-start(bf16[128,512]{1,0:T(8,128)(2,1)S(1)} %bitcast.32), channel_id=1, source_target_pairs={{0,16},{8,24},{16,32},{24,40},{32,48},{40,56},{48,64},{56,72},{64,... | collective-permute-start | bytes 393224 | tf_op jit(solution)/shard_map/ppermute | solution.py:30
  42.4 6.9 %collective-permute-start.3 = (bf16[128,512]{1,0:T(8,128)(2,1)S(1)}, bf16[128,512]{1,0:T(8,128)(2,1)S(1)}, u32[]{:S(2)}, u32[]{:S(2)}) collective-permute-start(bf16[128,512]{1,0:T(8,128)(2,1)S(1)} %bitcast.33), channel_id=1, source_target_pairs={{8,32},{24,48},{40,64},{56,80},{72,96},{88,112},{104,128},{120,144... | collective-permute-start | bytes 393224 | tf_op jit(solution)/shard_map/ppermute | solution.py:30
  49.4 1.3 collective-permute-start.1
  50.7 3.0 %collective-permute-start.4 = (bf16[128,512]{1,0:T(8,128)(2,1)S(1)}, bf16[128,512]{1,0:T(8,128)(2,1)S(1)}, u32[]{:S(2)}, u32[]{:S(2)}) collective-permute-start(bf16[128,512]{1,0:T(8,128)(2,1)S(1)} %collective-permute-done.2.refs_2_), channel_id=1, source_target_pairs={{0,8},{8,0},{1,9},{9,1},{2,10},{10,2},{3,11},{11,3},{4,12},{12,4},... | collective-permute-start | bytes 393224 | tf_op jit(solution)/shard_map/ppermute | solution.py:34
  53.7 0.9 dynamic_slice.3
  55.3 7.6 %attention_weights.1 = (bf16[4,512,1024]{2,1,0:T(8,128)(2,1)}, bf16[128,512]{1,0:T(8,128)(2,1)S(1)}, bf16[128,512]{1,0:T(8,128)(2,1)S(1)}, bf16[128,512]{1,0:T(8,128)(2,1)S(1)}, f32[128,512]{1,0:T(8,128)S(1)}) custom-call(s32[1]{0:T(128)} %bitcast.core_ref, s32[1,128]{1,0:T(1,128)S(1)} %copy-done.2, bf16[128,4096]{1,0:T(8,128)(2,1)} %bitcast.38, ...), custom_call_target="tpu_custom_call" | custom-call | flops 2147483648 | bytes 8388608 | tf_op jit(solution)/shard_map/attention_weights/pallas_call | solution.py:130
  62.9 1.9 %collective-permute-start.5 = (bf16[512,1024]{1,0:T(8,128)(2,1)S(1)}, bf16[512,1024]{1,0:T(8,128)(2,1)S(1)}, u32[]{:S(2)}, u32[]{:S(2)}) collective-permute-start(bf16[512,1024]{1,0:T(8,128)(2,1)S(1)} %bitcast.24), channel_id=1, source_target_pairs={{0,8},{8,0},{1,9},{9,1},{2,10},{10,2},{3,11},{11,3},{4,12},{12,4},... | collective-permute-start | bytes 3145736 | tf_op jit(solution)/shard_map/ppermute | solution.py:34
  65.7 15.7 %all-to-all-start.1 = ((bf16[8,128,256]{2,1,0:T(8,128)(2,1)}), bf16[8,128,256]{2,1,0:T(8,128)(2,1)S(1)}, u32[]{:S(2)}, u32[]{:S(2)}) async-start(bf16[8,128,256]{2,1,0:T(8,128)(2,1)} %broadcast_in_dim.6), calls=%async_computation.1 | async-start | bytes 1048576 | tf_op jit(solution)/shard_map/all_to_all | solution.py:233
  81.3 2.4 %collective-permute-start.7 = (bf16[128,512]{1,0:T(8,128)(2,1)S(1)}, bf16[128,512]{1,0:T(8,128)(2,1)S(1)}, u32[]{:S(2)}, u32[]{:S(2)}) collective-permute-start(bf16[128,512]{1,0:T(8,128)(2,1)S(1)} %get-tuple-element.35), channel_id=1, source_target_pairs={{0,8},{8,0},{1,9},{9,1},{2,10},{10,2},{3,11},{11,3},{4,12},{12,4},... | collective-permute-start | bytes 393224 | tf_op jit(solution)/shard_map/ppermute | solution.py:34
  83.7 2.6 %collective-permute-start.6 = (bf16[128,512]{1,0:T(8,128)(2,1)S(1)}, bf16[128,512]{1,0:T(8,128)(2,1)}, u32[]{:S(2)}, u32[]{:S(2)}) collective-permute-start(bf16[128,512]{1,0:T(8,128)(2,1)S(1)} %get-tuple-element.34), channel_id=1, source_target_pairs={{8,0},{24,16},{40,32},{56,48},{72,64},{88,80},{104,96},{120,112},{... | collective-permute-start | bytes 393224 | tf_op jit(solution)/shard_map/ppermute | solution.py:30
  86.3 1.3 collective-permute-start.9
  87.7 1.3 collective-permute-start.8
  89.0 10.3 %all-to-all-done.1 = bf16[8,128,256]{2,1,0:T(8,128)(2,1)S(1)} async-done(((bf16[8,128,256]{2,1,0:T(8,128)(2,1)}), bf16[8,128,256]{2,1,0:T(8,128)(2,1)S(1)}, u32[]{:S(2)}, u32[]{:S(2)}) %all-to-all-start.1) | async-done | bytes 524320 | tf_op jit(solution)/shard_map/all_to_all | solution.py:233
  100.1 18.0 %all_to_all.52 = bf16[8,128,512]{2,1,0:T(8,128)(2,1)S(1)} all-to-all(bf16[8,128,512]{2,1,0:T(8,128)(2,1)S(1)} %bitcast.29), channel_id=1, replica_groups=mesh['x'=4,'z'=8,'c'=2,'y'=8] {'x','c'}, dimensions={0} | all-to-all | bytes 2097152 | tf_op jit(solution)/shard_map/all_to_all | solution.py:256
  118.1 2.0 %group_product.1 = bf16[1024,256]{1,0:T(8,128)(2,1)S(1)} custom-call(s32[1]{0:T(128)} %bitcast.core_ref, bf16[512,1024]{1,0:T(8,128)(2,1)S(1)} %bitcast.26, bf16[512,1024]{1,0:T(8,128)(2,1)S(1)} %collective-permute-done.5.far_ref, bf16[1024,512]{1,0:T(8,128)(2,1)S(1)} %bitcast.27), custom_call_target="tpu_custom_call" | custom-call | tf_op jit(solution)/shard_map/group_product/pallas_call | solution.py:261
  120.9 7.8 %all-to-all-start.3 = ((bf16[64,16,256]{2,1,0:T(8,128)(2,1)}), bf16[64,16,256]{2,1,0:T(8,128)(2,1)S(1)}, u32[]{:S(2)}, u32[]{:S(2)}) async-start(bf16[64,16,256]{2,1,0:T(8,128)(2,1)} %bitcast.30), calls=%async_computation.3 | async-start | bytes 1048576 | tf_op jit(solution)/shard_map/all_to_all | solution.py:310
  128.8 2.9 %collective-permute-start.11 = (bf16[128,512]{1,0:T(8,128)(2,1)S(1)}, bf16[128,512]{1,0:T(8,128)(2,1)S(1)}, u32[]{:S(2)}, u32[]{:S(2)}) collective-permute-start(bf16[128,512]{1,0:T(8,128)(2,1)S(1)} %pad_maximum_fusion.1.refs_0_), channel_id=1, source_target_pairs={{0,16},{8,24},{16,32},{24,40},{32,48},{40,56},{48,64},{56,72},{64,... | collective-permute-start | bytes 393224 | tf_op jit(solution)/shard_map/ppermute | solution.py:30
  131.7 5.8 %collective-permute-start.12 = (bf16[128,512]{1,0:T(8,128)(2,1)S(1)}, bf16[128,512]{1,0:T(8,128)(2,1)S(1)}, u32[]{:S(2)}, u32[]{:S(2)}) collective-permute-start(bf16[128,512]{1,0:T(8,128)(2,1)S(1)} %pad_maximum_fusion.1.refs_0_), channel_id=1, source_target_pairs={{8,32},{24,48},{40,64},{56,80},{72,96},{88,112},{104,128},{120,144... | collective-permute-start | bytes 393224 | tf_op jit(solution)/shard_map/ppermute | solution.py:30
  137.5 1.3 collective-permute-start.10
  138.8 8.7 %collective-permute-start.13 = (bf16[128,512]{1,0:T(8,128)(2,1)S(1)}, bf16[128,512]{1,0:T(8,128)(2,1)S(1)}, u32[]{:S(2)}, u32[]{:S(2)}) collective-permute-start(bf16[128,512]{1,0:T(8,128)(2,1)S(1)} %collective-permute-done.11.refs_2_), channel_id=1, source_target_pairs={{0,8},{8,0},{1,9},{9,1},{2,10},{10,2},{3,11},{11,3},{4,12},{12,4},... | collective-permute-start | bytes 393224 | tf_op jit(solution)/shard_map/ppermute | solution.py:34
  147.6 0.9 collective-permute-done.13.refs_4_
  149.3 6.6 %key_gradient.1 = (bf16[128,512]{1,0:T(8,128)(2,1)S(1)}, bf16[128,512]{1,0:T(8,128)(2,1)S(1)}, bf16[128,512]{1,0:T(8,128)(2,1)S(1)}, f32[128,512]{1,0:T(8,128)S(1)}) custom-call(s32[1]{0:T(128)} %bitcast.core_ref, bf16[4,512,1024]{2,1,0:T(8,128)(2,1)} %get-tuple-element.38.weights_ref, bf16[128,4096]{1,0:T(8,128)(2,1)} %bitcast.39, ...), custom_call_target="tpu_custom_call" | custom-call | flops 2147483648 | bytes 8388608 | tf_op jit(solution)/shard_map/key_gradient/pallas_call | solution.py:145
  156.6 14.6 %all-to-all-start.4 = ((bf16[32,16,256]{2,1,0:T(8,128)(2,1)}), bf16[32,16,256]{2,1,0:T(8,128)(2,1)S(1)}, u32[]{:S(2)}, u32[]{:S(2)}) async-start(bf16[32,16,256]{2,1,0:T(8,128)(2,1)} %broadcast_in_dim.8), calls=%async_computation.4 | async-start | bytes 524288 | tf_op jit(solution)/shard_map/all_to_all | solution.py:287
  171.2 2.8 %collective-permute-start.16 = (bf16[128,512]{1,0:T(8,128)(2,1)S(1)}, bf16[128,512]{1,0:T(8,128)(2,1)S(1)}, u32[]{:S(2)}, u32[]{:S(2)}) collective-permute-start(bf16[128,512]{1,0:T(8,128)(2,1)S(1)} %get-tuple-element.50), channel_id=1, source_target_pairs={{0,8},{8,0},{1,9},{9,1},{2,10},{10,2},{3,11},{11,3},{4,12},{12,4},... | collective-permute-start | bytes 393224 | tf_op jit(solution)/shard_map/ppermute | solution.py:34
  174.1 1.9 %collective-permute-start.15 = (bf16[128,512]{1,0:T(8,128)(2,1)S(1)}, bf16[128,512]{1,0:T(8,128)(2,1)S(1)}, u32[]{:S(2)}, u32[]{:S(2)}) collective-permute-start(bf16[128,512]{1,0:T(8,128)(2,1)S(1)} %get-tuple-element.49), channel_id=1, source_target_pairs={{8,0},{24,16},{40,32},{56,48},{72,64},{88,80},{104,96},{120,112},{... | collective-permute-start | bytes 393224 | tf_op jit(solution)/shard_map/ppermute | solution.py:30
  176.0 1.3 collective-permute-start.18
  177.4 1.3 collective-permute-start.17
  178.7 2.2 %all-to-all-done.4 = bf16[32,16,256]{2,1,0:T(8,128)(2,1)S(1)} async-done(((bf16[32,16,256]{2,1,0:T(8,128)(2,1)}), bf16[32,16,256]{2,1,0:T(8,128)(2,1)S(1)}, u32[]{:S(2)}, u32[]{:S(2)}) %all-to-all-start.4) | async-done | bytes 262176 | tf_op jit(solution)/shard_map/all_to_all | solution.py:287
  180.9 5.6 %collective-permute-start.19 = (bf16[512,256]{1,0:T(8,128)(2,1)S(1)}, bf16[512,256]{1,0:T(8,128)(2,1)S(1)}, u32[]{:S(2)}, u32[]{:S(2)}) collective-permute-start(bf16[512,256]{1,0:T(8,128)(2,1)S(1)} %bitcast.37), channel_id=1, source_target_pairs={{0,8},{8,0},{1,9},{9,1},{2,10},{10,2},{3,11},{11,3},{4,12},{12,4},... | collective-permute-start | bytes 786440 | tf_op jit(solution)/shard_map/ppermute | solution.py:34
  187.7 0.8 pad_maximum_fusion
  (42 shorter events, 6.0 us)
Async XLA Ops:
  0.6 37.8 %copy-start.1 = (bf16[1,128,512]{2,1,0:T(8,128)(2,1)S(1)}, bf16[1,128,512]{2,1,0:T(8,128)(2,1)}, u32[]{:S(2)}) copy-start(bf16[1,128,512]{2,1,0:T(8,128)(2,1)} %param.7) | copy-start | bytes 393220
  0.6 54.6 %copy-start.2 = (s32[1,128]{1,0:T(1,128)S(1)}, s32[1,128]{1,0:T(1,128)}, u32[]{:S(2)}) copy-start(s32[1,128]{1,0:T(1,128)} %position_ref.1) | copy-start | bytes 1540
  33.6 29.4 %all-to-all-start = ((bf16[4,128,1024]{2,1,0:T(8,128)(2,1)}), bf16[4,128,1024]{2,1,0:T(8,128)(2,1)S(1)}, u32[]{:S(2)}, u32[]{:S(2)}) async-start(bf16[4,128,1024]{2,1,0:T(8,128)(2,1)} %bitcast.2), calls=%async_computation | async-start | bytes 2097152 | tf_op jit(solution)/shard_map/all_to_all | solution.py:221
  38.4 12.2 %collective-permute-start.2 = (bf16[128,512]{1,0:T(8,128)(2,1)S(1)}, bf16[128,512]{1,0:T(8,128)(2,1)S(1)}, u32[]{:S(2)}, u32[]{:S(2)}) collective-permute-start(bf16[128,512]{1,0:T(8,128)(2,1)S(1)} %bitcast.32), channel_id=1, source_target_pairs={{0,16},{8,24},{16,32},{24,40},{32,48},{40,56},{48,64},{56,72},{64,... | collective-permute-start | bytes 393224 | tf_op jit(solution)/shard_map/ppermute | solution.py:30
  42.4 12.8 %collective-permute-start.3 = (bf16[128,512]{1,0:T(8,128)(2,1)S(1)}, bf16[128,512]{1,0:T(8,128)(2,1)S(1)}, u32[]{:S(2)}, u32[]{:S(2)}) collective-permute-start(bf16[128,512]{1,0:T(8,128)(2,1)S(1)} %bitcast.33), channel_id=1, source_target_pairs={{8,32},{24,48},{40,64},{56,80},{72,96},{88,112},{104,128},{120,144... | collective-permute-start | bytes 393224 | tf_op jit(solution)/shard_map/ppermute | solution.py:30
  49.4 5.9 %collective-permute-start.1 = (bf16[128,512]{1,0:T(8,128)(2,1)S(1)}, bf16[128,512]{1,0:T(8,128)(2,1)S(1)}, u32[]{:S(2)}, u32[]{:S(2)}) collective-permute-start(bf16[128,512]{1,0:T(8,128)(2,1)S(1)} %bitcast.34), channel_id=1, source_target_pairs={{0,8},{16,24},{32,40},{48,56},{64,72},{80,88},{96,104},{112,120},{... | collective-permute-start | bytes 393224 | tf_op jit(solution)/shard_map/ppermute | solution.py:30
  50.7 4.6 %collective-permute-start.4 = (bf16[128,512]{1,0:T(8,128)(2,1)S(1)}, bf16[128,512]{1,0:T(8,128)(2,1)S(1)}, u32[]{:S(2)}, u32[]{:S(2)}) collective-permute-start(bf16[128,512]{1,0:T(8,128)(2,1)S(1)} %collective-permute-done.2.refs_2_), channel_id=1, source_target_pairs={{0,8},{8,0},{1,9},{9,1},{2,10},{10,2},{3,11},{11,3},{4,12},{12,4},... | collective-permute-start | bytes 393224 | tf_op jit(solution)/shard_map/ppermute | solution.py:34
  54.6 8.3 %collective-permute-start = (bf16[128,256]{1,0:T(8,128)(2,1)S(1)}, bf16[128,256]{1,0:T(8,128)(2,1)S(1)}, u32[]{:S(2)}, u32[]{:S(2)}) collective-permute-start(bf16[128,256]{1,0:T(8,128)(2,1)S(1)} %dynamic_slice.3), channel_id=1, source_target_pairs={{0,0},{128,1},{256,2},{384,3},{1,4},{129,5},{257,6},{385,7},{8,8},... | collective-permute-start | bytes 196616 | tf_op jit(solution)/shard_map/ppermute | solution.py:228
  62.9 36.4 %collective-permute-start.5 = (bf16[512,1024]{1,0:T(8,128)(2,1)S(1)}, bf16[512,1024]{1,0:T(8,128)(2,1)S(1)}, u32[]{:S(2)}, u32[]{:S(2)}) collective-permute-start(bf16[512,1024]{1,0:T(8,128)(2,1)S(1)} %bitcast.24), channel_id=1, source_target_pairs={{0,8},{8,0},{1,9},{9,1},{2,10},{10,2},{3,11},{11,3},{4,12},{12,4},... | collective-permute-start | bytes 3145736 | tf_op jit(solution)/shard_map/ppermute | solution.py:34
  65.7 33.6 %all-to-all-start.1 = ((bf16[8,128,256]{2,1,0:T(8,128)(2,1)}), bf16[8,128,256]{2,1,0:T(8,128)(2,1)S(1)}, u32[]{:S(2)}, u32[]{:S(2)}) async-start(bf16[8,128,256]{2,1,0:T(8,128)(2,1)} %broadcast_in_dim.6), calls=%async_computation.1 | async-start | bytes 1048576 | tf_op jit(solution)/shard_map/all_to_all | solution.py:233
  81.3 6.3 %collective-permute-start.7 = (bf16[128,512]{1,0:T(8,128)(2,1)S(1)}, bf16[128,512]{1,0:T(8,128)(2,1)S(1)}, u32[]{:S(2)}, u32[]{:S(2)}) collective-permute-start(bf16[128,512]{1,0:T(8,128)(2,1)S(1)} %get-tuple-element.35), channel_id=1, source_target_pairs={{0,8},{8,0},{1,9},{9,1},{2,10},{10,2},{3,11},{11,3},{4,12},{12,4},... | collective-permute-start | bytes 393224 | tf_op jit(solution)/shard_map/ppermute | solution.py:34
  83.7 3.9 %collective-permute-start.6 = (bf16[128,512]{1,0:T(8,128)(2,1)S(1)}, bf16[128,512]{1,0:T(8,128)(2,1)}, u32[]{:S(2)}, u32[]{:S(2)}) collective-permute-start(bf16[128,512]{1,0:T(8,128)(2,1)S(1)} %get-tuple-element.34), channel_id=1, source_target_pairs={{8,0},{24,16},{40,32},{56,48},{72,64},{88,80},{104,96},{120,112},{... | collective-permute-start | bytes 393224 | tf_op jit(solution)/shard_map/ppermute | solution.py:30
  86.3 13.7 %collective-permute-start.9 = (bf16[128,512]{1,0:T(8,128)(2,1)S(1)}, bf16[128,512]{1,0:T(8,128)(2,1)S(1)}, u32[]{:S(2)}, u32[]{:S(2)}) collective-permute-start(bf16[128,512]{1,0:T(8,128)(2,1)S(1)} %get-tuple-element.34), channel_id=1, source_target_pairs={{32,8},{48,24},{64,40},{80,56},{96,72},{112,88},{128,104},{144,120... | collective-permute-start | bytes 393224 | tf_op jit(solution)/shard_map/ppermute | solution.py:30
  87.7 12.3 %collective-permute-start.8 = (bf16[128,512]{1,0:T(8,128)(2,1)S(1)}, bf16[128,512]{1,0:T(8,128)(2,1)S(1)}, u32[]{:S(2)}, u32[]{:S(2)}) collective-permute-start(bf16[128,512]{1,0:T(8,128)(2,1)S(1)} %add_convert_fusion.2), channel_id=1, source_target_pairs={{16,0},{24,8},{32,16},{40,24},{48,32},{56,40},{64,48},{72,56},{80,... | collective-permute-start | bytes 393224 | tf_op jit(solution)/shard_map/ppermute | solution.py:30
  120.1 0.8 copy-start
  120.9 27.6 %all-to-all-start.3 = ((bf16[64,16,256]{2,1,0:T(8,128)(2,1)}), bf16[64,16,256]{2,1,0:T(8,128)(2,1)S(1)}, u32[]{:S(2)}, u32[]{:S(2)}) async-start(bf16[64,16,256]{2,1,0:T(8,128)(2,1)} %bitcast.30), calls=%async_computation.3 | async-start | bytes 1048576 | tf_op jit(solution)/shard_map/all_to_all | solution.py:310
  128.8 10.0 %collective-permute-start.11 = (bf16[128,512]{1,0:T(8,128)(2,1)S(1)}, bf16[128,512]{1,0:T(8,128)(2,1)S(1)}, u32[]{:S(2)}, u32[]{:S(2)}) collective-permute-start(bf16[128,512]{1,0:T(8,128)(2,1)S(1)} %pad_maximum_fusion.1.refs_0_), channel_id=1, source_target_pairs={{0,16},{8,24},{16,32},{24,40},{32,48},{40,56},{48,64},{56,72},{64,... | collective-permute-start | bytes 393224 | tf_op jit(solution)/shard_map/ppermute | solution.py:30
  131.7 15.8 %collective-permute-start.12 = (bf16[128,512]{1,0:T(8,128)(2,1)S(1)}, bf16[128,512]{1,0:T(8,128)(2,1)S(1)}, u32[]{:S(2)}, u32[]{:S(2)}) collective-permute-start(bf16[128,512]{1,0:T(8,128)(2,1)S(1)} %pad_maximum_fusion.1.refs_0_), channel_id=1, source_target_pairs={{8,32},{24,48},{40,64},{56,80},{72,96},{88,112},{104,128},{120,144... | collective-permute-start | bytes 393224 | tf_op jit(solution)/shard_map/ppermute | solution.py:30
  137.5 10.1 %collective-permute-start.10 = (bf16[128,512]{1,0:T(8,128)(2,1)S(1)}, bf16[128,512]{1,0:T(8,128)(2,1)S(1)}, u32[]{:S(2)}, u32[]{:S(2)}) collective-permute-start(bf16[128,512]{1,0:T(8,128)(2,1)S(1)} %pad_maximum_fusion.1.refs_0_), channel_id=1, source_target_pairs={{0,8},{16,24},{32,40},{48,56},{64,72},{80,88},{96,104},{112,120},{... | collective-permute-start | bytes 393224 | tf_op jit(solution)/shard_map/ppermute | solution.py:30
  138.8 9.7 %collective-permute-start.13 = (bf16[128,512]{1,0:T(8,128)(2,1)S(1)}, bf16[128,512]{1,0:T(8,128)(2,1)S(1)}, u32[]{:S(2)}, u32[]{:S(2)}) collective-permute-start(bf16[128,512]{1,0:T(8,128)(2,1)S(1)} %collective-permute-done.11.refs_2_), channel_id=1, source_target_pairs={{0,8},{8,0},{1,9},{9,1},{2,10},{10,2},{3,11},{11,3},{4,12},{12,4},... | collective-permute-start | bytes 393224 | tf_op jit(solution)/shard_map/ppermute | solution.py:34
  148.6 7.3 %collective-permute-start.14 = (bf16[16,256]{1,0:T(8,128)(2,1)S(1)}, bf16[16,256]{1,0:T(8,128)(2,1)S(1)}, u32[]{:S(2)}, u32[]{:S(2)}) collective-permute-start(bf16[16,256]{1,0:T(8,128)(2,1)S(1)} %multiply_convert_fusion), channel_id=1, source_target_pairs={{0,0},{1,128},{2,256},{3,384},{4,1},{5,129},{6,257},{7,385},{8,8},... | collective-permute-start | bytes 24584 | tf_op jit(solution)/shard_map/ppermute | solution.py:322
  156.6 24.3 %all-to-all-start.4 = ((bf16[32,16,256]{2,1,0:T(8,128)(2,1)}), bf16[32,16,256]{2,1,0:T(8,128)(2,1)S(1)}, u32[]{:S(2)}, u32[]{:S(2)}) async-start(bf16[32,16,256]{2,1,0:T(8,128)(2,1)} %broadcast_in_dim.8), calls=%async_computation.4 | async-start | bytes 524288 | tf_op jit(solution)/shard_map/all_to_all | solution.py:287
  171.2 6.1 %collective-permute-start.16 = (bf16[128,512]{1,0:T(8,128)(2,1)S(1)}, bf16[128,512]{1,0:T(8,128)(2,1)S(1)}, u32[]{:S(2)}, u32[]{:S(2)}) collective-permute-start(bf16[128,512]{1,0:T(8,128)(2,1)S(1)} %get-tuple-element.50), channel_id=1, source_target_pairs={{0,8},{8,0},{1,9},{9,1},{2,10},{10,2},{3,11},{11,3},{4,12},{12,4},... | collective-permute-start | bytes 393224 | tf_op jit(solution)/shard_map/ppermute | solution.py:34
  174.1 3.2 %collective-permute-start.15 = (bf16[128,512]{1,0:T(8,128)(2,1)S(1)}, bf16[128,512]{1,0:T(8,128)(2,1)S(1)}, u32[]{:S(2)}, u32[]{:S(2)}) collective-permute-start(bf16[128,512]{1,0:T(8,128)(2,1)S(1)} %get-tuple-element.49), channel_id=1, source_target_pairs={{8,0},{24,16},{40,32},{56,48},{72,64},{88,80},{104,96},{120,112},{... | collective-permute-start | bytes 393224 | tf_op jit(solution)/shard_map/ppermute | solution.py:30
  176.0 10.5 %collective-permute-start.18 = (bf16[128,512]{1,0:T(8,128)(2,1)S(1)}, bf16[128,512]{1,0:T(8,128)(2,1)S(1)}, u32[]{:S(2)}, u32[]{:S(2)}) collective-permute-start(bf16[128,512]{1,0:T(8,128)(2,1)S(1)} %get-tuple-element.49), channel_id=1, source_target_pairs={{32,8},{48,24},{64,40},{80,56},{96,72},{112,88},{128,104},{144,120... | collective-permute-start | bytes 393224 | tf_op jit(solution)/shard_map/ppermute | solution.py:30
  177.4 9.2 %collective-permute-start.17 = (bf16[128,512]{1,0:T(8,128)(2,1)S(1)}, bf16[128,512]{1,0:T(8,128)(2,1)S(1)}, u32[]{:S(2)}, u32[]{:S(2)}) collective-permute-start(bf16[128,512]{1,0:T(8,128)(2,1)S(1)} %add_convert_fusion.1), channel_id=1, source_target_pairs={{16,0},{24,8},{32,16},{40,24},{48,32},{56,40},{64,48},{72,56},{80,... | collective-permute-start | bytes 393224 | tf_op jit(solution)/shard_map/ppermute | solution.py:30
  180.9 6.8 %collective-permute-start.19 = (bf16[512,256]{1,0:T(8,128)(2,1)S(1)}, bf16[512,256]{1,0:T(8,128)(2,1)S(1)}, u32[]{:S(2)}, u32[]{:S(2)}) collective-permute-start(bf16[512,256]{1,0:T(8,128)(2,1)S(1)} %bitcast.37), channel_id=1, source_target_pairs={{0,8},{8,0},{1,9},{9,1},{2,10},{10,2},{3,11},{11,3},{4,12},{12,4},... | collective-permute-start | bytes 786440 | tf_op jit(solution)/shard_map/ppermute | solution.py:34

commit v6 on v4

v6 whole, which is shorter than its diff:
```python
import math

import jax
import jax.numpy as jnp
from jax import lax
from jax.experimental import pallas as pl
from jax.experimental.pallas import tpu as pltpu
from jax.sharding import Mesh, PartitionSpec as P

GROUP_WIDTH = 8
HEAD_SIZE = 128
SPAN = 3
BLOCK = 128
PAIR = 2 * HEAD_SIZE
GROUP_COLUMNS = GROUP_WIDTH * HEAD_SIZE
SPAN_ROWS = (SPAN + 1) * BLOCK
HEADS = 2
QUARTER = 1024
HALF = 256

DP = ("x", "z", "c")
ALL = ("x", "z", "c", "y")
OTHER_CORE = [(0, 1), (1, 0)]
masked_value = -1e30
NT = (((1,), (1,)), ((), ()))
TN = (((0,), (0,)), ((), ()))


def shift(block, chips):
    devices = range(lax.axis_size(DP))
    route = [(i, i + 2 * chips) for i in devices if i + 2 * chips in devices]
    return lax.ppermute(block, DP, route)


def swap(block):
    return lax.ppermute(block, "c", OTHER_CORE)


def plane_route():
    route = []
    for x in range(4):
        for z in range(8):
            for c in range(2):
                for y in range(8):
                    source = ((x * 8 + z) * 2 + c) * 8 + y
                    target = (((y % 4) * 8 + z) * 2 + c) * 8 + 2 * x + y // 4
                    route.append((source, target))
    return route


def in_hbm(array):
    return pltpu.with_memory_space_constraint(array, pltpu.HBM)


def span_blocks(chip_blocks):
    return shift(chip_blocks[BLOCK:], 2), shift(chip_blocks, 1), chip_blocks


def stacked(ref, pair):
    first = ref[:, pair * PAIR : pair * PAIR + HEAD_SIZE]
    second = ref[:, pair * PAIR + HEAD_SIZE : (pair + 1) * PAIR]
    return jnp.concatenate([first, second], axis=0)


def rows_at(block, count):
    return pl.ds(pl.multiple_of(block * BLOCK, BLOCK), count * BLOCK)


def store_gradients(total, out_refs):
    start = 0
    for out_ref in out_refs:
        rows = out_ref.shape[0]
        out_ref[...] = total[start : start + rows, :].astype(out_ref.dtype)
        start += rows


def weights_kernel(
    core_ref, own_position, other_position, own_query, other_query, own_grad, other_grad, *refs
):
    key_refs, weights_ref, out_refs, span_ref, total_ref = refs[:3], refs[3], refs[4:7], refs[7], refs[8]
    start = 0
    for key_ref in key_refs:
        span_ref[start : start + key_ref.shape[0], :] = key_ref[...]
        start += key_ref.shape[0]
    total_ref[...] = jnp.zeros_like(total_ref)
    keys_down = lax.broadcasted_iota(jnp.int32, (SPAN_ROWS, BLOCK), 0)
    queries_across = lax.broadcasted_iota(jnp.int32, (SPAN_ROWS, BLOCK), 1)
    offset = SPAN * BLOCK + queries_across - keys_down
    unit = (
        lax.broadcasted_iota(jnp.int32, (PAIR, BLOCK), 0) % BLOCK
        == lax.broadcasted_iota(jnp.int32, (PAIR, BLOCK), 1)
    )
    unit = jnp.where(unit, 1.0, 0.0).astype(jnp.bfloat16)
    score_scale = 1.0 / math.sqrt(HEAD_SIZE)
    sides = (
        (core_ref[0], own_position, own_query, own_grad),
        (1 - core_ref[0], other_position, other_query, other_grad),
    )
    for side, (block, position_ref, query_ref, grad_ref) in enumerate(sides):
        allowed = (offset >= 0) & (offset <= position_ref[...])
        mask = jnp.where(allowed, 0.0, masked_value).astype(jnp.bfloat16)
        keys = jnp.concatenate([span_ref[rows_at(block, SPAN + 1), :], mask], axis=1)
        total = jnp.zeros((SPAN_ROWS, HEAD_SIZE), jnp.float32)
        for pair in range(GROUP_WIDTH // 2):
            heads = jnp.concatenate([stacked(query_ref, pair), unit], axis=1)
            scores = lax.dot_general(keys, heads, NT, preferred_element_type=jnp.float32)
            top = jnp.max(scores, axis=0, keepdims=True)
            weights = jnp.exp((scores - top) * score_scale)
            weights = weights * (1.0 / jnp.sum(weights, axis=0, keepdims=True))
            low = weights.astype(jnp.bfloat16)
            weights_ref[0, side, :, pair * PAIR : (pair + 1) * PAIR] = low
            total += jnp.dot(low, stacked(grad_ref, pair), preferred_element_type=jnp.float32)
        total_ref[rows_at(block, SPAN + 1), :] += total
    store_gradients(total_ref[...], out_refs)


def scores_kernel(core_ref, weights_ref, own_query, other_query, own_grad, other_grad, *refs):
    value_refs, out_refs, span_ref, total_ref = refs[:3], refs[3:6], refs[6], refs[7]
    start = 0
    for value_ref in value_refs:
        span_ref[start : start + value_ref.shape[0], :] = value_ref[...]
        start += value_ref.shape[0]
    total_ref[...] = jnp.zeros_like(total_ref)
    sides = ((core_ref[0], own_query, own_grad), (1 - core_ref[0], other_query, other_grad))
    for side, (block, query_ref, grad_ref) in enumerate(sides):
        values = span_ref[rows_at(block, SPAN + 1), :]
        total = jnp.zeros((SPAN_ROWS, HEAD_SIZE), jnp.float32)
        for pair in range(GROUP_WIDTH // 2):
            prob_grad = lax.dot_general(
                values, stacked(grad_ref, pair), NT, preferred_element_type=jnp.float32
            )
            weights = weights_ref[0, side, :, pair * PAIR : (pair + 1) * PAIR].astype(jnp.float32)
            row_delta = jnp.sum(weights * prob_grad, axis=0, keepdims=True)
            low = (weights * (prob_grad - row_delta)).astype(jnp.bfloat16)
            total += jnp.dot(low, stacked(query_ref, pair), preferred_element_type=jnp.float32)
        total_ref[rows_at(block, SPAN + 1), :] += total
    store_gradients(total_ref[...] * (1.0 / math.sqrt(HEAD_SIZE)), out_refs)


in_smem = pl.BlockSpec(memory_space=pltpu.SMEM)
in_vmem = pl.BlockSpec(memory_space=pltpu.VMEM)
wide = pl.BlockSpec((BLOCK, GROUP_COLUMNS), lambda g, core: (0, HEADS * core[0] + g))
held = pl.BlockSpec((1, 2, SPAN_ROWS, GROUP_COLUMNS), lambda g, core: (g, 0, 0, 0))
position_spec = pl.BlockSpec((1, BLOCK), lambda g, core: (0, 0))
span_specs = [
    pl.BlockSpec((rows, HEAD_SIZE), lambda g, core: (0, g)) for rows in (BLOCK, 2 * BLOCK, 2 * BLOCK)
]
gradients = [
    jax.ShapeDtypeStruct((rows, HALF), kind)
    for rows, kind in (
        (BLOCK, jnp.bfloat16),
        (2 * BLOCK, jnp.bfloat16),
        (2 * BLOCK, jnp.float32),
    )
]
span_scratch = [
    pltpu.VMEM((SPAN_ROWS + BLOCK, HEAD_SIZE), jnp.bfloat16),
    pltpu.VMEM((SPAN_ROWS + BLOCK, HEAD_SIZE), jnp.float32),
]
KERNEL_FLOPS = 2 * 2 * SPAN_ROWS * BLOCK * HEADS * 2 * GROUP_COLUMNS
params = pltpu.CompilerParams(vmem_limit_bytes=20 * 1024 * 1024)


def attention_weights(core, positions, queries, grads, keys):
    return pl.pallas_call(
        weights_kernel,
        grid_spec=pltpu.PrefetchScalarGridSpec(
            num_scalar_prefetch=1,
            grid=(HEADS,),
            in_specs=[position_spec] * 2 + [wide] * 4 + span_specs,
            out_specs=[held] + span_specs,
            scratch_shapes=span_scratch,
        ),
        out_shape=[pltpu.HBM((HEADS, 2, SPAN_ROWS, GROUP_COLUMNS), jnp.bfloat16)] + gradients,
        compiler_params=params,
        cost_estimate=pl.CostEstimate(
            flops=2 * KERNEL_FLOPS, bytes_accessed=8 << 20, transcendentals=SPAN_ROWS * BLOCK * 32
        ),
        name="attention_weights",
    )(core, *positions, *queries, *grads, *keys)


def key_gradient(core, weights, queries, grads, values):
    return pl.pallas_call(
        scores_kernel,
        grid_spec=pltpu.PrefetchScalarGridSpec(
            num_scalar_prefetch=1,
            grid=(HEADS,),
            in_specs=[held] + [wide] * 4 + span_specs,
            out_specs=span_specs,
            scratch_shapes=span_scratch,
        ),
        out_shape=gradients,
        compiler_params=params,
        cost_estimate=pl.CostEstimate(
            flops=2 * KERNEL_FLOPS, bytes_accessed=8 << 20, transcendentals=0
        ),
        name="key_gradient",
    )(core, in_hbm(weights), *queries, *grads, *values)


def quarters_kernel(rows_ref, out_ref, sems):
    copies = [
        pltpu.make_async_copy(
            rows_ref.at[:, pl.ds(x * QUARTER, QUARTER)],
            out_ref.at[pl.ds(x * BLOCK, BLOCK), :],
            sems.at[x],
        )
        for x in range(4)
    ]
    for copy in copies:
        copy.start()
    for copy in copies:
        copy.wait()


def join_kernel(core_ref, own_ref, other_ref, out_ref):
    core = core_ref[0]
    for ref, block in ((own_ref, core), (other_ref, 1 - core)):
        half = jnp.where(core == 0, ref[:, :HALF], ref[:, HALF:])
        out_ref[rows_at(block, 1), :] = half


def partial_values_kernel(core_ref, near_ref, far_ref, weight_ref, out_ref):
    for rows_ref, core in ((near_ref, core_ref[0]), (far_ref, 1 - core_ref[0])):
        values = jnp.dot(rows_ref[...], weight_ref[...], preferred_element_type=jnp.float32)
        values = values.astype(jnp.bfloat16)
        for x in range(4):
            out_ref[rows_at(2 * x + core, 1), :] = values[x * BLOCK : (x + 1) * BLOCK]


def pack_kernel(two_ref, one_ref, own_ref, values_ref, out_ref):
    total = own_ref[...] + one_ref[...].astype(jnp.float32)
    last = total[BLOCK:] + two_ref[...].astype(jnp.float32)
    low = jnp.concatenate([total[:BLOCK], last], axis=0).astype(jnp.bfloat16)
    for x in range(4):
        rows = slice(x * 2 * BLOCK, (x + 1) * 2 * BLOCK)
        out_ref[rows, :HALF] = low
        out_ref[rows, HALF:] = values_ref[rows, :]


def product_kernel(core_ref, near_ref, far_ref, grads_ref, out_ref):
    total = None
    for rows_ref, core in ((near_ref, core_ref[0]), (far_ref, 1 - core_ref[0])):
        grads = [grads_ref[rows_at(2 * x + core, 1), :HALF] for x in range(4)]
        part = lax.dot_general(
            jnp.concatenate(grads, axis=0), rows_ref[...], TN, preferred_element_type=jnp.float32
        )
        total = part if total is None else total + part
    out_ref[...] = total.T.astype(jnp.bfloat16)


def column_quarters(rows):
    return pl.pallas_call(
        quarters_kernel,
        in_specs=[pl.BlockSpec(memory_space=pl.ANY)],
        out_specs=pl.BlockSpec(memory_space=pl.ANY),
        out_shape=jax.ShapeDtypeStruct((4 * BLOCK, QUARTER), jnp.bfloat16),
        scratch_shapes=[pltpu.SemaphoreType.DMA((4,))],
        compiler_params=params,
        name="quarters",
    )(rows)


def join_halves(core, own, other):
    return pl.pallas_call(
        join_kernel,
        in_specs=[in_smem, in_vmem, in_vmem],
        out_specs=in_vmem,
        out_shape=jax.ShapeDtypeStruct((2 * BLOCK, HALF), jnp.bfloat16),
        compiler_params=params,
        name="join_halves",
    )(core, own, other)


def projection_piece(w_value):
    route = [(target, source) for source, target in plane_route()]
    start = (lax.axis_index("x") * BLOCK, lax.axis_index("c") * HALF)
    return lax.ppermute(lax.dynamic_slice(w_value, start, (BLOCK, HALF)), ALL, route)


def projection_part(piece):
    copies = jnp.broadcast_to(piece[None], (8, BLOCK, HALF)).reshape(8 * BLOCK, HALF)
    return lax.all_to_all(copies, "y", 0, 0, tiled=True)


def partial_values(core, near, far, weight):
    return pl.pallas_call(
        partial_values_kernel,
        in_specs=[in_smem, in_vmem, in_vmem, in_vmem],
        out_specs=in_vmem,
        out_shape=jax.ShapeDtypeStruct((8 * BLOCK, HALF), jnp.bfloat16),
        compiler_params=params,
        name="partial_values",
    )(core, near, far, weight)


def exchange_packed(two, one, own, values):
    packed = pl.pallas_call(
        pack_kernel,
        in_specs=[in_vmem] * 4,
        out_specs=in_vmem,
        out_shape=jax.ShapeDtypeStruct((8 * BLOCK, 2 * HALF), jnp.bfloat16),
        compiler_params=params,
        name="pack",
    )(two, one, own, values)
    return lax.all_to_all(packed, "x", 0, 0, tiled=True)


def group_product(core, near, far, packed):
    rows = pl.BlockSpec((4 * BLOCK, HALF), lambda part: (0, part))
    return pl.pallas_call(
        product_kernel,
        grid=(QUARTER // HALF,),
        in_specs=[in_smem, rows, rows, pl.BlockSpec((8 * BLOCK, 2 * HALF), lambda part: (0, 0))],
        out_specs=pl.BlockSpec((HALF, HALF), lambda part: (part, 0)),
        out_shape=jax.ShapeDtypeStruct((QUARTER, HALF), jnp.bfloat16),
        compiler_params=params,
        name="group_product",
    )(core, near, far, packed)


def whole_shard(piece, even):
    rows, columns = piece.shape
    copies = jnp.broadcast_to(piece[None], (32, rows, columns)).reshape(32 * rows, columns)
    half = lax.all_to_all(copies, ("x", "z"), 0, 0, tiled=True)
    return both_halves(half, swap(half), even)


def both_halves(half, other, even):
    return jnp.concatenate([jnp.where(even, half, other), jnp.where(even, other, half)], axis=1)


def per_device(queries, key_rows, out_grad, inputs, w_value, doc_pos):
    queries, keys, grads, rows = queries[0], key_rows[0], out_grad[0], inputs[0]
    core = lax.axis_index("c").astype(jnp.int32).reshape(1)
    even = core[0] == 0
    weight = projection_piece(w_value)
    other_keys = swap(keys)
    near = lax.all_to_all(column_quarters(rows), "x", 0, 0, tiled=True)
    both_queries = (in_hbm(queries), swap(queries))
    both_grads = (in_hbm(grads), swap(grads))
    positions = (doc_pos, swap(doc_pos))
    other_keys, weight = lax.optimization_barrier((other_keys, weight))
    key_span = span_blocks(join_halves(core, keys, other_keys))
    weights, *value_parts = attention_weights(core, positions, both_queries, both_grads, key_span)
    near, weight, value_parts = lax.optimization_barrier((near, weight, value_parts))

    two, one, own = value_parts
    two, one = shift(two, -2), shift(one, -1)
    far = swap(near)
    values = partial_values(core, near, far, projection_part(weight))
    packed = exchange_packed(two, one, own, values)
    product = group_product(core, near, far, packed)
    pieces = lax.all_to_all(product, ("y", "z"), 0, 0, tiled=True)

    parts = packed.reshape(4, 2 * BLOCK, 2 * HALF)[:, :, HALF:].astype(jnp.float32)
    value_span = span_blocks(jnp.sum(parts, axis=0).astype(jnp.bfloat16))
    pieces, value_span = lax.optimization_barrier((pieces, value_span))
    key_parts = key_gradient(core, weights, both_queries, both_grads, value_span)

    pieces = pieces.reshape(64, -1, HALF).astype(jnp.float32)
    token_total = lax.axis_size(ALL) * BLOCK
    piece = (jnp.sum(pieces, axis=0) * (1.0 / math.sqrt(token_total))).astype(jnp.bfloat16)
    piece = lax.ppermute(piece, ALL, plane_route())
    piece, key_parts = lax.optimization_barrier((piece, key_parts))
    weight_grad = whole_shard(piece, even)

    two, one, own = key_parts
    two, one = shift(two, -2).astype(jnp.float32), shift(one, -1).astype(jnp.float32)
    first = (own[:BLOCK] + one[:BLOCK]).astype(jnp.bfloat16)
    second = (own[BLOCK:] + one[BLOCK:] + two).astype(jnp.bfloat16)
    received = swap(jnp.where(even, second, first))
    key_grad = both_halves(jnp.where(even, first, second), received, even)
    return (key_grad[None], weight_grad)


def solution(mesh):
    mesh = Mesh(mesh.devices.reshape(4, 8, 2, 8), ("x", "z", "c", "y"))
    tokens = P("y", DP, None)
    return jax.shard_map(
        per_device,
        mesh=mesh,
        in_specs=(tokens, tokens, tokens, tokens, P("y", None), P("y", DP)),
        out_specs=(tokens, P("y", None)),
        check_vma=False,
    )
```

time: 164 us -> 178 us (1.085)
  starting transfers between devices: 75.5 us -> 86.5 us
  Pallas kernels: 15.9 us -> 19.3 us
  local copies, waits for them, and re-layouts: 12.3 us -> 8.95 us
  blocking collectives: 21.1 us -> 23.2 us
    ppermute x4 -> x9, starting transfers between devices: 6.83 us -> 25.3 us  [the longest x7 23.9 us: swap(): return lax.ppermute(block, 'c', OTHER_CORE)]
    ppermute x12 -> x8, starting transfers between devices: 32.2 us -> 17.3 us  [shift(): return lax.ppermute(block, DP, route)]
    all_to_all x1, waiting for transfers between devices: 6.19 us -> 0.01 us  [whole_shard(): half = lax.all_to_all(copies, ('x', 'z'), 0, 0, tiled=True)]
    all_to_all x1, starting transfers between devices: 10.7 us -> 16.7 us  [projection_part(): return lax.all_to_all(copies, 'y', 0, 0, tiled=True)]
    unnamed x20, local copies, waits for them, and re-layouts: 9.84 us -> 5.7 us
    all_to_all x1, starting transfers between devices: 14 us -> 17.7 us  [whole_shard(): half = lax.all_to_all(copies, ('x', 'z'), 0, 0, tiled=True)]
    pallas_call x4 -> x5, Pallas kernels: 13.2 us -> 16.6 us  [the longest x1 8.61 us: attention_weights(): pl.pallas_call(weights_kernel, grid_spec=pltpu.PrefetchScalarGridSpec(num...]
    ppermute x12 -> x8, waiting for transfers between devices: 16.1 us -> 19.2 us  [shift(): return lax.ppermute(block, DP, route)]
  transfers between devices with their start and end apart: 20 -> 21, of which waited for: 7 -> 6; matrix products, arithmetic and copies ran while one was open for 2% -> 2% of each run, Pallas kernels for 8% -> 10%
where the time goes in v6:
time: 178 us; the launch traced here: 177 us
  starting transfers between devices  86.5 us (49%)
  waiting for transfers between devices  36.2 us (20%)
  blocking collectives  23.2 us (13%)
  Pallas kernels  19.3 us (11%)
  local copies, waits for them, and re-layouts  8.95 us (5%)
  other arithmetic  1.81 us (1%)
    ppermute x7, starting transfers between devices, swap(): return lax.ppermute(block, 'c', OTHER_CORE)  23.9 us
    all_to_all x1, blocking collectives, exchange_packed(): return lax.all_to_all(packed, 'x', 0, 0, tiled=True)  23.2 us
    ppermute x8, waiting for transfers between devices, shift(): return lax.ppermute(block, DP, route)  19.2 us
    all_to_all x1, starting transfers between devices, whole_shard(): half = lax.all_to_all(copies, ('x', 'z'), 0, 0, tiled=True)  17.7 us
    ppermute x8, starting transfers between devices, shift(): return lax.ppermute(block, DP, route)  17.3 us
    all_to_all x1, starting transfers between devices, projection_part(): return lax.all_to_all(copies, 'y', 0, 0, tiled=True)  16.7 us
    all_to_all x1, waiting for transfers between devices, projection_part(): return lax.all_to_all(copies, 'y', 0, 0, tiled=True)  15.4 us
    pallas_call x1, Pallas kernels, attention_weights(): pl.pallas_call(weights_kernel, grid_spec=pltpu.PrefetchScalarGridSpec(num...  8.61 us
  transfers between devices with their start and end apart: 21, of which 6 were waited for; matrix products, arithmetic and copies ran while one was open for 2% of the time, Pallas kernels for 10%

profile of v6, /device:TPU:1, one launch (start us, length us, event | category | flops | bytes accessed | tf_op | source)
XLA Modules:
  0.0 177.0 jit_solution(1886188613401239319)
XLA Ops:
  0.6 8.8 %collective-permute-start.3 = (bf16[128,4096]{1,0:T(8,128)(2,1)}, bf16[128,4096]{1,0:T(8,128)(2,1)S(1)}, u32[]{:S(2)}, u32[]{:S(2)}) collective-permute-start(bf16[128,4096]{1,0:T(8,128)(2,1)} %bitcast.29), channel_id=1, source_target_pairs={{0,8},{8,0},{1,9},{9,1},{2,10},{10,2},{3,11},{11,3},{4,12},{12,4},... | collective-permute-start | bytes 3145736 | tf_op jit(solution)/shard_map/ppermute | solution.py:36
  9.4 1.9 %collective-permute-start.4 = (bf16[128,4096]{1,0:T(8,128)(2,1)}, bf16[128,4096]{1,0:T(8,128)(2,1)S(1)}, u32[]{:S(2)}, u32[]{:S(2)}) collective-permute-start(bf16[128,4096]{1,0:T(8,128)(2,1)} %bitcast.32), channel_id=1, source_target_pairs={{0,8},{8,0},{1,9},{9,1},{2,10},{10,2},{3,11},{11,3},{4,12},{12,4},... | collective-permute-start | bytes 3145736 | tf_op jit(solution)/shard_map/ppermute | solution.py:36
  11.4 1.2 copy-done.5
  12.6 1.1 quarters.1
  13.7 3.5 %all-to-all-start = ((bf16[4,128,1024]{2,1,0:T(8,128)(2,1)}), bf16[4,128,1024]{2,1,0:T(8,128)(2,1)S(1)}, u32[]{:S(2)}, u32[]{:S(2)}) async-start(bf16[4,128,1024]{2,1,0:T(8,128)(2,1)} %bitcast.2), calls=%async_computation | async-start | bytes 2097152 | tf_op jit(solution)/shard_map/all_to_all | solution.py:340
  17.2 2.4 %collective-permute-start = (bf16[128,512]{1,0:T(8,128)(2,1)S(1)}, bf16[128,512]{1,0:T(8,128)(2,1)S(1)}, u32[]{:S(2)}, u32[]{:S(2)}) collective-permute-start(bf16[128,512]{1,0:T(8,128)(2,1)S(1)} %bitcast.27), channel_id=1, source_target_pairs={{0,8},{8,0},{1,9},{9,1},{2,10},{10,2},{3,11},{11,3},{4,12},{12,4},... | collective-permute-start | bytes 393224 | tf_op jit(solution)/shard_map/ppermute | solution.py:36
  21.8 1.3 collective-permute-start.6
  23.1 3.9 %collective-permute-start.5 = (bf16[128,256]{1,0:T(8,128)(2,1)S(1)}, bf16[128,256]{1,0:T(8,128)(2,1)S(1)}, u32[]{:S(2)}, u32[]{:S(2)}) collective-permute-start(bf16[128,256]{1,0:T(8,128)(2,1)S(1)} %slice.28), channel_id=1, source_target_pairs={{0,32},{8,40},{16,48},{24,56},{32,64},{40,72},{48,80},{56,88},{64,... | collective-permute-start | bytes 196616 | tf_op jit(solution)/shard_map/ppermute | solution.py:32
  27.0 2.5 %collective-permute-start.2 = (s32[1,128]{1,0:T(1,128)S(1)}, s32[1,128]{1,0:T(1,128)S(1)}, u32[]{:S(2)}, u32[]{:S(2)}) collective-permute-start(s32[1,128]{1,0:T(1,128)S(1)} %copy-done.8), channel_id=1, source_target_pairs={{0,8},{8,0},{1,9},{9,1},{2,10},{10,2},{3,11},{11,3},{4,12},{12,4},... | collective-permute-start | bytes 1544 | tf_op jit(solution)/shard_map/ppermute | solution.py:36
  30.4 8.6 %attention_weights.1 = (bf16[2,2,512,1024]{3,2,1,0:T(8,128)(2,1)}, bf16[128,256]{1,0:T(8,128)(2,1)S(1)}, bf16[256,256]{1,0:T(8,128)(2,1)S(1)}, f32[256,256]{1,0:T(8,128)S(1)}) custom-call(s32[1]{0:T(128)} %bitcast.core_ref, s32[1,128]{1,0:T(1,128)S(1)} %copy-done.8, s32[1,128]{1,0:T(1,128)S(1)} %collective-permute-done.2.other_position, ...), custom_call_target="tpu_custom_call" | custom-call | flops 2147483648 | bytes 8388608 | tf_op jit(solution)/shard_map/attention_weights/pallas_call | solution.py:165
  39.6 2.2 %collective-permute-start.7 = (bf16[512,1024]{1,0:T(8,128)(2,1)S(1)}, bf16[512,1024]{1,0:T(8,128)(2,1)S(1)}, u32[]{:S(2)}, u32[]{:S(2)}) collective-permute-start(bf16[512,1024]{1,0:T(8,128)(2,1)S(1)} %bitcast.19), channel_id=1, source_target_pairs={{0,8},{8,0},{1,9},{9,1},{2,10},{10,2},{3,11},{11,3},{4,12},{12,4},... | collective-permute-start | bytes 3145736 | tf_op jit(solution)/shard_map/ppermute | solution.py:36
  41.8 1.7 broadcast_in_dim.6
  43.5 16.7 %all-to-all-start.1 = ((bf16[8,128,256]{2,1,0:T(8,128)(2,1)}), bf16[8,128,256]{2,1,0:T(8,128)(2,1)S(1)}, u32[]{:S(2)}, u32[]{:S(2)}) async-start(bf16[8,128,256]{2,1,0:T(8,128)(2,1)} %broadcast_in_dim.6), calls=%async_computation.1 | async-start | bytes 1048576 | tf_op jit(solution)/shard_map/all_to_all | solution.py:284
  60.3 1.3 collective-permute-start.9
  61.5 1.3 collective-permute-start.8
  62.8 15.4 %all-to-all-done.1 = bf16[8,128,256]{2,1,0:T(8,128)(2,1)S(1)} async-done(((bf16[8,128,256]{2,1,0:T(8,128)(2,1)}), bf16[8,128,256]{2,1,0:T(8,128)(2,1)S(1)}, u32[]{:S(2)}, u32[]{:S(2)}) %all-to-all-start.1) | async-done | bytes 524320 | tf_op jit(solution)/shard_map/all_to_all | solution.py:284
  79.1 23.2 %all_to_all.52 = bf16[4,256,512]{2,1,0:T(8,128)(2,1)S(1)} all-to-all(bf16[4,256,512]{2,1,0:T(8,128)(2,1)S(1)} %bitcast.23), channel_id=1, replica_groups=mesh['x'=4,'z'=8,'c'=2,'y'=8] {'x'}, dimensions={0} | all-to-all | bytes 2097152 | tf_op jit(solution)/shard_map/all_to_all | solution.py:307
  102.2 2.0 %group_product.1 = bf16[1024,256]{1,0:T(8,128)(2,1)S(1)} custom-call(s32[1]{0:T(128)} %bitcast.core_ref, bf16[512,1024]{1,0:T(8,128)(2,1)S(1)} %bitcast.21, bf16[512,1024]{1,0:T(8,128)(2,1)S(1)} %collective-permute-done.7.far_ref, bf16[1024,512]{1,0:T(8,128)(2,1)S(1)} %bitcast.22), custom_call_target="tpu_custom_call" | custom-call | tf_op jit(solution)/shard_map/group_product/pallas_call | solution.py:312
  105.1 6.0 %all-to-all-start.3 = ((bf16[64,16,256]{2,1,0:T(8,128)(2,1)}), bf16[64,16,256]{2,1,0:T(8,128)(2,1)S(1)}, u32[]{:S(2)}, u32[]{:S(2)}) async-start(bf16[64,16,256]{2,1,0:T(8,128)(2,1)} %bitcast.24), calls=%async_computation.3 | async-start | bytes 1048576 | tf_op jit(solution)/shard_map/all_to_all | solution.py:355
  111.2 2.9 %collective-permute-start.11 = (bf16[256,256]{1,0:T(8,128)(2,1)S(1)}, bf16[256,256]{1,0:T(8,128)(2,1)S(1)}, u32[]{:S(2)}, u32[]{:S(2)}) collective-permute-start(bf16[256,256]{1,0:T(8,128)(2,1)S(1)} %slice_reduce_fusion.refs_2_), channel_id=1, source_target_pairs={{0,16},{8,24},{16,32},{24,40},{32,48},{40,56},{48,64},{56,72},{64,... | collective-permute-start | bytes 393224 | tf_op jit(solution)/shard_map/ppermute | solution.py:32
  114.1 4.0 %collective-permute-start.10 = (bf16[128,256]{1,0:T(8,128)(2,1)S(1)}, bf16[128,256]{1,0:T(8,128)(2,1)S(1)}, u32[]{:S(2)}, u32[]{:S(2)}) collective-permute-start(bf16[128,256]{1,0:T(8,128)(2,1)S(1)} %slice.30), channel_id=1, source_target_pairs={{0,32},{8,40},{16,48},{24,56},{32,64},{40,72},{48,80},{56,88},{64,... | collective-permute-start | bytes 196616 | tf_op jit(solution)/shard_map/ppermute | solution.py:32
  118.1 9.0 %collective-permute-done.10.refs_0_ = bf16[128,256]{1,0:T(8,128)(2,1)S(1)} collective-permute-done((bf16[128,256]{1,0:T(8,128)(2,1)S(1)}, bf16[128,256]{1,0:T(8,128)(2,1)S(1)}, u32[]{:S(2)}, u32[]{:S(2)}) %collective-permute-start.10) | collective-permute-done | bytes 65568 | tf_op jit(solution)/shard_map/ppermute | solution.py:32
  127.9 1.2 copy-done.2
  129.2 1.2 copy-done.4
  130.4 6.8 %key_gradient.1 = (bf16[128,256]{1,0:T(8,128)(2,1)S(1)}, bf16[256,256]{1,0:T(8,128)(2,1)S(1)}, f32[256,256]{1,0:T(8,128)S(1)}) custom-call(s32[1]{0:T(128)} %bitcast.core_ref, bf16[2,2,512,1024]{3,2,1,0:T(8,128)(2,1)} %get-tuple-element.35.weights_ref, bf16[128,4096]{1,0:T(8,128)(2,1)} %bitcast.31, bf16[128,4096]{1,0:T(8,128)(2,1)S(1)} %copy-done.2, ...), custom_call_target="tpu_custom_call" | custom-call | flops 2147483648 | bytes 8388608 | tf_op jit(solution)/shard_map/key_gradient/pallas_call | solution.py:184
  137.9 17.7 %all-to-all-start.4 = ((bf16[32,16,256]{2,1,0:T(8,128)(2,1)}), bf16[32,16,256]{2,1,0:T(8,128)(2,1)S(1)}, u32[]{:S(2)}, u32[]{:S(2)}) async-start(bf16[32,16,256]{2,1,0:T(8,128)(2,1)} %broadcast_in_dim.8), calls=%async_computation.4 | async-start | bytes 524288 | tf_op jit(solution)/shard_map/all_to_all | solution.py:326
  155.7 1.3 collective-permute-start.13
  157.0 1.3 collective-permute-start.14
  158.3 7.3 %collective-permute-done.13 = bf16[256,256]{1,0:T(8,128)(2,1)S(1)} collective-permute-done((bf16[256,256]{1,0:T(8,128)(2,1)S(1)}, bf16[256,256]{1,0:T(8,128)(2,1)S(1)}, u32[]{:S(2)}, u32[]{:S(2)}) %collective-permute-start.13) | collective-permute-done | bytes 131104 | tf_op jit(solution)/shard_map/ppermute | solution.py:32
  165.6 2.8 %collective-permute-done.14 = bf16[128,256]{1,0:T(8,128)(2,1)S(1)} collective-permute-done((bf16[128,256]{1,0:T(8,128)(2,1)S(1)}, bf16[128,256]{1,0:T(8,128)(2,1)S(1)}, u32[]{:S(2)}, u32[]{:S(2)}) %collective-permute-start.14) | collective-permute-done | bytes 65568 | tf_op jit(solution)/shard_map/ppermute | solution.py:32
  168.5 4.2 %collective-permute-start.15 = (bf16[128,256]{1,0:T(8,128)(2,1)S(1)}, bf16[128,256]{1,0:T(8,128)(2,1)S(1)}, u32[]{:S(2)}, u32[]{:S(2)}) collective-permute-start(bf16[128,256]{1,0:T(8,128)(2,1)S(1)} %get-tuple-element.46), channel_id=1, source_target_pairs={{0,8},{8,0},{1,9},{9,1},{2,10},{10,2},{3,11},{11,3},{4,12},{12,4},... | collective-permute-start | bytes 196616 | tf_op jit(solution)/shard_map/ppermute | solution.py:36
  172.7 1.9 %collective-permute-start.16 = (bf16[512,256]{1,0:T(8,128)(2,1)S(1)}, bf16[512,256]{1,0:T(8,128)(2,1)S(1)}, u32[]{:S(2)}, u32[]{:S(2)}) collective-permute-start(bf16[512,256]{1,0:T(8,128)(2,1)S(1)} %bitcast.35), channel_id=1, source_target_pairs={{0,8},{8,0},{1,9},{9,1},{2,10},{10,2},{3,11},{11,3},{4,12},{12,4},... | collective-permute-start | bytes 786440 | tf_op jit(solution)/shard_map/ppermute | solution.py:36
  (52 shorter events, 9.2 us)
Async XLA Ops:
  0.6 26.4 %copy-start.8 = (s32[1,128]{1,0:T(1,128)S(1)}, s32[1,128]{1,0:T(1,128)}, u32[]{:S(2)}) copy-start(s32[1,128]{1,0:T(1,128)} %own_position.1) | copy-start | bytes 1540
  0.6 29.7 %collective-permute-start.3 = (bf16[128,4096]{1,0:T(8,128)(2,1)}, bf16[128,4096]{1,0:T(8,128)(2,1)S(1)}, u32[]{:S(2)}, u32[]{:S(2)}) collective-permute-start(bf16[128,4096]{1,0:T(8,128)(2,1)} %bitcast.29), channel_id=1, source_target_pairs={{0,8},{8,0},{1,9},{9,1},{2,10},{10,2},{3,11},{11,3},{4,12},{12,4},... | collective-permute-start | bytes 3145736 | tf_op jit(solution)/shard_map/ppermute | solution.py:36
  9.4 20.9 %collective-permute-start.4 = (bf16[128,4096]{1,0:T(8,128)(2,1)}, bf16[128,4096]{1,0:T(8,128)(2,1)S(1)}, u32[]{:S(2)}, u32[]{:S(2)}) collective-permute-start(bf16[128,4096]{1,0:T(8,128)(2,1)} %bitcast.32), channel_id=1, source_target_pairs={{0,8},{8,0},{1,9},{9,1},{2,10},{10,2},{3,11},{11,3},{4,12},{12,4},... | collective-permute-start | bytes 3145736 | tf_op jit(solution)/shard_map/ppermute | solution.py:36
  11.4 1.2 copy-start.5
  12.6 4.6 %copy-start.6 = (bf16[1,128,512]{2,1,0:T(8,128)(2,1)S(1)}, bf16[1,128,512]{2,1,0:T(8,128)(2,1)}, u32[]{:S(2)}) copy-start(bf16[1,128,512]{2,1,0:T(8,128)(2,1)} %param.7) | copy-start | bytes 393220
  13.7 25.9 %all-to-all-start = ((bf16[4,128,1024]{2,1,0:T(8,128)(2,1)}), bf16[4,128,1024]{2,1,0:T(8,128)(2,1)S(1)}, u32[]{:S(2)}, u32[]{:S(2)}) async-start(bf16[4,128,1024]{2,1,0:T(8,128)(2,1)} %bitcast.2), calls=%async_computation | async-start | bytes 2097152 | tf_op jit(solution)/shard_map/all_to_all | solution.py:340
  17.2 4.0 %collective-permute-start = (bf16[128,512]{1,0:T(8,128)(2,1)S(1)}, bf16[128,512]{1,0:T(8,128)(2,1)S(1)}, u32[]{:S(2)}, u32[]{:S(2)}) collective-permute-start(bf16[128,512]{1,0:T(8,128)(2,1)S(1)} %bitcast.27), channel_id=1, source_target_pairs={{0,8},{8,0},{1,9},{9,1},{2,10},{10,2},{3,11},{11,3},{4,12},{12,4},... | collective-permute-start | bytes 393224 | tf_op jit(solution)/shard_map/ppermute | solution.py:36
  20.5 0.7 collective-permute-start.1
  21.2 0.6 copy-start.9
  21.8 8.5 %collective-permute-start.6 = (bf16[256,256]{1,0:T(8,128)(2,1)S(1)}, bf16[256,256]{1,0:T(8,128)(2,1)S(1)}, u32[]{:S(2)}, u32[]{:S(2)}) collective-permute-start(bf16[256,256]{1,0:T(8,128)(2,1)S(1)} %join_halves.1.refs_2_), channel_id=1, source_target_pairs={{0,16},{8,24},{16,32},{24,40},{32,48},{40,56},{48,64},{56,72},{64,... | collective-permute-start | bytes 393224 | tf_op jit(solution)/shard_map/ppermute | solution.py:32
  23.1 7.2 %collective-permute-start.5 = (bf16[128,256]{1,0:T(8,128)(2,1)S(1)}, bf16[128,256]{1,0:T(8,128)(2,1)S(1)}, u32[]{:S(2)}, u32[]{:S(2)}) collective-permute-start(bf16[128,256]{1,0:T(8,128)(2,1)S(1)} %slice.28), channel_id=1, source_target_pairs={{0,32},{8,40},{16,48},{24,56},{32,64},{40,72},{48,80},{56,88},{64,... | collective-permute-start | bytes 196616 | tf_op jit(solution)/shard_map/ppermute | solution.py:32
  27.0 3.3 %collective-permute-start.2 = (s32[1,128]{1,0:T(1,128)S(1)}, s32[1,128]{1,0:T(1,128)S(1)}, u32[]{:S(2)}, u32[]{:S(2)}) collective-permute-start(s32[1,128]{1,0:T(1,128)S(1)} %copy-done.8), channel_id=1, source_target_pairs={{0,8},{8,0},{1,9},{9,1},{2,10},{10,2},{3,11},{11,3},{4,12},{12,4},... | collective-permute-start | bytes 1544 | tf_op jit(solution)/shard_map/ppermute | solution.py:36
  30.3 9.3 %copy-start.1 = (bf16[128,4096]{1,0:T(8,128)(2,1)}, bf16[128,4096]{1,0:T(8,128)(2,1)S(1)}, u32[]{:S(2)}) copy-start(bf16[128,4096]{1,0:T(8,128)(2,1)S(1)} %collective-permute-done.3.other_query) | copy-start | bytes 3145732
  30.4 13.2 %copy-start.3 = (bf16[128,4096]{1,0:T(8,128)(2,1)}, bf16[128,4096]{1,0:T(8,128)(2,1)S(1)}, u32[]{:S(2)}) copy-start(bf16[128,4096]{1,0:T(8,128)(2,1)S(1)} %collective-permute-done.4.other_grad) | copy-start | bytes 3145732
  39.0 0.6 copy-start.7
  39.6 38.6 %collective-permute-start.7 = (bf16[512,1024]{1,0:T(8,128)(2,1)S(1)}, bf16[512,1024]{1,0:T(8,128)(2,1)S(1)}, u32[]{:S(2)}, u32[]{:S(2)}) collective-permute-start(bf16[512,1024]{1,0:T(8,128)(2,1)S(1)} %bitcast.19), channel_id=1, source_target_pairs={{0,8},{8,0},{1,9},{9,1},{2,10},{10,2},{3,11},{11,3},{4,12},{12,4},... | collective-permute-start | bytes 3145736 | tf_op jit(solution)/shard_map/ppermute | solution.py:36
  43.5 34.7 %all-to-all-start.1 = ((bf16[8,128,256]{2,1,0:T(8,128)(2,1)}), bf16[8,128,256]{2,1,0:T(8,128)(2,1)S(1)}, u32[]{:S(2)}, u32[]{:S(2)}) async-start(bf16[8,128,256]{2,1,0:T(8,128)(2,1)} %broadcast_in_dim.6), calls=%async_computation.1 | async-start | bytes 1048576 | tf_op jit(solution)/shard_map/all_to_all | solution.py:284
  60.3 18.7 %collective-permute-start.9 = (bf16[256,256]{1,0:T(8,128)(2,1)S(1)}, bf16[256,256]{1,0:T(8,128)(2,1)S(1)}, u32[]{:S(2)}, u32[]{:S(2)}) collective-permute-start(bf16[256,256]{1,0:T(8,128)(2,1)S(1)} %get-tuple-element.31), channel_id=1, source_target_pairs={{16,0},{24,8},{32,16},{40,24},{48,32},{56,40},{64,48},{72,56},{80,... | collective-permute-start | bytes 393224 | tf_op jit(solution)/shard_map/ppermute | solution.py:32
  61.5 17.4 %collective-permute-start.8 = (bf16[128,256]{1,0:T(8,128)(2,1)}, bf16[128,256]{1,0:T(8,128)(2,1)S(1)}, u32[]{:S(2)}, u32[]{:S(2)}) collective-permute-start(bf16[128,256]{1,0:T(8,128)(2,1)} %copy-done.7), channel_id=1, source_target_pairs={{32,0},{40,8},{48,16},{56,24},{64,32},{72,40},{80,48},{88,56},{96,... | collective-permute-start | bytes 196616 | tf_op jit(solution)/shard_map/ppermute | solution.py:32
  104.3 0.8 copy-start
  105.1 22.1 %all-to-all-start.3 = ((bf16[64,16,256]{2,1,0:T(8,128)(2,1)}), bf16[64,16,256]{2,1,0:T(8,128)(2,1)S(1)}, u32[]{:S(2)}, u32[]{:S(2)}) async-start(bf16[64,16,256]{2,1,0:T(8,128)(2,1)} %bitcast.24), calls=%async_computation.3 | async-start | bytes 1048576 | tf_op jit(solution)/shard_map/all_to_all | solution.py:355
  111.2 16.0 %collective-permute-start.11 = (bf16[256,256]{1,0:T(8,128)(2,1)S(1)}, bf16[256,256]{1,0:T(8,128)(2,1)S(1)}, u32[]{:S(2)}, u32[]{:S(2)}) collective-permute-start(bf16[256,256]{1,0:T(8,128)(2,1)S(1)} %slice_reduce_fusion.refs_2_), channel_id=1, source_target_pairs={{0,16},{8,24},{16,32},{24,40},{32,48},{40,56},{48,64},{56,72},{64,... | collective-permute-start | bytes 393224 | tf_op jit(solution)/shard_map/ppermute | solution.py:32
  114.1 13.0 %collective-permute-start.10 = (bf16[128,256]{1,0:T(8,128)(2,1)S(1)}, bf16[128,256]{1,0:T(8,128)(2,1)S(1)}, u32[]{:S(2)}, u32[]{:S(2)}) collective-permute-start(bf16[128,256]{1,0:T(8,128)(2,1)S(1)} %slice.30), channel_id=1, source_target_pairs={{0,32},{8,40},{16,48},{24,56},{32,64},{40,72},{48,80},{56,88},{64,... | collective-permute-start | bytes 196616 | tf_op jit(solution)/shard_map/ppermute | solution.py:32
  127.3 9.9 %collective-permute-start.12 = (bf16[16,256]{1,0:T(8,128)(2,1)S(1)}, bf16[16,256]{1,0:T(8,128)(2,1)S(1)}, u32[]{:S(2)}, u32[]{:S(2)}) collective-permute-start(bf16[16,256]{1,0:T(8,128)(2,1)S(1)} %multiply_convert_fusion), channel_id=1, source_target_pairs={{0,0},{1,128},{2,256},{3,384},{4,1},{5,129},{6,257},{7,385},{8,8},... | collective-permute-start | bytes 24584 | tf_op jit(solution)/shard_map/ppermute | solution.py:365
  127.9 1.2 copy-start.2
  129.2 1.2 copy-start.4
  137.9 34.8 %all-to-all-start.4 = ((bf16[32,16,256]{2,1,0:T(8,128)(2,1)}), bf16[32,16,256]{2,1,0:T(8,128)(2,1)S(1)}, u32[]{:S(2)}, u32[]{:S(2)}) async-start(bf16[32,16,256]{2,1,0:T(8,128)(2,1)} %broadcast_in_dim.8), calls=%async_computation.4 | async-start | bytes 524288 | tf_op jit(solution)/shard_map/all_to_all | solution.py:326
  155.7 9.9 %collective-permute-start.13 = (bf16[256,256]{1,0:T(8,128)(2,1)S(1)}, bf16[256,256]{1,0:T(8,128)(2,1)S(1)}, u32[]{:S(2)}, u32[]{:S(2)}) collective-permute-start(bf16[256,256]{1,0:T(8,128)(2,1)S(1)} %get-tuple-element.43), channel_id=1, source_target_pairs={{16,0},{24,8},{32,16},{40,24},{48,32},{56,40},{64,48},{72,56},{80,... | collective-permute-start | bytes 393224 | tf_op jit(solution)/shard_map/ppermute | solution.py:32
  157.0 11.5 %collective-permute-start.14 = (bf16[128,256]{1,0:T(8,128)(2,1)S(1)}, bf16[128,256]{1,0:T(8,128)(2,1)S(1)}, u32[]{:S(2)}, u32[]{:S(2)}) collective-permute-start(bf16[128,256]{1,0:T(8,128)(2,1)S(1)} %get-tuple-element.44), channel_id=1, source_target_pairs={{32,0},{40,8},{48,16},{56,24},{64,32},{72,40},{80,48},{88,56},{96,... | collective-permute-start | bytes 196616 | tf_op jit(solution)/shard_map/ppermute | solution.py:32
  168.5 6.1 %collective-permute-start.15 = (bf16[128,256]{1,0:T(8,128)(2,1)S(1)}, bf16[128,256]{1,0:T(8,128)(2,1)S(1)}, u32[]{:S(2)}, u32[]{:S(2)}) collective-permute-start(bf16[128,256]{1,0:T(8,128)(2,1)S(1)} %get-tuple-element.46), channel_id=1, source_target_pairs={{0,8},{8,0},{1,9},{9,1},{2,10},{10,2},{3,11},{11,3},{4,12},{12,4},... | collective-permute-start | bytes 196616 | tf_op jit(solution)/shard_map/ppermute | solution.py:36
  172.7 3.4 %collective-permute-start.16 = (bf16[512,256]{1,0:T(8,128)(2,1)S(1)}, bf16[512,256]{1,0:T(8,128)(2,1)S(1)}, u32[]{:S(2)}, u32[]{:S(2)}) collective-permute-start(bf16[512,256]{1,0:T(8,128)(2,1)S(1)} %bitcast.35), channel_id=1, source_target_pairs={{0,8},{8,0},{1,9},{9,1},{2,10},{10,2},{3,11},{11,3},{4,12},{12,4},... | collective-permute-start | bytes 786440 | tf_op jit(solution)/shard_map/ppermute | solution.py:36

commit v7 on v6

--- a/solution.py
+++ b/solution.py
@@ -337,37 +337,41 @@
     even = core[0] == 0
     weight = projection_piece(w_value)
     other_keys = swap(keys)
-    near = lax.all_to_all(column_quarters(rows), "x", 0, 0, tiled=True)
-    both_queries = (in_hbm(queries), swap(queries))
-    both_grads = (in_hbm(grads), swap(grads))
-    positions = (doc_pos, swap(doc_pos))
-    other_keys, weight = lax.optimization_barrier((other_keys, weight))
+    others = (swap(queries), swap(grads), swap(doc_pos))
+    quarters = column_quarters(rows)
     key_span = span_blocks(join_halves(core, keys, other_keys))
+    weight, quarters, key_span, others = lax.optimization_barrier(
+        (projection_part(weight), quarters, key_span, others)
+    )
+    near = lax.all_to_all(quarters, "x", 0, 0, tiled=True)
+    both_queries, both_grads = (in_hbm(queries), others[0]), (in_hbm(grads), others[1])
+    positions = (doc_pos, others[2])
     weights, *value_parts = attention_weights(core, positions, both_queries, both_grads, key_span)
-    near, weight, value_parts = lax.optimization_barrier((near, weight, value_parts))
 
     two, one, own = value_parts
     two, one = shift(two, -2), shift(one, -1)
+    near, own = lax.optimization_barrier((near, own))
     far = swap(near)
-    values = partial_values(core, near, far, projection_part(weight))
+    values = partial_values(core, near, far, weight)
     packed = exchange_packed(two, one, own, values)
     product = group_product(core, near, far, packed)
-    pieces = lax.all_to_all(product, ("y", "z"), 0, 0, tiled=True)
-
     parts = packed.reshape(4, 2 * BLOCK, 2 * HALF)[:, :, HALF:].astype(jnp.float32)
     value_span = span_blocks(jnp.sum(parts, axis=0).astype(jnp.bfloat16))
-    pieces, value_span = lax.optimization_barrier((pieces, value_span))
+    product, value_span = lax.optimization_barrier((product, value_span))
+    pieces = lax.all_to_all(product, ("y", "z"), 0, 0, tiled=True)
     key_parts = key_gradient(core, weights, both_queries, both_grads, value_span)
+    pieces, key_parts = lax.optimization_barrier((pieces, key_parts))
 
     pieces = pieces.reshape(64, -1, HALF).astype(jnp.float32)
     token_total = lax.axis_size(ALL) * BLOCK
     piece = (jnp.sum(pieces, axis=0) * (1.0 / math.sqrt(token_total))).astype(jnp.bfloat16)
     piece = lax.ppermute(piece, ALL, plane_route())
-    piece, key_parts = lax.optimization_barrier((piece, key_parts))
+    two, one, own = key_parts
+    two, one = shift(two, -2), shift(one, -1)
+    piece, two, one = lax.optimization_barrier((piece, two, one))
     weight_grad = whole_shard(piece, even)
 
-    two, one, own = key_parts
-    two, one = shift(two, -2).astype(jnp.float32), shift(one, -1).astype(jnp.float32)
+    two, one = two.astype(jnp.float32), one.astype(jnp.float32)
     first = (own[:BLOCK] + one[:BLOCK]).astype(jnp.bfloat16)
     second = (own[BLOCK:] + one[BLOCK:] + two).astype(jnp.bfloat16)
     received = swap(jnp.where(even, second, first))

time: 178 us -> 178 us (level)
  starting transfers between devices: 86.5 us -> 106 us
  waiting for transfers between devices: 36.2 us -> 22.3 us
  blocking collectives: 23.2 us -> 18 us
    ppermute x7, starting transfers between devices: 23.9 us -> 41.1 us  [swap(): return lax.ppermute(block, 'c', OTHER_CORE)]
    all_to_all x1, waiting for transfers between devices: 15.4 us -> 0.01 us  [projection_part(): return lax.all_to_all(copies, 'y', 0, 0, tiled=True)]
    ppermute x8, waiting for transfers between devices: 19.2 us -> 9.37 us  [shift(): return lax.ppermute(block, DP, route)]
    all_to_all x1, waiting for transfers between devices: 0.01 us -> 6.98 us  [per_device(): pieces = lax.all_to_all(product, ('y', 'z'), 0, 0, tiled=True)]
    all_to_all x1, starting transfers between devices: 16.7 us -> 9.9 us  [projection_part(): return lax.all_to_all(copies, 'y', 0, 0, tiled=True)]
    all_to_all x1, starting transfers between devices: 6.03 us -> 12.9 us  [per_device(): pieces = lax.all_to_all(product, ('y', 'z'), 0, 0, tiled=True)]
    all_to_all x1, blocking collectives: 23.2 us -> 18 us  [exchange_packed(): return lax.all_to_all(packed, 'x', 0, 0, tiled=True)]
    all_to_all x1, starting transfers between devices: 17.7 us -> 12.7 us  [whole_shard(): half = lax.all_to_all(copies, ('x', 'z'), 0, 0, tiled=True)]
  transfers between devices with their start and end apart: 21 -> 21, of which waited for: 6 -> 7; matrix products, arithmetic and copies ran while one was open for 2% -> 1% of each run, Pallas kernels for 10% -> 11%
where the time goes in v7:
time: 178 us; the launch traced here: 177 us
  starting transfers between devices  106 us (60%)
  waiting for transfers between devices  22.3 us (13%)
  Pallas kernels  19.6 us (11%)
  blocking collectives  18 us (10%)
  local copies, waits for them, and re-layouts  7.98 us (4%)
  other arithmetic  1.81 us (1%)
    ppermute x7, starting transfers between devices, swap(): return lax.ppermute(block, 'c', OTHER_CORE)  41.1 us
    ppermute x8, starting transfers between devices, shift(): return lax.ppermute(block, DP, route)  22 us
    all_to_all x1, blocking collectives, exchange_packed(): return lax.all_to_all(packed, 'x', 0, 0, tiled=True)  18 us
    all_to_all x1, starting transfers between devices, per_device(): pieces = lax.all_to_all(product, ('y', 'z'), 0, 0, tiled=True)  12.9 us
    all_to_all x1, starting transfers between devices, whole_shard(): half = lax.all_to_all(copies, ('x', 'z'), 0, 0, tiled=True)  12.7 us
    all_to_all x1, starting transfers between devices, projection_part(): return lax.all_to_all(copies, 'y', 0, 0, tiled=True)  9.9 us
    ppermute x8, waiting for transfers between devices, shift(): return lax.ppermute(block, DP, route)  9.37 us
    pallas_call x1, Pallas kernels, attention_weights(): pl.pallas_call(weights_kernel, grid_spec=pltpu.PrefetchScalarGridSpec(num...  8.14 us
  transfers between devices with their start and end apart: 21, of which 7 were waited for; matrix products, arithmetic and copies ran while one was open for 1% of the time, Pallas kernels for 11%

profile of v7, /device:TPU:1, one launch (start us, length us, event | category | flops | bytes accessed | tf_op | source)
XLA Modules:
  0.0 177.0 jit_solution(17025733905775673191)
XLA Ops:
  0.6 8.8 %collective-permute-start.4 = (bf16[128,4096]{1,0:T(8,128)(2,1)}, bf16[128,4096]{1,0:T(8,128)(2,1)S(1)}, u32[]{:S(2)}, u32[]{:S(2)}) collective-permute-start(bf16[128,4096]{1,0:T(8,128)(2,1)} %bitcast.28), channel_id=1, source_target_pairs={{0,8},{8,0},{1,9},{9,1},{2,10},{10,2},{3,11},{11,3},{4,12},{12,4},... | collective-permute-start | bytes 3145736 | tf_op jit(solution)/shard_map/ppermute | solution.py:36
  9.4 1.9 %collective-permute-start.5 = (bf16[128,4096]{1,0:T(8,128)(2,1)}, bf16[128,4096]{1,0:T(8,128)(2,1)S(1)}, u32[]{:S(2)}, u32[]{:S(2)}) collective-permute-start(bf16[128,4096]{1,0:T(8,128)(2,1)} %bitcast.31), channel_id=1, source_target_pairs={{0,8},{8,0},{1,9},{9,1},{2,10},{10,2},{3,11},{11,3},{4,12},{12,4},... | collective-permute-start | bytes 3145736 | tf_op jit(solution)/shard_map/ppermute | solution.py:36
  13.7 9.9 %all-to-all-start = ((bf16[8,128,256]{2,1,0:T(8,128)(2,1)}), bf16[8,128,256]{2,1,0:T(8,128)(2,1)S(1)}, u32[]{:S(2)}, u32[]{:S(2)}) async-start(bf16[8,128,256]{2,1,0:T(8,128)(2,1)} %broadcast_in_dim.6), calls=%async_computation | async-start | bytes 1048576 | tf_op jit(solution)/shard_map/all_to_all | solution.py:284
  23.6 3.7 %collective-permute-start.1 = (bf16[128,512]{1,0:T(8,128)(2,1)}, bf16[128,512]{1,0:T(8,128)(2,1)S(1)}, u32[]{:S(2)}, u32[]{:S(2)}) collective-permute-start(bf16[128,512]{1,0:T(8,128)(2,1)} %bitcast.26), channel_id=1, source_target_pairs={{0,8},{8,0},{1,9},{9,1},{2,10},{10,2},{3,11},{11,3},{4,12},{12,4},... | collective-permute-start | bytes 393224 | tf_op jit(solution)/shard_map/ppermute | solution.py:36
  27.4 1.2 collective-permute-done.1.other_ref
  29.5 4.0 %collective-permute-start.3 = (bf16[256,256]{1,0:T(8,128)(2,1)S(1)}, bf16[256,256]{1,0:T(8,128)(2,1)S(1)}, u32[]{:S(2)}, u32[]{:S(2)}) collective-permute-start(bf16[256,256]{1,0:T(8,128)(2,1)S(1)} %join_halves.1.refs_2_), channel_id=1, source_target_pairs={{0,16},{8,24},{16,32},{24,40},{32,48},{40,56},{48,64},{56,72},{64,... | collective-permute-start | bytes 393224 | tf_op jit(solution)/shard_map/ppermute | solution.py:32
  33.5 5.8 %collective-permute-start.2 = (bf16[128,256]{1,0:T(8,128)(2,1)S(1)}, bf16[128,256]{1,0:T(8,128)(2,1)S(1)}, u32[]{:S(2)}, u32[]{:S(2)}) collective-permute-start(bf16[128,256]{1,0:T(8,128)(2,1)S(1)} %slice.28), channel_id=1, source_target_pairs={{0,32},{8,40},{16,48},{24,56},{32,64},{40,72},{48,80},{56,88},{64,... | collective-permute-start | bytes 196616 | tf_op jit(solution)/shard_map/ppermute | solution.py:32
  39.3 2.8 %collective-permute-start.6 = (s32[1,128]{1,0:T(1,128)}, s32[1,128]{1,0:T(1,128)S(1)}, u32[]{:S(2)}, u32[]{:S(2)}) collective-permute-start(s32[1,128]{1,0:T(1,128)} %own_position.1), channel_id=1, source_target_pairs={{0,8},{8,0},{1,9},{9,1},{2,10},{10,2},{3,11},{11,3},{4,12},{12,4},... | collective-permute-start | bytes 1544 | tf_op jit(solution)/shard_map/ppermute | solution.py:36
  42.1 1.2 copy-done.3
  43.4 1.0 quarters.1
  45.4 6.3 %all-to-all-start.1 = ((bf16[4,128,1024]{2,1,0:T(8,128)(2,1)}), bf16[4,128,1024]{2,1,0:T(8,128)(2,1)S(1)}, u32[]{:S(2)}, u32[]{:S(2)}) async-start(bf16[4,128,1024]{2,1,0:T(8,128)(2,1)} %bitcast.6), calls=%async_computation.1 | async-start | bytes 2097152 | tf_op jit(solution)/shard_map/all_to_all | solution.py:346
  51.8 1.2 copy-done.1
  53.0 8.1 %attention_weights.1 = (bf16[2,2,512,1024]{3,2,1,0:T(8,128)(2,1)}, bf16[128,256]{1,0:T(8,128)(2,1)S(1)}, bf16[256,256]{1,0:T(8,128)(2,1)S(1)}, f32[256,256]{1,0:T(8,128)S(1)}) custom-call(s32[1]{0:T(128)} %bitcast.core_ref, s32[1,128]{1,0:T(1,128)S(1)} %copy-done.5, s32[1,128]{1,0:T(1,128)S(1)} %collective-permute-done.6.other_position, ...), custom_call_target="tpu_custom_call" | custom-call | flops 2147483648 | bytes 8388608 | tf_op jit(solution)/shard_map/attention_weights/pallas_call | solution.py:165
  61.1 3.7 %all-to-all-done.1 = bf16[4,128,1024]{2,1,0:T(8,128)(2,1)S(1)} async-done(((bf16[4,128,1024]{2,1,0:T(8,128)(2,1)}), bf16[4,128,1024]{2,1,0:T(8,128)(2,1)S(1)}, u32[]{:S(2)}, u32[]{:S(2)}) %all-to-all-start.1) | async-done | bytes 1048608 | tf_op jit(solution)/shard_map/all_to_all | solution.py:346
  64.9 4.8 %collective-permute-start.7 = (bf16[512,1024]{1,0:T(8,128)(2,1)S(1)}, bf16[512,1024]{1,0:T(8,128)(2,1)S(1)}, u32[]{:S(2)}, u32[]{:S(2)}) collective-permute-start(bf16[512,1024]{1,0:T(8,128)(2,1)S(1)} %bitcast.19), channel_id=1, source_target_pairs={{0,8},{8,0},{1,9},{9,1},{2,10},{10,2},{3,11},{11,3},{4,12},{12,4},... | collective-permute-start | bytes 3145736 | tf_op jit(solution)/shard_map/ppermute | solution.py:36
  69.7 1.3 collective-permute-start.9
  71.0 1.3 collective-permute-start.8
  73.1 5.4 %collective-permute-done.8.two_ref = bf16[128,256]{1,0:T(8,128)(2,1)S(1)} collective-permute-done((bf16[128,256]{1,0:T(8,128)(2,1)S(1)}, bf16[128,256]{1,0:T(8,128)(2,1)S(1)}, u32[]{:S(2)}, u32[]{:S(2)}) %collective-permute-start.8) | collective-permute-done | bytes 65568 | tf_op jit(solution)/shard_map/ppermute | solution.py:32
  78.6 18.0 %all_to_all.53 = bf16[4,256,512]{2,1,0:T(8,128)(2,1)S(1)} all-to-all(bf16[4,256,512]{2,1,0:T(8,128)(2,1)S(1)} %bitcast.23), channel_id=1, replica_groups=mesh['x'=4,'z'=8,'c'=2,'y'=8] {'x'}, dimensions={0} | all-to-all | bytes 2097152 | tf_op jit(solution)/shard_map/all_to_all | solution.py:307
  96.7 1.3 collective-permute-start.11
  98.0 5.8 %collective-permute-start.10 = (bf16[128,256]{1,0:T(8,128)(2,1)S(1)}, bf16[128,256]{1,0:T(8,128)(2,1)S(1)}, u32[]{:S(2)}, u32[]{:S(2)}) collective-permute-start(bf16[128,256]{1,0:T(8,128)(2,1)S(1)} %slice.30), channel_id=1, source_target_pairs={{0,32},{8,40},{16,48},{24,56},{32,64},{40,72},{48,80},{56,88},{64,... | collective-permute-start | bytes 196616 | tf_op jit(solution)/shard_map/ppermute | solution.py:32
  103.8 2.8 %group_product.1 = bf16[1024,256]{1,0:T(8,128)(2,1)} custom-call(s32[1]{0:T(128)} %bitcast.core_ref, bf16[512,1024]{1,0:T(8,128)(2,1)S(1)} %bitcast.21, bf16[512,1024]{1,0:T(8,128)(2,1)S(1)} %collective-permute-done.7.far_ref, bf16[1024,512]{1,0:T(8,128)(2,1)S(1)} %bitcast.22), custom_call_target="tpu_custom_call" | custom-call | tf_op jit(solution)/shard_map/group_product/pallas_call | solution.py:312
  106.6 12.9 %all-to-all-start.3 = ((bf16[64,16,256]{2,1,0:T(8,128)(2,1)}), bf16[64,16,256]{2,1,0:T(8,128)(2,1)S(1)}, u32[]{:S(2)}, u32[]{:S(2)}) async-start(bf16[64,16,256]{2,1,0:T(8,128)(2,1)} %bitcast.10), calls=%async_computation.3 | async-start | bytes 1048576 | tf_op jit(solution)/shard_map/all_to_all | solution.py:361
  119.5 1.2 copy-done.2
  120.7 6.8 %key_gradient.1 = (bf16[128,256]{1,0:T(8,128)(2,1)S(1)}, bf16[256,256]{1,0:T(8,128)(2,1)S(1)}, f32[256,256]{1,0:T(8,128)S(1)}) custom-call(s32[1]{0:T(128)} %bitcast.core_ref, bf16[2,2,512,1024]{3,2,1,0:T(8,128)(2,1)} %get-tuple-element.44.weights_ref, bf16[128,4096]{1,0:T(8,128)(2,1)} %bitcast.30, bf16[128,4096]{1,0:T(8,128)(2,1)S(1)} %collective-permute-done.4.other_query, ...), custom_call_target="tpu_custom_call" | custom-call | flops 2147483648 | bytes 8388608 | tf_op jit(solution)/shard_map/key_gradient/pallas_call | solution.py:184
  127.5 7.0 %all-to-all-done.3 = bf16[64,16,256]{2,1,0:T(8,128)(2,1)S(1)} async-done(((bf16[64,16,256]{2,1,0:T(8,128)(2,1)}), bf16[64,16,256]{2,1,0:T(8,128)(2,1)S(1)}, u32[]{:S(2)}, u32[]{:S(2)}) %all-to-all-start.3) | async-done | bytes 524320 | tf_op jit(solution)/shard_map/all_to_all | solution.py:361
  134.5 1.3 collective-permute-start.14
  135.8 1.3 collective-permute-start.13
  137.9 3.9 %collective-permute-done.13 = bf16[128,256]{1,0:T(8,128)(2,1)S(1)} collective-permute-done((bf16[128,256]{1,0:T(8,128)(2,1)S(1)}, bf16[128,256]{1,0:T(8,128)(2,1)S(1)}, u32[]{:S(2)}, u32[]{:S(2)}) %collective-permute-start.13) | collective-permute-done | bytes 65568 | tf_op jit(solution)/shard_map/ppermute | solution.py:32
  142.5 12.7 %all-to-all-start.4 = ((bf16[32,16,256]{2,1,0:T(8,128)(2,1)}), bf16[32,16,256]{2,1,0:T(8,128)(2,1)S(1)}, u32[]{:S(2)}, u32[]{:S(2)}) async-start(bf16[32,16,256]{2,1,0:T(8,128)(2,1)} %broadcast_in_dim.8), calls=%async_computation.4 | async-start | bytes 524288 | tf_op jit(solution)/shard_map/all_to_all | solution.py:326
  155.3 8.9 %collective-permute-start.15 = (bf16[128,256]{1,0:T(8,128)(2,1)S(1)}, bf16[128,256]{1,0:T(8,128)(2,1)S(1)}, u32[]{:S(2)}, u32[]{:S(2)}) collective-permute-start(bf16[128,256]{1,0:T(8,128)(2,1)S(1)} %get-tuple-element.58), channel_id=1, source_target_pairs={{0,8},{8,0},{1,9},{9,1},{2,10},{10,2},{3,11},{11,3},{4,12},{12,4},... | collective-permute-start | bytes 196616 | tf_op jit(solution)/shard_map/ppermute | solution.py:36
  164.9 10.1 %collective-permute-start.16 = (bf16[512,256]{1,0:T(8,128)(2,1)S(1)}, bf16[512,256]{1,0:T(8,128)(2,1)S(1)}, u32[]{:S(2)}, u32[]{:S(2)}) collective-permute-start(bf16[512,256]{1,0:T(8,128)(2,1)S(1)} %bitcast.34), channel_id=1, source_target_pairs={{0,8},{8,0},{1,9},{9,1},{2,10},{10,2},{3,11},{11,3},{4,12},{12,4},... | collective-permute-start | bytes 786440 | tf_op jit(solution)/shard_map/ppermute | solution.py:36
  (44 shorter events, 9.4 us)
Async XLA Ops:
  0.6 51.1 %copy-start.5 = (s32[1,128]{1,0:T(1,128)S(1)}, s32[1,128]{1,0:T(1,128)}, u32[]{:S(2)}) copy-start(s32[1,128]{1,0:T(1,128)} %own_position.1) | copy-start | bytes 1540
  0.6 43.8 %collective-permute-start.4 = (bf16[128,4096]{1,0:T(8,128)(2,1)}, bf16[128,4096]{1,0:T(8,128)(2,1)S(1)}, u32[]{:S(2)}, u32[]{:S(2)}) collective-permute-start(bf16[128,4096]{1,0:T(8,128)(2,1)} %bitcast.28), channel_id=1, source_target_pairs={{0,8},{8,0},{1,9},{9,1},{2,10},{10,2},{3,11},{11,3},{4,12},{12,4},... | collective-permute-start | bytes 3145736 | tf_op jit(solution)/shard_map/ppermute | solution.py:36
  9.4 35.0 %collective-permute-start.5 = (bf16[128,4096]{1,0:T(8,128)(2,1)}, bf16[128,4096]{1,0:T(8,128)(2,1)S(1)}, u32[]{:S(2)}, u32[]{:S(2)}) collective-permute-start(bf16[128,4096]{1,0:T(8,128)(2,1)} %bitcast.31), channel_id=1, source_target_pairs={{0,8},{8,0},{1,9},{9,1},{2,10},{10,2},{3,11},{11,3},{4,12},{12,4},... | collective-permute-start | bytes 3145736 | tf_op jit(solution)/shard_map/ppermute | solution.py:36
  12.2 0.7 collective-permute-start
  13.7 30.7 %all-to-all-start = ((bf16[8,128,256]{2,1,0:T(8,128)(2,1)}), bf16[8,128,256]{2,1,0:T(8,128)(2,1)S(1)}, u32[]{:S(2)}, u32[]{:S(2)}) async-start(bf16[8,128,256]{2,1,0:T(8,128)(2,1)} %broadcast_in_dim.6), calls=%async_computation | async-start | bytes 1048576 | tf_op jit(solution)/shard_map/all_to_all | solution.py:284
  23.6 4.9 %collective-permute-start.1 = (bf16[128,512]{1,0:T(8,128)(2,1)}, bf16[128,512]{1,0:T(8,128)(2,1)S(1)}, u32[]{:S(2)}, u32[]{:S(2)}) collective-permute-start(bf16[128,512]{1,0:T(8,128)(2,1)} %bitcast.26), channel_id=1, source_target_pairs={{0,8},{8,0},{1,9},{9,1},{2,10},{10,2},{3,11},{11,3},{4,12},{12,4},... | collective-permute-start | bytes 393224 | tf_op jit(solution)/shard_map/ppermute | solution.py:36
  28.5 0.9 copy-start.4
  29.5 15.0 %collective-permute-start.3 = (bf16[256,256]{1,0:T(8,128)(2,1)S(1)}, bf16[256,256]{1,0:T(8,128)(2,1)S(1)}, u32[]{:S(2)}, u32[]{:S(2)}) collective-permute-start(bf16[256,256]{1,0:T(8,128)(2,1)S(1)} %join_halves.1.refs_2_), channel_id=1, source_target_pairs={{0,16},{8,24},{16,32},{24,40},{32,48},{40,56},{48,64},{56,72},{64,... | collective-permute-start | bytes 393224 | tf_op jit(solution)/shard_map/ppermute | solution.py:32
  33.5 10.9 %collective-permute-start.2 = (bf16[128,256]{1,0:T(8,128)(2,1)S(1)}, bf16[128,256]{1,0:T(8,128)(2,1)S(1)}, u32[]{:S(2)}, u32[]{:S(2)}) collective-permute-start(bf16[128,256]{1,0:T(8,128)(2,1)S(1)} %slice.28), channel_id=1, source_target_pairs={{0,32},{8,40},{16,48},{24,56},{32,64},{40,72},{48,80},{56,88},{64,... | collective-permute-start | bytes 196616 | tf_op jit(solution)/shard_map/ppermute | solution.py:32
  39.3 5.1 %collective-permute-start.6 = (s32[1,128]{1,0:T(1,128)}, s32[1,128]{1,0:T(1,128)S(1)}, u32[]{:S(2)}, u32[]{:S(2)}) collective-permute-start(s32[1,128]{1,0:T(1,128)} %own_position.1), channel_id=1, source_target_pairs={{0,8},{8,0},{1,9},{9,1},{2,10},{10,2},{3,11},{11,3},{4,12},{12,4},... | collective-permute-start | bytes 1544 | tf_op jit(solution)/shard_map/ppermute | solution.py:36
  42.1 1.2 copy-start.3
  44.4 1.0 copy-start
  45.4 19.4 %all-to-all-start.1 = ((bf16[4,128,1024]{2,1,0:T(8,128)(2,1)}), bf16[4,128,1024]{2,1,0:T(8,128)(2,1)S(1)}, u32[]{:S(2)}, u32[]{:S(2)}) async-start(bf16[4,128,1024]{2,1,0:T(8,128)(2,1)} %bitcast.6), calls=%async_computation.1 | async-start | bytes 2097152 | tf_op jit(solution)/shard_map/all_to_all | solution.py:346
  51.8 1.2 copy-start.1
  64.9 7.4 %collective-permute-start.7 = (bf16[512,1024]{1,0:T(8,128)(2,1)S(1)}, bf16[512,1024]{1,0:T(8,128)(2,1)S(1)}, u32[]{:S(2)}, u32[]{:S(2)}) collective-permute-start(bf16[512,1024]{1,0:T(8,128)(2,1)S(1)} %bitcast.19), channel_id=1, source_target_pairs={{0,8},{8,0},{1,9},{9,1},{2,10},{10,2},{3,11},{11,3},{4,12},{12,4},... | collective-permute-start | bytes 3145736 | tf_op jit(solution)/shard_map/ppermute | solution.py:36
  69.7 8.8 %collective-permute-start.9 = (bf16[256,256]{1,0:T(8,128)(2,1)S(1)}, bf16[256,256]{1,0:T(8,128)(2,1)S(1)}, u32[]{:S(2)}, u32[]{:S(2)}) collective-permute-start(bf16[256,256]{1,0:T(8,128)(2,1)S(1)} %get-tuple-element.40), channel_id=1, source_target_pairs={{16,0},{24,8},{32,16},{40,24},{48,32},{56,40},{64,48},{72,56},{80,... | collective-permute-start | bytes 393224 | tf_op jit(solution)/shard_map/ppermute | solution.py:32
  71.0 7.5 %collective-permute-start.8 = (bf16[128,256]{1,0:T(8,128)(2,1)S(1)}, bf16[128,256]{1,0:T(8,128)(2,1)S(1)}, u32[]{:S(2)}, u32[]{:S(2)}) collective-permute-start(bf16[128,256]{1,0:T(8,128)(2,1)S(1)} %get-tuple-element.39), channel_id=1, source_target_pairs={{32,0},{40,8},{48,16},{56,24},{64,32},{72,40},{80,48},{88,56},{96,... | collective-permute-start | bytes 196616 | tf_op jit(solution)/shard_map/ppermute | solution.py:32
  96.7 10.0 %collective-permute-start.11 = (bf16[256,256]{1,0:T(8,128)(2,1)S(1)}, bf16[256,256]{1,0:T(8,128)(2,1)S(1)}, u32[]{:S(2)}, u32[]{:S(2)}) collective-permute-start(bf16[256,256]{1,0:T(8,128)(2,1)S(1)} %slice_reduce_fusion.refs_2_), channel_id=1, source_target_pairs={{0,16},{8,24},{16,32},{24,40},{32,48},{40,56},{48,64},{56,72},{64,... | collective-permute-start | bytes 393224 | tf_op jit(solution)/shard_map/ppermute | solution.py:32
  98.0 8.6 %collective-permute-start.10 = (bf16[128,256]{1,0:T(8,128)(2,1)S(1)}, bf16[128,256]{1,0:T(8,128)(2,1)S(1)}, u32[]{:S(2)}, u32[]{:S(2)}) collective-permute-start(bf16[128,256]{1,0:T(8,128)(2,1)S(1)} %slice.30), channel_id=1, source_target_pairs={{0,32},{8,40},{16,48},{24,56},{32,64},{40,72},{48,80},{56,88},{64,... | collective-permute-start | bytes 196616 | tf_op jit(solution)/shard_map/ppermute | solution.py:32
  106.6 27.9 %all-to-all-start.3 = ((bf16[64,16,256]{2,1,0:T(8,128)(2,1)}), bf16[64,16,256]{2,1,0:T(8,128)(2,1)S(1)}, u32[]{:S(2)}, u32[]{:S(2)}) async-start(bf16[64,16,256]{2,1,0:T(8,128)(2,1)} %bitcast.10), calls=%async_computation.3 | async-start | bytes 1048576 | tf_op jit(solution)/shard_map/all_to_all | solution.py:361
  119.5 1.2 copy-start.2
  134.5 7.3 %collective-permute-start.14 = (bf16[256,256]{1,0:T(8,128)(2,1)S(1)}, bf16[256,256]{1,0:T(8,128)(2,1)S(1)}, u32[]{:S(2)}, u32[]{:S(2)}) collective-permute-start(bf16[256,256]{1,0:T(8,128)(2,1)S(1)} %get-tuple-element.54), channel_id=1, source_target_pairs={{16,0},{24,8},{32,16},{40,24},{48,32},{56,40},{64,48},{72,56},{80,... | collective-permute-start | bytes 393224 | tf_op jit(solution)/shard_map/ppermute | solution.py:32
  135.8 6.0 %collective-permute-start.13 = (bf16[128,256]{1,0:T(8,128)(2,1)S(1)}, bf16[128,256]{1,0:T(8,128)(2,1)S(1)}, u32[]{:S(2)}, u32[]{:S(2)}) collective-permute-start(bf16[128,256]{1,0:T(8,128)(2,1)S(1)} %get-tuple-element.53), channel_id=1, source_target_pairs={{32,0},{40,8},{48,16},{56,24},{64,32},{72,40},{80,48},{88,56},{96,... | collective-permute-start | bytes 196616 | tf_op jit(solution)/shard_map/ppermute | solution.py:32
  137.2 0.7 collective-permute-start.12
  142.5 22.4 %all-to-all-start.4 = ((bf16[32,16,256]{2,1,0:T(8,128)(2,1)}), bf16[32,16,256]{2,1,0:T(8,128)(2,1)S(1)}, u32[]{:S(2)}, u32[]{:S(2)}) async-start(bf16[32,16,256]{2,1,0:T(8,128)(2,1)} %broadcast_in_dim.8), calls=%async_computation.4 | async-start | bytes 524288 | tf_op jit(solution)/shard_map/all_to_all | solution.py:326
  155.3 19.7 %collective-permute-start.15 = (bf16[128,256]{1,0:T(8,128)(2,1)S(1)}, bf16[128,256]{1,0:T(8,128)(2,1)S(1)}, u32[]{:S(2)}, u32[]{:S(2)}) collective-permute-start(bf16[128,256]{1,0:T(8,128)(2,1)S(1)} %get-tuple-element.58), channel_id=1, source_target_pairs={{0,8},{8,0},{1,9},{9,1},{2,10},{10,2},{3,11},{11,3},{4,12},{12,4},... | collective-permute-start | bytes 196616 | tf_op jit(solution)/shard_map/ppermute | solution.py:36
  164.9 11.2 %collective-permute-start.16 = (bf16[512,256]{1,0:T(8,128)(2,1)S(1)}, bf16[512,256]{1,0:T(8,128)(2,1)S(1)}, u32[]{:S(2)}, u32[]{:S(2)}) collective-permute-start(bf16[512,256]{1,0:T(8,128)(2,1)S(1)} %bitcast.34), channel_id=1, source_target_pairs={{0,8},{8,0},{1,9},{9,1},{2,10},{10,2},{3,11},{11,3},{4,12},{12,4},... | collective-permute-start | bytes 786440 | tf_op jit(solution)/shard_map/ppermute | solution.py:36

commit v8 on v6

--- a/solution.py
+++ b/solution.py
@@ -221,28 +221,18 @@
         out_ref[rows_at(block, 1), :] = half
 
 
-def partial_values_kernel(core_ref, near_ref, far_ref, weight_ref, out_ref):
-    for rows_ref, core in ((near_ref, core_ref[0]), (far_ref, 1 - core_ref[0])):
-        values = jnp.dot(rows_ref[...], weight_ref[...], preferred_element_type=jnp.float32)
-        values = values.astype(jnp.bfloat16)
-        for x in range(4):
-            out_ref[rows_at(2 * x + core, 1), :] = values[x * BLOCK : (x + 1) * BLOCK]
-
-
-def pack_kernel(two_ref, one_ref, own_ref, values_ref, out_ref):
+def pack_kernel(two_ref, one_ref, own_ref, out_ref):
     total = own_ref[...] + one_ref[...].astype(jnp.float32)
     last = total[BLOCK:] + two_ref[...].astype(jnp.float32)
     low = jnp.concatenate([total[:BLOCK], last], axis=0).astype(jnp.bfloat16)
     for x in range(4):
-        rows = slice(x * 2 * BLOCK, (x + 1) * 2 * BLOCK)
-        out_ref[rows, :HALF] = low
-        out_ref[rows, HALF:] = values_ref[rows, :]
+        out_ref[x * 2 * BLOCK : (x + 1) * 2 * BLOCK, :] = low
 
 
 def product_kernel(core_ref, near_ref, far_ref, grads_ref, out_ref):
     total = None
     for rows_ref, core in ((near_ref, core_ref[0]), (far_ref, 1 - core_ref[0])):
-        grads = [grads_ref[rows_at(2 * x + core, 1), :HALF] for x in range(4)]
+        grads = [grads_ref[rows_at(2 * x + core, 1), :] for x in range(4)]
         part = lax.dot_general(
             jnp.concatenate(grads, axis=0), rows_ref[...], TN, preferred_element_type=jnp.float32
         )
@@ -273,51 +263,29 @@
     )(core, own, other)
 
 
-def projection_piece(w_value):
-    route = [(target, source) for source, target in plane_route()]
-    start = (lax.axis_index("x") * BLOCK, lax.axis_index("c") * HALF)
-    return lax.ppermute(lax.dynamic_slice(w_value, start, (BLOCK, HALF)), ALL, route)
-
-
-def projection_part(piece):
-    copies = jnp.broadcast_to(piece[None], (8, BLOCK, HALF)).reshape(8 * BLOCK, HALF)
-    return lax.all_to_all(copies, "y", 0, 0, tiled=True)
-
-
-def partial_values(core, near, far, weight):
-    return pl.pallas_call(
-        partial_values_kernel,
-        in_specs=[in_smem, in_vmem, in_vmem, in_vmem],
+def exchange_value_grad(two, one, own):
+    packed = pl.pallas_call(
+        pack_kernel,
+        in_specs=[in_vmem] * 3,
         out_specs=in_vmem,
         out_shape=jax.ShapeDtypeStruct((8 * BLOCK, HALF), jnp.bfloat16),
         compiler_params=params,
-        name="partial_values",
-    )(core, near, far, weight)
-
-
-def exchange_packed(two, one, own, values):
-    packed = pl.pallas_call(
-        pack_kernel,
-        in_specs=[in_vmem] * 4,
-        out_specs=in_vmem,
-        out_shape=jax.ShapeDtypeStruct((8 * BLOCK, 2 * HALF), jnp.bfloat16),
-        compiler_params=params,
         name="pack",
-    )(two, one, own, values)
+    )(two, one, own)
     return lax.all_to_all(packed, "x", 0, 0, tiled=True)
 
 
-def group_product(core, near, far, packed):
+def group_product(core, near, far, value_grads):
     rows = pl.BlockSpec((4 * BLOCK, HALF), lambda part: (0, part))
     return pl.pallas_call(
         product_kernel,
         grid=(QUARTER // HALF,),
-        in_specs=[in_smem, rows, rows, pl.BlockSpec((8 * BLOCK, 2 * HALF), lambda part: (0, 0))],
+        in_specs=[in_smem, rows, rows, pl.BlockSpec((8 * BLOCK, HALF), lambda part: (0, 0))],
         out_specs=pl.BlockSpec((HALF, HALF), lambda part: (part, 0)),
         out_shape=jax.ShapeDtypeStruct((QUARTER, HALF), jnp.bfloat16),
         compiler_params=params,
         name="group_product",
-    )(core, near, far, packed)
+    )(core, near, far, value_grads)
 
 
 def whole_shard(piece, even):
@@ -335,27 +303,25 @@
     queries, keys, grads, rows = queries[0], key_rows[0], out_grad[0], inputs[0]
     core = lax.axis_index("c").astype(jnp.int32).reshape(1)
     even = core[0] == 0
-    weight = projection_piece(w_value)
-    other_keys = swap(keys)
-    near = lax.all_to_all(column_quarters(rows), "x", 0, 0, tiled=True)
-    both_queries = (in_hbm(queries), swap(queries))
-    both_grads = (in_hbm(grads), swap(grads))
-    positions = (doc_pos, swap(doc_pos))
-    other_keys, weight = lax.optimization_barrier((other_keys, weight))
-    key_span = span_blocks(join_halves(core, keys, other_keys))
+    whole_weight = lax.all_gather(w_value, "y", axis=0, tiled=True)
+    key_span = span_blocks(join_halves(core, keys, swap(keys)))
+    others = (swap(queries), swap(grads), swap(doc_pos))
+    quarters, key_span, others = lax.optimization_barrier((column_quarters(rows), key_span, others))
+    near = lax.all_to_all(quarters, "x", 0, 0, tiled=True)
+    both_queries, both_grads = (in_hbm(queries), others[0]), (in_hbm(grads), others[1])
+    positions = (doc_pos, others[2])
     weights, *value_parts = attention_weights(core, positions, both_queries, both_grads, key_span)
-    near, weight, value_parts = lax.optimization_barrier((near, weight, value_parts))
 
     two, one, own = value_parts
     two, one = shift(two, -2), shift(one, -1)
+    near, two, one = lax.optimization_barrier((near, two, one))
     far = swap(near)
-    values = partial_values(core, near, far, projection_part(weight))
-    packed = exchange_packed(two, one, own, values)
-    product = group_product(core, near, far, packed)
+    product = group_product(core, near, far, exchange_value_grad(two, one, own))
+    rows, product = lax.optimization_barrier((rows, product))
     pieces = lax.all_to_all(product, ("y", "z"), 0, 0, tiled=True)
 
-    parts = packed.reshape(4, 2 * BLOCK, 2 * HALF)[:, :, HALF:].astype(jnp.float32)
-    value_span = span_blocks(jnp.sum(parts, axis=0).astype(jnp.bfloat16))
+    values = jnp.dot(rows, whole_weight, preferred_element_type=jnp.float32).astype(jnp.bfloat16)
+    value_span = span_blocks(join_halves(core, values, swap(values)))
     pieces, value_span = lax.optimization_barrier((pieces, value_span))
     key_parts = key_gradient(core, weights, both_queries, both_grads, value_span)
 

time: 178 us -> 167 us (0.938)
  between operations: 1.04 us -> 14.4 us
  waiting for transfers between devices: 36.2 us -> 23.1 us
  blocking collectives: 23.2 us -> 14.8 us
  starting transfers between devices: 86.5 us -> 81.8 us
  matrix products: 0 us -> 2.91 us
    all_to_all x2 -> x1, waiting for transfers between devices: 15.4 us -> 0.01 us  [per_device(): near = lax.all_to_all(quarters, 'x', 0, 0, tiled=True)]
    all_to_all x2 -> x1, starting transfers between devices: 20.3 us -> 6.42 us  [per_device(): near = lax.all_to_all(quarters, 'x', 0, 0, tiled=True)]
    all_to_all x1, blocking collectives: 23.2 us -> 14.8 us  [exchange_value_grad(): return lax.all_to_all(packed, 'x', 0, 0, tiled=True)]
    all_to_all x1, starting transfers between devices: 6.03 us -> 13.1 us  [per_device(): pieces = lax.all_to_all(product, ('y', 'z'), 0, 0, tiled=True)]
    ppermute x7 -> x8, starting transfers between devices: 23.9 us -> 29.4 us  [swap(): return lax.ppermute(block, 'c', OTHER_CORE)]
    dot_general x0 -> x1, matrix products: none -> 2.91 us  [per_device(): jnp.dot(rows, whole_weight, preferred_element_type=jnp.float32)]
    all_to_all x1, starting transfers between devices: 17.7 us -> 15.3 us  [whole_shard(): half = lax.all_to_all(copies, ('x', 'z'), 0, 0, tiled=True)]
    unnamed x20 -> x24, local copies, waits for them, and re-layouts: 5.7 us -> 6.63 us
  transfers between devices with their start and end apart: 21 -> 21, of which waited for: 6 -> 8; matrix products, arithmetic and copies ran while one was open for 2% -> 2% of each run, Pallas kernels for 10% -> 11%
where the time goes in v8:
time: 167 us; the launch traced here: 166 us
  starting transfers between devices  81.8 us (49%)
  waiting for transfers between devices  23.1 us (14%)
  Pallas kernels  19 us (11%)
  blocking collectives  14.8 us (9%)
  between operations  14.4 us (9%)
  local copies, waits for them, and re-layouts  7.36 us (4%)
  matrix products  2.91 us (2%)
  other arithmetic  2.78 us (2%)
    ppermute x8, starting transfers between devices, swap(): return lax.ppermute(block, 'c', OTHER_CORE)  29.4 us
    ppermute x8, waiting for transfers between devices, shift(): return lax.ppermute(block, DP, route)  17.9 us
    ppermute x8, starting transfers between devices, shift(): return lax.ppermute(block, DP, route)  16.8 us
    all_to_all x1, starting transfers between devices, whole_shard(): half = lax.all_to_all(copies, ('x', 'z'), 0, 0, tiled=True)  15.3 us
    all_to_all x1, blocking collectives, exchange_value_grad(): return lax.all_to_all(packed, 'x', 0, 0, tiled=True)  14.8 us
    all_to_all x1, starting transfers between devices, per_device(): pieces = lax.all_to_all(product, ('y', 'z'), 0, 0, tiled=True)  13.1 us
    pallas_call x1, Pallas kernels, attention_weights(): pl.pallas_call(weights_kernel, grid_spec=pltpu.PrefetchScalarGridSpec(num...  8.28 us
    pallas_call x1, Pallas kernels, key_gradient(): pl.pallas_call(scores_kernel, grid_spec=pltpu.PrefetchScalarGridSpec(num_...  6.83 us
  transfers between devices with their start and end apart: 21, of which 8 were waited for; matrix products, arithmetic and copies ran while one was open for 2% of the time, Pallas kernels for 11%

profile of v8, /device:TPU:1, one launch (start us, length us, event | category | flops | bytes accessed | tf_op | source)
XLA Modules:
  0.0 166.2 jit_solution(6949468265716741461)
XLA Ops:
  7.9 8.8 %collective-permute-start.3 = (bf16[128,4096]{1,0:T(8,128)(2,1)}, bf16[128,4096]{1,0:T(8,128)(2,1)S(1)}, u32[]{:S(2)}, u32[]{:S(2)}) collective-permute-start(bf16[128,4096]{1,0:T(8,128)(2,1)} %bitcast.28), channel_id=1, source_target_pairs={{0,8},{8,0},{1,9},{9,1},{2,10},{10,2},{3,11},{11,3},{4,12},{12,4},... | collective-permute-start | bytes 3145736 | tf_op jit(solution)/shard_map/ppermute | solution.py:36
  16.7 1.9 %collective-permute-start.4 = (bf16[128,4096]{1,0:T(8,128)(2,1)}, bf16[128,4096]{1,0:T(8,128)(2,1)S(1)}, u32[]{:S(2)}, u32[]{:S(2)}) collective-permute-start(bf16[128,4096]{1,0:T(8,128)(2,1)} %bitcast.31), channel_id=1, source_target_pairs={{0,8},{8,0},{1,9},{9,1},{2,10},{10,2},{3,11},{11,3},{4,12},{12,4},... | collective-permute-start | bytes 3145736 | tf_op jit(solution)/shard_map/ppermute | solution.py:36
  18.6 2.4 %collective-permute-start = (bf16[128,512]{1,0:T(8,128)(2,1)}, bf16[128,512]{1,0:T(8,128)(2,1)S(1)}, u32[]{:S(2)}, u32[]{:S(2)}) collective-permute-start(bf16[128,512]{1,0:T(8,128)(2,1)} %bitcast.26), channel_id=1, source_target_pairs={{0,8},{8,0},{1,9},{9,1},{2,10},{10,2},{3,11},{11,3},{4,12},{12,4},... | collective-permute-start | bytes 393224 | tf_op jit(solution)/shard_map/ppermute | solution.py:36
  21.1 1.2 collective-permute-done.other_ref
  23.1 1.3 collective-permute-start.2
  24.5 3.1 %collective-permute-start.1 = (bf16[128,256]{1,0:T(8,128)(2,1)S(1)}, bf16[128,256]{1,0:T(8,128)(2,1)S(1)}, u32[]{:S(2)}, u32[]{:S(2)}) collective-permute-start(bf16[128,256]{1,0:T(8,128)(2,1)S(1)} %slice.24), channel_id=1, source_target_pairs={{0,32},{8,40},{16,48},{24,56},{32,64},{40,72},{48,80},{56,88},{64,... | collective-permute-start | bytes 196616 | tf_op jit(solution)/shard_map/ppermute | solution.py:32
  27.6 2.8 %collective-permute-start.5 = (s32[1,128]{1,0:T(1,128)}, s32[1,128]{1,0:T(1,128)S(1)}, u32[]{:S(2)}, u32[]{:S(2)}) collective-permute-start(s32[1,128]{1,0:T(1,128)} %own_position.1), channel_id=1, source_target_pairs={{0,8},{8,0},{1,9},{9,1},{2,10},{10,2},{3,11},{11,3},{4,12},{12,4},... | collective-permute-start | bytes 1544 | tf_op jit(solution)/shard_map/ppermute | solution.py:36
  30.5 1.2 copy-done
  34.0 6.4 %all-to-all-start = ((bf16[4,128,1024]{2,1,0:T(8,128)(2,1)}), bf16[4,128,1024]{2,1,0:T(8,128)(2,1)S(1)}, u32[]{:S(2)}, u32[]{:S(2)}) async-start(bf16[4,128,1024]{2,1,0:T(8,128)(2,1)} %bitcast.5), calls=%async_computation | async-start | bytes 2097152 | tf_op jit(solution)/shard_map/all_to_all | solution.py:310
  42.2 8.3 %attention_weights.1 = (bf16[2,2,512,1024]{3,2,1,0:T(8,128)(2,1)}, bf16[128,256]{1,0:T(8,128)(2,1)S(1)}, bf16[256,256]{1,0:T(8,128)(2,1)S(1)}, f32[256,256]{1,0:T(8,128)S(1)}) custom-call(s32[1]{0:T(128)} %bitcast.1.core_ref, s32[1,128]{1,0:T(1,128)S(1)} %copy-done.11, s32[1,128]{1,0:T(1,128)S(1)} %collective-permute-done.5.other_position, ...), custom_call_target="tpu_custom_call" | custom-call | flops 2147483648 | bytes 8388608 | tf_op jit(solution)/shard_map/attention_weights/pallas_call | solution.py:165
  50.5 1.4 collective-permute-start.7
  51.9 1.3 collective-permute-start.6
  53.2 6.3 %collective-permute-done.6.two_ref = bf16[128,256]{1,0:T(8,128)(2,1)S(1)} collective-permute-done((bf16[128,256]{1,0:T(8,128)(2,1)S(1)}, bf16[128,256]{1,0:T(8,128)(2,1)S(1)}, u32[]{:S(2)}, u32[]{:S(2)}) %collective-permute-start.6) | collective-permute-done | bytes 65568 | tf_op jit(solution)/shard_map/ppermute | solution.py:32
  60.1 3.7 %collective-permute-start.8 = (bf16[512,1024]{1,0:T(8,128)(2,1)S(1)}, bf16[512,1024]{1,0:T(8,128)(2,1)S(1)}, u32[]{:S(2)}, u32[]{:S(2)}) collective-permute-start(bf16[512,1024]{1,0:T(8,128)(2,1)S(1)} %bitcast.20), channel_id=1, source_target_pairs={{0,8},{8,0},{1,9},{9,1},{2,10},{10,2},{3,11},{11,3},{4,12},{12,4},... | collective-permute-start | bytes 3145736 | tf_op jit(solution)/shard_map/ppermute | solution.py:36
  64.8 14.8 %all_to_all.44 = bf16[4,256,256]{2,1,0:T(8,128)(2,1)S(1)} all-to-all(bf16[4,256,256]{2,1,0:T(8,128)(2,1)S(1)} %bitcast.24), channel_id=1, replica_groups=mesh['x'=4,'z'=8,'c'=2,'y'=8] {'x'}, dimensions={0} | all-to-all | bytes 1048576 | tf_op jit(solution)/shard_map/all_to_all | solution.py:275
  79.6 2.8 %group_product.1 = bf16[1024,256]{1,0:T(8,128)(2,1)} custom-call(s32[1]{0:T(128)} %bitcast.1.core_ref, bf16[512,1024]{1,0:T(8,128)(2,1)S(1)} %bitcast.21, bf16[512,1024]{1,0:T(8,128)(2,1)S(1)} %collective-permute-done.8.far_ref, bf16[1024,256]{1,0:T(8,128)(2,1)S(1)} %bitcast.25), custom_call_target="tpu_custom_call" | custom-call | tf_op jit(solution)/shard_map/group_product/pallas_call | solution.py:280
  82.4 13.1 %all-to-all-start.2 = ((bf16[64,16,256]{2,1,0:T(8,128)(2,1)}), bf16[64,16,256]{2,1,0:T(8,128)(2,1)}, u32[]{:S(2)}, u32[]{:S(2)}) async-start(bf16[64,16,256]{2,1,0:T(8,128)(2,1)} %bitcast.9), calls=%async_computation.2 | async-start | bytes 1048576 | tf_op jit(solution)/shard_map/all_to_all | solution.py:321
  95.5 2.9 %convolution_convert_fusion.own_ref = bf16[128,512]{1,0:T(8,128)(2,1)S(1)} fusion(bf16[128,4096]{1,0:T(8,128)(2,1)S(1)} %bitcast.23, bf16[4096,512]{1,0:T(8,128)(2,1)} %all-gather.2.cloned.1.call-done), kind=kOutput, calls=%fused_computation | convolution fusion | flops 536936448 | bytes 5373952 | tf_op jit(solution)/shard_map/dot_general | solution.py:323
  98.5 3.3 %collective-permute-start.9 = (bf16[128,512]{1,0:T(8,128)(2,1)S(1)}, bf16[128,512]{1,0:T(8,128)(2,1)S(1)}, u32[]{:S(2)}, u32[]{:S(2)}) collective-permute-start(bf16[128,512]{1,0:T(8,128)(2,1)S(1)} %convolution_convert_fusion.own_ref), channel_id=1, source_target_pairs={{0,8},{8,0},{1,9},{9,1},{2,10},{10,2},{3,11},{11,3},{4,12},{12,4},... | collective-permute-start | bytes 393224 | tf_op jit(solution)/shard_map/ppermute | solution.py:36
  102.7 3.1 %collective-permute-start.11 = (bf16[256,256]{1,0:T(8,128)(2,1)S(1)}, bf16[256,256]{1,0:T(8,128)(2,1)S(1)}, u32[]{:S(2)}, u32[]{:S(2)}) collective-permute-start(bf16[256,256]{1,0:T(8,128)(2,1)S(1)} %join_halves.3.refs_2_), channel_id=1, source_target_pairs={{0,16},{8,24},{16,32},{24,40},{32,48},{40,56},{48,64},{56,72},{64,... | collective-permute-start | bytes 393224 | tf_op jit(solution)/shard_map/ppermute | solution.py:32
  105.9 4.0 %collective-permute-start.10 = (bf16[128,256]{1,0:T(8,128)(2,1)S(1)}, bf16[128,256]{1,0:T(8,128)(2,1)S(1)}, u32[]{:S(2)}, u32[]{:S(2)}) collective-permute-start(bf16[128,256]{1,0:T(8,128)(2,1)S(1)} %slice.25), channel_id=1, source_target_pairs={{0,32},{8,40},{16,48},{24,56},{32,64},{40,72},{48,80},{56,88},{64,... | collective-permute-start | bytes 196616 | tf_op jit(solution)/shard_map/ppermute | solution.py:32
  109.9 1.6 all-to-all-done.2
  111.5 2.3 %collective-permute-done.10.refs_0_ = bf16[128,256]{1,0:T(8,128)(2,1)S(1)} collective-permute-done((bf16[128,256]{1,0:T(8,128)(2,1)S(1)}, bf16[128,256]{1,0:T(8,128)(2,1)S(1)}, u32[]{:S(2)}, u32[]{:S(2)}) %collective-permute-start.10) | collective-permute-done | bytes 65568 | tf_op jit(solution)/shard_map/ppermute | solution.py:32
  113.8 1.1 convert_reduce_fusion
  115.6 6.8 %key_gradient.1 = (bf16[128,256]{1,0:T(8,128)(2,1)S(1)}, bf16[256,256]{1,0:T(8,128)(2,1)S(1)}, f32[256,256]{1,0:T(8,128)S(1)}) custom-call(s32[1]{0:T(128)} %bitcast.1.core_ref, bf16[2,2,512,1024]{3,2,1,0:T(8,128)(2,1)} %get-tuple-element.45.weights_ref, bf16[128,4096]{1,0:T(8,128)(2,1)} %bitcast.30, ...), custom_call_target="tpu_custom_call" | custom-call | flops 2147483648 | bytes 8388608 | tf_op jit(solution)/shard_map/key_gradient/pallas_call | solution.py:184
  123.2 15.3 %all-to-all-start.3 = ((bf16[32,16,256]{2,1,0:T(8,128)(2,1)}), bf16[32,16,256]{2,1,0:T(8,128)(2,1)S(1)}, u32[]{:S(2)}, u32[]{:S(2)}) async-start(bf16[32,16,256]{2,1,0:T(8,128)(2,1)} %broadcast_in_dim.10), calls=%async_computation.3 | async-start | bytes 524288 | tf_op jit(solution)/shard_map/all_to_all | solution.py:294
  138.5 1.3 collective-permute-start.13
  139.8 1.3 collective-permute-start.14
  141.1 5.8 %collective-permute-done.13 = bf16[256,256]{1,0:T(8,128)(2,1)S(1)} collective-permute-done((bf16[256,256]{1,0:T(8,128)(2,1)S(1)}, bf16[256,256]{1,0:T(8,128)(2,1)S(1)}, u32[]{:S(2)}, u32[]{:S(2)}) %collective-permute-start.13) | collective-permute-done | bytes 131104 | tf_op jit(solution)/shard_map/ppermute | solution.py:32
  147.0 3.4 %collective-permute-done.14 = bf16[128,256]{1,0:T(8,128)(2,1)S(1)} collective-permute-done((bf16[128,256]{1,0:T(8,128)(2,1)S(1)}, bf16[128,256]{1,0:T(8,128)(2,1)S(1)}, u32[]{:S(2)}, u32[]{:S(2)}) %collective-permute-start.14) | collective-permute-done | bytes 65568 | tf_op jit(solution)/shard_map/ppermute | solution.py:32
  150.5 4.6 %collective-permute-start.15 = (bf16[128,256]{1,0:T(8,128)(2,1)S(1)}, bf16[128,256]{1,0:T(8,128)(2,1)S(1)}, u32[]{:S(2)}, u32[]{:S(2)}) collective-permute-start(bf16[128,256]{1,0:T(8,128)(2,1)S(1)} %get-tuple-element.56), channel_id=1, source_target_pairs={{0,8},{8,0},{1,9},{9,1},{2,10},{10,2},{3,11},{11,3},{4,12},{12,4},... | collective-permute-start | bytes 196616 | tf_op jit(solution)/shard_map/ppermute | solution.py:36
  155.1 1.9 %collective-permute-start.16 = (bf16[512,256]{1,0:T(8,128)(2,1)S(1)}, bf16[512,256]{1,0:T(8,128)(2,1)S(1)}, u32[]{:S(2)}, u32[]{:S(2)}) collective-permute-start(bf16[512,256]{1,0:T(8,128)(2,1)S(1)} %bitcast.34), channel_id=1, source_target_pairs={{0,8},{8,0},{1,9},{9,1},{2,10},{10,2},{3,11},{11,3},{4,12},{12,4},... | collective-permute-start | bytes 786440 | tf_op jit(solution)/shard_map/ppermute | solution.py:36
  (55 shorter events, 12.1 us)
Async XLA Ops:
  7.2 33.3 %copy-start.11 = (s32[1,128]{1,0:T(1,128)S(1)}, s32[1,128]{1,0:T(1,128)}, u32[]{:S(2)}) copy-start(s32[1,128]{1,0:T(1,128)} %own_position.1) | copy-start | bytes 1540
  7.2 88.4 %all-gather.2.cloned.1.call-start = ((), (), s32[]{:S(2)}) async-start(), calls=%async_computation.4 | async-start | bytes 4718592 | tf_op jit(solution)/shard_map/all_gather | solution.py:306
  7.9 26.1 %collective-permute-start.3 = (bf16[128,4096]{1,0:T(8,128)(2,1)}, bf16[128,4096]{1,0:T(8,128)(2,1)S(1)}, u32[]{:S(2)}, u32[]{:S(2)}) collective-permute-start(bf16[128,4096]{1,0:T(8,128)(2,1)} %bitcast.28), channel_id=1, source_target_pairs={{0,8},{8,0},{1,9},{9,1},{2,10},{10,2},{3,11},{11,3},{4,12},{12,4},... | collective-permute-start | bytes 3145736 | tf_op jit(solution)/shard_map/ppermute | solution.py:36
  16.7 17.3 %collective-permute-start.4 = (bf16[128,4096]{1,0:T(8,128)(2,1)}, bf16[128,4096]{1,0:T(8,128)(2,1)S(1)}, u32[]{:S(2)}, u32[]{:S(2)}) collective-permute-start(bf16[128,4096]{1,0:T(8,128)(2,1)} %bitcast.31), channel_id=1, source_target_pairs={{0,8},{8,0},{1,9},{9,1},{2,10},{10,2},{3,11},{11,3},{4,12},{12,4},... | collective-permute-start | bytes 3145736 | tf_op jit(solution)/shard_map/ppermute | solution.py:36
  18.6 3.6 %collective-permute-start = (bf16[128,512]{1,0:T(8,128)(2,1)}, bf16[128,512]{1,0:T(8,128)(2,1)S(1)}, u32[]{:S(2)}, u32[]{:S(2)}) collective-permute-start(bf16[128,512]{1,0:T(8,128)(2,1)} %bitcast.26), channel_id=1, source_target_pairs={{0,8},{8,0},{1,9},{9,1},{2,10},{10,2},{3,11},{11,3},{4,12},{12,4},... | collective-permute-start | bytes 393224 | tf_op jit(solution)/shard_map/ppermute | solution.py:36
  22.2 0.9 copy-start.4
  23.1 10.2 %collective-permute-start.2 = (bf16[256,256]{1,0:T(8,128)(2,1)S(1)}, bf16[256,256]{1,0:T(8,128)(2,1)S(1)}, u32[]{:S(2)}, u32[]{:S(2)}) collective-permute-start(bf16[256,256]{1,0:T(8,128)(2,1)S(1)} %join_halves.2.refs_2_), channel_id=1, source_target_pairs={{0,16},{8,24},{16,32},{24,40},{32,48},{40,56},{48,64},{56,72},{64,... | collective-permute-start | bytes 393224 | tf_op jit(solution)/shard_map/ppermute | solution.py:32
  24.5 8.3 %collective-permute-start.1 = (bf16[128,256]{1,0:T(8,128)(2,1)S(1)}, bf16[128,256]{1,0:T(8,128)(2,1)S(1)}, u32[]{:S(2)}, u32[]{:S(2)}) collective-permute-start(bf16[128,256]{1,0:T(8,128)(2,1)S(1)} %slice.24), channel_id=1, source_target_pairs={{0,32},{8,40},{16,48},{24,56},{32,64},{40,72},{48,80},{56,88},{64,... | collective-permute-start | bytes 196616 | tf_op jit(solution)/shard_map/ppermute | solution.py:32
  27.6 5.1 %collective-permute-start.5 = (s32[1,128]{1,0:T(1,128)}, s32[1,128]{1,0:T(1,128)S(1)}, u32[]{:S(2)}, u32[]{:S(2)}) collective-permute-start(s32[1,128]{1,0:T(1,128)} %own_position.1), channel_id=1, source_target_pairs={{0,8},{8,0},{1,9},{9,1},{2,10},{10,2},{3,11},{11,3},{4,12},{12,4},... | collective-permute-start | bytes 1544 | tf_op jit(solution)/shard_map/ppermute | solution.py:36
  30.5 1.2 copy-start
  32.7 0.6 copy-start.9
  33.4 0.7 copy-start.7
  34.0 6.4 %copy-start.2 = (bf16[128,4096]{1,0:T(8,128)(2,1)}, bf16[128,4096]{1,0:T(8,128)(2,1)S(1)}, u32[]{:S(2)}) copy-start(bf16[128,4096]{1,0:T(8,128)(2,1)S(1)} %collective-permute-done.4.other_grad) | copy-start | bytes 3145732
  34.0 26.1 %all-to-all-start = ((bf16[4,128,1024]{2,1,0:T(8,128)(2,1)}), bf16[4,128,1024]{2,1,0:T(8,128)(2,1)S(1)}, u32[]{:S(2)}, u32[]{:S(2)}) async-start(bf16[4,128,1024]{2,1,0:T(8,128)(2,1)} %bitcast.5), calls=%async_computation | async-start | bytes 2097152 | tf_op jit(solution)/shard_map/all_to_all | solution.py:310
  40.5 0.9 copy-start.8
  41.4 0.8 copy-start.10
  50.5 45.0 %copy-start.1 = (bf16[1,128,4096]{2,1,0:T(8,128)(2,1)S(1)}, bf16[1,128,4096]{2,1,0:T(8,128)(2,1)}, u32[]{:S(2)}) copy-start(bf16[1,128,4096]{2,1,0:T(8,128)(2,1)} %param.9) | copy-start | bytes 3145732
  50.5 9.7 %collective-permute-start.7 = (bf16[256,256]{1,0:T(8,128)(2,1)S(1)}, bf16[256,256]{1,0:T(8,128)(2,1)S(1)}, u32[]{:S(2)}, u32[]{:S(2)}) collective-permute-start(bf16[256,256]{1,0:T(8,128)(2,1)S(1)} %get-tuple-element.37), channel_id=1, source_target_pairs={{16,0},{24,8},{32,16},{40,24},{48,32},{56,40},{64,48},{72,56},{80,... | collective-permute-start | bytes 393224 | tf_op jit(solution)/shard_map/ppermute | solution.py:32
  51.9 7.6 %collective-permute-start.6 = (bf16[128,256]{1,0:T(8,128)(2,1)S(1)}, bf16[128,256]{1,0:T(8,128)(2,1)S(1)}, u32[]{:S(2)}, u32[]{:S(2)}) collective-permute-start(bf16[128,256]{1,0:T(8,128)(2,1)S(1)} %get-tuple-element.36), channel_id=1, source_target_pairs={{32,0},{40,8},{48,16},{56,24},{64,32},{72,40},{80,48},{88,56},{96,... | collective-permute-start | bytes 196616 | tf_op jit(solution)/shard_map/ppermute | solution.py:32
  60.1 19.4 %collective-permute-start.8 = (bf16[512,1024]{1,0:T(8,128)(2,1)S(1)}, bf16[512,1024]{1,0:T(8,128)(2,1)S(1)}, u32[]{:S(2)}, u32[]{:S(2)}) collective-permute-start(bf16[512,1024]{1,0:T(8,128)(2,1)S(1)} %bitcast.20), channel_id=1, source_target_pairs={{0,8},{8,0},{1,9},{9,1},{2,10},{10,2},{3,11},{11,3},{4,12},{12,4},... | collective-permute-start | bytes 3145736 | tf_op jit(solution)/shard_map/ppermute | solution.py:36
  63.9 0.8 copy-start.6
  82.4 33.3 %copy-start.3 = (bf16[128,4096]{1,0:T(8,128)(2,1)S(1)}, bf16[128,4096]{1,0:T(8,128)(2,1)}, u32[]{:S(2)}) copy-start(bf16[128,4096]{1,0:T(8,128)(2,1)} %copy-done.2) | copy-start | bytes 3145732
  82.4 29.1 %all-to-all-start.2 = ((bf16[64,16,256]{2,1,0:T(8,128)(2,1)}), bf16[64,16,256]{2,1,0:T(8,128)(2,1)}, u32[]{:S(2)}, u32[]{:S(2)}) async-start(bf16[64,16,256]{2,1,0:T(8,128)(2,1)} %bitcast.9), calls=%async_computation.2 | async-start | bytes 1048576 | tf_op jit(solution)/shard_map/all_to_all | solution.py:321
  98.5 4.3 %collective-permute-start.9 = (bf16[128,512]{1,0:T(8,128)(2,1)S(1)}, bf16[128,512]{1,0:T(8,128)(2,1)S(1)}, u32[]{:S(2)}, u32[]{:S(2)}) collective-permute-start(bf16[128,512]{1,0:T(8,128)(2,1)S(1)} %convolution_convert_fusion.own_ref), channel_id=1, source_target_pairs={{0,8},{8,0},{1,9},{9,1},{2,10},{10,2},{3,11},{11,3},{4,12},{12,4},... | collective-permute-start | bytes 393224 | tf_op jit(solution)/shard_map/ppermute | solution.py:36
  102.7 11.1 %collective-permute-start.11 = (bf16[256,256]{1,0:T(8,128)(2,1)S(1)}, bf16[256,256]{1,0:T(8,128)(2,1)S(1)}, u32[]{:S(2)}, u32[]{:S(2)}) collective-permute-start(bf16[256,256]{1,0:T(8,128)(2,1)S(1)} %join_halves.3.refs_2_), channel_id=1, source_target_pairs={{0,16},{8,24},{16,32},{24,40},{32,48},{40,56},{48,64},{56,72},{64,... | collective-permute-start | bytes 393224 | tf_op jit(solution)/shard_map/ppermute | solution.py:32
  105.9 7.9 %collective-permute-start.10 = (bf16[128,256]{1,0:T(8,128)(2,1)S(1)}, bf16[128,256]{1,0:T(8,128)(2,1)S(1)}, u32[]{:S(2)}, u32[]{:S(2)}) collective-permute-start(bf16[128,256]{1,0:T(8,128)(2,1)S(1)} %slice.25), channel_id=1, source_target_pairs={{0,32},{8,40},{16,48},{24,56},{32,64},{40,72},{48,80},{56,88},{64,... | collective-permute-start | bytes 196616 | tf_op jit(solution)/shard_map/ppermute | solution.py:32
  114.9 7.5 %collective-permute-start.12 = (bf16[16,256]{1,0:T(8,128)(2,1)S(1)}, bf16[16,256]{1,0:T(8,128)(2,1)S(1)}, u32[]{:S(2)}, u32[]{:S(2)}) collective-permute-start(bf16[16,256]{1,0:T(8,128)(2,1)S(1)} %multiply_convert_fusion), channel_id=1, source_target_pairs={{0,0},{1,128},{2,256},{3,384},{4,1},{5,129},{6,257},{7,385},{8,8},... | collective-permute-start | bytes 24584 | tf_op jit(solution)/shard_map/ppermute | solution.py:331
  123.2 31.9 %all-to-all-start.3 = ((bf16[32,16,256]{2,1,0:T(8,128)(2,1)}), bf16[32,16,256]{2,1,0:T(8,128)(2,1)S(1)}, u32[]{:S(2)}, u32[]{:S(2)}) async-start(bf16[32,16,256]{2,1,0:T(8,128)(2,1)} %broadcast_in_dim.10), calls=%async_computation.3 | async-start | bytes 524288 | tf_op jit(solution)/shard_map/all_to_all | solution.py:294
  138.5 8.4 %collective-permute-start.13 = (bf16[256,256]{1,0:T(8,128)(2,1)S(1)}, bf16[256,256]{1,0:T(8,128)(2,1)S(1)}, u32[]{:S(2)}, u32[]{:S(2)}) collective-permute-start(bf16[256,256]{1,0:T(8,128)(2,1)S(1)} %get-tuple-element.53), channel_id=1, source_target_pairs={{16,0},{24,8},{32,16},{40,24},{48,32},{56,40},{64,48},{72,56},{80,... | collective-permute-start | bytes 393224 | tf_op jit(solution)/shard_map/ppermute | solution.py:32
  139.8 10.6 %collective-permute-start.14 = (bf16[128,256]{1,0:T(8,128)(2,1)S(1)}, bf16[128,256]{1,0:T(8,128)(2,1)S(1)}, u32[]{:S(2)}, u32[]{:S(2)}) collective-permute-start(bf16[128,256]{1,0:T(8,128)(2,1)S(1)} %get-tuple-element.54), channel_id=1, source_target_pairs={{32,0},{40,8},{48,16},{56,24},{64,32},{72,40},{80,48},{88,56},{96,... | collective-permute-start | bytes 196616 | tf_op jit(solution)/shard_map/ppermute | solution.py:32
  150.5 6.5 %collective-permute-start.15 = (bf16[128,256]{1,0:T(8,128)(2,1)S(1)}, bf16[128,256]{1,0:T(8,128)(2,1)S(1)}, u32[]{:S(2)}, u32[]{:S(2)}) collective-permute-start(bf16[128,256]{1,0:T(8,128)(2,1)S(1)} %get-tuple-element.56), channel_id=1, source_target_pairs={{0,8},{8,0},{1,9},{9,1},{2,10},{10,2},{3,11},{11,3},{4,12},{12,4},... | collective-permute-start | bytes 196616 | tf_op jit(solution)/shard_map/ppermute | solution.py:36
  155.1 3.4 %collective-permute-start.16 = (bf16[512,256]{1,0:T(8,128)(2,1)S(1)}, bf16[512,256]{1,0:T(8,128)(2,1)S(1)}, u32[]{:S(2)}, u32[]{:S(2)}) collective-permute-start(bf16[512,256]{1,0:T(8,128)(2,1)S(1)} %bitcast.34), channel_id=1, source_target_pairs={{0,8},{8,0},{1,9},{9,1},{2,10},{10,2},{3,11},{11,3},{4,12},{12,4},... | collective-permute-start | bytes 786440 | tf_op jit(solution)/shard_map/ppermute | solution.py:36
  (1 other events, 0.6 us)
Sparse Core Ops, SparseCore 0:
  10.1 62.6 all-gather.1

commit v9 on v5

--- a/solution.py
+++ b/solution.py
@@ -171,31 +171,21 @@
         copy.wait()
 
 
-def partial_values_kernel(core_ref, near_ref, far_ref, weight_ref, out_ref):
-    for rows_ref, core in ((near_ref, core_ref[0]), (far_ref, 1 - core_ref[0])):
-        values = jnp.dot(rows_ref[...], weight_ref[...], preferred_element_type=jnp.float32)
-        values = values.astype(jnp.bfloat16)
-        for x in range(4):
-            rows = pl.ds(pl.multiple_of((2 * x + core) * BLOCK, BLOCK), BLOCK)
-            out_ref[rows, :] = values[x * BLOCK : (x + 1) * BLOCK]
-
-
-def pack_kernel(core_ref, own_ref, two_ref, across_ref, three_ref, values_ref, out_ref):
+def pack_kernel(core_ref, own_ref, two_ref, across_ref, three_ref, out_ref):
     last = jnp.where(core_ref[0] == 0, across_ref[...], three_ref[...])
     total = own_ref[...] + two_ref[...].astype(jnp.float32) + last.astype(jnp.float32)
     low = total.astype(jnp.bfloat16)
     for device in range(8):
         core = device % 2
         rows = slice(device * BLOCK, (device + 1) * BLOCK)
-        out_ref[rows, :HALF] = low[:, core * HALF : (core + 1) * HALF]
-        out_ref[rows, HALF:] = values_ref[rows, :]
+        out_ref[rows, :] = low[:, core * HALF : (core + 1) * HALF]
 
 
 def product_kernel(core_ref, near_ref, far_ref, grads_ref, out_ref):
     total = None
     for rows_ref, core in ((near_ref, core_ref[0]), (far_ref, 1 - core_ref[0])):
         grads = [
-            grads_ref[pl.ds(pl.multiple_of((2 * x + core) * BLOCK, BLOCK), BLOCK), :HALF]
+            grads_ref[pl.ds(pl.multiple_of((2 * x + core) * BLOCK, BLOCK), BLOCK), :]
             for x in range(4)
         ]
         part = lax.dot_general(
@@ -217,56 +207,33 @@
         scratch_shapes=[pltpu.SemaphoreType.DMA((4,))],
         compiler_params=params,
         name="quarters",
-    )(in_hbm(rows))
+    )(rows)
     return lax.all_to_all(quarters, "x", 0, 0, tiled=True)
 
 
-def projection_piece(w_value):
-    route = [(target, source) for source, target in plane_route()]
-    start = (lax.axis_index("x") * BLOCK, lax.axis_index("c") * HALF)
-    piece = lax.dynamic_slice(w_value, start, (BLOCK, HALF))
-    return lax.ppermute(piece, ("x", "z", "c", "y"), route)
-
-
-def projection_part(piece):
-    copies = jnp.broadcast_to(piece[None], (8, BLOCK, HALF)).reshape(8 * BLOCK, HALF)
-    return lax.all_to_all(copies, "y", 0, 0, tiled=True)
-
-
-def partial_values(core, near, far, weight):
-    return pl.pallas_call(
-        partial_values_kernel,
-        in_specs=[in_smem, in_vmem, in_vmem, in_vmem],
+def exchange_value_grad(core, own, received):
+    packed = pl.pallas_call(
+        pack_kernel,
+        in_specs=[in_smem] + [in_vmem] * 4,
         out_specs=in_vmem,
         out_shape=jax.ShapeDtypeStruct((8 * BLOCK, HALF), jnp.bfloat16),
         compiler_params=params,
-        name="partial_values",
-    )(core, near, far, weight)
-
-
-def exchange_packed(core, own, received, values):
-    packed = pl.pallas_call(
-        pack_kernel,
-        in_specs=[in_smem] + [in_vmem] * 5,
-        out_specs=in_vmem,
-        out_shape=jax.ShapeDtypeStruct((8 * BLOCK, 2 * HALF), jnp.bfloat16),
-        compiler_params=params,
         name="pack",
-    )(core, own, *received, values)
+    )(core, own, *received)
     return lax.all_to_all(packed, ("x", "c"), 0, 0, tiled=True)
 
 
-def group_product(core, near, far, packed):
+def group_product(core, near, far, value_grads):
     rows = pl.BlockSpec((4 * BLOCK, HALF), lambda part: (0, part))
     return pl.pallas_call(
         product_kernel,
         grid=(QUARTER // HALF,),
-        in_specs=[in_smem, rows, rows, pl.BlockSpec((8 * BLOCK, 2 * HALF), lambda part: (0, 0))],
+        in_specs=[in_smem, rows, rows, pl.BlockSpec((8 * BLOCK, HALF), lambda part: (0, 0))],
         out_specs=pl.BlockSpec((HALF, HALF), lambda part: (part, 0)),
         out_shape=jax.ShapeDtypeStruct((QUARTER, HALF), jnp.bfloat16),
         compiler_params=params,
         name="group_product",
-    )(core, near, far, packed)
+    )(core, near, far, value_grads)
 
 
 def plane_route():
@@ -296,33 +263,29 @@
     queries, keys, grads, rows = queries[0], key_rows[0], out_grad[0], inputs[0]
     core = lax.axis_index("c").astype(jnp.int32).reshape(1)
     even = core[0] == 0
+    whole_weight = lax.all_gather(w_value, "y", axis=0, tiled=True)
     key_blocks = from_earlier(keys)
     near = exchange_rows(rows)
-    weight = projection_piece(w_value)
     weights, *value_parts = attention_weights(core, doc_pos, queries, grads, (keys,) + key_blocks)
-    near, weight, value_parts = lax.optimization_barrier((near, weight, value_parts))
-
     received = to_earlier(value_parts, even)
+    near, received = lax.optimization_barrier((near, received))
+
     far = swap(near)
-    values = partial_values(core, near, far, projection_part(weight))
-    packed = exchange_packed(core, value_parts[SPAN], received, values)
-    product = group_product(core, near, far, packed)
+    value_grads = exchange_value_grad(core, value_parts[SPAN], received)
+    values = jnp.dot(rows, whole_weight, preferred_element_type=jnp.float32).astype(jnp.bfloat16)
+    value_blocks = from_earlier(values)
+    value_grads, value_blocks = lax.optimization_barrier((value_grads, value_blocks))
+    product = group_product(core, near, far, value_grads)
     pieces = lax.all_to_all(product, ("y", "z"), 0, 0, tiled=True)
-
-    parts = packed.reshape(4, 2, BLOCK, 2 * HALF)[..., HALF:].astype(jnp.float32)
-    values = jnp.sum(parts, axis=0).astype(jnp.bfloat16)
-    values = jnp.concatenate([values[0], values[1]], axis=1)
-    value_blocks = from_earlier(values)
-    pieces, value_blocks = lax.optimization_barrier((pieces, value_blocks))
     key_parts = key_gradient(core, weights, queries, grads, (values,) + value_blocks)
+    two, across, three = to_earlier(key_parts, even)
+    pieces, two, across, three = lax.optimization_barrier((pieces, two, across, three))
 
     pieces = pieces.reshape(64, -1, HALF).astype(jnp.float32)
     token_total = lax.axis_size(("x", "z", "c", "y")) * BLOCK
     piece = (jnp.sum(pieces, axis=0) * (1.0 / math.sqrt(token_total))).astype(jnp.bfloat16)
     piece = lax.ppermute(piece, ("x", "z", "c", "y"), plane_route())
-    piece, key_parts = lax.optimization_barrier((piece, key_parts))
     weight_grad = whole_shard(piece)
-    two, across, three = to_earlier(key_parts, even)
     key_grad = key_parts[SPAN] + two.astype(jnp.float32)
     key_grad = key_grad + jnp.where(even, across, three).astype(jnp.float32)
     return (key_grad.astype(jnp.bfloat16)[None], weight_grad)

time: 190 us -> 169 us (0.89)
  Pallas kernels: 50 us -> 20.5 us
  starting transfers between devices: 101 us -> 75.9 us
  between operations: 1.05 us -> 14.4 us
  waiting for transfers between devices: 13.9 us -> 24.1 us
  blocking collectives: 18 us -> 26 us
  matrix products: 0 us -> 2.97 us
  local copies, waits for them, and re-layouts: 3.21 us -> 1.25 us
    pallas_call x1, Pallas kernels: 32.9 us -> 1.06 us  [exchange_rows(): pl.pallas_call(quarters_kernel, in_specs=[pl.BlockSpec(memory_space=pl.AN...]
    all_to_all x2 -> x1, starting transfers between devices: 30.3 us -> 6.1 us  [exchange_value_grad(): return lax.all_to_all(packed, ('x', 'c'), 0, 0, tiled=True)]
    ppermute x12, waiting for transfers between devices: 0.03 us -> 14.9 us  [shift(): return lax.ppermute(block, DP, route)]
    all_to_all x2 -> x1, waiting for transfers between devices: 12.5 us -> 0.01 us  [exchange_value_grad(): return lax.all_to_all(packed, ('x', 'c'), 0, 0, tiled=True)]
    all_to_all x1, blocking collectives: 18 us -> 26 us  [whole_shard(): half = lax.all_to_all(copies, ('x', 'z'), 0, 0, tiled=True)]
    all_gather x0 -> x1, waiting for transfers between devices: none -> 7.14 us  [per_device(): whole_weight = lax.all_gather(w_value, 'y', axis=0, tiled=True)]
    ppermute x6, starting transfers between devices: 24.5 us -> 20.7 us  [swap(): return lax.ppermute(block, 'c', OTHER_CORE)]
    all_to_all x1, starting transfers between devices: 4.85 us -> 7.86 us  [exchange_rows(): return lax.all_to_all(quarters, 'x', 0, 0, tiled=True)]
  transfers between devices with their start and end apart: 24 -> 23, of which waited for: 4 -> 7; matrix products, arithmetic and copies ran while one was open for 1% -> 2% of each run, Pallas kernels for 8% -> 10%
where the time goes in v9:
time: 169 us; the launch traced here: 167 us
  starting transfers between devices  75.9 us (45%)
  blocking collectives  26 us (15%)
  waiting for transfers between devices  24.1 us (14%)
  Pallas kernels  20.5 us (12%)
  between operations  14.4 us (9%)
  matrix products  2.97 us (2%)
  other arithmetic  1.82 us (1%)
    ppermute x12, starting transfers between devices, shift(): return lax.ppermute(block, DP, route)  31.8 us
    all_to_all x1, blocking collectives, whole_shard(): half = lax.all_to_all(copies, ('x', 'z'), 0, 0, tiled=True)  26 us
    ppermute x6, starting transfers between devices, swap(): return lax.ppermute(block, 'c', OTHER_CORE)  20.7 us
    ppermute x12, waiting for transfers between devices, shift(): return lax.ppermute(block, DP, route)  14.9 us
    all_to_all x1, starting transfers between devices, per_device(): pieces = lax.all_to_all(product, ('y', 'z'), 0, 0, tiled=True)  8.79 us
    all_to_all x1, starting transfers between devices, exchange_rows(): return lax.all_to_all(quarters, 'x', 0, 0, tiled=True)  7.86 us
    pallas_call x1, Pallas kernels, attention_weights(): pl.pallas_call(weights_kernel, grid=(KEY_HEADS,), in_specs=[in_smem, pl.B...  7.83 us
    all_gather x1, waiting for transfers between devices, per_device(): whole_weight = lax.all_gather(w_value, 'y', axis=0, tiled=True)  7.14 us
  transfers between devices with their start and end apart: 23, of which 7 were waited for; matrix products, arithmetic and copies ran while one was open for 2% of the time, Pallas kernels for 10%

profile of v9, /device:TPU:1, one launch (start us, length us, event | category | flops | bytes accessed | tf_op | source)
XLA Modules:
  0.0 166.9 jit_solution(11846733314287197999)
XLA Ops:
  7.9 4.8 %collective-permute-start.1 = (bf16[128,512]{1,0:T(8,128)(2,1)}, bf16[128,512]{1,0:T(8,128)(2,1)S(1)}, u32[]{:S(2)}, u32[]{:S(2)}) collective-permute-start(bf16[128,512]{1,0:T(8,128)(2,1)} %bitcast.25), channel_id=1, source_target_pairs={{0,16},{8,24},{16,32},{24,40},{32,48},{40,56},{48,64},{56,72},{64,... | collective-permute-start | bytes 393224 | tf_op jit(solution)/shard_map/ppermute | solution.py:30
  12.8 6.6 %collective-permute-start.2 = (bf16[128,512]{1,0:T(8,128)(2,1)}, bf16[128,512]{1,0:T(8,128)(2,1)S(1)}, u32[]{:S(2)}, u32[]{:S(2)}) collective-permute-start(bf16[128,512]{1,0:T(8,128)(2,1)} %bitcast.26), channel_id=1, source_target_pairs={{8,32},{24,48},{40,64},{56,80},{72,96},{88,112},{104,128},{120,144... | collective-permute-start | bytes 393224 | tf_op jit(solution)/shard_map/ppermute | solution.py:30
  19.4 1.3 collective-permute-start
  20.7 3.0 %collective-permute-start.3 = (bf16[128,512]{1,0:T(8,128)(2,1)S(1)}, bf16[128,512]{1,0:T(8,128)(2,1)S(1)}, u32[]{:S(2)}, u32[]{:S(2)}) collective-permute-start(bf16[128,512]{1,0:T(8,128)(2,1)S(1)} %collective-permute-done.1.refs_2_), channel_id=1, source_target_pairs={{0,8},{8,0},{1,9},{9,1},{2,10},{10,2},{3,11},{11,3},{4,12},{12,4},... | collective-permute-start | bytes 393224 | tf_op jit(solution)/shard_map/ppermute | solution.py:34
  23.8 1.2 copy-done
  25.0 1.1 quarters.1
  26.1 7.9 %all-to-all-start = ((bf16[4,128,1024]{2,1,0:T(8,128)(2,1)}), bf16[4,128,1024]{2,1,0:T(8,128)(2,1)S(1)}, u32[]{:S(2)}, u32[]{:S(2)}) async-start(bf16[4,128,1024]{2,1,0:T(8,128)(2,1)} %bitcast.5), calls=%async_computation | async-start | bytes 2097152 | tf_op jit(solution)/shard_map/all_to_all | solution.py:211
  34.0 7.8 %attention_weights.1 = (bf16[4,512,1024]{2,1,0:T(8,128)(2,1)}, bf16[128,512]{1,0:T(8,128)(2,1)S(1)}, bf16[128,512]{1,0:T(8,128)(2,1)S(1)}, bf16[128,512]{1,0:T(8,128)(2,1)S(1)}, f32[128,512]{1,0:T(8,128)S(1)}) custom-call(s32[1]{0:T(128)} %bitcast.core_ref, s32[1,128]{1,0:T(1,128)S(1)} %copy-done.3, bf16[128,4096]{1,0:T(8,128)(2,1)} %bitcast.30, ...), custom_call_target="tpu_custom_call" | custom-call | flops 2147483648 | bytes 8388608 | tf_op jit(solution)/shard_map/attention_weights/pallas_call | solution.py:130
  41.8 2.2 %collective-permute-start.5 = (bf16[128,512]{1,0:T(8,128)(2,1)S(1)}, bf16[128,512]{1,0:T(8,128)(2,1)S(1)}, u32[]{:S(2)}, u32[]{:S(2)}) collective-permute-start(bf16[128,512]{1,0:T(8,128)(2,1)S(1)} %get-tuple-element.28), channel_id=1, source_target_pairs={{0,8},{8,0},{1,9},{9,1},{2,10},{10,2},{3,11},{11,3},{4,12},{12,4},... | collective-permute-start | bytes 393224 | tf_op jit(solution)/shard_map/ppermute | solution.py:34
  44.0 2.1 %collective-permute-start.4 = (bf16[128,512]{1,0:T(8,128)(2,1)S(1)}, bf16[128,512]{1,0:T(8,128)(2,1)S(1)}, u32[]{:S(2)}, u32[]{:S(2)}) collective-permute-start(bf16[128,512]{1,0:T(8,128)(2,1)S(1)} %get-tuple-element.27), channel_id=1, source_target_pairs={{8,0},{24,16},{40,32},{56,48},{72,64},{88,80},{104,96},{120,112},{... | collective-permute-start | bytes 393224 | tf_op jit(solution)/shard_map/ppermute | solution.py:30
  46.2 1.3 collective-permute-start.7
  47.5 1.3 collective-permute-start.6
  48.8 6.8 %collective-permute-done.7.three_ref = bf16[128,512]{1,0:T(8,128)(2,1)S(1)} collective-permute-done((bf16[128,512]{1,0:T(8,128)(2,1)S(1)}, bf16[128,512]{1,0:T(8,128)(2,1)S(1)}, u32[]{:S(2)}, u32[]{:S(2)}) %collective-permute-start.7) | collective-permute-done | bytes 131104 | tf_op jit(solution)/shard_map/ppermute | solution.py:30
  56.1 2.5 %collective-permute-start.12 = (bf16[512,1024]{1,0:T(8,128)(2,1)S(1)}, bf16[512,1024]{1,0:T(8,128)(2,1)}, u32[]{:S(2)}, u32[]{:S(2)}) collective-permute-start(bf16[512,1024]{1,0:T(8,128)(2,1)S(1)} %bitcast.21), channel_id=1, source_target_pairs={{0,8},{8,0},{1,9},{9,1},{2,10},{10,2},{3,11},{11,3},{4,12},{12,4},... | collective-permute-start | bytes 3145736 | tf_op jit(solution)/shard_map/ppermute | solution.py:34
  59.5 6.1 %all-to-all-start.1 = ((bf16[8,128,256]{2,1,0:T(8,128)(2,1)}), bf16[8,128,256]{2,1,0:T(8,128)(2,1)S(1)}, u32[]{:S(2)}, u32[]{:S(2)}) async-start(bf16[8,128,256]{2,1,0:T(8,128)(2,1)} %bitcast.7), calls=%async_computation.1 | async-start | bytes 1048576 | tf_op jit(solution)/shard_map/all_to_all | solution.py:223
  65.6 7.1 %all-gather.2.cloned.1.call-done = bf16[4096,512]{1,0:T(8,128)(2,1)} async-done(((bf16[512,512]{1,0:T(8,128)(2,1)}), bf16[4096,512]{1,0:T(8,128)(2,1)}) %all-gather.2.cloned.1.call-update) | async-done | bytes 4194320 | tf_op jit(solution)/shard_map/all_gather | solution.py:266
  72.8 3.0 %convolution_convert_fusion.refs_0_ = bf16[128,512]{1,0:T(8,128)(2,1)S(1)} fusion(bf16[4096,512]{1,0:T(8,128)(2,1)} %all-gather.2.cloned.1.call-done, bf16[1,128,4096]{2,1,0:T(8,128)(2,1)S(1)} %copy-done.1), kind=kOutput, calls=%fused_computation | convolution fusion | flops 536936448 | bytes 5373952 | tf_op jit(solution)/shard_map/dot_general | solution.py:275
  75.7 3.3 %collective-permute-start.9 = (bf16[128,512]{1,0:T(8,128)(2,1)S(1)}, bf16[128,512]{1,0:T(8,128)(2,1)S(1)}, u32[]{:S(2)}, u32[]{:S(2)}) collective-permute-start(bf16[128,512]{1,0:T(8,128)(2,1)S(1)} %convolution_convert_fusion.refs_0_), channel_id=1, source_target_pairs={{0,16},{8,24},{16,32},{24,40},{32,48},{40,56},{48,64},{56,72},{64,... | collective-permute-start | bytes 393224 | tf_op jit(solution)/shard_map/ppermute | solution.py:30
  79.0 5.2 %collective-permute-start.10 = (bf16[128,512]{1,0:T(8,128)(2,1)S(1)}, bf16[128,512]{1,0:T(8,128)(2,1)S(1)}, u32[]{:S(2)}, u32[]{:S(2)}) collective-permute-start(bf16[128,512]{1,0:T(8,128)(2,1)S(1)} %convolution_convert_fusion.refs_0_), channel_id=1, source_target_pairs={{8,32},{24,48},{40,64},{56,80},{72,96},{88,112},{104,128},{120,144... | collective-permute-start | bytes 393224 | tf_op jit(solution)/shard_map/ppermute | solution.py:30
  84.2 1.3 collective-permute-start.8
  85.5 3.0 %collective-permute-start.11 = (bf16[128,512]{1,0:T(8,128)(2,1)S(1)}, bf16[128,512]{1,0:T(8,128)(2,1)S(1)}, u32[]{:S(2)}, u32[]{:S(2)}) collective-permute-start(bf16[128,512]{1,0:T(8,128)(2,1)S(1)} %collective-permute-done.9.refs_2_), channel_id=1, source_target_pairs={{0,8},{8,0},{1,9},{9,1},{2,10},{10,2},{3,11},{11,3},{4,12},{12,4},... | collective-permute-start | bytes 393224 | tf_op jit(solution)/shard_map/ppermute | solution.py:34
  88.6 0.9 collective-permute-done.11.refs_4_
  89.5 4.2 %group_product.1 = bf16[1024,256]{1,0:T(8,128)(2,1)} custom-call(s32[1]{0:T(128)} %bitcast.core_ref, bf16[512,1024]{1,0:T(8,128)(2,1)S(1)} %bitcast.22, bf16[512,1024]{1,0:T(8,128)(2,1)} %collective-permute-done.12.far_ref, bf16[1024,256]{1,0:T(8,128)(2,1)S(1)} %bitcast.24), custom_call_target="tpu_custom_call" | custom-call | tf_op jit(solution)/shard_map/group_product/pallas_call | solution.py:228
  93.7 8.8 %all-to-all-start.2 = ((bf16[64,16,256]{2,1,0:T(8,128)(2,1)}), bf16[64,16,256]{2,1,0:T(8,128)(2,1)S(1)}, u32[]{:S(2)}, u32[]{:S(2)}) async-start(bf16[64,16,256]{2,1,0:T(8,128)(2,1)} %bitcast.9), calls=%async_computation.2 | async-start | bytes 1048576 | tf_op jit(solution)/shard_map/all_to_all | solution.py:279
  102.5 6.6 %key_gradient.1 = (bf16[128,512]{1,0:T(8,128)(2,1)S(1)}, bf16[128,512]{1,0:T(8,128)(2,1)S(1)}, bf16[128,512]{1,0:T(8,128)(2,1)S(1)}, f32[128,512]{1,0:T(8,128)S(1)}) custom-call(s32[1]{0:T(128)} %bitcast.core_ref, bf16[4,512,1024]{2,1,0:T(8,128)(2,1)} %get-tuple-element.24.weights_ref, bf16[128,4096]{1,0:T(8,128)(2,1)} %bitcast.31, ...), custom_call_target="tpu_custom_call" | custom-call | flops 2147483648 | bytes 8388608 | tf_op jit(solution)/shard_map/key_gradient/pallas_call | solution.py:145
  109.1 3.5 %collective-permute-start.14 = (bf16[128,512]{1,0:T(8,128)(2,1)S(1)}, bf16[128,512]{1,0:T(8,128)(2,1)S(1)}, u32[]{:S(2)}, u32[]{:S(2)}) collective-permute-start(bf16[128,512]{1,0:T(8,128)(2,1)S(1)} %get-tuple-element.41), channel_id=1, source_target_pairs={{0,8},{8,0},{1,9},{9,1},{2,10},{10,2},{3,11},{11,3},{4,12},{12,4},... | collective-permute-start | bytes 393224 | tf_op jit(solution)/shard_map/ppermute | solution.py:34
  112.6 1.9 %collective-permute-start.13 = (bf16[128,512]{1,0:T(8,128)(2,1)S(1)}, bf16[128,512]{1,0:T(8,128)(2,1)S(1)}, u32[]{:S(2)}, u32[]{:S(2)}) collective-permute-start(bf16[128,512]{1,0:T(8,128)(2,1)S(1)} %get-tuple-element.40), channel_id=1, source_target_pairs={{8,0},{24,16},{40,32},{56,48},{72,64},{88,80},{104,96},{120,112},{... | collective-permute-start | bytes 393224 | tf_op jit(solution)/shard_map/ppermute | solution.py:30
  114.5 1.3 collective-permute-start.16
  115.9 1.3 collective-permute-start.15
  117.2 6.9 %collective-permute-done.16 = bf16[128,512]{1,0:T(8,128)(2,1)S(1)} collective-permute-done((bf16[128,512]{1,0:T(8,128)(2,1)S(1)}, bf16[128,512]{1,0:T(8,128)(2,1)S(1)}, u32[]{:S(2)}, u32[]{:S(2)}) %collective-permute-start.16) | collective-permute-done | bytes 131104 | tf_op jit(solution)/shard_map/ppermute | solution.py:30
  125.6 26.0 %all_to_all.45 = bf16[32,16,256]{2,1,0:T(8,128)(2,1)S(1)} all-to-all(bf16[32,16,256]{2,1,0:T(8,128)(2,1)S(1)} %broadcast_in_dim.10), channel_id=1, replica_groups=mesh['x'=4,'z'=8,'c'=2,'y'=8] {'x','z'}, dimensions={0} | all-to-all | bytes 524288 | tf_op jit(solution)/shard_map/all_to_all | solution.py:254
  151.6 6.4 %collective-permute-start.18 = (bf16[512,256]{1,0:T(8,128)(2,1)S(1)}, bf16[512,256]{1,0:T(8,128)(2,1)S(1)}, u32[]{:S(2)}, u32[]{:S(2)}) collective-permute-start(bf16[512,256]{1,0:T(8,128)(2,1)S(1)} %bitcast.29), channel_id=1, source_target_pairs={{0,8},{8,0},{1,9},{9,1},{2,10},{10,2},{3,11},{11,3},{4,12},{12,4},... | collective-permute-start | bytes 786440 | tf_op jit(solution)/shard_map/ppermute | solution.py:34
  (38 shorter events, 5.7 us)
Async XLA Ops:
  7.2 26.8 %copy-start.2 = (bf16[1,128,512]{2,1,0:T(8,128)(2,1)S(1)}, bf16[1,128,512]{2,1,0:T(8,128)(2,1)}, u32[]{:S(2)}) copy-start(bf16[1,128,512]{2,1,0:T(8,128)(2,1)} %param.7) | copy-start | bytes 393220
  7.2 26.8 %copy-start.3 = (s32[1,128]{1,0:T(1,128)S(1)}, s32[1,128]{1,0:T(1,128)}, u32[]{:S(2)}) copy-start(s32[1,128]{1,0:T(1,128)} %position_ref.1) | copy-start | bytes 1540
  7.2 65.6 %all-gather.2.cloned.1.call-start = ((), (), s32[]{:S(2)}) async-start(), calls=%async_computation.4 | async-start | bytes 4718592 | tf_op jit(solution)/shard_map/all_gather | solution.py:266
  7.9 12.8 %collective-permute-start.1 = (bf16[128,512]{1,0:T(8,128)(2,1)}, bf16[128,512]{1,0:T(8,128)(2,1)S(1)}, u32[]{:S(2)}, u32[]{:S(2)}) collective-permute-start(bf16[128,512]{1,0:T(8,128)(2,1)} %bitcast.25), channel_id=1, source_target_pairs={{0,16},{8,24},{16,32},{24,40},{32,48},{40,56},{48,64},{56,72},{64,... | collective-permute-start | bytes 393224 | tf_op jit(solution)/shard_map/ppermute | solution.py:30
  12.8 21.2 %collective-permute-start.2 = (bf16[128,512]{1,0:T(8,128)(2,1)}, bf16[128,512]{1,0:T(8,128)(2,1)S(1)}, u32[]{:S(2)}, u32[]{:S(2)}) collective-permute-start(bf16[128,512]{1,0:T(8,128)(2,1)} %bitcast.26), channel_id=1, source_target_pairs={{8,32},{24,48},{40,64},{56,80},{72,96},{88,112},{104,128},{120,144... | collective-permute-start | bytes 393224 | tf_op jit(solution)/shard_map/ppermute | solution.py:30
  19.4 14.5 %collective-permute-start = (bf16[128,512]{1,0:T(8,128)(2,1)}, bf16[128,512]{1,0:T(8,128)(2,1)S(1)}, u32[]{:S(2)}, u32[]{:S(2)}) collective-permute-start(bf16[128,512]{1,0:T(8,128)(2,1)} %bitcast.27), channel_id=1, source_target_pairs={{0,8},{16,24},{32,40},{48,56},{64,72},{80,88},{96,104},{112,120},{... | collective-permute-start | bytes 393224 | tf_op jit(solution)/shard_map/ppermute | solution.py:30
  20.7 13.2 %collective-permute-start.3 = (bf16[128,512]{1,0:T(8,128)(2,1)S(1)}, bf16[128,512]{1,0:T(8,128)(2,1)S(1)}, u32[]{:S(2)}, u32[]{:S(2)}) collective-permute-start(bf16[128,512]{1,0:T(8,128)(2,1)S(1)} %collective-permute-done.1.refs_2_), channel_id=1, source_target_pairs={{0,8},{8,0},{1,9},{9,1},{2,10},{10,2},{3,11},{11,3},{4,12},{12,4},... | collective-permute-start | bytes 393224 | tf_op jit(solution)/shard_map/ppermute | solution.py:34
  23.8 1.2 copy-start
  26.1 30.1 %all-to-all-start = ((bf16[4,128,1024]{2,1,0:T(8,128)(2,1)}), bf16[4,128,1024]{2,1,0:T(8,128)(2,1)S(1)}, u32[]{:S(2)}, u32[]{:S(2)}) async-start(bf16[4,128,1024]{2,1,0:T(8,128)(2,1)} %bitcast.5), calls=%async_computation | async-start | bytes 2097152 | tf_op jit(solution)/shard_map/all_to_all | solution.py:211
  34.0 38.8 %copy-start.1 = (bf16[1,128,4096]{2,1,0:T(8,128)(2,1)S(1)}, bf16[1,128,4096]{2,1,0:T(8,128)(2,1)}, u32[]{:S(2)}) copy-start(bf16[1,128,4096]{2,1,0:T(8,128)(2,1)} %param.9) | copy-start | bytes 3145732
  41.8 5.6 %collective-permute-start.5 = (bf16[128,512]{1,0:T(8,128)(2,1)S(1)}, bf16[128,512]{1,0:T(8,128)(2,1)S(1)}, u32[]{:S(2)}, u32[]{:S(2)}) collective-permute-start(bf16[128,512]{1,0:T(8,128)(2,1)S(1)} %get-tuple-element.28), channel_id=1, source_target_pairs={{0,8},{8,0},{1,9},{9,1},{2,10},{10,2},{3,11},{11,3},{4,12},{12,4},... | collective-permute-start | bytes 393224 | tf_op jit(solution)/shard_map/ppermute | solution.py:34
  44.0 3.5 %collective-permute-start.4 = (bf16[128,512]{1,0:T(8,128)(2,1)S(1)}, bf16[128,512]{1,0:T(8,128)(2,1)S(1)}, u32[]{:S(2)}, u32[]{:S(2)}) collective-permute-start(bf16[128,512]{1,0:T(8,128)(2,1)S(1)} %get-tuple-element.27), channel_id=1, source_target_pairs={{8,0},{24,16},{40,32},{56,48},{72,64},{88,80},{104,96},{120,112},{... | collective-permute-start | bytes 393224 | tf_op jit(solution)/shard_map/ppermute | solution.py:30
  46.2 9.5 %collective-permute-start.7 = (bf16[128,512]{1,0:T(8,128)(2,1)S(1)}, bf16[128,512]{1,0:T(8,128)(2,1)S(1)}, u32[]{:S(2)}, u32[]{:S(2)}) collective-permute-start(bf16[128,512]{1,0:T(8,128)(2,1)S(1)} %get-tuple-element.27), channel_id=1, source_target_pairs={{32,8},{48,24},{64,40},{80,56},{96,72},{112,88},{128,104},{144,120... | collective-permute-start | bytes 393224 | tf_op jit(solution)/shard_map/ppermute | solution.py:30
  47.5 8.6 %collective-permute-start.6 = (bf16[128,512]{1,0:T(8,128)(2,1)S(1)}, bf16[128,512]{1,0:T(8,128)(2,1)S(1)}, u32[]{:S(2)}, u32[]{:S(2)}) collective-permute-start(bf16[128,512]{1,0:T(8,128)(2,1)S(1)} %add_convert_fusion.2), channel_id=1, source_target_pairs={{16,0},{24,8},{32,16},{40,24},{48,32},{56,40},{64,48},{72,56},{80,... | collective-permute-start | bytes 393224 | tf_op jit(solution)/shard_map/ppermute | solution.py:30
  56.1 33.4 %collective-permute-start.12 = (bf16[512,1024]{1,0:T(8,128)(2,1)S(1)}, bf16[512,1024]{1,0:T(8,128)(2,1)}, u32[]{:S(2)}, u32[]{:S(2)}) collective-permute-start(bf16[512,1024]{1,0:T(8,128)(2,1)S(1)} %bitcast.21), channel_id=1, source_target_pairs={{0,8},{8,0},{1,9},{9,1},{2,10},{10,2},{3,11},{11,3},{4,12},{12,4},... | collective-permute-start | bytes 3145736 | tf_op jit(solution)/shard_map/ppermute | solution.py:34
  59.5 29.1 %all-to-all-start.1 = ((bf16[8,128,256]{2,1,0:T(8,128)(2,1)}), bf16[8,128,256]{2,1,0:T(8,128)(2,1)S(1)}, u32[]{:S(2)}, u32[]{:S(2)}) async-start(bf16[8,128,256]{2,1,0:T(8,128)(2,1)} %bitcast.7), calls=%async_computation.1 | async-start | bytes 1048576 | tf_op jit(solution)/shard_map/all_to_all | solution.py:223
  75.7 9.8 %collective-permute-start.9 = (bf16[128,512]{1,0:T(8,128)(2,1)S(1)}, bf16[128,512]{1,0:T(8,128)(2,1)S(1)}, u32[]{:S(2)}, u32[]{:S(2)}) collective-permute-start(bf16[128,512]{1,0:T(8,128)(2,1)S(1)} %convolution_convert_fusion.refs_0_), channel_id=1, source_target_pairs={{0,16},{8,24},{16,32},{24,40},{32,48},{40,56},{48,64},{56,72},{64,... | collective-permute-start | bytes 393224 | tf_op jit(solution)/shard_map/ppermute | solution.py:30
  79.0 9.6 %collective-permute-start.10 = (bf16[128,512]{1,0:T(8,128)(2,1)S(1)}, bf16[128,512]{1,0:T(8,128)(2,1)S(1)}, u32[]{:S(2)}, u32[]{:S(2)}) collective-permute-start(bf16[128,512]{1,0:T(8,128)(2,1)S(1)} %convolution_convert_fusion.refs_0_), channel_id=1, source_target_pairs={{8,32},{24,48},{40,64},{56,80},{72,96},{88,112},{104,128},{120,144... | collective-permute-start | bytes 393224 | tf_op jit(solution)/shard_map/ppermute | solution.py:30
  84.2 4.4 %collective-permute-start.8 = (bf16[128,512]{1,0:T(8,128)(2,1)S(1)}, bf16[128,512]{1,0:T(8,128)(2,1)S(1)}, u32[]{:S(2)}, u32[]{:S(2)}) collective-permute-start(bf16[128,512]{1,0:T(8,128)(2,1)S(1)} %convolution_convert_fusion.refs_0_), channel_id=1, source_target_pairs={{0,8},{16,24},{32,40},{48,56},{64,72},{80,88},{96,104},{112,120},{... | collective-permute-start | bytes 393224 | tf_op jit(solution)/shard_map/ppermute | solution.py:30
  85.5 4.0 %collective-permute-start.11 = (bf16[128,512]{1,0:T(8,128)(2,1)S(1)}, bf16[128,512]{1,0:T(8,128)(2,1)S(1)}, u32[]{:S(2)}, u32[]{:S(2)}) collective-permute-start(bf16[128,512]{1,0:T(8,128)(2,1)S(1)} %collective-permute-done.9.refs_2_), channel_id=1, source_target_pairs={{0,8},{8,0},{1,9},{9,1},{2,10},{10,2},{3,11},{11,3},{4,12},{12,4},... | collective-permute-start | bytes 393224 | tf_op jit(solution)/shard_map/ppermute | solution.py:34
  93.7 31.1 %all-to-all-start.2 = ((bf16[64,16,256]{2,1,0:T(8,128)(2,1)}), bf16[64,16,256]{2,1,0:T(8,128)(2,1)S(1)}, u32[]{:S(2)}, u32[]{:S(2)}) async-start(bf16[64,16,256]{2,1,0:T(8,128)(2,1)} %bitcast.9), calls=%async_computation.2 | async-start | bytes 1048576 | tf_op jit(solution)/shard_map/all_to_all | solution.py:279
  109.1 6.7 %collective-permute-start.14 = (bf16[128,512]{1,0:T(8,128)(2,1)S(1)}, bf16[128,512]{1,0:T(8,128)(2,1)S(1)}, u32[]{:S(2)}, u32[]{:S(2)}) collective-permute-start(bf16[128,512]{1,0:T(8,128)(2,1)S(1)} %get-tuple-element.41), channel_id=1, source_target_pairs={{0,8},{8,0},{1,9},{9,1},{2,10},{10,2},{3,11},{11,3},{4,12},{12,4},... | collective-permute-start | bytes 393224 | tf_op jit(solution)/shard_map/ppermute | solution.py:34
  112.6 3.2 %collective-permute-start.13 = (bf16[128,512]{1,0:T(8,128)(2,1)S(1)}, bf16[128,512]{1,0:T(8,128)(2,1)S(1)}, u32[]{:S(2)}, u32[]{:S(2)}) collective-permute-start(bf16[128,512]{1,0:T(8,128)(2,1)S(1)} %get-tuple-element.40), channel_id=1, source_target_pairs={{8,0},{24,16},{40,32},{56,48},{72,64},{88,80},{104,96},{120,112},{... | collective-permute-start | bytes 393224 | tf_op jit(solution)/shard_map/ppermute | solution.py:30
  114.5 9.6 %collective-permute-start.16 = (bf16[128,512]{1,0:T(8,128)(2,1)S(1)}, bf16[128,512]{1,0:T(8,128)(2,1)S(1)}, u32[]{:S(2)}, u32[]{:S(2)}) collective-permute-start(bf16[128,512]{1,0:T(8,128)(2,1)S(1)} %get-tuple-element.40), channel_id=1, source_target_pairs={{32,8},{48,24},{64,40},{80,56},{96,72},{112,88},{128,104},{144,120... | collective-permute-start | bytes 393224 | tf_op jit(solution)/shard_map/ppermute | solution.py:30
  115.9 8.9 %collective-permute-start.15 = (bf16[128,512]{1,0:T(8,128)(2,1)S(1)}, bf16[128,512]{1,0:T(8,128)(2,1)S(1)}, u32[]{:S(2)}, u32[]{:S(2)}) collective-permute-start(bf16[128,512]{1,0:T(8,128)(2,1)S(1)} %add_convert_fusion.1), channel_id=1, source_target_pairs={{16,0},{24,8},{32,16},{40,24},{48,32},{56,40},{64,48},{72,56},{80,... | collective-permute-start | bytes 393224 | tf_op jit(solution)/shard_map/ppermute | solution.py:30
  124.9 0.7 collective-permute-start.17
  151.6 7.6 %collective-permute-start.18 = (bf16[512,256]{1,0:T(8,128)(2,1)S(1)}, bf16[512,256]{1,0:T(8,128)(2,1)S(1)}, u32[]{:S(2)}, u32[]{:S(2)}) collective-permute-start(bf16[512,256]{1,0:T(8,128)(2,1)S(1)} %bitcast.29), channel_id=1, source_target_pairs={{0,8},{8,0},{1,9},{9,1},{2,10},{10,2},{3,11},{11,3},{4,12},{12,4},... | collective-permute-start | bytes 786440 | tf_op jit(solution)/shard_map/ppermute | solution.py:34
Sparse Core Ops, SparseCore 0:
  10.1 62.6 all-gather.1

commit v10 on v5

--- a/solution.py
+++ b/solution.py
@@ -19,6 +19,7 @@
 DP = ("x", "z", "c")
 OTHER_CORE = [(0, 1), (1, 0)]
 QUARTER = 1024
+SHARD = 512
 HALF = 256
 masked_value = -1e30
 NT = (((1,), (1,)), ((), ()))
@@ -156,19 +157,13 @@
     )(core, in_hbm(weights), in_hbm(queries), in_hbm(grads), *values)
 
 
-def quarters_kernel(rows_ref, out_ref, sems):
-    copies = [
-        pltpu.make_async_copy(
-            rows_ref.at[:, pl.ds(x * QUARTER, QUARTER)],
-            out_ref.at[pl.ds(x * BLOCK, BLOCK), :],
-            sems.at[x],
-        )
-        for x in range(4)
-    ]
-    for copy in copies:
-        copy.start()
-    for copy in copies:
-        copy.wait()
+def quarters_kernel(rows_ref, out_ref):
+    for x in range(4):
+        for shard in range(8):
+            start = shard * SHARD + x * BLOCK
+            out_ref[x * BLOCK : (x + 1) * BLOCK, shard * BLOCK : (shard + 1) * BLOCK] = rows_ref[
+                :, start : start + BLOCK
+            ]
 
 
 def partial_values_kernel(core_ref, near_ref, far_ref, weight_ref, out_ref):
@@ -211,24 +206,21 @@
 def exchange_rows(rows):
     quarters = pl.pallas_call(
         quarters_kernel,
-        in_specs=[pl.BlockSpec(memory_space=pl.ANY)],
-        out_specs=pl.BlockSpec(memory_space=pl.ANY),
+        in_specs=[in_vmem],
+        out_specs=in_vmem,
         out_shape=jax.ShapeDtypeStruct((4 * BLOCK, QUARTER), jnp.bfloat16),
-        scratch_shapes=[pltpu.SemaphoreType.DMA((4,))],
         compiler_params=params,
         name="quarters",
-    )(in_hbm(rows))
+    )(rows)
     return lax.all_to_all(quarters, "x", 0, 0, tiled=True)
 
 
-def projection_piece(w_value):
-    route = [(target, source) for source, target in plane_route()]
+def projection_part(w_value):
     start = (lax.axis_index("x") * BLOCK, lax.axis_index("c") * HALF)
-    piece = lax.dynamic_slice(w_value, start, (BLOCK, HALF))
-    return lax.ppermute(piece, ("x", "z", "c", "y"), route)
-
-
-def projection_part(piece):
+    return lax.dynamic_slice(w_value, start, (BLOCK, HALF))
+
+
+def gathered_over_y(piece):
     copies = jnp.broadcast_to(piece[None], (8, BLOCK, HALF)).reshape(8 * BLOCK, HALF)
     return lax.all_to_all(copies, "y", 0, 0, tiled=True)
 
@@ -267,18 +259,6 @@
         compiler_params=params,
         name="group_product",
     )(core, near, far, packed)
-
-
-def plane_route():
-    route = []
-    for x in range(4):
-        for z in range(8):
-            for c in range(2):
-                for y in range(8):
-                    source = ((x * 8 + z) * 2 + c) * 8 + y
-                    target = (((y % 4) * 8 + z) * 2 + c) * 8 + 2 * x + y // 4
-                    route.append((source, target))
-    return route
 
 
 def whole_shard(piece):
@@ -298,13 +278,13 @@
     even = core[0] == 0
     key_blocks = from_earlier(keys)
     near = exchange_rows(rows)
-    weight = projection_piece(w_value)
+    piece = projection_part(w_value)
     weights, *value_parts = attention_weights(core, doc_pos, queries, grads, (keys,) + key_blocks)
-    near, weight, value_parts = lax.optimization_barrier((near, weight, value_parts))
+    near, piece, value_parts = lax.optimization_barrier((near, piece, value_parts))
 
     received = to_earlier(value_parts, even)
     far = swap(near)
-    values = partial_values(core, near, far, projection_part(weight))
+    values = partial_values(core, near, far, gathered_over_y(piece))
     packed = exchange_packed(core, value_parts[SPAN], received, values)
     product = group_product(core, near, far, packed)
     pieces = lax.all_to_all(product, ("y", "z"), 0, 0, tiled=True)
@@ -319,8 +299,6 @@
     pieces = pieces.reshape(64, -1, HALF).astype(jnp.float32)
     token_total = lax.axis_size(("x", "z", "c", "y")) * BLOCK
     piece = (jnp.sum(pieces, axis=0) * (1.0 / math.sqrt(token_total))).astype(jnp.bfloat16)
-    piece = lax.ppermute(piece, ("x", "z", "c", "y"), plane_route())
-    piece, key_parts = lax.optimization_barrier((piece, key_parts))
     weight_grad = whole_shard(piece)
     two, across, three = to_earlier(key_parts, even)
     key_grad = key_parts[SPAN] + two.astype(jnp.float32)

time: 190 us -> 150 us (0.79)
  Pallas kernels: 50 us -> 18.2 us
  starting transfers between devices: 101 us -> 80.4 us
  blocking collectives: 18 us -> 24.2 us
  waiting for transfers between devices: 13.9 us -> 17.7 us
    pallas_call x1, Pallas kernels: 32.9 us -> 1.2 us  [exchange_rows(): pl.pallas_call(quarters_kernel, in_specs=[in_vmem], out_specs=in_vmem, ou...]
    all_to_all x1, starting transfers between devices: 15.7 us -> 6.82 us  [gathered_over_y(): return lax.all_to_all(copies, 'y', 0, 0, tiled=True)]
    all_to_all x1, starting transfers between devices: 14.6 us -> 8.28 us  [whole_shard(): half = lax.all_to_all(copies, ('x', 'z'), 0, 0, tiled=True)]
    all_to_all x1, blocking collectives: 18 us -> 24.2 us  [exchange_packed(): return lax.all_to_all(packed, ('x', 'c'), 0, 0, tiled=True)]
    ppermute x12, waiting for transfers between devices: 0.03 us -> 5.52 us  [shift(): return lax.ppermute(block, DP, route)]
    ppermute x6, starting transfers between devices: 24.5 us -> 20.8 us  [swap(): return lax.ppermute(block, 'c', OTHER_CORE)]
    all_to_all x1, waiting for transfers between devices: 2.23 us -> 0.01 us  [whole_shard(): half = lax.all_to_all(copies, ('x', 'z'), 0, 0, tiled=True)]
  transfers between devices with their start and end apart: 24 -> 22, of which waited for: 4 -> 5; matrix products, arithmetic and copies ran while one was open for 1% -> 1% of each run, Pallas kernels for 8% -> 10%
where the time goes in v10:
time: 150 us; the launch traced here: 147 us
  starting transfers between devices  80.4 us (54%)
  blocking collectives  24.2 us (16%)
  Pallas kernels  18.2 us (12%)
  waiting for transfers between devices  17.7 us (12%)
  local copies, waits for them, and re-layouts  3.59 us (2%)
  other arithmetic  1.91 us (1%)
    ppermute x12, starting transfers between devices, shift(): return lax.ppermute(block, DP, route)  31.9 us
    all_to_all x1, blocking collectives, exchange_packed(): return lax.all_to_all(packed, ('x', 'c'), 0, 0, tiled=True)  24.2 us
    ppermute x6, starting transfers between devices, swap(): return lax.ppermute(block, 'c', OTHER_CORE)  20.8 us
    all_to_all x1, waiting for transfers between devices, gathered_over_y(): return lax.all_to_all(copies, 'y', 0, 0, tiled=True)  10.3 us
    all_to_all x1, starting transfers between devices, whole_shard(): half = lax.all_to_all(copies, ('x', 'z'), 0, 0, tiled=True)  8.28 us
    all_to_all x1, starting transfers between devices, per_device(): pieces = lax.all_to_all(product, ('y', 'z'), 0, 0, tiled=True)  7.7 us
    pallas_call x1, Pallas kernels, attention_weights(): pl.pallas_call(weights_kernel, grid=(KEY_HEADS,), in_specs=[in_smem, pl.B...  7.62 us
    all_to_all x1, starting transfers between devices, gathered_over_y(): return lax.all_to_all(copies, 'y', 0, 0, tiled=True)  6.82 us
  transfers between devices with their start and end apart: 22, of which 5 were waited for; matrix products, arithmetic and copies ran while one was open for 1% of the time, Pallas kernels for 10%

profile of v10, /device:TPU:1, one launch (start us, length us, event | category | flops | bytes accessed | tf_op | source)
XLA Modules:
  0.0 147.1 jit_solution(12157042519726492729)
XLA Ops:
  0.7 1.2 copy-done.1
  1.9 1.2 quarters.1
  3.1 4.8 %all-to-all-start = ((bf16[4,128,1024]{2,1,0:T(8,128)(2,1)}), bf16[4,128,1024]{2,1,0:T(8,128)(2,1)S(1)}, u32[]{:S(2)}, u32[]{:S(2)}) async-start(bf16[4,128,1024]{2,1,0:T(8,128)(2,1)} %bitcast.5), calls=%async_computation | async-start | bytes 2097152 | tf_op jit(solution)/shard_map/all_to_all | solution.py:215
  7.9 4.0 %collective-permute-start.1 = (bf16[128,512]{1,0:T(8,128)(2,1)S(1)}, bf16[128,512]{1,0:T(8,128)(2,1)S(1)}, u32[]{:S(2)}, u32[]{:S(2)}) collective-permute-start(bf16[128,512]{1,0:T(8,128)(2,1)S(1)} %bitcast.33), channel_id=1, source_target_pairs={{0,16},{8,24},{16,32},{24,40},{32,48},{40,56},{48,64},{56,72},{64,... | collective-permute-start | bytes 393224 | tf_op jit(solution)/shard_map/ppermute | solution.py:31
  11.9 6.9 %collective-permute-start.2 = (bf16[128,512]{1,0:T(8,128)(2,1)S(1)}, bf16[128,512]{1,0:T(8,128)(2,1)S(1)}, u32[]{:S(2)}, u32[]{:S(2)}) collective-permute-start(bf16[128,512]{1,0:T(8,128)(2,1)S(1)} %bitcast.34), channel_id=1, source_target_pairs={{8,32},{24,48},{40,64},{56,80},{72,96},{88,112},{104,128},{120,144... | collective-permute-start | bytes 393224 | tf_op jit(solution)/shard_map/ppermute | solution.py:31
  18.9 1.3 collective-permute-start
  20.2 3.0 %collective-permute-start.3 = (bf16[128,512]{1,0:T(8,128)(2,1)S(1)}, bf16[128,512]{1,0:T(8,128)(2,1)S(1)}, u32[]{:S(2)}, u32[]{:S(2)}) collective-permute-start(bf16[128,512]{1,0:T(8,128)(2,1)S(1)} %collective-permute-done.1.refs_2_), channel_id=1, source_target_pairs={{0,8},{8,0},{1,9},{9,1},{2,10},{10,2},{3,11},{11,3},{4,12},{12,4},... | collective-permute-start | bytes 393224 | tf_op jit(solution)/shard_map/ppermute | solution.py:35
  24.2 7.6 %attention_weights.1 = (bf16[4,512,1024]{2,1,0:T(8,128)(2,1)}, bf16[128,512]{1,0:T(8,128)(2,1)S(1)}, bf16[128,512]{1,0:T(8,128)(2,1)S(1)}, bf16[128,512]{1,0:T(8,128)(2,1)S(1)}, f32[128,512]{1,0:T(8,128)S(1)}) custom-call(s32[1]{0:T(128)} %bitcast.core_ref, s32[1,128]{1,0:T(1,128)S(1)} %copy-done.3, bf16[128,4096]{1,0:T(8,128)(2,1)} %bitcast.38, ...), custom_call_target="tpu_custom_call" | custom-call | flops 2147483648 | bytes 8388608 | tf_op jit(solution)/shard_map/attention_weights/pallas_call | solution.py:131
  31.8 2.3 %collective-permute-start.8 = (bf16[512,1024]{1,0:T(8,128)(2,1)S(1)}, bf16[512,1024]{1,0:T(8,128)(2,1)S(1)}, u32[]{:S(2)}, u32[]{:S(2)}) collective-permute-start(bf16[512,1024]{1,0:T(8,128)(2,1)S(1)} %bitcast.24), channel_id=1, source_target_pairs={{0,8},{8,0},{1,9},{9,1},{2,10},{10,2},{3,11},{11,3},{4,12},{12,4},... | collective-permute-start | bytes 3145736 | tf_op jit(solution)/shard_map/ppermute | solution.py:35
  34.9 6.8 %all-to-all-start.1 = ((bf16[8,128,256]{2,1,0:T(8,128)(2,1)}), bf16[8,128,256]{2,1,0:T(8,128)(2,1)S(1)}, u32[]{:S(2)}, u32[]{:S(2)}) async-start(bf16[8,128,256]{2,1,0:T(8,128)(2,1)} %broadcast_in_dim.6), calls=%async_computation.1 | async-start | bytes 1048576 | tf_op jit(solution)/shard_map/all_to_all | solution.py:225
  41.7 2.3 %collective-permute-start.5 = (bf16[128,512]{1,0:T(8,128)(2,1)S(1)}, bf16[128,512]{1,0:T(8,128)(2,1)S(1)}, u32[]{:S(2)}, u32[]{:S(2)}) collective-permute-start(bf16[128,512]{1,0:T(8,128)(2,1)S(1)} %get-tuple-element.30), channel_id=1, source_target_pairs={{0,8},{8,0},{1,9},{9,1},{2,10},{10,2},{3,11},{11,3},{4,12},{12,4},... | collective-permute-start | bytes 393224 | tf_op jit(solution)/shard_map/ppermute | solution.py:35
  44.1 2.6 %collective-permute-start.4 = (bf16[128,512]{1,0:T(8,128)(2,1)S(1)}, bf16[128,512]{1,0:T(8,128)(2,1)}, u32[]{:S(2)}, u32[]{:S(2)}) collective-permute-start(bf16[128,512]{1,0:T(8,128)(2,1)S(1)} %get-tuple-element.29), channel_id=1, source_target_pairs={{8,0},{24,16},{40,32},{56,48},{72,64},{88,80},{104,96},{120,112},{... | collective-permute-start | bytes 393224 | tf_op jit(solution)/shard_map/ppermute | solution.py:31
  46.7 1.3 collective-permute-start.7
  48.1 1.3 collective-permute-start.6
  49.4 10.3 %all-to-all-done.1 = bf16[8,128,256]{2,1,0:T(8,128)(2,1)S(1)} async-done(((bf16[8,128,256]{2,1,0:T(8,128)(2,1)}), bf16[8,128,256]{2,1,0:T(8,128)(2,1)S(1)}, u32[]{:S(2)}, u32[]{:S(2)}) %all-to-all-start.1) | async-done | bytes 524320 | tf_op jit(solution)/shard_map/all_to_all | solution.py:225
  60.5 24.2 %all_to_all.52 = bf16[8,128,512]{2,1,0:T(8,128)(2,1)S(1)} all-to-all(bf16[8,128,512]{2,1,0:T(8,128)(2,1)S(1)} %bitcast.29), channel_id=1, replica_groups=mesh['x'=4,'z'=8,'c'=2,'y'=8] {'x','c'}, dimensions={0} | all-to-all | bytes 2097152 | tf_op jit(solution)/shard_map/all_to_all | solution.py:248
  84.8 2.0 %group_product.1 = bf16[1024,256]{1,0:T(8,128)(2,1)S(1)} custom-call(s32[1]{0:T(128)} %bitcast.core_ref, bf16[512,1024]{1,0:T(8,128)(2,1)S(1)} %bitcast.26, bf16[512,1024]{1,0:T(8,128)(2,1)S(1)} %collective-permute-done.8.far_ref, bf16[1024,512]{1,0:T(8,128)(2,1)S(1)} %bitcast.27), custom_call_target="tpu_custom_call" | custom-call | tf_op jit(solution)/shard_map/group_product/pallas_call | solution.py:253
  87.6 7.7 %all-to-all-start.3 = ((bf16[64,16,256]{2,1,0:T(8,128)(2,1)}), bf16[64,16,256]{2,1,0:T(8,128)(2,1)S(1)}, u32[]{:S(2)}, u32[]{:S(2)}) async-start(bf16[64,16,256]{2,1,0:T(8,128)(2,1)} %bitcast.30), calls=%async_computation.3 | async-start | bytes 1048576 | tf_op jit(solution)/shard_map/all_to_all | solution.py:290
  95.4 2.9 %collective-permute-start.10 = (bf16[128,512]{1,0:T(8,128)(2,1)S(1)}, bf16[128,512]{1,0:T(8,128)(2,1)S(1)}, u32[]{:S(2)}, u32[]{:S(2)}) collective-permute-start(bf16[128,512]{1,0:T(8,128)(2,1)S(1)} %pad_maximum_fusion.1.refs_0_), channel_id=1, source_target_pairs={{0,16},{8,24},{16,32},{24,40},{32,48},{40,56},{48,64},{56,72},{64,... | collective-permute-start | bytes 393224 | tf_op jit(solution)/shard_map/ppermute | solution.py:31
  98.3 5.8 %collective-permute-start.11 = (bf16[128,512]{1,0:T(8,128)(2,1)S(1)}, bf16[128,512]{1,0:T(8,128)(2,1)S(1)}, u32[]{:S(2)}, u32[]{:S(2)}) collective-permute-start(bf16[128,512]{1,0:T(8,128)(2,1)S(1)} %pad_maximum_fusion.1.refs_0_), channel_id=1, source_target_pairs={{8,32},{24,48},{40,64},{56,80},{72,96},{88,112},{104,128},{120,144... | collective-permute-start | bytes 393224 | tf_op jit(solution)/shard_map/ppermute | solution.py:31
  104.1 1.3 collective-permute-start.9
  105.4 8.7 %collective-permute-start.12 = (bf16[128,512]{1,0:T(8,128)(2,1)S(1)}, bf16[128,512]{1,0:T(8,128)(2,1)S(1)}, u32[]{:S(2)}, u32[]{:S(2)}) collective-permute-start(bf16[128,512]{1,0:T(8,128)(2,1)S(1)} %collective-permute-done.10.refs_2_), channel_id=1, source_target_pairs={{0,8},{8,0},{1,9},{9,1},{2,10},{10,2},{3,11},{11,3},{4,12},{12,4},... | collective-permute-start | bytes 393224 | tf_op jit(solution)/shard_map/ppermute | solution.py:35
  114.2 0.9 collective-permute-done.12.refs_4_
  115.9 8.3 %all-to-all-start.4 = ((bf16[32,16,256]{2,1,0:T(8,128)(2,1)}), bf16[32,16,256]{2,1,0:T(8,128)(2,1)S(1)}, u32[]{:S(2)}, u32[]{:S(2)}) async-start(bf16[32,16,256]{2,1,0:T(8,128)(2,1)} %broadcast_in_dim.8), calls=%async_computation.4 | async-start | bytes 524288 | tf_op jit(solution)/shard_map/all_to_all | solution.py:267
  124.2 6.6 %key_gradient.1 = (bf16[128,512]{1,0:T(8,128)(2,1)S(1)}, bf16[128,512]{1,0:T(8,128)(2,1)S(1)}, bf16[128,512]{1,0:T(8,128)(2,1)S(1)}, f32[128,512]{1,0:T(8,128)S(1)}) custom-call(s32[1]{0:T(128)} %bitcast.core_ref, bf16[4,512,1024]{2,1,0:T(8,128)(2,1)} %get-tuple-element.22.weights_ref, bf16[128,4096]{1,0:T(8,128)(2,1)} %bitcast.39, ...), custom_call_target="tpu_custom_call" | custom-call | flops 2147483648 | bytes 8388608 | tf_op jit(solution)/shard_map/key_gradient/pallas_call | solution.py:146
  130.8 2.6 %collective-permute-start.14 = (bf16[128,512]{1,0:T(8,128)(2,1)S(1)}, bf16[128,512]{1,0:T(8,128)(2,1)S(1)}, u32[]{:S(2)}, u32[]{:S(2)}) collective-permute-start(bf16[128,512]{1,0:T(8,128)(2,1)S(1)} %get-tuple-element.40), channel_id=1, source_target_pairs={{0,8},{8,0},{1,9},{9,1},{2,10},{10,2},{3,11},{11,3},{4,12},{12,4},... | collective-permute-start | bytes 393224 | tf_op jit(solution)/shard_map/ppermute | solution.py:35
  133.4 1.9 %collective-permute-start.13 = (bf16[128,512]{1,0:T(8,128)(2,1)S(1)}, bf16[128,512]{1,0:T(8,128)(2,1)S(1)}, u32[]{:S(2)}, u32[]{:S(2)}) collective-permute-start(bf16[128,512]{1,0:T(8,128)(2,1)S(1)} %get-tuple-element.39), channel_id=1, source_target_pairs={{8,0},{24,16},{40,32},{56,48},{72,64},{88,80},{104,96},{120,112},{... | collective-permute-start | bytes 393224 | tf_op jit(solution)/shard_map/ppermute | solution.py:31
  135.3 1.3 collective-permute-start.16
  136.7 1.3 collective-permute-start.15
  138.0 1.9 %collective-permute-start.17 = (bf16[512,256]{1,0:T(8,128)(2,1)S(1)}, bf16[512,256]{1,0:T(8,128)(2,1)S(1)}, u32[]{:S(2)}, u32[]{:S(2)}) collective-permute-start(bf16[512,256]{1,0:T(8,128)(2,1)S(1)} %bitcast.37), channel_id=1, source_target_pairs={{0,8},{8,0},{1,9},{9,1},{2,10},{10,2},{3,11},{11,3},{4,12},{12,4},... | collective-permute-start | bytes 786440 | tf_op jit(solution)/shard_map/ppermute | solution.py:35
  139.9 4.2 %collective-permute-done.16 = bf16[128,512]{1,0:T(8,128)(2,1)S(1)} collective-permute-done((bf16[128,512]{1,0:T(8,128)(2,1)S(1)}, bf16[128,512]{1,0:T(8,128)(2,1)S(1)}, u32[]{:S(2)}, u32[]{:S(2)}) %collective-permute-start.16) | collective-permute-done | bytes 131104 | tf_op jit(solution)/shard_map/ppermute | solution.py:31
  144.1 1.3 collective-permute-done.15
  (41 shorter events, 6.1 us)
Async XLA Ops:
  0.6 23.5 %copy-start.3 = (s32[1,128]{1,0:T(1,128)S(1)}, s32[1,128]{1,0:T(1,128)}, u32[]{:S(2)}) copy-start(s32[1,128]{1,0:T(1,128)} %position_ref.1) | copy-start | bytes 1540
  0.6 1.2 copy-start.1
  1.9 6.0 %copy-start.2 = (bf16[1,128,512]{2,1,0:T(8,128)(2,1)S(1)}, bf16[1,128,512]{2,1,0:T(8,128)(2,1)}, u32[]{:S(2)}) copy-start(bf16[1,128,512]{2,1,0:T(8,128)(2,1)} %param.7) | copy-start | bytes 393220
  3.1 28.7 %all-to-all-start = ((bf16[4,128,1024]{2,1,0:T(8,128)(2,1)}), bf16[4,128,1024]{2,1,0:T(8,128)(2,1)S(1)}, u32[]{:S(2)}, u32[]{:S(2)}) async-start(bf16[4,128,1024]{2,1,0:T(8,128)(2,1)} %bitcast.5), calls=%async_computation | async-start | bytes 2097152 | tf_op jit(solution)/shard_map/all_to_all | solution.py:215
  7.9 12.2 %collective-permute-start.1 = (bf16[128,512]{1,0:T(8,128)(2,1)S(1)}, bf16[128,512]{1,0:T(8,128)(2,1)S(1)}, u32[]{:S(2)}, u32[]{:S(2)}) collective-permute-start(bf16[128,512]{1,0:T(8,128)(2,1)S(1)} %bitcast.33), channel_id=1, source_target_pairs={{0,16},{8,24},{16,32},{24,40},{32,48},{40,56},{48,64},{56,72},{64,... | collective-permute-start | bytes 393224 | tf_op jit(solution)/shard_map/ppermute | solution.py:31
  11.9 11.3 %collective-permute-start.2 = (bf16[128,512]{1,0:T(8,128)(2,1)S(1)}, bf16[128,512]{1,0:T(8,128)(2,1)S(1)}, u32[]{:S(2)}, u32[]{:S(2)}) collective-permute-start(bf16[128,512]{1,0:T(8,128)(2,1)S(1)} %bitcast.34), channel_id=1, source_target_pairs={{8,32},{24,48},{40,64},{56,80},{72,96},{88,112},{104,128},{120,144... | collective-permute-start | bytes 393224 | tf_op jit(solution)/shard_map/ppermute | solution.py:31
  18.9 4.4 %collective-permute-start = (bf16[128,512]{1,0:T(8,128)(2,1)S(1)}, bf16[128,512]{1,0:T(8,128)(2,1)S(1)}, u32[]{:S(2)}, u32[]{:S(2)}) collective-permute-start(bf16[128,512]{1,0:T(8,128)(2,1)S(1)} %bitcast.35), channel_id=1, source_target_pairs={{0,8},{16,24},{32,40},{48,56},{64,72},{80,88},{96,104},{112,120},{... | collective-permute-start | bytes 393224 | tf_op jit(solution)/shard_map/ppermute | solution.py:31
  20.2 4.0 %collective-permute-start.3 = (bf16[128,512]{1,0:T(8,128)(2,1)S(1)}, bf16[128,512]{1,0:T(8,128)(2,1)S(1)}, u32[]{:S(2)}, u32[]{:S(2)}) collective-permute-start(bf16[128,512]{1,0:T(8,128)(2,1)S(1)} %collective-permute-done.1.refs_2_), channel_id=1, source_target_pairs={{0,8},{8,0},{1,9},{9,1},{2,10},{10,2},{3,11},{11,3},{4,12},{12,4},... | collective-permute-start | bytes 393224 | tf_op jit(solution)/shard_map/ppermute | solution.py:35
  23.2 10.9 %dynamic-slice-start = ((bf16[512,512]{1,0:T(8,128)(2,1)}, s32[]{:T(128)}, s32[]{:T(128)}), bf16[128,256]{1,0:T(8,128)(2,1)S(1)}, s32[]{:S(2)}) async-start(bf16[512,512]{1,0:T(8,128)(2,1)} %param.10, s32[]{:T(128)} %select_n.34, s32[]{:T(128)} %select_n.35), calls=%async_computation.5 | async-start | bytes 131584 | tf_op jit(solution)/shard_map/dynamic_slice | solution.py:220
  31.8 27.9 %collective-permute-start.8 = (bf16[512,1024]{1,0:T(8,128)(2,1)S(1)}, bf16[512,1024]{1,0:T(8,128)(2,1)S(1)}, u32[]{:S(2)}, u32[]{:S(2)}) collective-permute-start(bf16[512,1024]{1,0:T(8,128)(2,1)S(1)} %bitcast.24), channel_id=1, source_target_pairs={{0,8},{8,0},{1,9},{9,1},{2,10},{10,2},{3,11},{11,3},{4,12},{12,4},... | collective-permute-start | bytes 3145736 | tf_op jit(solution)/shard_map/ppermute | solution.py:35
  34.9 24.8 %all-to-all-start.1 = ((bf16[8,128,256]{2,1,0:T(8,128)(2,1)}), bf16[8,128,256]{2,1,0:T(8,128)(2,1)S(1)}, u32[]{:S(2)}, u32[]{:S(2)}) async-start(bf16[8,128,256]{2,1,0:T(8,128)(2,1)} %broadcast_in_dim.6), calls=%async_computation.1 | async-start | bytes 1048576 | tf_op jit(solution)/shard_map/all_to_all | solution.py:225
  41.7 6.3 %collective-permute-start.5 = (bf16[128,512]{1,0:T(8,128)(2,1)S(1)}, bf16[128,512]{1,0:T(8,128)(2,1)S(1)}, u32[]{:S(2)}, u32[]{:S(2)}) collective-permute-start(bf16[128,512]{1,0:T(8,128)(2,1)S(1)} %get-tuple-element.30), channel_id=1, source_target_pairs={{0,8},{8,0},{1,9},{9,1},{2,10},{10,2},{3,11},{11,3},{4,12},{12,4},... | collective-permute-start | bytes 393224 | tf_op jit(solution)/shard_map/ppermute | solution.py:35
  44.1 3.9 %collective-permute-start.4 = (bf16[128,512]{1,0:T(8,128)(2,1)S(1)}, bf16[128,512]{1,0:T(8,128)(2,1)}, u32[]{:S(2)}, u32[]{:S(2)}) collective-permute-start(bf16[128,512]{1,0:T(8,128)(2,1)S(1)} %get-tuple-element.29), channel_id=1, source_target_pairs={{8,0},{24,16},{40,32},{56,48},{72,64},{88,80},{104,96},{120,112},{... | collective-permute-start | bytes 393224 | tf_op jit(solution)/shard_map/ppermute | solution.py:31
  46.7 13.7 %collective-permute-start.7 = (bf16[128,512]{1,0:T(8,128)(2,1)S(1)}, bf16[128,512]{1,0:T(8,128)(2,1)S(1)}, u32[]{:S(2)}, u32[]{:S(2)}) collective-permute-start(bf16[128,512]{1,0:T(8,128)(2,1)S(1)} %get-tuple-element.29), channel_id=1, source_target_pairs={{32,8},{48,24},{64,40},{80,56},{96,72},{112,88},{128,104},{144,120... | collective-permute-start | bytes 393224 | tf_op jit(solution)/shard_map/ppermute | solution.py:31
  48.1 12.3 %collective-permute-start.6 = (bf16[128,512]{1,0:T(8,128)(2,1)S(1)}, bf16[128,512]{1,0:T(8,128)(2,1)S(1)}, u32[]{:S(2)}, u32[]{:S(2)}) collective-permute-start(bf16[128,512]{1,0:T(8,128)(2,1)S(1)} %add_convert_fusion.2), channel_id=1, source_target_pairs={{16,0},{24,8},{32,16},{40,24},{48,32},{56,40},{64,48},{72,56},{80,... | collective-permute-start | bytes 393224 | tf_op jit(solution)/shard_map/ppermute | solution.py:31
  86.8 0.8 copy-start
  87.6 27.5 %all-to-all-start.3 = ((bf16[64,16,256]{2,1,0:T(8,128)(2,1)}), bf16[64,16,256]{2,1,0:T(8,128)(2,1)S(1)}, u32[]{:S(2)}, u32[]{:S(2)}) async-start(bf16[64,16,256]{2,1,0:T(8,128)(2,1)} %bitcast.30), calls=%async_computation.3 | async-start | bytes 1048576 | tf_op jit(solution)/shard_map/all_to_all | solution.py:290
  95.4 10.0 %collective-permute-start.10 = (bf16[128,512]{1,0:T(8,128)(2,1)S(1)}, bf16[128,512]{1,0:T(8,128)(2,1)S(1)}, u32[]{:S(2)}, u32[]{:S(2)}) collective-permute-start(bf16[128,512]{1,0:T(8,128)(2,1)S(1)} %pad_maximum_fusion.1.refs_0_), channel_id=1, source_target_pairs={{0,16},{8,24},{16,32},{24,40},{32,48},{40,56},{48,64},{56,72},{64,... | collective-permute-start | bytes 393224 | tf_op jit(solution)/shard_map/ppermute | solution.py:31
  98.3 15.8 %collective-permute-start.11 = (bf16[128,512]{1,0:T(8,128)(2,1)S(1)}, bf16[128,512]{1,0:T(8,128)(2,1)S(1)}, u32[]{:S(2)}, u32[]{:S(2)}) collective-permute-start(bf16[128,512]{1,0:T(8,128)(2,1)S(1)} %pad_maximum_fusion.1.refs_0_), channel_id=1, source_target_pairs={{8,32},{24,48},{40,64},{56,80},{72,96},{88,112},{104,128},{120,144... | collective-permute-start | bytes 393224 | tf_op jit(solution)/shard_map/ppermute | solution.py:31
  104.1 10.1 %collective-permute-start.9 = (bf16[128,512]{1,0:T(8,128)(2,1)S(1)}, bf16[128,512]{1,0:T(8,128)(2,1)S(1)}, u32[]{:S(2)}, u32[]{:S(2)}) collective-permute-start(bf16[128,512]{1,0:T(8,128)(2,1)S(1)} %pad_maximum_fusion.1.refs_0_), channel_id=1, source_target_pairs={{0,8},{16,24},{32,40},{48,56},{64,72},{80,88},{96,104},{112,120},{... | collective-permute-start | bytes 393224 | tf_op jit(solution)/shard_map/ppermute | solution.py:31
  105.4 9.7 %collective-permute-start.12 = (bf16[128,512]{1,0:T(8,128)(2,1)S(1)}, bf16[128,512]{1,0:T(8,128)(2,1)S(1)}, u32[]{:S(2)}, u32[]{:S(2)}) collective-permute-start(bf16[128,512]{1,0:T(8,128)(2,1)S(1)} %collective-permute-done.10.refs_2_), channel_id=1, source_target_pairs={{0,8},{8,0},{1,9},{9,1},{2,10},{10,2},{3,11},{11,3},{4,12},{12,4},... | collective-permute-start | bytes 393224 | tf_op jit(solution)/shard_map/ppermute | solution.py:35
  115.9 22.1 %all-to-all-start.4 = ((bf16[32,16,256]{2,1,0:T(8,128)(2,1)}), bf16[32,16,256]{2,1,0:T(8,128)(2,1)S(1)}, u32[]{:S(2)}, u32[]{:S(2)}) async-start(bf16[32,16,256]{2,1,0:T(8,128)(2,1)} %broadcast_in_dim.8), calls=%async_computation.4 | async-start | bytes 524288 | tf_op jit(solution)/shard_map/all_to_all | solution.py:267
  130.8 5.8 %collective-permute-start.14 = (bf16[128,512]{1,0:T(8,128)(2,1)S(1)}, bf16[128,512]{1,0:T(8,128)(2,1)S(1)}, u32[]{:S(2)}, u32[]{:S(2)}) collective-permute-start(bf16[128,512]{1,0:T(8,128)(2,1)S(1)} %get-tuple-element.40), channel_id=1, source_target_pairs={{0,8},{8,0},{1,9},{9,1},{2,10},{10,2},{3,11},{11,3},{4,12},{12,4},... | collective-permute-start | bytes 393224 | tf_op jit(solution)/shard_map/ppermute | solution.py:35
  133.4 3.2 %collective-permute-start.13 = (bf16[128,512]{1,0:T(8,128)(2,1)S(1)}, bf16[128,512]{1,0:T(8,128)(2,1)S(1)}, u32[]{:S(2)}, u32[]{:S(2)}) collective-permute-start(bf16[128,512]{1,0:T(8,128)(2,1)S(1)} %get-tuple-element.39), channel_id=1, source_target_pairs={{8,0},{24,16},{40,32},{56,48},{72,64},{88,80},{104,96},{120,112},{... | collective-permute-start | bytes 393224 | tf_op jit(solution)/shard_map/ppermute | solution.py:31
  135.3 8.8 %collective-permute-start.16 = (bf16[128,512]{1,0:T(8,128)(2,1)S(1)}, bf16[128,512]{1,0:T(8,128)(2,1)S(1)}, u32[]{:S(2)}, u32[]{:S(2)}) collective-permute-start(bf16[128,512]{1,0:T(8,128)(2,1)S(1)} %get-tuple-element.39), channel_id=1, source_target_pairs={{32,8},{48,24},{64,40},{80,56},{96,72},{112,88},{128,104},{144,120... | collective-permute-start | bytes 393224 | tf_op jit(solution)/shard_map/ppermute | solution.py:31
  136.7 8.7 %collective-permute-start.15 = (bf16[128,512]{1,0:T(8,128)(2,1)S(1)}, bf16[128,512]{1,0:T(8,128)(2,1)S(1)}, u32[]{:S(2)}, u32[]{:S(2)}) collective-permute-start(bf16[128,512]{1,0:T(8,128)(2,1)S(1)} %add_convert_fusion.1), channel_id=1, source_target_pairs={{16,0},{24,8},{32,16},{40,24},{48,32},{56,40},{64,48},{72,56},{80,... | collective-permute-start | bytes 393224 | tf_op jit(solution)/shard_map/ppermute | solution.py:31
  138.0 8.1 %collective-permute-start.17 = (bf16[512,256]{1,0:T(8,128)(2,1)S(1)}, bf16[512,256]{1,0:T(8,128)(2,1)S(1)}, u32[]{:S(2)}, u32[]{:S(2)}) collective-permute-start(bf16[512,256]{1,0:T(8,128)(2,1)S(1)} %bitcast.37), channel_id=1, source_target_pairs={{0,8},{8,0},{1,9},{9,1},{2,10},{10,2},{3,11},{11,3},{4,12},{12,4},... | collective-permute-start | bytes 786440 | tf_op jit(solution)/shard_map/ppermute | solution.py:35

commit v11 on v10

--- a/solution.py
+++ b/solution.py
@@ -78,13 +78,13 @@
         == lax.broadcasted_iota(jnp.int32, (PAIR, BLOCK), 1)
     )
     unit = jnp.where(unit, 1.0, 0.0).astype(jnp.bfloat16)
-    score_scale = 1.0 / math.sqrt(HEAD_SIZE)
+    score_scale = math.log2(math.e) / math.sqrt(HEAD_SIZE)
     total = jnp.zeros((SPAN_ROWS, HEAD_SIZE), jnp.float32)
     for pair in range(GROUP_WIDTH // 2):
         heads = jnp.concatenate([stacked(query_ref, pair), unit], axis=1)
         scores = lax.dot_general(keys, heads, NT, preferred_element_type=jnp.float32)
         top = jnp.max(scores, axis=0, keepdims=True)
-        weights = jnp.exp((scores - top) * score_scale)
+        weights = jnp.exp2((scores - top) * score_scale)
         weights = weights * (1.0 / jnp.sum(weights, axis=0, keepdims=True))
         low = weights.astype(jnp.bfloat16)
         weights_ref[0, :, pair * PAIR : (pair + 1) * PAIR] = low
@@ -217,12 +217,8 @@
 
 def projection_part(w_value):
     start = (lax.axis_index("x") * BLOCK, lax.axis_index("c") * HALF)
-    return lax.dynamic_slice(w_value, start, (BLOCK, HALF))
-
-
-def gathered_over_y(piece):
-    copies = jnp.broadcast_to(piece[None], (8, BLOCK, HALF)).reshape(8 * BLOCK, HALF)
-    return lax.all_to_all(copies, "y", 0, 0, tiled=True)
+    piece = lax.dynamic_slice(w_value, start, (BLOCK, HALF))
+    return jnp.broadcast_to(piece[None], (8, BLOCK, HALF)).reshape(8 * BLOCK, HALF)
 
 
 def partial_values(core, near, far, weight):
@@ -255,7 +251,7 @@
         grid=(QUARTER // HALF,),
         in_specs=[in_smem, rows, rows, pl.BlockSpec((8 * BLOCK, 2 * HALF), lambda part: (0, 0))],
         out_specs=pl.BlockSpec((HALF, HALF), lambda part: (part, 0)),
-        out_shape=jax.ShapeDtypeStruct((QUARTER, HALF), jnp.bfloat16),
+        out_shape=pltpu.HBM((QUARTER, HALF), jnp.bfloat16),
         compiler_params=params,
         name="group_product",
     )(core, near, far, packed)
@@ -278,13 +274,13 @@
     even = core[0] == 0
     key_blocks = from_earlier(keys)
     near = exchange_rows(rows)
-    piece = projection_part(w_value)
+    near, piece, key_blocks = lax.optimization_barrier((near, projection_part(w_value), key_blocks))
+    part = lax.all_to_all(piece, "y", 0, 0, tiled=True)
     weights, *value_parts = attention_weights(core, doc_pos, queries, grads, (keys,) + key_blocks)
-    near, piece, value_parts = lax.optimization_barrier((near, piece, value_parts))
 
     received = to_earlier(value_parts, even)
     far = swap(near)
-    values = partial_values(core, near, far, gathered_over_y(piece))
+    values = partial_values(core, near, far, part)
     packed = exchange_packed(core, value_parts[SPAN], received, values)
     product = group_product(core, near, far, packed)
     pieces = lax.all_to_all(product, ("y", "z"), 0, 0, tiled=True)

time: 150 us -> 150 us (level)
  starting transfers between devices: 80.4 us -> 86.4 us
  waiting for transfers between devices: 17.7 us -> 12.6 us
  blocking collectives: 24.2 us -> 22.7 us
    all_to_all x1, waiting for transfers between devices: 10.3 us -> 2.79 us  [per_device(): part = lax.all_to_all(piece, 'y', 0, 0, tiled=True)]
    ppermute x6, starting transfers between devices: 20.8 us -> 24.3 us  [swap(): return lax.ppermute(block, 'c', OTHER_CORE)]
    ppermute x12, waiting for transfers between devices: 5.52 us -> 8.75 us  [shift(): return lax.ppermute(block, DP, route)]
    all_to_all x1, starting transfers between devices: 7.7 us -> 10.9 us  [per_device(): pieces = lax.all_to_all(product, ('y', 'z'), 0, 0, tiled=True)]
    all_to_all x1, blocking collectives: 24.2 us -> 22.7 us  [exchange_packed(): return lax.all_to_all(packed, ('x', 'c'), 0, 0, tiled=True)]
  transfers between devices with their start and end apart: 22 -> 22, of which waited for: 5 -> 6; matrix products, arithmetic and copies ran while one was open for 1% -> 1% of each run, Pallas kernels for 10% -> 10%
where the time goes in v11:
time: 150 us; the launch traced here: 148 us
  starting transfers between devices  86.4 us (58%)
  blocking collectives  22.7 us (15%)
  Pallas kernels  18.7 us (12%)
  waiting for transfers between devices  12.6 us (8%)
  local copies, waits for them, and re-layouts  4.55 us (3%)
  other arithmetic  1.9 us (1%)
    ppermute x12, starting transfers between devices, shift(): return lax.ppermute(block, DP, route)  31.4 us
    ppermute x6, starting transfers between devices, swap(): return lax.ppermute(block, 'c', OTHER_CORE)  24.3 us
    all_to_all x1, blocking collectives, exchange_packed(): return lax.all_to_all(packed, ('x', 'c'), 0, 0, tiled=True)  22.7 us
    all_to_all x1, starting transfers between devices, per_device(): pieces = lax.all_to_all(product, ('y', 'z'), 0, 0, tiled=True)  10.9 us
    ppermute x12, waiting for transfers between devices, shift(): return lax.ppermute(block, DP, route)  8.75 us
    all_to_all x1, starting transfers between devices, whole_shard(): half = lax.all_to_all(copies, ('x', 'z'), 0, 0, tiled=True)  8.26 us
    pallas_call x1, Pallas kernels, attention_weights(): pl.pallas_call(weights_kernel, grid=(KEY_HEADS,), in_specs=[in_smem, pl.B...  7.29 us
    all_to_all x1, starting transfers between devices, per_device(): part = lax.all_to_all(piece, 'y', 0, 0, tiled=True)  6.74 us
  transfers between devices with their start and end apart: 22, of which 6 were waited for; matrix products, arithmetic and copies ran while one was open for 1% of the time, Pallas kernels for 10%

profile of v11, /device:TPU:1, one launch (start us, length us, event | category | flops | bytes accessed | tf_op | source)
XLA Modules:
  0.0 147.9 jit_solution(14601482154458091627)
XLA Ops:
  0.7 1.2 copy-done
  1.9 1.2 quarters.1
  3.1 4.8 %all-to-all-start = ((bf16[4,128,1024]{2,1,0:T(8,128)(2,1)}), bf16[4,128,1024]{2,1,0:T(8,128)(2,1)S(1)}, u32[]{:S(2)}, u32[]{:S(2)}) async-start(bf16[4,128,1024]{2,1,0:T(8,128)(2,1)} %bitcast.5), calls=%async_computation | async-start | bytes 2097152 | tf_op jit(solution)/shard_map/all_to_all | solution.py:215
  7.9 4.0 %collective-permute-start.1 = (bf16[128,512]{1,0:T(8,128)(2,1)S(1)}, bf16[128,512]{1,0:T(8,128)(2,1)S(1)}, u32[]{:S(2)}, u32[]{:S(2)}) collective-permute-start(bf16[128,512]{1,0:T(8,128)(2,1)S(1)} %bitcast.34), channel_id=1, source_target_pairs={{0,16},{8,24},{16,32},{24,40},{32,48},{40,56},{48,64},{56,72},{64,... | collective-permute-start | bytes 393224 | tf_op jit(solution)/shard_map/ppermute | solution.py:31
  11.9 6.9 %collective-permute-start.2 = (bf16[128,512]{1,0:T(8,128)(2,1)S(1)}, bf16[128,512]{1,0:T(8,128)(2,1)S(1)}, u32[]{:S(2)}, u32[]{:S(2)}) collective-permute-start(bf16[128,512]{1,0:T(8,128)(2,1)S(1)} %bitcast.35), channel_id=1, source_target_pairs={{8,32},{24,48},{40,64},{56,80},{72,96},{88,112},{104,128},{120,144... | collective-permute-start | bytes 393224 | tf_op jit(solution)/shard_map/ppermute | solution.py:31
  18.8 1.3 collective-permute-start
  20.2 3.0 %collective-permute-start.3 = (bf16[128,512]{1,0:T(8,128)(2,1)S(1)}, bf16[128,512]{1,0:T(8,128)(2,1)S(1)}, u32[]{:S(2)}, u32[]{:S(2)}) collective-permute-start(bf16[128,512]{1,0:T(8,128)(2,1)S(1)} %collective-permute-done.1.refs_2_), channel_id=1, source_target_pairs={{0,8},{8,0},{1,9},{9,1},{2,10},{10,2},{3,11},{11,3},{4,12},{12,4},... | collective-permute-start | bytes 393224 | tf_op jit(solution)/shard_map/ppermute | solution.py:35
  25.0 5.9 %collective-permute-start.8 = (bf16[512,1024]{1,0:T(8,128)(2,1)S(1)}, bf16[512,1024]{1,0:T(8,128)(2,1)S(1)}, u32[]{:S(2)}, u32[]{:S(2)}) collective-permute-start(bf16[512,1024]{1,0:T(8,128)(2,1)S(1)} %bitcast.26), channel_id=1, source_target_pairs={{0,8},{8,0},{1,9},{9,1},{2,10},{10,2},{3,11},{11,3},{4,12},{12,4},... | collective-permute-start | bytes 3145736 | tf_op jit(solution)/shard_map/ppermute | solution.py:35
  31.0 6.7 %all-to-all-start.1 = ((bf16[8,128,256]{2,1,0:T(8,128)(2,1)}), bf16[8,128,256]{2,1,0:T(8,128)(2,1)S(1)}, u32[]{:S(2)}, u32[]{:S(2)}) async-start(bf16[8,128,256]{2,1,0:T(8,128)(2,1)} %broadcast_in_dim.6), calls=%async_computation.1 | async-start | bytes 1048576 | tf_op jit(solution)/shard_map/all_to_all | solution.py:278
  38.6 7.3 %attention_weights.1 = (bf16[4,512,1024]{2,1,0:T(8,128)(2,1)}, bf16[128,512]{1,0:T(8,128)(2,1)}, bf16[128,512]{1,0:T(8,128)(2,1)S(1)}, bf16[128,512]{1,0:T(8,128)(2,1)}, f32[128,512]{1,0:T(8,128)S(1)}) custom-call(s32[1]{0:T(128)} %bitcast.core_ref, s32[1,128]{1,0:T(1,128)S(1)} %copy-done.4, bf16[128,4096]{1,0:T(8,128)(2,1)} %bitcast.40, ...), custom_call_target="tpu_custom_call" | custom-call | flops 2147483648 | bytes 8388608 | tf_op jit(solution)/shard_map/attention_weights/pallas_call | solution.py:131
  45.9 2.2 %collective-permute-start.5 = (bf16[128,512]{1,0:T(8,128)(2,1)}, bf16[128,512]{1,0:T(8,128)(2,1)S(1)}, u32[]{:S(2)}, u32[]{:S(2)}) collective-permute-start(bf16[128,512]{1,0:T(8,128)(2,1)} %get-tuple-element.30), channel_id=1, source_target_pairs={{0,8},{8,0},{1,9},{9,1},{2,10},{10,2},{3,11},{11,3},{4,12},{12,4},... | collective-permute-start | bytes 393224 | tf_op jit(solution)/shard_map/ppermute | solution.py:35
  48.1 2.1 %collective-permute-start.4 = (bf16[128,512]{1,0:T(8,128)(2,1)}, bf16[128,512]{1,0:T(8,128)(2,1)S(1)}, u32[]{:S(2)}, u32[]{:S(2)}) collective-permute-start(bf16[128,512]{1,0:T(8,128)(2,1)} %get-tuple-element.29), channel_id=1, source_target_pairs={{8,0},{24,16},{40,32},{56,48},{72,64},{88,80},{104,96},{120,112},{... | collective-permute-start | bytes 393224 | tf_op jit(solution)/shard_map/ppermute | solution.py:31
  50.2 1.3 collective-permute-start.7
  51.6 1.3 collective-permute-start.6
  52.9 2.8 %all-to-all-done.1 = bf16[8,128,256]{2,1,0:T(8,128)(2,1)S(1)} async-done(((bf16[8,128,256]{2,1,0:T(8,128)(2,1)}), bf16[8,128,256]{2,1,0:T(8,128)(2,1)S(1)}, u32[]{:S(2)}, u32[]{:S(2)}) %all-to-all-start.1) | async-done | bytes 524320 | tf_op jit(solution)/shard_map/all_to_all | solution.py:278
  56.5 3.2 %collective-permute-done.7.three_ref = bf16[128,512]{1,0:T(8,128)(2,1)S(1)} collective-permute-done((bf16[128,512]{1,0:T(8,128)(2,1)}, bf16[128,512]{1,0:T(8,128)(2,1)S(1)}, u32[]{:S(2)}, u32[]{:S(2)}) %collective-permute-start.7) | collective-permute-done | bytes 131104 | tf_op jit(solution)/shard_map/ppermute | solution.py:31
  59.8 22.7 %all_to_all.55 = bf16[8,128,512]{2,1,0:T(8,128)(2,1)S(1)} all-to-all(bf16[8,128,512]{2,1,0:T(8,128)(2,1)S(1)} %bitcast.31), channel_id=1, replica_groups=mesh['x'=4,'z'=8,'c'=2,'y'=8] {'x','c'}, dimensions={0} | all-to-all | bytes 2097152 | tf_op jit(solution)/shard_map/all_to_all | solution.py:244
  82.5 2.8 %group_product.1 = bf16[1024,256]{1,0:T(8,128)(2,1)} custom-call(s32[1]{0:T(128)} %bitcast.core_ref, bf16[512,1024]{1,0:T(8,128)(2,1)S(1)} %bitcast.28, bf16[512,1024]{1,0:T(8,128)(2,1)S(1)} %collective-permute-done.8.far_ref, bf16[1024,512]{1,0:T(8,128)(2,1)S(1)} %bitcast.29), custom_call_target="tpu_custom_call" | custom-call | tf_op jit(solution)/shard_map/group_product/pallas_call | solution.py:249
  85.3 10.9 %all-to-all-start.3 = ((bf16[64,16,256]{2,1,0:T(8,128)(2,1)}), bf16[64,16,256]{2,1,0:T(8,128)(2,1)S(1)}, u32[]{:S(2)}, u32[]{:S(2)}) async-start(bf16[64,16,256]{2,1,0:T(8,128)(2,1)} %bitcast.38), calls=%async_computation.3 | async-start | bytes 1048576 | tf_op jit(solution)/shard_map/all_to_all | solution.py:286
  96.3 2.9 %collective-permute-start.10 = (bf16[128,512]{1,0:T(8,128)(2,1)S(1)}, bf16[128,512]{1,0:T(8,128)(2,1)S(1)}, u32[]{:S(2)}, u32[]{:S(2)}) collective-permute-start(bf16[128,512]{1,0:T(8,128)(2,1)S(1)} %pad_maximum_fusion.1.refs_0_), channel_id=1, source_target_pairs={{0,16},{8,24},{16,32},{24,40},{32,48},{40,56},{48,64},{56,72},{64,... | collective-permute-start | bytes 393224 | tf_op jit(solution)/shard_map/ppermute | solution.py:31
  99.2 5.8 %collective-permute-start.11 = (bf16[128,512]{1,0:T(8,128)(2,1)S(1)}, bf16[128,512]{1,0:T(8,128)(2,1)S(1)}, u32[]{:S(2)}, u32[]{:S(2)}) collective-permute-start(bf16[128,512]{1,0:T(8,128)(2,1)S(1)} %pad_maximum_fusion.1.refs_0_), channel_id=1, source_target_pairs={{8,32},{24,48},{40,64},{56,80},{72,96},{88,112},{104,128},{120,144... | collective-permute-start | bytes 393224 | tf_op jit(solution)/shard_map/ppermute | solution.py:31
  105.0 1.3 collective-permute-start.9
  106.3 8.7 %collective-permute-start.12 = (bf16[128,512]{1,0:T(8,128)(2,1)S(1)}, bf16[128,512]{1,0:T(8,128)(2,1)S(1)}, u32[]{:S(2)}, u32[]{:S(2)}) collective-permute-start(bf16[128,512]{1,0:T(8,128)(2,1)S(1)} %collective-permute-done.10.refs_2_), channel_id=1, source_target_pairs={{0,8},{8,0},{1,9},{9,1},{2,10},{10,2},{3,11},{11,3},{4,12},{12,4},... | collective-permute-start | bytes 393224 | tf_op jit(solution)/shard_map/ppermute | solution.py:35
  116.8 8.3 %all-to-all-start.4 = ((bf16[32,16,256]{2,1,0:T(8,128)(2,1)}), bf16[32,16,256]{2,1,0:T(8,128)(2,1)S(1)}, u32[]{:S(2)}, u32[]{:S(2)}) async-start(bf16[32,16,256]{2,1,0:T(8,128)(2,1)} %broadcast_in_dim.8), calls=%async_computation.4 | async-start | bytes 524288 | tf_op jit(solution)/shard_map/all_to_all | solution.py:263
  125.1 6.6 %key_gradient.1 = (bf16[128,512]{1,0:T(8,128)(2,1)S(1)}, bf16[128,512]{1,0:T(8,128)(2,1)S(1)}, bf16[128,512]{1,0:T(8,128)(2,1)S(1)}, f32[128,512]{1,0:T(8,128)S(1)}) custom-call(s32[1]{0:T(128)} %bitcast.core_ref, bf16[4,512,1024]{2,1,0:T(8,128)(2,1)} %get-tuple-element.26.weights_ref, bf16[128,4096]{1,0:T(8,128)(2,1)} %bitcast.41, ...), custom_call_target="tpu_custom_call" | custom-call | flops 2147483648 | bytes 8388608 | tf_op jit(solution)/shard_map/key_gradient/pallas_call | solution.py:146
  131.7 2.5 %collective-permute-start.14 = (bf16[128,512]{1,0:T(8,128)(2,1)S(1)}, bf16[128,512]{1,0:T(8,128)(2,1)S(1)}, u32[]{:S(2)}, u32[]{:S(2)}) collective-permute-start(bf16[128,512]{1,0:T(8,128)(2,1)S(1)} %get-tuple-element.40), channel_id=1, source_target_pairs={{0,8},{8,0},{1,9},{9,1},{2,10},{10,2},{3,11},{11,3},{4,12},{12,4},... | collective-permute-start | bytes 393224 | tf_op jit(solution)/shard_map/ppermute | solution.py:35
  134.2 1.9 %collective-permute-start.13 = (bf16[128,512]{1,0:T(8,128)(2,1)S(1)}, bf16[128,512]{1,0:T(8,128)(2,1)S(1)}, u32[]{:S(2)}, u32[]{:S(2)}) collective-permute-start(bf16[128,512]{1,0:T(8,128)(2,1)S(1)} %get-tuple-element.39), channel_id=1, source_target_pairs={{8,0},{24,16},{40,32},{56,48},{72,64},{88,80},{104,96},{120,112},{... | collective-permute-start | bytes 393224 | tf_op jit(solution)/shard_map/ppermute | solution.py:31
  136.1 1.3 collective-permute-start.16
  137.5 1.3 collective-permute-start.15
  138.8 1.9 %collective-permute-start.17 = (bf16[512,256]{1,0:T(8,128)(2,1)S(1)}, bf16[512,256]{1,0:T(8,128)(2,1)S(1)}, u32[]{:S(2)}, u32[]{:S(2)}) collective-permute-start(bf16[512,256]{1,0:T(8,128)(2,1)S(1)} %bitcast.39), channel_id=1, source_target_pairs={{0,8},{8,0},{1,9},{9,1},{2,10},{10,2},{3,11},{11,3},{4,12},{12,4},... | collective-permute-start | bytes 786440 | tf_op jit(solution)/shard_map/ppermute | solution.py:35
  140.8 4.2 %collective-permute-done.16 = bf16[128,512]{1,0:T(8,128)(2,1)S(1)} collective-permute-done((bf16[128,512]{1,0:T(8,128)(2,1)S(1)}, bf16[128,512]{1,0:T(8,128)(2,1)S(1)}, u32[]{:S(2)}, u32[]{:S(2)}) %collective-permute-start.16) | collective-permute-done | bytes 131104 | tf_op jit(solution)/shard_map/ppermute | solution.py:31
  145.0 1.3 collective-permute-done.15
  (42 shorter events, 7.1 us)
Async XLA Ops:
  0.6 37.1 %copy-start.4 = (s32[1,128]{1,0:T(1,128)S(1)}, s32[1,128]{1,0:T(1,128)}, u32[]{:S(2)}) copy-start(s32[1,128]{1,0:T(1,128)} %position_ref.1) | copy-start | bytes 1540
  0.6 1.2 copy-start
  1.9 6.0 %copy-start.1 = (bf16[1,128,512]{2,1,0:T(8,128)(2,1)S(1)}, bf16[1,128,512]{2,1,0:T(8,128)(2,1)}, u32[]{:S(2)}) copy-start(bf16[1,128,512]{2,1,0:T(8,128)(2,1)} %param.7) | copy-start | bytes 393220
  3.1 21.1 %all-to-all-start = ((bf16[4,128,1024]{2,1,0:T(8,128)(2,1)}), bf16[4,128,1024]{2,1,0:T(8,128)(2,1)S(1)}, u32[]{:S(2)}, u32[]{:S(2)}) async-start(bf16[4,128,1024]{2,1,0:T(8,128)(2,1)} %bitcast.5), calls=%async_computation | async-start | bytes 2097152 | tf_op jit(solution)/shard_map/all_to_all | solution.py:215
  7.9 12.2 %collective-permute-start.1 = (bf16[128,512]{1,0:T(8,128)(2,1)S(1)}, bf16[128,512]{1,0:T(8,128)(2,1)S(1)}, u32[]{:S(2)}, u32[]{:S(2)}) collective-permute-start(bf16[128,512]{1,0:T(8,128)(2,1)S(1)} %bitcast.34), channel_id=1, source_target_pairs={{0,16},{8,24},{16,32},{24,40},{32,48},{40,56},{48,64},{56,72},{64,... | collective-permute-start | bytes 393224 | tf_op jit(solution)/shard_map/ppermute | solution.py:31
  11.9 12.2 %collective-permute-start.2 = (bf16[128,512]{1,0:T(8,128)(2,1)S(1)}, bf16[128,512]{1,0:T(8,128)(2,1)S(1)}, u32[]{:S(2)}, u32[]{:S(2)}) collective-permute-start(bf16[128,512]{1,0:T(8,128)(2,1)S(1)} %bitcast.35), channel_id=1, source_target_pairs={{8,32},{24,48},{40,64},{56,80},{72,96},{88,112},{104,128},{120,144... | collective-permute-start | bytes 393224 | tf_op jit(solution)/shard_map/ppermute | solution.py:31
  18.8 5.2 %collective-permute-start = (bf16[128,512]{1,0:T(8,128)(2,1)S(1)}, bf16[128,512]{1,0:T(8,128)(2,1)S(1)}, u32[]{:S(2)}, u32[]{:S(2)}) collective-permute-start(bf16[128,512]{1,0:T(8,128)(2,1)S(1)} %bitcast.36), channel_id=1, source_target_pairs={{0,8},{16,24},{32,40},{48,56},{64,72},{80,88},{96,104},{112,120},{... | collective-permute-start | bytes 393224 | tf_op jit(solution)/shard_map/ppermute | solution.py:31
  20.2 4.0 %collective-permute-start.3 = (bf16[128,512]{1,0:T(8,128)(2,1)S(1)}, bf16[128,512]{1,0:T(8,128)(2,1)S(1)}, u32[]{:S(2)}, u32[]{:S(2)}) collective-permute-start(bf16[128,512]{1,0:T(8,128)(2,1)S(1)} %collective-permute-done.1.refs_2_), channel_id=1, source_target_pairs={{0,8},{8,0},{1,9},{9,1},{2,10},{10,2},{3,11},{11,3},{4,12},{12,4},... | collective-permute-start | bytes 393224 | tf_op jit(solution)/shard_map/ppermute | solution.py:35
  24.2 13.5 %copy-start.2 = (bf16[128,512]{1,0:T(8,128)(2,1)}, bf16[128,512]{1,0:T(8,128)(2,1)S(1)}, u32[]{:S(2)}) copy-start(bf16[128,512]{1,0:T(8,128)(2,1)S(1)} %collective-permute-done.3.refs_4_) | copy-start | bytes 393220
  25.0 30.7 %collective-permute-start.8 = (bf16[512,1024]{1,0:T(8,128)(2,1)S(1)}, bf16[512,1024]{1,0:T(8,128)(2,1)S(1)}, u32[]{:S(2)}, u32[]{:S(2)}) collective-permute-start(bf16[512,1024]{1,0:T(8,128)(2,1)S(1)} %bitcast.26), channel_id=1, source_target_pairs={{0,8},{8,0},{1,9},{9,1},{2,10},{10,2},{3,11},{11,3},{4,12},{12,4},... | collective-permute-start | bytes 3145736 | tf_op jit(solution)/shard_map/ppermute | solution.py:35
  31.0 24.8 %all-to-all-start.1 = ((bf16[8,128,256]{2,1,0:T(8,128)(2,1)}), bf16[8,128,256]{2,1,0:T(8,128)(2,1)S(1)}, u32[]{:S(2)}, u32[]{:S(2)}) async-start(bf16[8,128,256]{2,1,0:T(8,128)(2,1)} %broadcast_in_dim.6), calls=%async_computation.1 | async-start | bytes 1048576 | tf_op jit(solution)/shard_map/all_to_all | solution.py:278
  37.7 0.9 copy-start.3
  45.9 5.6 %collective-permute-start.5 = (bf16[128,512]{1,0:T(8,128)(2,1)}, bf16[128,512]{1,0:T(8,128)(2,1)S(1)}, u32[]{:S(2)}, u32[]{:S(2)}) collective-permute-start(bf16[128,512]{1,0:T(8,128)(2,1)} %get-tuple-element.30), channel_id=1, source_target_pairs={{0,8},{8,0},{1,9},{9,1},{2,10},{10,2},{3,11},{11,3},{4,12},{12,4},... | collective-permute-start | bytes 393224 | tf_op jit(solution)/shard_map/ppermute | solution.py:35
  48.1 3.5 %collective-permute-start.4 = (bf16[128,512]{1,0:T(8,128)(2,1)}, bf16[128,512]{1,0:T(8,128)(2,1)S(1)}, u32[]{:S(2)}, u32[]{:S(2)}) collective-permute-start(bf16[128,512]{1,0:T(8,128)(2,1)} %get-tuple-element.29), channel_id=1, source_target_pairs={{8,0},{24,16},{40,32},{56,48},{72,64},{88,80},{104,96},{120,112},{... | collective-permute-start | bytes 393224 | tf_op jit(solution)/shard_map/ppermute | solution.py:31
  50.2 9.4 %collective-permute-start.7 = (bf16[128,512]{1,0:T(8,128)(2,1)}, bf16[128,512]{1,0:T(8,128)(2,1)S(1)}, u32[]{:S(2)}, u32[]{:S(2)}) collective-permute-start(bf16[128,512]{1,0:T(8,128)(2,1)} %get-tuple-element.29), channel_id=1, source_target_pairs={{32,8},{48,24},{64,40},{80,56},{96,72},{112,88},{128,104},{144,120... | collective-permute-start | bytes 393224 | tf_op jit(solution)/shard_map/ppermute | solution.py:31
  51.6 8.1 %collective-permute-start.6 = (bf16[128,512]{1,0:T(8,128)(2,1)S(1)}, bf16[128,512]{1,0:T(8,128)(2,1)S(1)}, u32[]{:S(2)}, u32[]{:S(2)}) collective-permute-start(bf16[128,512]{1,0:T(8,128)(2,1)S(1)} %add_convert_fusion.2), channel_id=1, source_target_pairs={{16,0},{24,8},{32,16},{40,24},{48,32},{56,40},{64,48},{72,56},{80,... | collective-permute-start | bytes 393224 | tf_op jit(solution)/shard_map/ppermute | solution.py:31
  85.3 30.7 %all-to-all-start.3 = ((bf16[64,16,256]{2,1,0:T(8,128)(2,1)}), bf16[64,16,256]{2,1,0:T(8,128)(2,1)S(1)}, u32[]{:S(2)}, u32[]{:S(2)}) async-start(bf16[64,16,256]{2,1,0:T(8,128)(2,1)} %bitcast.38), calls=%async_computation.3 | async-start | bytes 1048576 | tf_op jit(solution)/shard_map/all_to_all | solution.py:286
  96.3 10.0 %collective-permute-start.10 = (bf16[128,512]{1,0:T(8,128)(2,1)S(1)}, bf16[128,512]{1,0:T(8,128)(2,1)S(1)}, u32[]{:S(2)}, u32[]{:S(2)}) collective-permute-start(bf16[128,512]{1,0:T(8,128)(2,1)S(1)} %pad_maximum_fusion.1.refs_0_), channel_id=1, source_target_pairs={{0,16},{8,24},{16,32},{24,40},{32,48},{40,56},{48,64},{56,72},{64,... | collective-permute-start | bytes 393224 | tf_op jit(solution)/shard_map/ppermute | solution.py:31
  99.2 15.8 %collective-permute-start.11 = (bf16[128,512]{1,0:T(8,128)(2,1)S(1)}, bf16[128,512]{1,0:T(8,128)(2,1)S(1)}, u32[]{:S(2)}, u32[]{:S(2)}) collective-permute-start(bf16[128,512]{1,0:T(8,128)(2,1)S(1)} %pad_maximum_fusion.1.refs_0_), channel_id=1, source_target_pairs={{8,32},{24,48},{40,64},{56,80},{72,96},{88,112},{104,128},{120,144... | collective-permute-start | bytes 393224 | tf_op jit(solution)/shard_map/ppermute | solution.py:31
  105.0 10.0 %collective-permute-start.9 = (bf16[128,512]{1,0:T(8,128)(2,1)S(1)}, bf16[128,512]{1,0:T(8,128)(2,1)S(1)}, u32[]{:S(2)}, u32[]{:S(2)}) collective-permute-start(bf16[128,512]{1,0:T(8,128)(2,1)S(1)} %pad_maximum_fusion.1.refs_0_), channel_id=1, source_target_pairs={{0,8},{16,24},{32,40},{48,56},{64,72},{80,88},{96,104},{112,120},{... | collective-permute-start | bytes 393224 | tf_op jit(solution)/shard_map/ppermute | solution.py:31
  106.3 9.7 %collective-permute-start.12 = (bf16[128,512]{1,0:T(8,128)(2,1)S(1)}, bf16[128,512]{1,0:T(8,128)(2,1)S(1)}, u32[]{:S(2)}, u32[]{:S(2)}) collective-permute-start(bf16[128,512]{1,0:T(8,128)(2,1)S(1)} %collective-permute-done.10.refs_2_), channel_id=1, source_target_pairs={{0,8},{8,0},{1,9},{9,1},{2,10},{10,2},{3,11},{11,3},{4,12},{12,4},... | collective-permute-start | bytes 393224 | tf_op jit(solution)/shard_map/ppermute | solution.py:35
  116.8 22.0 %all-to-all-start.4 = ((bf16[32,16,256]{2,1,0:T(8,128)(2,1)}), bf16[32,16,256]{2,1,0:T(8,128)(2,1)S(1)}, u32[]{:S(2)}, u32[]{:S(2)}) async-start(bf16[32,16,256]{2,1,0:T(8,128)(2,1)} %broadcast_in_dim.8), calls=%async_computation.4 | async-start | bytes 524288 | tf_op jit(solution)/shard_map/all_to_all | solution.py:263
  131.7 5.8 %collective-permute-start.14 = (bf16[128,512]{1,0:T(8,128)(2,1)S(1)}, bf16[128,512]{1,0:T(8,128)(2,1)S(1)}, u32[]{:S(2)}, u32[]{:S(2)}) collective-permute-start(bf16[128,512]{1,0:T(8,128)(2,1)S(1)} %get-tuple-element.40), channel_id=1, source_target_pairs={{0,8},{8,0},{1,9},{9,1},{2,10},{10,2},{3,11},{11,3},{4,12},{12,4},... | collective-permute-start | bytes 393224 | tf_op jit(solution)/shard_map/ppermute | solution.py:35
  134.2 3.2 %collective-permute-start.13 = (bf16[128,512]{1,0:T(8,128)(2,1)S(1)}, bf16[128,512]{1,0:T(8,128)(2,1)S(1)}, u32[]{:S(2)}, u32[]{:S(2)}) collective-permute-start(bf16[128,512]{1,0:T(8,128)(2,1)S(1)} %get-tuple-element.39), channel_id=1, source_target_pairs={{8,0},{24,16},{40,32},{56,48},{72,64},{88,80},{104,96},{120,112},{... | collective-permute-start | bytes 393224 | tf_op jit(solution)/shard_map/ppermute | solution.py:31
  136.1 8.8 %collective-permute-start.16 = (bf16[128,512]{1,0:T(8,128)(2,1)S(1)}, bf16[128,512]{1,0:T(8,128)(2,1)S(1)}, u32[]{:S(2)}, u32[]{:S(2)}) collective-permute-start(bf16[128,512]{1,0:T(8,128)(2,1)S(1)} %get-tuple-element.39), channel_id=1, source_target_pairs={{32,8},{48,24},{64,40},{80,56},{96,72},{112,88},{128,104},{144,120... | collective-permute-start | bytes 393224 | tf_op jit(solution)/shard_map/ppermute | solution.py:31
  137.5 8.7 %collective-permute-start.15 = (bf16[128,512]{1,0:T(8,128)(2,1)S(1)}, bf16[128,512]{1,0:T(8,128)(2,1)S(1)}, u32[]{:S(2)}, u32[]{:S(2)}) collective-permute-start(bf16[128,512]{1,0:T(8,128)(2,1)S(1)} %add_convert_fusion.1), channel_id=1, source_target_pairs={{16,0},{24,8},{32,16},{40,24},{48,32},{56,40},{64,48},{72,56},{80,... | collective-permute-start | bytes 393224 | tf_op jit(solution)/shard_map/ppermute | solution.py:31
  138.8 8.1 %collective-permute-start.17 = (bf16[512,256]{1,0:T(8,128)(2,1)S(1)}, bf16[512,256]{1,0:T(8,128)(2,1)S(1)}, u32[]{:S(2)}, u32[]{:S(2)}) collective-permute-start(bf16[512,256]{1,0:T(8,128)(2,1)S(1)} %bitcast.39), channel_id=1, source_target_pairs={{0,8},{8,0},{1,9},{9,1},{2,10},{10,2},{3,11},{11,3},{4,12},{12,4},... | collective-permute-start | bytes 786440 | tf_op jit(solution)/shard_map/ppermute | solution.py:35

commit v12 on v11

--- a/solution.py
+++ b/solution.py
@@ -80,15 +80,16 @@
     unit = jnp.where(unit, 1.0, 0.0).astype(jnp.bfloat16)
     score_scale = math.log2(math.e) / math.sqrt(HEAD_SIZE)
     total = jnp.zeros((SPAN_ROWS, HEAD_SIZE), jnp.float32)
-    for pair in range(GROUP_WIDTH // 2):
-        heads = jnp.concatenate([stacked(query_ref, pair), unit], axis=1)
-        scores = lax.dot_general(keys, heads, NT, preferred_element_type=jnp.float32)
-        top = jnp.max(scores, axis=0, keepdims=True)
-        weights = jnp.exp2((scores - top) * score_scale)
-        weights = weights * (1.0 / jnp.sum(weights, axis=0, keepdims=True))
-        low = weights.astype(jnp.bfloat16)
-        weights_ref[0, :, pair * PAIR : (pair + 1) * PAIR] = low
-        total += jnp.dot(low, stacked(grad_ref, pair), preferred_element_type=jnp.float32)
+    heads = jnp.concatenate([stacked(query_ref, pair) for pair in range(GROUP_WIDTH // 2)], axis=0)
+    heads = jnp.concatenate([heads, jnp.concatenate([unit] * (GROUP_WIDTH // 2), axis=0)], axis=1)
+    scores = lax.dot_general(keys, heads, NT, preferred_element_type=jnp.float32)
+    top = jnp.max(scores, axis=0, keepdims=True)
+    weights = jnp.exp2((scores - top) * score_scale)
+    weights = weights * (1.0 / jnp.sum(weights, axis=0, keepdims=True))
+    low = weights.astype(jnp.bfloat16)
+    weights_ref[0] = low
+    grads = jnp.concatenate([stacked(grad_ref, pair) for pair in range(GROUP_WIDTH // 2)], axis=0)
+    total = jnp.dot(low, grads, preferred_element_type=jnp.float32)
     for block, out_ref in enumerate(out_refs):
         out_ref[...] = total[block * BLOCK : (block + 1) * BLOCK].astype(out_ref.dtype)
 
@@ -97,14 +98,14 @@
     value_refs, out_refs = refs[:5], refs[5:]
     values = span_rows(core_ref, *value_refs)
     total = jnp.zeros((SPAN_ROWS, HEAD_SIZE), jnp.float32)
-    for pair in range(GROUP_WIDTH // 2):
-        prob_grad = lax.dot_general(
-            values, stacked(grad_ref, pair), NT, preferred_element_type=jnp.float32
-        )
-        weights = weights_ref[0, :, pair * PAIR : (pair + 1) * PAIR].astype(jnp.float32)
-        row_delta = jnp.sum(weights * prob_grad, axis=0, keepdims=True)
-        low = (weights * (prob_grad - row_delta)).astype(jnp.bfloat16)
-        total += jnp.dot(low, stacked(query_ref, pair), preferred_element_type=jnp.float32)
+    pairs = range(GROUP_WIDTH // 2)
+    grads = jnp.concatenate([stacked(grad_ref, pair) for pair in pairs], axis=0)
+    prob_grad = lax.dot_general(values, grads, NT, preferred_element_type=jnp.float32)
+    weights = weights_ref[0].astype(jnp.float32)
+    row_delta = jnp.sum(weights * prob_grad, axis=0, keepdims=True)
+    low = (weights * (prob_grad - row_delta)).astype(jnp.bfloat16)
+    queries = jnp.concatenate([stacked(query_ref, pair) for pair in pairs], axis=0)
+    total = jnp.dot(low, queries, preferred_element_type=jnp.float32)
     total = total * (1.0 / math.sqrt(HEAD_SIZE))
     for block, out_ref in enumerate(out_refs):
         out_ref[...] = total[block * BLOCK : (block + 1) * BLOCK].astype(out_ref.dtype)
@@ -175,22 +176,21 @@
             out_ref[rows, :] = values[x * BLOCK : (x + 1) * BLOCK]
 
 
-def pack_kernel(core_ref, own_ref, two_ref, across_ref, three_ref, values_ref, out_ref):
+def pack_kernel(core_ref, own_ref, two_ref, across_ref, three_ref, out_ref):
     last = jnp.where(core_ref[0] == 0, across_ref[...], three_ref[...])
     total = own_ref[...] + two_ref[...].astype(jnp.float32) + last.astype(jnp.float32)
     low = total.astype(jnp.bfloat16)
     for device in range(8):
         core = device % 2
         rows = slice(device * BLOCK, (device + 1) * BLOCK)
-        out_ref[rows, :HALF] = low[:, core * HALF : (core + 1) * HALF]
-        out_ref[rows, HALF:] = values_ref[rows, :]
+        out_ref[rows, :] = low[:, core * HALF : (core + 1) * HALF]
 
 
 def product_kernel(core_ref, near_ref, far_ref, grads_ref, out_ref):
     total = None
     for rows_ref, core in ((near_ref, core_ref[0]), (far_ref, 1 - core_ref[0])):
         grads = [
-            grads_ref[pl.ds(pl.multiple_of((2 * x + core) * BLOCK, BLOCK), BLOCK), :HALF]
+            grads_ref[pl.ds(pl.multiple_of((2 * x + core) * BLOCK, BLOCK), BLOCK), :]
             for x in range(4)
         ]
         part = lax.dot_general(
@@ -232,29 +232,36 @@
     )(core, near, far, weight)
 
 
-def exchange_packed(core, own, received, values):
+def exchange_value_grad(core, own, received):
     packed = pl.pallas_call(
         pack_kernel,
-        in_specs=[in_smem] + [in_vmem] * 5,
+        in_specs=[in_smem] + [in_vmem] * 4,
         out_specs=in_vmem,
-        out_shape=jax.ShapeDtypeStruct((8 * BLOCK, 2 * HALF), jnp.bfloat16),
+        out_shape=jax.ShapeDtypeStruct((8 * BLOCK, HALF), jnp.bfloat16),
         compiler_params=params,
         name="pack",
-    )(core, own, *received, values)
+    )(core, own, *received)
     return lax.all_to_all(packed, ("x", "c"), 0, 0, tiled=True)
 
 
-def group_product(core, near, far, packed):
+def exchange_values(values):
+    parts = lax.all_to_all(values, ("x", "c"), 0, 0, tiled=True)
+    parts = parts.reshape(4, 2, BLOCK, HALF).astype(jnp.float32)
+    values = jnp.sum(parts, axis=0).astype(jnp.bfloat16)
+    return jnp.concatenate([values[0], values[1]], axis=1)
+
+
+def group_product(core, near, far, value_grads):
     rows = pl.BlockSpec((4 * BLOCK, HALF), lambda part: (0, part))
     return pl.pallas_call(
         product_kernel,
         grid=(QUARTER // HALF,),
-        in_specs=[in_smem, rows, rows, pl.BlockSpec((8 * BLOCK, 2 * HALF), lambda part: (0, 0))],
+        in_specs=[in_smem, rows, rows, pl.BlockSpec((8 * BLOCK, HALF), lambda part: (0, 0))],
         out_specs=pl.BlockSpec((HALF, HALF), lambda part: (part, 0)),
-        out_shape=pltpu.HBM((QUARTER, HALF), jnp.bfloat16),
+        out_shape=jax.ShapeDtypeStruct((QUARTER, HALF), jnp.bfloat16),
         compiler_params=params,
         name="group_product",
-    )(core, near, far, packed)
+    )(core, near, far, value_grads)
 
 
 def whole_shard(piece):
@@ -278,25 +285,25 @@
     part = lax.all_to_all(piece, "y", 0, 0, tiled=True)
     weights, *value_parts = attention_weights(core, doc_pos, queries, grads, (keys,) + key_blocks)
 
-    received = to_earlier(value_parts, even)
+    two, across, three = to_earlier(value_parts, even)
+    part, across = lax.optimization_barrier((part, across))
     far = swap(near)
-    values = partial_values(core, near, far, part)
-    packed = exchange_packed(core, value_parts[SPAN], received, values)
-    product = group_product(core, near, far, packed)
+    values = exchange_values(partial_values(core, near, far, part))
+    values, two, across, three = lax.optimization_barrier((values, two, across, three))
+    value_grads = exchange_value_grad(core, value_parts[SPAN], (two, across, three))
+    value_blocks = from_earlier(values)
+    value_grads, value_blocks = lax.optimization_barrier((value_grads, value_blocks))
+    product = group_product(core, near, far, value_grads)
     pieces = lax.all_to_all(product, ("y", "z"), 0, 0, tiled=True)
 
-    parts = packed.reshape(4, 2, BLOCK, 2 * HALF)[..., HALF:].astype(jnp.float32)
-    values = jnp.sum(parts, axis=0).astype(jnp.bfloat16)
-    values = jnp.concatenate([values[0], values[1]], axis=1)
-    value_blocks = from_earlier(values)
-    pieces, value_blocks = lax.optimization_barrier((pieces, value_blocks))
     key_parts = key_gradient(core, weights, queries, grads, (values,) + value_blocks)
+    two, across, three = to_earlier(key_parts, even)
+    pieces, two, across, three = lax.optimization_barrier((pieces, two, across, three))
 
     pieces = pieces.reshape(64, -1, HALF).astype(jnp.float32)
     token_total = lax.axis_size(("x", "z", "c", "y")) * BLOCK
     piece = (jnp.sum(pieces, axis=0) * (1.0 / math.sqrt(token_total))).astype(jnp.bfloat16)
     weight_grad = whole_shard(piece)
-    two, across, three = to_earlier(key_parts, even)
     key_grad = key_parts[SPAN] + two.astype(jnp.float32)
     key_grad = key_grad + jnp.where(even, across, three).astype(jnp.float32)
     return (key_grad.astype(jnp.bfloat16)[None], weight_grad)

time: 150 us -> 154 us (1.027)
  waiting for transfers between devices: 12.6 us -> 22.3 us
  blocking collectives: 22.7 us -> 19.3 us
  starting transfers between devices: 86.4 us -> 83.3 us
    all_to_all x1 -> x2, waiting for transfers between devices: 0.01 us -> 4.98 us  [the longest x1 4.98 us: exchange_values(): parts = lax.all_to_all(values, ('x', 'c'), 0, 0, tiled=True)]
    all_to_all x1 -> x2, starting transfers between devices: 8.26 us -> 13.2 us  [the longest x1 7.54 us: exchange_value_grad(): return lax.all_to_all(packed, ('x', 'c'), 0, 0, tiled=True)]
    ppermute x12, starting transfers between devices: 31.4 us -> 27.6 us  [shift(): return lax.ppermute(block, DP, route)]
    all_to_all x1, blocking collectives: 22.7 us -> 19.3 us  [whole_shard(): half = lax.all_to_all(copies, ('x', 'z'), 0, 0, tiled=True)]
    all_to_all x1, waiting for transfers between devices: 2.79 us -> 6.12 us  [per_device(): part = lax.all_to_all(piece, 'y', 0, 0, tiled=True)]
    all_to_all x1, starting transfers between devices: 10.9 us -> 8.52 us  [per_device(): pieces = lax.all_to_all(product, ('y', 'z'), 0, 0, tiled=True)]
    ppermute x6, starting transfers between devices: 24.3 us -> 22.4 us  [swap(): return lax.ppermute(block, 'c', OTHER_CORE)]
  transfers between devices with their start and end apart: 22 -> 23, of which waited for: 6 -> 10; matrix products, arithmetic and copies ran while one was open for 1% -> 2% of each run, Pallas kernels for 10% -> 9%
where the time goes in v12:
time: 154 us; the launch traced here: 153 us
  starting transfers between devices  83.3 us (54%)
  waiting for transfers between devices  22.3 us (14%)
  Pallas kernels  19.7 us (13%)
  blocking collectives  19.3 us (13%)
  local copies, waits for them, and re-layouts  4.51 us (3%)
  other arithmetic  2.95 us (2%)
    ppermute x12, starting transfers between devices, shift(): return lax.ppermute(block, DP, route)  27.6 us
    ppermute x6, starting transfers between devices, swap(): return lax.ppermute(block, 'c', OTHER_CORE)  22.4 us
    all_to_all x1, blocking collectives, whole_shard(): half = lax.all_to_all(copies, ('x', 'z'), 0, 0, tiled=True)  19.3 us
    ppermute x12, waiting for transfers between devices, shift(): return lax.ppermute(block, DP, route)  8.66 us
    all_to_all x1, starting transfers between devices, per_device(): pieces = lax.all_to_all(product, ('y', 'z'), 0, 0, tiled=True)  8.52 us
    all_to_all x1, starting transfers between devices, exchange_value_grad(): return lax.all_to_all(packed, ('x', 'c'), 0, 0, tiled=True)  7.54 us
    pallas_call x1, Pallas kernels, attention_weights(): pl.pallas_call(weights_kernel, grid=(KEY_HEADS,), in_specs=[in_smem, pl.B...  6.97 us
    all_to_all x1, starting transfers between devices, per_device(): part = lax.all_to_all(piece, 'y', 0, 0, tiled=True)  6.74 us
  transfers between devices with their start and end apart: 23, of which 10 were waited for; matrix products, arithmetic and copies ran while one was open for 2% of the time, Pallas kernels for 9%

profile of v12, /device:TPU:1, one launch (start us, length us, event | category | flops | bytes accessed | tf_op | source)
XLA Modules:
  0.0 153.0 jit_solution(14478101126464199657)
XLA Ops:
  0.7 1.2 copy-done
  3.0 4.8 %all-to-all-start = ((bf16[4,128,1024]{2,1,0:T(8,128)(2,1)}), bf16[4,128,1024]{2,1,0:T(8,128)(2,1)S(1)}, u32[]{:S(2)}, u32[]{:S(2)}) async-start(bf16[4,128,1024]{2,1,0:T(8,128)(2,1)} %bitcast.5), calls=%async_computation | async-start | bytes 2097152 | tf_op jit(solution)/shard_map/all_to_all | solution.py:215
  7.9 4.0 %collective-permute-start.1 = (bf16[128,512]{1,0:T(8,128)(2,1)S(1)}, bf16[128,512]{1,0:T(8,128)(2,1)S(1)}, u32[]{:S(2)}, u32[]{:S(2)}) collective-permute-start(bf16[128,512]{1,0:T(8,128)(2,1)S(1)} %bitcast.33), channel_id=1, source_target_pairs={{0,16},{8,24},{16,32},{24,40},{32,48},{40,56},{48,64},{56,72},{64,... | collective-permute-start | bytes 393224 | tf_op jit(solution)/shard_map/ppermute | solution.py:31
  11.9 6.9 %collective-permute-start.2 = (bf16[128,512]{1,0:T(8,128)(2,1)S(1)}, bf16[128,512]{1,0:T(8,128)(2,1)S(1)}, u32[]{:S(2)}, u32[]{:S(2)}) collective-permute-start(bf16[128,512]{1,0:T(8,128)(2,1)S(1)} %bitcast.34), channel_id=1, source_target_pairs={{8,32},{24,48},{40,64},{56,80},{72,96},{88,112},{104,128},{120,144... | collective-permute-start | bytes 393224 | tf_op jit(solution)/shard_map/ppermute | solution.py:31
  18.8 1.3 collective-permute-start
  20.1 3.0 %collective-permute-start.3 = (bf16[128,512]{1,0:T(8,128)(2,1)S(1)}, bf16[128,512]{1,0:T(8,128)(2,1)S(1)}, u32[]{:S(2)}, u32[]{:S(2)}) collective-permute-start(bf16[128,512]{1,0:T(8,128)(2,1)S(1)} %collective-permute-done.1.refs_2_), channel_id=1, source_target_pairs={{0,8},{8,0},{1,9},{9,1},{2,10},{10,2},{3,11},{11,3},{4,12},{12,4},... | collective-permute-start | bytes 393224 | tf_op jit(solution)/shard_map/ppermute | solution.py:35
  25.0 5.9 %collective-permute-start.4 = (bf16[512,1024]{1,0:T(8,128)(2,1)S(1)}, bf16[512,1024]{1,0:T(8,128)(2,1)S(1)}, u32[]{:S(2)}, u32[]{:S(2)}) collective-permute-start(bf16[512,1024]{1,0:T(8,128)(2,1)S(1)} %bitcast.27), channel_id=1, source_target_pairs={{0,8},{8,0},{1,9},{9,1},{2,10},{10,2},{3,11},{11,3},{4,12},{12,4},... | collective-permute-start | bytes 3145736 | tf_op jit(solution)/shard_map/ppermute | solution.py:35
  30.9 6.7 %all-to-all-start.1 = ((bf16[8,128,256]{2,1,0:T(8,128)(2,1)}), bf16[8,128,256]{2,1,0:T(8,128)(2,1)S(1)}, u32[]{:S(2)}, u32[]{:S(2)}) async-start(bf16[8,128,256]{2,1,0:T(8,128)(2,1)} %broadcast_in_dim.6), calls=%async_computation.1 | async-start | bytes 1048576 | tf_op jit(solution)/shard_map/all_to_all | solution.py:285
  38.6 7.0 %attention_weights.1 = (bf16[4,512,1024]{2,1,0:T(8,128)(2,1)}, bf16[128,512]{1,0:T(8,128)(2,1)S(1)}, bf16[128,512]{1,0:T(8,128)(2,1)S(1)}, bf16[128,512]{1,0:T(8,128)(2,1)S(1)}, f32[128,512]{1,0:T(8,128)S(1)}) custom-call(s32[1]{0:T(128)} %bitcast.core_ref, s32[1,128]{1,0:T(1,128)S(1)} %copy-done.6, bf16[128,4096]{1,0:T(8,128)(2,1)} %bitcast.38, ...), custom_call_target="tpu_custom_call" | custom-call | flops 2147483648 | bytes 8388608 | tf_op jit(solution)/shard_map/attention_weights/pallas_call | solution.py:132
  46.2 2.3 %collective-permute-start.5 = (bf16[128,512]{1,0:T(8,128)(2,1)S(1)}, bf16[128,512]{1,0:T(8,128)(2,1)S(1)}, u32[]{:S(2)}, u32[]{:S(2)}) collective-permute-start(bf16[128,512]{1,0:T(8,128)(2,1)S(1)} %get-tuple-element.39), channel_id=1, source_target_pairs={{0,8},{8,0},{1,9},{9,1},{2,10},{10,2},{3,11},{11,3},{4,12},{12,4},... | collective-permute-start | bytes 393224 | tf_op jit(solution)/shard_map/ppermute | solution.py:35
  49.6 6.1 %all-to-all-done.1 = bf16[8,128,256]{2,1,0:T(8,128)(2,1)S(1)} async-done(((bf16[8,128,256]{2,1,0:T(8,128)(2,1)}), bf16[8,128,256]{2,1,0:T(8,128)(2,1)S(1)}, u32[]{:S(2)}, u32[]{:S(2)}) %all-to-all-start.1) | async-done | bytes 524320 | tf_op jit(solution)/shard_map/all_to_all | solution.py:285
  55.7 1.5 %partial_values.1 = bf16[1024,256]{1,0:T(8,128)(2,1)} custom-call(s32[1]{0:T(128)} %bitcast.core_ref, bf16[512,1024]{1,0:T(8,128)(2,1)S(1)} %bitcast.28, bf16[512,1024]{1,0:T(8,128)(2,1)S(1)} %collective-permute-done.4.far_ref, bf16[1024,256]{1,0:T(8,128)(2,1)S(1)} %bitcast.31), custom_call_target="tpu_custom_call" | custom-call | tf_op jit(solution)/shard_map/partial_values/pallas_call | solution.py:225
  57.2 5.7 %all-to-all-start.2 = ((bf16[8,128,256]{2,1,0:T(8,128)(2,1)}), bf16[8,128,256]{2,1,0:T(8,128)(2,1)}, u32[]{:S(2)}, u32[]{:S(2)}) async-start(bf16[8,128,256]{2,1,0:T(8,128)(2,1)} %bitcast.10), calls=%async_computation.2 | async-start | bytes 1048576 | tf_op jit(solution)/shard_map/all_to_all | solution.py:248
  62.9 1.9 %collective-permute-start.6 = (bf16[128,512]{1,0:T(8,128)(2,1)S(1)}, bf16[128,512]{1,0:T(8,128)(2,1)S(1)}, u32[]{:S(2)}, u32[]{:S(2)}) collective-permute-start(bf16[128,512]{1,0:T(8,128)(2,1)S(1)} %copy-done.5), channel_id=1, source_target_pairs={{8,0},{24,16},{40,32},{56,48},{72,64},{88,80},{104,96},{120,112},{... | collective-permute-start | bytes 393224 | tf_op jit(solution)/shard_map/ppermute | solution.py:31
  64.9 1.3 collective-permute-start.8
  66.2 1.3 collective-permute-start.7
  67.5 5.0 %all-to-all-done.2 = bf16[8,128,256]{2,1,0:T(8,128)(2,1)} async-done(((bf16[8,128,256]{2,1,0:T(8,128)(2,1)}), bf16[8,128,256]{2,1,0:T(8,128)(2,1)}, u32[]{:S(2)}, u32[]{:S(2)}) %all-to-all-start.2) | async-done | bytes 524320 | tf_op jit(solution)/shard_map/all_to_all | solution.py:248
  75.6 7.5 %all-to-all-start.3 = ((bf16[8,128,256]{2,1,0:T(8,128)(2,1)}), bf16[8,128,256]{2,1,0:T(8,128)(2,1)S(1)}, u32[]{:S(2)}, u32[]{:S(2)}) async-start(bf16[8,128,256]{2,1,0:T(8,128)(2,1)} %bitcast.14), calls=%async_computation.3 | async-start | bytes 1048576 | tf_op jit(solution)/shard_map/all_to_all | solution.py:244
  83.1 3.1 %collective-permute-start.10 = (bf16[128,512]{1,0:T(8,128)(2,1)S(1)}, bf16[128,512]{1,0:T(8,128)(2,1)S(1)}, u32[]{:S(2)}, u32[]{:S(2)}) collective-permute-start(bf16[128,512]{1,0:T(8,128)(2,1)S(1)} %pad_maximum_fusion.1.refs_0_), channel_id=1, source_target_pairs={{0,16},{8,24},{16,32},{24,40},{32,48},{40,56},{48,64},{56,72},{64,... | collective-permute-start | bytes 393224 | tf_op jit(solution)/shard_map/ppermute | solution.py:31
  86.2 2.0 %collective-permute-start.11 = (bf16[128,512]{1,0:T(8,128)(2,1)S(1)}, bf16[128,512]{1,0:T(8,128)(2,1)S(1)}, u32[]{:S(2)}, u32[]{:S(2)}) collective-permute-start(bf16[128,512]{1,0:T(8,128)(2,1)S(1)} %pad_maximum_fusion.1.refs_0_), channel_id=1, source_target_pairs={{8,32},{24,48},{40,64},{56,80},{72,96},{88,112},{104,128},{120,144... | collective-permute-start | bytes 393224 | tf_op jit(solution)/shard_map/ppermute | solution.py:31
  88.2 1.3 collective-permute-start.9
  89.5 3.0 %collective-permute-start.12 = (bf16[128,512]{1,0:T(8,128)(2,1)S(1)}, bf16[128,512]{1,0:T(8,128)(2,1)S(1)}, u32[]{:S(2)}, u32[]{:S(2)}) collective-permute-start(bf16[128,512]{1,0:T(8,128)(2,1)S(1)} %collective-permute-done.10.refs_2_), channel_id=1, source_target_pairs={{0,8},{8,0},{1,9},{9,1},{2,10},{10,2},{3,11},{11,3},{4,12},{12,4},... | collective-permute-start | bytes 393224 | tf_op jit(solution)/shard_map/ppermute | solution.py:35
  93.5 2.8 %group_product.1 = bf16[1024,256]{1,0:T(8,128)(2,1)} custom-call(s32[1]{0:T(128)} %bitcast.core_ref, bf16[512,1024]{1,0:T(8,128)(2,1)S(1)} %bitcast.29, bf16[512,1024]{1,0:T(8,128)(2,1)S(1)} %collective-permute-done.4.far_ref, bf16[1024,256]{1,0:T(8,128)(2,1)S(1)} %bitcast.30), custom_call_target="tpu_custom_call" | custom-call | tf_op jit(solution)/shard_map/group_product/pallas_call | solution.py:256
  96.4 8.5 %all-to-all-start.4 = ((bf16[64,16,256]{2,1,0:T(8,128)(2,1)}), bf16[64,16,256]{2,1,0:T(8,128)(2,1)S(1)}, u32[]{:S(2)}, u32[]{:S(2)}) async-start(bf16[64,16,256]{2,1,0:T(8,128)(2,1)} %bitcast.16), calls=%async_computation.4 | async-start | bytes 1048576 | tf_op jit(solution)/shard_map/all_to_all | solution.py:297
  104.9 6.4 %key_gradient.1 = (bf16[128,512]{1,0:T(8,128)(2,1)S(1)}, bf16[128,512]{1,0:T(8,128)(2,1)S(1)}, bf16[128,512]{1,0:T(8,128)(2,1)S(1)}, f32[128,512]{1,0:T(8,128)S(1)}) custom-call(s32[1]{0:T(128)} %bitcast.core_ref, bf16[4,512,1024]{2,1,0:T(8,128)(2,1)} %get-tuple-element.36.weights_ref, bf16[128,4096]{1,0:T(8,128)(2,1)} %bitcast.39, ...), custom_call_target="tpu_custom_call" | custom-call | flops 2147483648 | bytes 8388608 | tf_op jit(solution)/shard_map/key_gradient/pallas_call | solution.py:147
  111.3 2.6 %collective-permute-start.14 = (bf16[128,512]{1,0:T(8,128)(2,1)S(1)}, bf16[128,512]{1,0:T(8,128)(2,1)S(1)}, u32[]{:S(2)}, u32[]{:S(2)}) collective-permute-start(bf16[128,512]{1,0:T(8,128)(2,1)S(1)} %get-tuple-element.57), channel_id=1, source_target_pairs={{0,8},{8,0},{1,9},{9,1},{2,10},{10,2},{3,11},{11,3},{4,12},{12,4},... | collective-permute-start | bytes 393224 | tf_op jit(solution)/shard_map/ppermute | solution.py:35
  113.8 1.9 %collective-permute-start.13 = (bf16[128,512]{1,0:T(8,128)(2,1)S(1)}, bf16[128,512]{1,0:T(8,128)(2,1)S(1)}, u32[]{:S(2)}, u32[]{:S(2)}) collective-permute-start(bf16[128,512]{1,0:T(8,128)(2,1)S(1)} %get-tuple-element.56), channel_id=1, source_target_pairs={{8,0},{24,16},{40,32},{56,48},{72,64},{88,80},{104,96},{120,112},{... | collective-permute-start | bytes 393224 | tf_op jit(solution)/shard_map/ppermute | solution.py:31
  115.8 1.3 collective-permute-start.16
  117.1 1.3 collective-permute-start.15
  118.4 7.1 %collective-permute-done.16 = bf16[128,512]{1,0:T(8,128)(2,1)S(1)} collective-permute-done((bf16[128,512]{1,0:T(8,128)(2,1)S(1)}, bf16[128,512]{1,0:T(8,128)(2,1)S(1)}, u32[]{:S(2)}, u32[]{:S(2)}) %collective-permute-start.16) | collective-permute-done | bytes 131104 | tf_op jit(solution)/shard_map/ppermute | solution.py:31
  126.1 19.3 %all_to_all.66 = bf16[32,16,256]{2,1,0:T(8,128)(2,1)S(1)} all-to-all(bf16[32,16,256]{2,1,0:T(8,128)(2,1)S(1)} %broadcast_in_dim.8), channel_id=1, replica_groups=mesh['x'=4,'z'=8,'c'=2,'y'=8] {'x','z'}, dimensions={0} | all-to-all | bytes 524288 | tf_op jit(solution)/shard_map/all_to_all | solution.py:270
  145.4 5.5 %collective-permute-start.17 = (bf16[512,256]{1,0:T(8,128)(2,1)S(1)}, bf16[512,256]{1,0:T(8,128)(2,1)S(1)}, u32[]{:S(2)}, u32[]{:S(2)}) collective-permute-start(bf16[512,256]{1,0:T(8,128)(2,1)S(1)} %bitcast.37), channel_id=1, source_target_pairs={{0,8},{8,0},{1,9},{9,1},{2,10},{10,2},{3,11},{11,3},{4,12},{12,4},... | collective-permute-start | bytes 786440 | tf_op jit(solution)/shard_map/ppermute | solution.py:35
  (48 shorter events, 12.3 us)
Async XLA Ops:
  0.6 37.1 %copy-start.6 = (s32[1,128]{1,0:T(1,128)S(1)}, s32[1,128]{1,0:T(1,128)}, u32[]{:S(2)}) copy-start(s32[1,128]{1,0:T(1,128)} %position_ref.1) | copy-start | bytes 1540
  0.6 1.2 copy-start
  1.9 6.0 %copy-start.1 = (bf16[1,128,512]{2,1,0:T(8,128)(2,1)S(1)}, bf16[1,128,512]{2,1,0:T(8,128)(2,1)}, u32[]{:S(2)}) copy-start(bf16[1,128,512]{2,1,0:T(8,128)(2,1)} %param.7) | copy-start | bytes 393220
  3.0 21.1 %all-to-all-start = ((bf16[4,128,1024]{2,1,0:T(8,128)(2,1)}), bf16[4,128,1024]{2,1,0:T(8,128)(2,1)S(1)}, u32[]{:S(2)}, u32[]{:S(2)}) async-start(bf16[4,128,1024]{2,1,0:T(8,128)(2,1)} %bitcast.5), calls=%async_computation | async-start | bytes 2097152 | tf_op jit(solution)/shard_map/all_to_all | solution.py:215
  7.9 12.2 %collective-permute-start.1 = (bf16[128,512]{1,0:T(8,128)(2,1)S(1)}, bf16[128,512]{1,0:T(8,128)(2,1)S(1)}, u32[]{:S(2)}, u32[]{:S(2)}) collective-permute-start(bf16[128,512]{1,0:T(8,128)(2,1)S(1)} %bitcast.33), channel_id=1, source_target_pairs={{0,16},{8,24},{16,32},{24,40},{32,48},{40,56},{48,64},{56,72},{64,... | collective-permute-start | bytes 393224 | tf_op jit(solution)/shard_map/ppermute | solution.py:31
  11.9 12.2 %collective-permute-start.2 = (bf16[128,512]{1,0:T(8,128)(2,1)S(1)}, bf16[128,512]{1,0:T(8,128)(2,1)S(1)}, u32[]{:S(2)}, u32[]{:S(2)}) collective-permute-start(bf16[128,512]{1,0:T(8,128)(2,1)S(1)} %bitcast.34), channel_id=1, source_target_pairs={{8,32},{24,48},{40,64},{56,80},{72,96},{88,112},{104,128},{120,144... | collective-permute-start | bytes 393224 | tf_op jit(solution)/shard_map/ppermute | solution.py:31
  18.8 5.2 %collective-permute-start = (bf16[128,512]{1,0:T(8,128)(2,1)S(1)}, bf16[128,512]{1,0:T(8,128)(2,1)S(1)}, u32[]{:S(2)}, u32[]{:S(2)}) collective-permute-start(bf16[128,512]{1,0:T(8,128)(2,1)S(1)} %bitcast.35), channel_id=1, source_target_pairs={{0,8},{16,24},{32,40},{48,56},{64,72},{80,88},{96,104},{112,120},{... | collective-permute-start | bytes 393224 | tf_op jit(solution)/shard_map/ppermute | solution.py:31
  20.1 4.0 %collective-permute-start.3 = (bf16[128,512]{1,0:T(8,128)(2,1)S(1)}, bf16[128,512]{1,0:T(8,128)(2,1)S(1)}, u32[]{:S(2)}, u32[]{:S(2)}) collective-permute-start(bf16[128,512]{1,0:T(8,128)(2,1)S(1)} %collective-permute-done.1.refs_2_), channel_id=1, source_target_pairs={{0,8},{8,0},{1,9},{9,1},{2,10},{10,2},{3,11},{11,3},{4,12},{12,4},... | collective-permute-start | bytes 393224 | tf_op jit(solution)/shard_map/ppermute | solution.py:35
  24.1 13.5 %copy-start.2 = (bf16[128,512]{1,0:T(8,128)(2,1)}, bf16[128,512]{1,0:T(8,128)(2,1)S(1)}, u32[]{:S(2)}) copy-start(bf16[128,512]{1,0:T(8,128)(2,1)S(1)} %collective-permute-done.3.refs_4_) | copy-start | bytes 393220
  25.0 30.7 %collective-permute-start.4 = (bf16[512,1024]{1,0:T(8,128)(2,1)S(1)}, bf16[512,1024]{1,0:T(8,128)(2,1)S(1)}, u32[]{:S(2)}, u32[]{:S(2)}) collective-permute-start(bf16[512,1024]{1,0:T(8,128)(2,1)S(1)} %bitcast.27), channel_id=1, source_target_pairs={{0,8},{8,0},{1,9},{9,1},{2,10},{10,2},{3,11},{11,3},{4,12},{12,4},... | collective-permute-start | bytes 3145736 | tf_op jit(solution)/shard_map/ppermute | solution.py:35
  30.9 24.8 %all-to-all-start.1 = ((bf16[8,128,256]{2,1,0:T(8,128)(2,1)}), bf16[8,128,256]{2,1,0:T(8,128)(2,1)S(1)}, u32[]{:S(2)}, u32[]{:S(2)}) async-start(bf16[8,128,256]{2,1,0:T(8,128)(2,1)} %broadcast_in_dim.6), calls=%async_computation.1 | async-start | bytes 1048576 | tf_op jit(solution)/shard_map/all_to_all | solution.py:285
  37.7 0.9 copy-start.3
  45.6 0.7 copy-start.4
  46.2 16.7 %copy-start.5 = (bf16[128,512]{1,0:T(8,128)(2,1)S(1)}, bf16[128,512]{1,0:T(8,128)(2,1)}, u32[]{:S(2)}) copy-start(bf16[128,512]{1,0:T(8,128)(2,1)} %copy-done.4) | copy-start | bytes 393220
  46.2 3.4 %collective-permute-start.5 = (bf16[128,512]{1,0:T(8,128)(2,1)S(1)}, bf16[128,512]{1,0:T(8,128)(2,1)S(1)}, u32[]{:S(2)}, u32[]{:S(2)}) collective-permute-start(bf16[128,512]{1,0:T(8,128)(2,1)S(1)} %get-tuple-element.39), channel_id=1, source_target_pairs={{0,8},{8,0},{1,9},{9,1},{2,10},{10,2},{3,11},{11,3},{4,12},{12,4},... | collective-permute-start | bytes 393224 | tf_op jit(solution)/shard_map/ppermute | solution.py:35
  57.2 15.3 %all-to-all-start.2 = ((bf16[8,128,256]{2,1,0:T(8,128)(2,1)}), bf16[8,128,256]{2,1,0:T(8,128)(2,1)}, u32[]{:S(2)}, u32[]{:S(2)}) async-start(bf16[8,128,256]{2,1,0:T(8,128)(2,1)} %bitcast.10), calls=%async_computation.2 | async-start | bytes 1048576 | tf_op jit(solution)/shard_map/all_to_all | solution.py:248
  62.9 3.2 %collective-permute-start.6 = (bf16[128,512]{1,0:T(8,128)(2,1)S(1)}, bf16[128,512]{1,0:T(8,128)(2,1)S(1)}, u32[]{:S(2)}, u32[]{:S(2)}) collective-permute-start(bf16[128,512]{1,0:T(8,128)(2,1)S(1)} %copy-done.5), channel_id=1, source_target_pairs={{8,0},{24,16},{40,32},{56,48},{72,64},{88,80},{104,96},{120,112},{... | collective-permute-start | bytes 393224 | tf_op jit(solution)/shard_map/ppermute | solution.py:31
  64.9 9.0 %collective-permute-start.8 = (bf16[128,512]{1,0:T(8,128)(2,1)S(1)}, bf16[128,512]{1,0:T(8,128)(2,1)S(1)}, u32[]{:S(2)}, u32[]{:S(2)}) collective-permute-start(bf16[128,512]{1,0:T(8,128)(2,1)S(1)} %copy-done.5), channel_id=1, source_target_pairs={{32,8},{48,24},{64,40},{80,56},{96,72},{112,88},{128,104},{144,120... | collective-permute-start | bytes 393224 | tf_op jit(solution)/shard_map/ppermute | solution.py:31
  66.2 8.5 %collective-permute-start.7 = (bf16[128,512]{1,0:T(8,128)(2,1)S(1)}, bf16[128,512]{1,0:T(8,128)(2,1)S(1)}, u32[]{:S(2)}, u32[]{:S(2)}) collective-permute-start(bf16[128,512]{1,0:T(8,128)(2,1)S(1)} %add_convert_fusion.2), channel_id=1, source_target_pairs={{16,0},{24,8},{32,16},{40,24},{48,32},{56,40},{64,48},{72,56},{80,... | collective-permute-start | bytes 393224 | tf_op jit(solution)/shard_map/ppermute | solution.py:31
  75.6 17.9 %all-to-all-start.3 = ((bf16[8,128,256]{2,1,0:T(8,128)(2,1)}), bf16[8,128,256]{2,1,0:T(8,128)(2,1)S(1)}, u32[]{:S(2)}, u32[]{:S(2)}) async-start(bf16[8,128,256]{2,1,0:T(8,128)(2,1)} %bitcast.14), calls=%async_computation.3 | async-start | bytes 1048576 | tf_op jit(solution)/shard_map/all_to_all | solution.py:244
  83.1 6.4 %collective-permute-start.10 = (bf16[128,512]{1,0:T(8,128)(2,1)S(1)}, bf16[128,512]{1,0:T(8,128)(2,1)S(1)}, u32[]{:S(2)}, u32[]{:S(2)}) collective-permute-start(bf16[128,512]{1,0:T(8,128)(2,1)S(1)} %pad_maximum_fusion.1.refs_0_), channel_id=1, source_target_pairs={{0,16},{8,24},{16,32},{24,40},{32,48},{40,56},{48,64},{56,72},{64,... | collective-permute-start | bytes 393224 | tf_op jit(solution)/shard_map/ppermute | solution.py:31
  86.2 6.3 %collective-permute-start.11 = (bf16[128,512]{1,0:T(8,128)(2,1)S(1)}, bf16[128,512]{1,0:T(8,128)(2,1)S(1)}, u32[]{:S(2)}, u32[]{:S(2)}) collective-permute-start(bf16[128,512]{1,0:T(8,128)(2,1)S(1)} %pad_maximum_fusion.1.refs_0_), channel_id=1, source_target_pairs={{8,32},{24,48},{40,64},{56,80},{72,96},{88,112},{104,128},{120,144... | collective-permute-start | bytes 393224 | tf_op jit(solution)/shard_map/ppermute | solution.py:31
  88.2 4.4 %collective-permute-start.9 = (bf16[128,512]{1,0:T(8,128)(2,1)S(1)}, bf16[128,512]{1,0:T(8,128)(2,1)S(1)}, u32[]{:S(2)}, u32[]{:S(2)}) collective-permute-start(bf16[128,512]{1,0:T(8,128)(2,1)S(1)} %pad_maximum_fusion.1.refs_0_), channel_id=1, source_target_pairs={{0,8},{16,24},{32,40},{48,56},{64,72},{80,88},{96,104},{112,120},{... | collective-permute-start | bytes 393224 | tf_op jit(solution)/shard_map/ppermute | solution.py:31
  89.5 4.0 %collective-permute-start.12 = (bf16[128,512]{1,0:T(8,128)(2,1)S(1)}, bf16[128,512]{1,0:T(8,128)(2,1)S(1)}, u32[]{:S(2)}, u32[]{:S(2)}) collective-permute-start(bf16[128,512]{1,0:T(8,128)(2,1)S(1)} %collective-permute-done.10.refs_2_), channel_id=1, source_target_pairs={{0,8},{8,0},{1,9},{9,1},{2,10},{10,2},{3,11},{11,3},{4,12},{12,4},... | collective-permute-start | bytes 393224 | tf_op jit(solution)/shard_map/ppermute | solution.py:35
  96.4 29.7 %all-to-all-start.4 = ((bf16[64,16,256]{2,1,0:T(8,128)(2,1)}), bf16[64,16,256]{2,1,0:T(8,128)(2,1)S(1)}, u32[]{:S(2)}, u32[]{:S(2)}) async-start(bf16[64,16,256]{2,1,0:T(8,128)(2,1)} %bitcast.16), calls=%async_computation.4 | async-start | bytes 1048576 | tf_op jit(solution)/shard_map/all_to_all | solution.py:297
  111.3 5.8 %collective-permute-start.14 = (bf16[128,512]{1,0:T(8,128)(2,1)S(1)}, bf16[128,512]{1,0:T(8,128)(2,1)S(1)}, u32[]{:S(2)}, u32[]{:S(2)}) collective-permute-start(bf16[128,512]{1,0:T(8,128)(2,1)S(1)} %get-tuple-element.57), channel_id=1, source_target_pairs={{0,8},{8,0},{1,9},{9,1},{2,10},{10,2},{3,11},{11,3},{4,12},{12,4},... | collective-permute-start | bytes 393224 | tf_op jit(solution)/shard_map/ppermute | solution.py:35
  113.8 3.2 %collective-permute-start.13 = (bf16[128,512]{1,0:T(8,128)(2,1)S(1)}, bf16[128,512]{1,0:T(8,128)(2,1)S(1)}, u32[]{:S(2)}, u32[]{:S(2)}) collective-permute-start(bf16[128,512]{1,0:T(8,128)(2,1)S(1)} %get-tuple-element.56), channel_id=1, source_target_pairs={{8,0},{24,16},{40,32},{56,48},{72,64},{88,80},{104,96},{120,112},{... | collective-permute-start | bytes 393224 | tf_op jit(solution)/shard_map/ppermute | solution.py:31
  115.8 9.8 %collective-permute-start.16 = (bf16[128,512]{1,0:T(8,128)(2,1)S(1)}, bf16[128,512]{1,0:T(8,128)(2,1)S(1)}, u32[]{:S(2)}, u32[]{:S(2)}) collective-permute-start(bf16[128,512]{1,0:T(8,128)(2,1)S(1)} %get-tuple-element.56), channel_id=1, source_target_pairs={{32,8},{48,24},{64,40},{80,56},{96,72},{112,88},{128,104},{144,120... | collective-permute-start | bytes 393224 | tf_op jit(solution)/shard_map/ppermute | solution.py:31
  117.1 8.9 %collective-permute-start.15 = (bf16[128,512]{1,0:T(8,128)(2,1)S(1)}, bf16[128,512]{1,0:T(8,128)(2,1)S(1)}, u32[]{:S(2)}, u32[]{:S(2)}) collective-permute-start(bf16[128,512]{1,0:T(8,128)(2,1)S(1)} %add_convert_fusion.1), channel_id=1, source_target_pairs={{16,0},{24,8},{32,16},{40,24},{48,32},{56,40},{64,48},{72,56},{80,... | collective-permute-start | bytes 393224 | tf_op jit(solution)/shard_map/ppermute | solution.py:31
  145.4 6.6 %collective-permute-start.17 = (bf16[512,256]{1,0:T(8,128)(2,1)S(1)}, bf16[512,256]{1,0:T(8,128)(2,1)S(1)}, u32[]{:S(2)}, u32[]{:S(2)}) collective-permute-start(bf16[512,256]{1,0:T(8,128)(2,1)S(1)} %bitcast.37), channel_id=1, source_target_pairs={{0,8},{8,0},{1,9},{9,1},{2,10},{10,2},{3,11},{11,3},{4,12},{12,4},... | collective-permute-start | bytes 786440 | tf_op jit(solution)/shard_map/ppermute | solution.py:35

commit v13 on v11

--- a/solution.py
+++ b/solution.py
@@ -80,15 +80,16 @@
     unit = jnp.where(unit, 1.0, 0.0).astype(jnp.bfloat16)
     score_scale = math.log2(math.e) / math.sqrt(HEAD_SIZE)
     total = jnp.zeros((SPAN_ROWS, HEAD_SIZE), jnp.float32)
-    for pair in range(GROUP_WIDTH // 2):
-        heads = jnp.concatenate([stacked(query_ref, pair), unit], axis=1)
-        scores = lax.dot_general(keys, heads, NT, preferred_element_type=jnp.float32)
-        top = jnp.max(scores, axis=0, keepdims=True)
-        weights = jnp.exp2((scores - top) * score_scale)
-        weights = weights * (1.0 / jnp.sum(weights, axis=0, keepdims=True))
-        low = weights.astype(jnp.bfloat16)
-        weights_ref[0, :, pair * PAIR : (pair + 1) * PAIR] = low
-        total += jnp.dot(low, stacked(grad_ref, pair), preferred_element_type=jnp.float32)
+    heads = jnp.concatenate([stacked(query_ref, pair) for pair in range(GROUP_WIDTH // 2)], axis=0)
+    heads = jnp.concatenate([heads, jnp.concatenate([unit] * (GROUP_WIDTH // 2), axis=0)], axis=1)
+    scores = lax.dot_general(keys, heads, NT, preferred_element_type=jnp.float32)
+    top = jnp.max(scores, axis=0, keepdims=True)
+    weights = jnp.exp2((scores - top) * score_scale)
+    weights = weights * (1.0 / jnp.sum(weights, axis=0, keepdims=True))
+    low = weights.astype(jnp.bfloat16)
+    weights_ref[0] = low
+    grads = jnp.concatenate([stacked(grad_ref, pair) for pair in range(GROUP_WIDTH // 2)], axis=0)
+    total = jnp.dot(low, grads, preferred_element_type=jnp.float32)
     for block, out_ref in enumerate(out_refs):
         out_ref[...] = total[block * BLOCK : (block + 1) * BLOCK].astype(out_ref.dtype)
 
@@ -97,14 +98,14 @@
     value_refs, out_refs = refs[:5], refs[5:]
     values = span_rows(core_ref, *value_refs)
     total = jnp.zeros((SPAN_ROWS, HEAD_SIZE), jnp.float32)
-    for pair in range(GROUP_WIDTH // 2):
-        prob_grad = lax.dot_general(
-            values, stacked(grad_ref, pair), NT, preferred_element_type=jnp.float32
-        )
-        weights = weights_ref[0, :, pair * PAIR : (pair + 1) * PAIR].astype(jnp.float32)
-        row_delta = jnp.sum(weights * prob_grad, axis=0, keepdims=True)
-        low = (weights * (prob_grad - row_delta)).astype(jnp.bfloat16)
-        total += jnp.dot(low, stacked(query_ref, pair), preferred_element_type=jnp.float32)
+    pairs = range(GROUP_WIDTH // 2)
+    grads = jnp.concatenate([stacked(grad_ref, pair) for pair in pairs], axis=0)
+    prob_grad = lax.dot_general(values, grads, NT, preferred_element_type=jnp.float32)
+    weights = weights_ref[0].astype(jnp.float32)
+    row_delta = jnp.sum(weights * prob_grad, axis=0, keepdims=True)
+    low = (weights * (prob_grad - row_delta)).astype(jnp.bfloat16)
+    queries = jnp.concatenate([stacked(query_ref, pair) for pair in pairs], axis=0)
+    total = jnp.dot(low, queries, preferred_element_type=jnp.float32)
     total = total * (1.0 / math.sqrt(HEAD_SIZE))
     for block, out_ref in enumerate(out_refs):
         out_ref[...] = total[block * BLOCK : (block + 1) * BLOCK].astype(out_ref.dtype)
@@ -251,7 +252,7 @@
         grid=(QUARTER // HALF,),
         in_specs=[in_smem, rows, rows, pl.BlockSpec((8 * BLOCK, 2 * HALF), lambda part: (0, 0))],
         out_specs=pl.BlockSpec((HALF, HALF), lambda part: (part, 0)),
-        out_shape=pltpu.HBM((QUARTER, HALF), jnp.bfloat16),
+        out_shape=jax.ShapeDtypeStruct((QUARTER, HALF), jnp.bfloat16),
         compiler_params=params,
         name="group_product",
     )(core, near, far, packed)
@@ -278,10 +279,11 @@
     part = lax.all_to_all(piece, "y", 0, 0, tiled=True)
     weights, *value_parts = attention_weights(core, doc_pos, queries, grads, (keys,) + key_blocks)
 
-    received = to_earlier(value_parts, even)
+    two, across, three = to_earlier(value_parts, even)
+    near, part, across = lax.optimization_barrier((near, part, across))
     far = swap(near)
     values = partial_values(core, near, far, part)
-    packed = exchange_packed(core, value_parts[SPAN], received, values)
+    packed = exchange_packed(core, value_parts[SPAN], (two, across, three), values)
     product = group_product(core, near, far, packed)
     pieces = lax.all_to_all(product, ("y", "z"), 0, 0, tiled=True)
 

time: 150 us -> 151 us (level)
  blocking collectives: 22.7 us -> 25.3 us
  starting transfers between devices: 86.4 us -> 84.4 us
  waiting for transfers between devices: 12.6 us -> 14.6 us
    all_to_all x1, starting transfers between devices: 10.9 us -> 4.64 us  [per_device(): pieces = lax.all_to_all(product, ('y', 'z'), 0, 0, tiled=True)]
    ppermute x6, starting transfers between devices: 24.3 us -> 28.6 us  [swap(): return lax.ppermute(block, 'c', OTHER_CORE)]
    ppermute x12, waiting for transfers between devices: 8.75 us -> 12.6 us  [shift(): return lax.ppermute(block, DP, route)]
    all_to_all x1, waiting for transfers between devices: 2.79 us -> 0.01 us  [per_device(): part = lax.all_to_all(piece, 'y', 0, 0, tiled=True)]
    all_to_all x1, blocking collectives: 22.7 us -> 25.3 us  [exchange_packed(): return lax.all_to_all(packed, ('x', 'c'), 0, 0, tiled=True)]
  transfers between devices with their start and end apart: 22 -> 22, of which waited for: 6 -> 7; matrix products, arithmetic and copies ran while one was open for 1% -> 1% of each run, Pallas kernels for 10% -> 9%
where the time goes in v13:
time: 151 us; the launch traced here: 149 us
  starting transfers between devices  84.4 us (56%)
  blocking collectives  25.3 us (17%)
  Pallas kernels  17.4 us (12%)
  waiting for transfers between devices  14.6 us (10%)
  local copies, waits for them, and re-layouts  4.43 us (3%)
  other arithmetic  1.9 us (1%)
    ppermute x12, starting transfers between devices, shift(): return lax.ppermute(block, DP, route)  31.2 us
    ppermute x6, starting transfers between devices, swap(): return lax.ppermute(block, 'c', OTHER_CORE)  28.6 us
    all_to_all x1, blocking collectives, exchange_packed(): return lax.all_to_all(packed, ('x', 'c'), 0, 0, tiled=True)  25.3 us
    ppermute x12, waiting for transfers between devices, shift(): return lax.ppermute(block, DP, route)  12.6 us
    all_to_all x1, starting transfers between devices, whole_shard(): half = lax.all_to_all(copies, ('x', 'z'), 0, 0, tiled=True)  8.33 us
    pallas_call x1, Pallas kernels, attention_weights(): pl.pallas_call(weights_kernel, grid=(KEY_HEADS,), in_specs=[in_smem, pl.B...  6.98 us
    all_to_all x1, starting transfers between devices, per_device(): part = lax.all_to_all(piece, 'y', 0, 0, tiled=True)  6.82 us
    pallas_call x1, Pallas kernels, key_gradient(): pl.pallas_call(scores_kernel, grid=(KEY_HEADS,), in_specs=[in_smem, held,...  6.38 us
  transfers between devices with their start and end apart: 22, of which 7 were waited for; matrix products, arithmetic and copies ran while one was open for 1% of the time, Pallas kernels for 9%

profile of v13, /device:TPU:1, one launch (start us, length us, event | category | flops | bytes accessed | tf_op | source)
XLA Modules:
  0.0 149.0 jit_solution(15503214321473401007)
XLA Ops:
  0.7 1.2 copy-done.1
  1.9 1.2 quarters.1
  3.1 4.8 %all-to-all-start = ((bf16[4,128,1024]{2,1,0:T(8,128)(2,1)}), bf16[4,128,1024]{2,1,0:T(8,128)(2,1)S(1)}, u32[]{:S(2)}, u32[]{:S(2)}) async-start(bf16[4,128,1024]{2,1,0:T(8,128)(2,1)} %bitcast.5), calls=%async_computation | async-start | bytes 2097152 | tf_op jit(solution)/shard_map/all_to_all | solution.py:216
  7.9 4.0 %collective-permute-start.1 = (bf16[128,512]{1,0:T(8,128)(2,1)S(1)}, bf16[128,512]{1,0:T(8,128)(2,1)S(1)}, u32[]{:S(2)}, u32[]{:S(2)}) collective-permute-start(bf16[128,512]{1,0:T(8,128)(2,1)S(1)} %bitcast.35), channel_id=1, source_target_pairs={{0,16},{8,24},{16,32},{24,40},{32,48},{40,56},{48,64},{56,72},{64,... | collective-permute-start | bytes 393224 | tf_op jit(solution)/shard_map/ppermute | solution.py:31
  11.9 6.9 %collective-permute-start.2 = (bf16[128,512]{1,0:T(8,128)(2,1)S(1)}, bf16[128,512]{1,0:T(8,128)(2,1)S(1)}, u32[]{:S(2)}, u32[]{:S(2)}) collective-permute-start(bf16[128,512]{1,0:T(8,128)(2,1)S(1)} %bitcast.36), channel_id=1, source_target_pairs={{8,32},{24,48},{40,64},{56,80},{72,96},{88,112},{104,128},{120,144... | collective-permute-start | bytes 393224 | tf_op jit(solution)/shard_map/ppermute | solution.py:31
  18.9 1.3 collective-permute-start
  20.2 3.0 %collective-permute-start.3 = (bf16[128,512]{1,0:T(8,128)(2,1)S(1)}, bf16[128,512]{1,0:T(8,128)(2,1)S(1)}, u32[]{:S(2)}, u32[]{:S(2)}) collective-permute-start(bf16[128,512]{1,0:T(8,128)(2,1)S(1)} %collective-permute-done.1.refs_2_), channel_id=1, source_target_pairs={{0,8},{8,0},{1,9},{9,1},{2,10},{10,2},{3,11},{11,3},{4,12},{12,4},... | collective-permute-start | bytes 393224 | tf_op jit(solution)/shard_map/ppermute | solution.py:35
  25.0 6.8 %all-to-all-start.1 = ((bf16[8,128,256]{2,1,0:T(8,128)(2,1)}), bf16[8,128,256]{2,1,0:T(8,128)(2,1)S(1)}, u32[]{:S(2)}, u32[]{:S(2)}) async-start(bf16[8,128,256]{2,1,0:T(8,128)(2,1)} %bitcast.8), calls=%async_computation.1 | async-start | bytes 1048576 | tf_op jit(solution)/shard_map/all_to_all | solution.py:279
  31.8 7.0 %attention_weights.1 = (bf16[4,512,1024]{2,1,0:T(8,128)(2,1)}, bf16[128,512]{1,0:T(8,128)(2,1)S(1)}, bf16[128,512]{1,0:T(8,128)(2,1)S(1)}, bf16[128,512]{1,0:T(8,128)(2,1)S(1)}, f32[128,512]{1,0:T(8,128)S(1)}) custom-call(s32[1]{0:T(128)} %bitcast.core_ref, s32[1,128]{1,0:T(1,128)S(1)} %copy-done.3, bf16[128,4096]{1,0:T(8,128)(2,1)} %bitcast.40, ...), custom_call_target="tpu_custom_call" | custom-call | flops 2147483648 | bytes 8388608 | tf_op jit(solution)/shard_map/attention_weights/pallas_call | solution.py:132
  38.8 6.1 %collective-permute-start.5 = (bf16[128,512]{1,0:T(8,128)(2,1)S(1)}, bf16[128,512]{1,0:T(8,128)(2,1)S(1)}, u32[]{:S(2)}, u32[]{:S(2)}) collective-permute-start(bf16[128,512]{1,0:T(8,128)(2,1)S(1)} %get-tuple-element.33), channel_id=1, source_target_pairs={{0,8},{8,0},{1,9},{9,1},{2,10},{10,2},{3,11},{11,3},{4,12},{12,4},... | collective-permute-start | bytes 393224 | tf_op jit(solution)/shard_map/ppermute | solution.py:35
  45.9 6.2 %collective-permute-start.8 = (bf16[512,1024]{1,0:T(8,128)(2,1)S(1)}, bf16[512,1024]{1,0:T(8,128)(2,1)S(1)}, u32[]{:S(2)}, u32[]{:S(2)}) collective-permute-start(bf16[512,1024]{1,0:T(8,128)(2,1)S(1)} %bitcast.26), channel_id=1, source_target_pairs={{0,8},{8,0},{1,9},{9,1},{2,10},{10,2},{3,11},{11,3},{4,12},{12,4},... | collective-permute-start | bytes 3145736 | tf_op jit(solution)/shard_map/ppermute | solution.py:35
  52.2 1.9 %collective-permute-start.4 = (bf16[128,512]{1,0:T(8,128)(2,1)S(1)}, bf16[128,512]{1,0:T(8,128)(2,1)S(1)}, u32[]{:S(2)}, u32[]{:S(2)}) collective-permute-start(bf16[128,512]{1,0:T(8,128)(2,1)S(1)} %get-tuple-element.32), channel_id=1, source_target_pairs={{8,0},{24,16},{40,32},{56,48},{72,64},{88,80},{104,96},{120,112},{... | collective-permute-start | bytes 393224 | tf_op jit(solution)/shard_map/ppermute | solution.py:31
  54.1 1.3 collective-permute-start.7
  55.5 1.3 collective-permute-start.6
  57.5 4.0 %collective-permute-done.7.three_ref = bf16[128,512]{1,0:T(8,128)(2,1)S(1)} collective-permute-done((bf16[128,512]{1,0:T(8,128)(2,1)S(1)}, bf16[128,512]{1,0:T(8,128)(2,1)S(1)}, u32[]{:S(2)}, u32[]{:S(2)}) %collective-permute-start.7) | collective-permute-done | bytes 131104 | tf_op jit(solution)/shard_map/ppermute | solution.py:31
  61.5 3.0 %collective-permute-done.6.two_ref = bf16[128,512]{1,0:T(8,128)(2,1)S(1)} collective-permute-done((bf16[128,512]{1,0:T(8,128)(2,1)S(1)}, bf16[128,512]{1,0:T(8,128)(2,1)S(1)}, u32[]{:S(2)}, u32[]{:S(2)}) %collective-permute-start.6) | collective-permute-done | bytes 131104 | tf_op jit(solution)/shard_map/ppermute | solution.py:31
  64.7 25.3 %all_to_all.56 = bf16[8,128,512]{2,1,0:T(8,128)(2,1)S(1)} all-to-all(bf16[8,128,512]{2,1,0:T(8,128)(2,1)S(1)} %bitcast.31), channel_id=1, replica_groups=mesh['x'=4,'z'=8,'c'=2,'y'=8] {'x','c'}, dimensions={0} | all-to-all | bytes 2097152 | tf_op jit(solution)/shard_map/all_to_all | solution.py:245
  89.9 2.0 %group_product.1 = bf16[1024,256]{1,0:T(8,128)(2,1)S(1)} custom-call(s32[1]{0:T(128)} %bitcast.core_ref, bf16[512,1024]{1,0:T(8,128)(2,1)S(1)} %bitcast.28, bf16[512,1024]{1,0:T(8,128)(2,1)S(1)} %collective-permute-done.8.far_ref, bf16[1024,512]{1,0:T(8,128)(2,1)S(1)} %bitcast.29), custom_call_target="tpu_custom_call" | custom-call | tf_op jit(solution)/shard_map/group_product/pallas_call | solution.py:250
  92.8 4.6 %all-to-all-start.3 = ((bf16[64,16,256]{2,1,0:T(8,128)(2,1)}), bf16[64,16,256]{2,1,0:T(8,128)(2,1)S(1)}, u32[]{:S(2)}, u32[]{:S(2)}) async-start(bf16[64,16,256]{2,1,0:T(8,128)(2,1)} %bitcast.33), calls=%async_computation.3 | async-start | bytes 1048576 | tf_op jit(solution)/shard_map/all_to_all | solution.py:288
  97.5 2.9 %collective-permute-start.10 = (bf16[128,512]{1,0:T(8,128)(2,1)S(1)}, bf16[128,512]{1,0:T(8,128)(2,1)S(1)}, u32[]{:S(2)}, u32[]{:S(2)}) collective-permute-start(bf16[128,512]{1,0:T(8,128)(2,1)S(1)} %pad_maximum_fusion.1.refs_0_), channel_id=1, source_target_pairs={{0,16},{8,24},{16,32},{24,40},{32,48},{40,56},{48,64},{56,72},{64,... | collective-permute-start | bytes 393224 | tf_op jit(solution)/shard_map/ppermute | solution.py:31
  100.4 5.8 %collective-permute-start.11 = (bf16[128,512]{1,0:T(8,128)(2,1)S(1)}, bf16[128,512]{1,0:T(8,128)(2,1)S(1)}, u32[]{:S(2)}, u32[]{:S(2)}) collective-permute-start(bf16[128,512]{1,0:T(8,128)(2,1)S(1)} %pad_maximum_fusion.1.refs_0_), channel_id=1, source_target_pairs={{8,32},{24,48},{40,64},{56,80},{72,96},{88,112},{104,128},{120,144... | collective-permute-start | bytes 393224 | tf_op jit(solution)/shard_map/ppermute | solution.py:31
  106.2 1.3 collective-permute-start.9
  107.5 8.7 %collective-permute-start.12 = (bf16[128,512]{1,0:T(8,128)(2,1)S(1)}, bf16[128,512]{1,0:T(8,128)(2,1)S(1)}, u32[]{:S(2)}, u32[]{:S(2)}) collective-permute-start(bf16[128,512]{1,0:T(8,128)(2,1)S(1)} %collective-permute-done.10.refs_2_), channel_id=1, source_target_pairs={{0,8},{8,0},{1,9},{9,1},{2,10},{10,2},{3,11},{11,3},{4,12},{12,4},... | collective-permute-start | bytes 393224 | tf_op jit(solution)/shard_map/ppermute | solution.py:35
  118.0 8.3 %all-to-all-start.4 = ((bf16[32,16,256]{2,1,0:T(8,128)(2,1)}), bf16[32,16,256]{2,1,0:T(8,128)(2,1)S(1)}, u32[]{:S(2)}, u32[]{:S(2)}) async-start(bf16[32,16,256]{2,1,0:T(8,128)(2,1)} %broadcast_in_dim.8), calls=%async_computation.4 | async-start | bytes 524288 | tf_op jit(solution)/shard_map/all_to_all | solution.py:264
  126.3 6.4 %key_gradient.1 = (bf16[128,512]{1,0:T(8,128)(2,1)S(1)}, bf16[128,512]{1,0:T(8,128)(2,1)S(1)}, bf16[128,512]{1,0:T(8,128)(2,1)S(1)}, f32[128,512]{1,0:T(8,128)S(1)}) custom-call(s32[1]{0:T(128)} %bitcast.core_ref, bf16[4,512,1024]{2,1,0:T(8,128)(2,1)} %get-tuple-element.29.weights_ref, bf16[128,4096]{1,0:T(8,128)(2,1)} %bitcast.41, ...), custom_call_target="tpu_custom_call" | custom-call | flops 2147483648 | bytes 8388608 | tf_op jit(solution)/shard_map/key_gradient/pallas_call | solution.py:147
  132.7 2.5 %collective-permute-start.14 = (bf16[128,512]{1,0:T(8,128)(2,1)S(1)}, bf16[128,512]{1,0:T(8,128)(2,1)S(1)}, u32[]{:S(2)}, u32[]{:S(2)}) collective-permute-start(bf16[128,512]{1,0:T(8,128)(2,1)S(1)} %get-tuple-element.46), channel_id=1, source_target_pairs={{0,8},{8,0},{1,9},{9,1},{2,10},{10,2},{3,11},{11,3},{4,12},{12,4},... | collective-permute-start | bytes 393224 | tf_op jit(solution)/shard_map/ppermute | solution.py:35
  135.3 1.9 %collective-permute-start.13 = (bf16[128,512]{1,0:T(8,128)(2,1)S(1)}, bf16[128,512]{1,0:T(8,128)(2,1)S(1)}, u32[]{:S(2)}, u32[]{:S(2)}) collective-permute-start(bf16[128,512]{1,0:T(8,128)(2,1)S(1)} %get-tuple-element.45), channel_id=1, source_target_pairs={{8,0},{24,16},{40,32},{56,48},{72,64},{88,80},{104,96},{120,112},{... | collective-permute-start | bytes 393224 | tf_op jit(solution)/shard_map/ppermute | solution.py:31
  137.2 1.3 collective-permute-start.16
  138.6 1.3 collective-permute-start.15
  139.9 1.9 %collective-permute-start.17 = (bf16[512,256]{1,0:T(8,128)(2,1)S(1)}, bf16[512,256]{1,0:T(8,128)(2,1)S(1)}, u32[]{:S(2)}, u32[]{:S(2)}) collective-permute-start(bf16[512,256]{1,0:T(8,128)(2,1)S(1)} %bitcast.39), channel_id=1, source_target_pairs={{0,8},{8,0},{1,9},{9,1},{2,10},{10,2},{3,11},{11,3},{4,12},{12,4},... | collective-permute-start | bytes 786440 | tf_op jit(solution)/shard_map/ppermute | solution.py:35
  141.8 4.2 %collective-permute-done.16 = bf16[128,512]{1,0:T(8,128)(2,1)S(1)} collective-permute-done((bf16[128,512]{1,0:T(8,128)(2,1)S(1)}, bf16[128,512]{1,0:T(8,128)(2,1)S(1)}, u32[]{:S(2)}, u32[]{:S(2)}) %collective-permute-start.16) | collective-permute-done | bytes 131104 | tf_op jit(solution)/shard_map/ppermute | solution.py:31
  146.0 1.3 collective-permute-done.15
  (40 shorter events, 8.0 us)
Async XLA Ops:
  0.6 31.2 %copy-start.3 = (s32[1,128]{1,0:T(1,128)S(1)}, s32[1,128]{1,0:T(1,128)}, u32[]{:S(2)}) copy-start(s32[1,128]{1,0:T(1,128)} %position_ref.1) | copy-start | bytes 1540
  0.6 1.2 copy-start.1
  1.9 6.1 %copy-start.2 = (bf16[1,128,512]{2,1,0:T(8,128)(2,1)S(1)}, bf16[1,128,512]{2,1,0:T(8,128)(2,1)}, u32[]{:S(2)}) copy-start(bf16[1,128,512]{2,1,0:T(8,128)(2,1)} %param.7) | copy-start | bytes 393220
  3.1 21.1 %all-to-all-start = ((bf16[4,128,1024]{2,1,0:T(8,128)(2,1)}), bf16[4,128,1024]{2,1,0:T(8,128)(2,1)S(1)}, u32[]{:S(2)}, u32[]{:S(2)}) async-start(bf16[4,128,1024]{2,1,0:T(8,128)(2,1)} %bitcast.5), calls=%async_computation | async-start | bytes 2097152 | tf_op jit(solution)/shard_map/all_to_all | solution.py:216
  7.9 12.2 %collective-permute-start.1 = (bf16[128,512]{1,0:T(8,128)(2,1)S(1)}, bf16[128,512]{1,0:T(8,128)(2,1)S(1)}, u32[]{:S(2)}, u32[]{:S(2)}) collective-permute-start(bf16[128,512]{1,0:T(8,128)(2,1)S(1)} %bitcast.35), channel_id=1, source_target_pairs={{0,16},{8,24},{16,32},{24,40},{32,48},{40,56},{48,64},{56,72},{64,... | collective-permute-start | bytes 393224 | tf_op jit(solution)/shard_map/ppermute | solution.py:31
  11.9 12.2 %collective-permute-start.2 = (bf16[128,512]{1,0:T(8,128)(2,1)S(1)}, bf16[128,512]{1,0:T(8,128)(2,1)S(1)}, u32[]{:S(2)}, u32[]{:S(2)}) collective-permute-start(bf16[128,512]{1,0:T(8,128)(2,1)S(1)} %bitcast.36), channel_id=1, source_target_pairs={{8,32},{24,48},{40,64},{56,80},{72,96},{88,112},{104,128},{120,144... | collective-permute-start | bytes 393224 | tf_op jit(solution)/shard_map/ppermute | solution.py:31
  18.9 5.2 %collective-permute-start = (bf16[128,512]{1,0:T(8,128)(2,1)S(1)}, bf16[128,512]{1,0:T(8,128)(2,1)S(1)}, u32[]{:S(2)}, u32[]{:S(2)}) collective-permute-start(bf16[128,512]{1,0:T(8,128)(2,1)S(1)} %bitcast.37), channel_id=1, source_target_pairs={{0,8},{16,24},{32,40},{48,56},{64,72},{80,88},{96,104},{112,120},{... | collective-permute-start | bytes 393224 | tf_op jit(solution)/shard_map/ppermute | solution.py:31
  20.2 4.0 %collective-permute-start.3 = (bf16[128,512]{1,0:T(8,128)(2,1)S(1)}, bf16[128,512]{1,0:T(8,128)(2,1)S(1)}, u32[]{:S(2)}, u32[]{:S(2)}) collective-permute-start(bf16[128,512]{1,0:T(8,128)(2,1)S(1)} %collective-permute-done.1.refs_2_), channel_id=1, source_target_pairs={{0,8},{8,0},{1,9},{9,1},{2,10},{10,2},{3,11},{11,3},{4,12},{12,4},... | collective-permute-start | bytes 393224 | tf_op jit(solution)/shard_map/ppermute | solution.py:35
  25.0 20.9 %all-to-all-start.1 = ((bf16[8,128,256]{2,1,0:T(8,128)(2,1)}), bf16[8,128,256]{2,1,0:T(8,128)(2,1)S(1)}, u32[]{:S(2)}, u32[]{:S(2)}) async-start(bf16[8,128,256]{2,1,0:T(8,128)(2,1)} %bitcast.8), calls=%async_computation.1 | async-start | bytes 1048576 | tf_op jit(solution)/shard_map/all_to_all | solution.py:279
  38.8 7.1 %collective-permute-start.5 = (bf16[128,512]{1,0:T(8,128)(2,1)S(1)}, bf16[128,512]{1,0:T(8,128)(2,1)S(1)}, u32[]{:S(2)}, u32[]{:S(2)}) collective-permute-start(bf16[128,512]{1,0:T(8,128)(2,1)S(1)} %get-tuple-element.33), channel_id=1, source_target_pairs={{0,8},{8,0},{1,9},{9,1},{2,10},{10,2},{3,11},{11,3},{4,12},{12,4},... | collective-permute-start | bytes 393224 | tf_op jit(solution)/shard_map/ppermute | solution.py:35
  45.9 10.9 %collective-permute-start.8 = (bf16[512,1024]{1,0:T(8,128)(2,1)S(1)}, bf16[512,1024]{1,0:T(8,128)(2,1)S(1)}, u32[]{:S(2)}, u32[]{:S(2)}) collective-permute-start(bf16[512,1024]{1,0:T(8,128)(2,1)S(1)} %bitcast.26), channel_id=1, source_target_pairs={{0,8},{8,0},{1,9},{9,1},{2,10},{10,2},{3,11},{11,3},{4,12},{12,4},... | collective-permute-start | bytes 3145736 | tf_op jit(solution)/shard_map/ppermute | solution.py:35
  52.2 3.2 %collective-permute-start.4 = (bf16[128,512]{1,0:T(8,128)(2,1)S(1)}, bf16[128,512]{1,0:T(8,128)(2,1)S(1)}, u32[]{:S(2)}, u32[]{:S(2)}) collective-permute-start(bf16[128,512]{1,0:T(8,128)(2,1)S(1)} %get-tuple-element.32), channel_id=1, source_target_pairs={{8,0},{24,16},{40,32},{56,48},{72,64},{88,80},{104,96},{120,112},{... | collective-permute-start | bytes 393224 | tf_op jit(solution)/shard_map/ppermute | solution.py:31
  54.1 7.4 %collective-permute-start.7 = (bf16[128,512]{1,0:T(8,128)(2,1)S(1)}, bf16[128,512]{1,0:T(8,128)(2,1)S(1)}, u32[]{:S(2)}, u32[]{:S(2)}) collective-permute-start(bf16[128,512]{1,0:T(8,128)(2,1)S(1)} %get-tuple-element.32), channel_id=1, source_target_pairs={{32,8},{48,24},{64,40},{80,56},{96,72},{112,88},{128,104},{144,120... | collective-permute-start | bytes 393224 | tf_op jit(solution)/shard_map/ppermute | solution.py:31
  55.5 9.1 %collective-permute-start.6 = (bf16[128,512]{1,0:T(8,128)(2,1)S(1)}, bf16[128,512]{1,0:T(8,128)(2,1)S(1)}, u32[]{:S(2)}, u32[]{:S(2)}) collective-permute-start(bf16[128,512]{1,0:T(8,128)(2,1)S(1)} %add_convert_fusion.2), channel_id=1, source_target_pairs={{16,0},{24,8},{32,16},{40,24},{48,32},{56,40},{64,48},{72,56},{80,... | collective-permute-start | bytes 393224 | tf_op jit(solution)/shard_map/ppermute | solution.py:31
  92.0 0.8 copy-start
  92.8 24.4 %all-to-all-start.3 = ((bf16[64,16,256]{2,1,0:T(8,128)(2,1)}), bf16[64,16,256]{2,1,0:T(8,128)(2,1)S(1)}, u32[]{:S(2)}, u32[]{:S(2)}) async-start(bf16[64,16,256]{2,1,0:T(8,128)(2,1)} %bitcast.33), calls=%async_computation.3 | async-start | bytes 1048576 | tf_op jit(solution)/shard_map/all_to_all | solution.py:288
  97.5 10.0 %collective-permute-start.10 = (bf16[128,512]{1,0:T(8,128)(2,1)S(1)}, bf16[128,512]{1,0:T(8,128)(2,1)S(1)}, u32[]{:S(2)}, u32[]{:S(2)}) collective-permute-start(bf16[128,512]{1,0:T(8,128)(2,1)S(1)} %pad_maximum_fusion.1.refs_0_), channel_id=1, source_target_pairs={{0,16},{8,24},{16,32},{24,40},{32,48},{40,56},{48,64},{56,72},{64,... | collective-permute-start | bytes 393224 | tf_op jit(solution)/shard_map/ppermute | solution.py:31
  100.4 15.8 %collective-permute-start.11 = (bf16[128,512]{1,0:T(8,128)(2,1)S(1)}, bf16[128,512]{1,0:T(8,128)(2,1)S(1)}, u32[]{:S(2)}, u32[]{:S(2)}) collective-permute-start(bf16[128,512]{1,0:T(8,128)(2,1)S(1)} %pad_maximum_fusion.1.refs_0_), channel_id=1, source_target_pairs={{8,32},{24,48},{40,64},{56,80},{72,96},{88,112},{104,128},{120,144... | collective-permute-start | bytes 393224 | tf_op jit(solution)/shard_map/ppermute | solution.py:31
  106.2 10.0 %collective-permute-start.9 = (bf16[128,512]{1,0:T(8,128)(2,1)S(1)}, bf16[128,512]{1,0:T(8,128)(2,1)S(1)}, u32[]{:S(2)}, u32[]{:S(2)}) collective-permute-start(bf16[128,512]{1,0:T(8,128)(2,1)S(1)} %pad_maximum_fusion.1.refs_0_), channel_id=1, source_target_pairs={{0,8},{16,24},{32,40},{48,56},{64,72},{80,88},{96,104},{112,120},{... | collective-permute-start | bytes 393224 | tf_op jit(solution)/shard_map/ppermute | solution.py:31
  107.5 9.7 %collective-permute-start.12 = (bf16[128,512]{1,0:T(8,128)(2,1)S(1)}, bf16[128,512]{1,0:T(8,128)(2,1)S(1)}, u32[]{:S(2)}, u32[]{:S(2)}) collective-permute-start(bf16[128,512]{1,0:T(8,128)(2,1)S(1)} %collective-permute-done.10.refs_2_), channel_id=1, source_target_pairs={{0,8},{8,0},{1,9},{9,1},{2,10},{10,2},{3,11},{11,3},{4,12},{12,4},... | collective-permute-start | bytes 393224 | tf_op jit(solution)/shard_map/ppermute | solution.py:35
  118.0 21.9 %all-to-all-start.4 = ((bf16[32,16,256]{2,1,0:T(8,128)(2,1)}), bf16[32,16,256]{2,1,0:T(8,128)(2,1)S(1)}, u32[]{:S(2)}, u32[]{:S(2)}) async-start(bf16[32,16,256]{2,1,0:T(8,128)(2,1)} %broadcast_in_dim.8), calls=%async_computation.4 | async-start | bytes 524288 | tf_op jit(solution)/shard_map/all_to_all | solution.py:264
  132.7 5.8 %collective-permute-start.14 = (bf16[128,512]{1,0:T(8,128)(2,1)S(1)}, bf16[128,512]{1,0:T(8,128)(2,1)S(1)}, u32[]{:S(2)}, u32[]{:S(2)}) collective-permute-start(bf16[128,512]{1,0:T(8,128)(2,1)S(1)} %get-tuple-element.46), channel_id=1, source_target_pairs={{0,8},{8,0},{1,9},{9,1},{2,10},{10,2},{3,11},{11,3},{4,12},{12,4},... | collective-permute-start | bytes 393224 | tf_op jit(solution)/shard_map/ppermute | solution.py:35
  135.3 3.2 %collective-permute-start.13 = (bf16[128,512]{1,0:T(8,128)(2,1)S(1)}, bf16[128,512]{1,0:T(8,128)(2,1)S(1)}, u32[]{:S(2)}, u32[]{:S(2)}) collective-permute-start(bf16[128,512]{1,0:T(8,128)(2,1)S(1)} %get-tuple-element.45), channel_id=1, source_target_pairs={{8,0},{24,16},{40,32},{56,48},{72,64},{88,80},{104,96},{120,112},{... | collective-permute-start | bytes 393224 | tf_op jit(solution)/shard_map/ppermute | solution.py:31
  137.2 8.8 %collective-permute-start.16 = (bf16[128,512]{1,0:T(8,128)(2,1)S(1)}, bf16[128,512]{1,0:T(8,128)(2,1)S(1)}, u32[]{:S(2)}, u32[]{:S(2)}) collective-permute-start(bf16[128,512]{1,0:T(8,128)(2,1)S(1)} %get-tuple-element.45), channel_id=1, source_target_pairs={{32,8},{48,24},{64,40},{80,56},{96,72},{112,88},{128,104},{144,120... | collective-permute-start | bytes 393224 | tf_op jit(solution)/shard_map/ppermute | solution.py:31
  138.6 8.7 %collective-permute-start.15 = (bf16[128,512]{1,0:T(8,128)(2,1)S(1)}, bf16[128,512]{1,0:T(8,128)(2,1)S(1)}, u32[]{:S(2)}, u32[]{:S(2)}) collective-permute-start(bf16[128,512]{1,0:T(8,128)(2,1)S(1)} %add_convert_fusion.1), channel_id=1, source_target_pairs={{16,0},{24,8},{32,16},{40,24},{48,32},{56,40},{64,48},{72,56},{80,... | collective-permute-start | bytes 393224 | tf_op jit(solution)/shard_map/ppermute | solution.py:31
  139.9 8.1 %collective-permute-start.17 = (bf16[512,256]{1,0:T(8,128)(2,1)S(1)}, bf16[512,256]{1,0:T(8,128)(2,1)S(1)}, u32[]{:S(2)}, u32[]{:S(2)}) collective-permute-start(bf16[512,256]{1,0:T(8,128)(2,1)S(1)} %bitcast.39), channel_id=1, source_target_pairs={{0,8},{8,0},{1,9},{9,1},{2,10},{10,2},{3,11},{11,3},{4,12},{12,4},... | collective-permute-start | bytes 786440 | tf_op jit(solution)/shard_map/ppermute | solution.py:35

commit v14 on v13

--- a/solution.py
+++ b/solution.py
@@ -279,11 +279,10 @@
     part = lax.all_to_all(piece, "y", 0, 0, tiled=True)
     weights, *value_parts = attention_weights(core, doc_pos, queries, grads, (keys,) + key_blocks)
 
-    two, across, three = to_earlier(value_parts, even)
-    near, part, across = lax.optimization_barrier((near, part, across))
+    received = to_earlier(value_parts, even)
     far = swap(near)
     values = partial_values(core, near, far, part)
-    packed = exchange_packed(core, value_parts[SPAN], (two, across, three), values)
+    packed = exchange_packed(core, value_parts[SPAN], received, values)
     product = group_product(core, near, far, packed)
     pieces = lax.all_to_all(product, ("y", "z"), 0, 0, tiled=True)
 

time: 151 us -> 150 us (level)
  blocking collectives: 25.3 us -> 22.7 us
  starting transfers between devices: 84.4 us -> 86.4 us
  waiting for transfers between devices: 14.6 us -> 12.6 us
    all_to_all x1, starting transfers between devices: 4.64 us -> 10.9 us  [per_device(): pieces = lax.all_to_all(product, ('y', 'z'), 0, 0, tiled=True)]
    ppermute x6, starting transfers between devices: 28.6 us -> 24.4 us  [swap(): return lax.ppermute(block, 'c', OTHER_CORE)]
    ppermute x12, waiting for transfers between devices: 12.6 us -> 8.38 us  [shift(): return lax.ppermute(block, DP, route)]
    all_to_all x1, waiting for transfers between devices: 0.01 us -> 3.16 us  [per_device(): part = lax.all_to_all(piece, 'y', 0, 0, tiled=True)]
    all_to_all x1, blocking collectives: 25.3 us -> 22.7 us  [exchange_packed(): return lax.all_to_all(packed, ('x', 'c'), 0, 0, tiled=True)]
  transfers between devices with their start and end apart: 22 -> 22, of which waited for: 7 -> 6; matrix products, arithmetic and copies ran while one was open for 1% -> 1% of each run, Pallas kernels for 9% -> 10%
where the time goes in v14:
time: 150 us; the launch traced here: 147 us
  starting transfers between devices  86.4 us (58%)
  blocking collectives  22.7 us (15%)
  Pallas kernels  17.3 us (12%)
  waiting for transfers between devices  12.6 us (8%)
  local copies, waits for them, and re-layouts  5.34 us (4%)
  other arithmetic  1.9 us (1%)
    ppermute x12, starting transfers between devices, shift(): return lax.ppermute(block, DP, route)  31.4 us
    ppermute x6, starting transfers between devices, swap(): return lax.ppermute(block, 'c', OTHER_CORE)  24.4 us
    all_to_all x1, blocking collectives, exchange_packed(): return lax.all_to_all(packed, ('x', 'c'), 0, 0, tiled=True)  22.7 us
    all_to_all x1, starting transfers between devices, per_device(): pieces = lax.all_to_all(product, ('y', 'z'), 0, 0, tiled=True)  10.9 us
    ppermute x12, waiting for transfers between devices, shift(): return lax.ppermute(block, DP, route)  8.38 us
    all_to_all x1, starting transfers between devices, whole_shard(): half = lax.all_to_all(copies, ('x', 'z'), 0, 0, tiled=True)  8.22 us
    pallas_call x1, Pallas kernels, attention_weights(): pl.pallas_call(weights_kernel, grid=(KEY_HEADS,), in_specs=[in_smem, pl.B...  6.92 us
    all_to_all x1, starting transfers between devices, per_device(): part = lax.all_to_all(piece, 'y', 0, 0, tiled=True)  6.74 us
  transfers between devices with their start and end apart: 22, of which 6 were waited for; matrix products, arithmetic and copies ran while one was open for 1% of the time, Pallas kernels for 10%

profile of v14, /device:TPU:1, one launch (start us, length us, event | category | flops | bytes accessed | tf_op | source)
XLA Modules:
  0.0 147.3 jit_solution(6169242399266598352)
XLA Ops:
  0.7 1.2 copy-done.1
  1.9 1.2 quarters.1
  3.1 4.8 %all-to-all-start = ((bf16[4,128,1024]{2,1,0:T(8,128)(2,1)}), bf16[4,128,1024]{2,1,0:T(8,128)(2,1)S(1)}, u32[]{:S(2)}, u32[]{:S(2)}) async-start(bf16[4,128,1024]{2,1,0:T(8,128)(2,1)} %bitcast.5), calls=%async_computation | async-start | bytes 2097152 | tf_op jit(solution)/shard_map/all_to_all | solution.py:216
  7.9 4.0 %collective-permute-start.1 = (bf16[128,512]{1,0:T(8,128)(2,1)S(1)}, bf16[128,512]{1,0:T(8,128)(2,1)S(1)}, u32[]{:S(2)}, u32[]{:S(2)}) collective-permute-start(bf16[128,512]{1,0:T(8,128)(2,1)S(1)} %bitcast.35), channel_id=1, source_target_pairs={{0,16},{8,24},{16,32},{24,40},{32,48},{40,56},{48,64},{56,72},{64,... | collective-permute-start | bytes 393224 | tf_op jit(solution)/shard_map/ppermute | solution.py:31
  11.9 6.9 %collective-permute-start.2 = (bf16[128,512]{1,0:T(8,128)(2,1)S(1)}, bf16[128,512]{1,0:T(8,128)(2,1)S(1)}, u32[]{:S(2)}, u32[]{:S(2)}) collective-permute-start(bf16[128,512]{1,0:T(8,128)(2,1)S(1)} %bitcast.36), channel_id=1, source_target_pairs={{8,32},{24,48},{40,64},{56,80},{72,96},{88,112},{104,128},{120,144... | collective-permute-start | bytes 393224 | tf_op jit(solution)/shard_map/ppermute | solution.py:31
  18.8 1.3 collective-permute-start
  20.1 3.0 %collective-permute-start.3 = (bf16[128,512]{1,0:T(8,128)(2,1)S(1)}, bf16[128,512]{1,0:T(8,128)(2,1)S(1)}, u32[]{:S(2)}, u32[]{:S(2)}) collective-permute-start(bf16[128,512]{1,0:T(8,128)(2,1)S(1)} %collective-permute-done.1.refs_2_), channel_id=1, source_target_pairs={{0,8},{8,0},{1,9},{9,1},{2,10},{10,2},{3,11},{11,3},{4,12},{12,4},... | collective-permute-start | bytes 393224 | tf_op jit(solution)/shard_map/ppermute | solution.py:35
  25.0 5.9 %collective-permute-start.8 = (bf16[512,1024]{1,0:T(8,128)(2,1)S(1)}, bf16[512,1024]{1,0:T(8,128)(2,1)S(1)}, u32[]{:S(2)}, u32[]{:S(2)}) collective-permute-start(bf16[512,1024]{1,0:T(8,128)(2,1)S(1)} %bitcast.26), channel_id=1, source_target_pairs={{0,8},{8,0},{1,9},{9,1},{2,10},{10,2},{3,11},{11,3},{4,12},{12,4},... | collective-permute-start | bytes 3145736 | tf_op jit(solution)/shard_map/ppermute | solution.py:35
  31.0 6.7 %all-to-all-start.1 = ((bf16[8,128,256]{2,1,0:T(8,128)(2,1)}), bf16[8,128,256]{2,1,0:T(8,128)(2,1)S(1)}, u32[]{:S(2)}, u32[]{:S(2)}) async-start(bf16[8,128,256]{2,1,0:T(8,128)(2,1)} %broadcast_in_dim.6), calls=%async_computation.1 | async-start | bytes 1048576 | tf_op jit(solution)/shard_map/all_to_all | solution.py:279
  38.6 6.9 %attention_weights.1 = (bf16[4,512,1024]{2,1,0:T(8,128)(2,1)}, bf16[128,512]{1,0:T(8,128)(2,1)}, bf16[128,512]{1,0:T(8,128)(2,1)S(1)}, bf16[128,512]{1,0:T(8,128)(2,1)}, f32[128,512]{1,0:T(8,128)S(1)}) custom-call(s32[1]{0:T(128)} %bitcast.core_ref, s32[1,128]{1,0:T(1,128)S(1)} %copy-done.5, bf16[128,4096]{1,0:T(8,128)(2,1)} %bitcast.40, ...), custom_call_target="tpu_custom_call" | custom-call | flops 2147483648 | bytes 8388608 | tf_op jit(solution)/shard_map/attention_weights/pallas_call | solution.py:132
  45.5 2.2 %collective-permute-start.5 = (bf16[128,512]{1,0:T(8,128)(2,1)}, bf16[128,512]{1,0:T(8,128)(2,1)S(1)}, u32[]{:S(2)}, u32[]{:S(2)}) collective-permute-start(bf16[128,512]{1,0:T(8,128)(2,1)} %get-tuple-element.30), channel_id=1, source_target_pairs={{0,8},{8,0},{1,9},{9,1},{2,10},{10,2},{3,11},{11,3},{4,12},{12,4},... | collective-permute-start | bytes 393224 | tf_op jit(solution)/shard_map/ppermute | solution.py:35
  47.7 2.1 %collective-permute-start.4 = (bf16[128,512]{1,0:T(8,128)(2,1)}, bf16[128,512]{1,0:T(8,128)(2,1)S(1)}, u32[]{:S(2)}, u32[]{:S(2)}) collective-permute-start(bf16[128,512]{1,0:T(8,128)(2,1)} %get-tuple-element.29), channel_id=1, source_target_pairs={{8,0},{24,16},{40,32},{56,48},{72,64},{88,80},{104,96},{120,112},{... | collective-permute-start | bytes 393224 | tf_op jit(solution)/shard_map/ppermute | solution.py:31
  49.9 1.3 collective-permute-start.7
  51.3 1.3 collective-permute-start.6
  52.6 3.2 %all-to-all-done.1 = bf16[8,128,256]{2,1,0:T(8,128)(2,1)S(1)} async-done(((bf16[8,128,256]{2,1,0:T(8,128)(2,1)}), bf16[8,128,256]{2,1,0:T(8,128)(2,1)S(1)}, u32[]{:S(2)}, u32[]{:S(2)}) %all-to-all-start.1) | async-done | bytes 524320 | tf_op jit(solution)/shard_map/all_to_all | solution.py:279
  56.5 2.9 %collective-permute-done.7.three_ref = bf16[128,512]{1,0:T(8,128)(2,1)S(1)} collective-permute-done((bf16[128,512]{1,0:T(8,128)(2,1)}, bf16[128,512]{1,0:T(8,128)(2,1)S(1)}, u32[]{:S(2)}, u32[]{:S(2)}) %collective-permute-start.7) | collective-permute-done | bytes 131104 | tf_op jit(solution)/shard_map/ppermute | solution.py:31
  59.4 22.7 %all_to_all.55 = bf16[8,128,512]{2,1,0:T(8,128)(2,1)S(1)} all-to-all(bf16[8,128,512]{2,1,0:T(8,128)(2,1)S(1)} %bitcast.31), channel_id=1, replica_groups=mesh['x'=4,'z'=8,'c'=2,'y'=8] {'x','c'}, dimensions={0} | all-to-all | bytes 2097152 | tf_op jit(solution)/shard_map/all_to_all | solution.py:245
  82.1 2.0 %group_product.1 = bf16[1024,256]{1,0:T(8,128)(2,1)S(1)} custom-call(s32[1]{0:T(128)} %bitcast.core_ref, bf16[512,1024]{1,0:T(8,128)(2,1)S(1)} %bitcast.28, bf16[512,1024]{1,0:T(8,128)(2,1)S(1)} %collective-permute-done.8.far_ref, bf16[1024,512]{1,0:T(8,128)(2,1)S(1)} %bitcast.29), custom_call_target="tpu_custom_call" | custom-call | tf_op jit(solution)/shard_map/group_product/pallas_call | solution.py:250
  84.9 10.9 %all-to-all-start.3 = ((bf16[64,16,256]{2,1,0:T(8,128)(2,1)}), bf16[64,16,256]{2,1,0:T(8,128)(2,1)S(1)}, u32[]{:S(2)}, u32[]{:S(2)}) async-start(bf16[64,16,256]{2,1,0:T(8,128)(2,1)} %bitcast.33), calls=%async_computation.3 | async-start | bytes 1048576 | tf_op jit(solution)/shard_map/all_to_all | solution.py:287
  95.9 2.9 %collective-permute-start.10 = (bf16[128,512]{1,0:T(8,128)(2,1)S(1)}, bf16[128,512]{1,0:T(8,128)(2,1)S(1)}, u32[]{:S(2)}, u32[]{:S(2)}) collective-permute-start(bf16[128,512]{1,0:T(8,128)(2,1)S(1)} %pad_maximum_fusion.1.refs_0_), channel_id=1, source_target_pairs={{0,16},{8,24},{16,32},{24,40},{32,48},{40,56},{48,64},{56,72},{64,... | collective-permute-start | bytes 393224 | tf_op jit(solution)/shard_map/ppermute | solution.py:31
  98.8 5.8 %collective-permute-start.11 = (bf16[128,512]{1,0:T(8,128)(2,1)S(1)}, bf16[128,512]{1,0:T(8,128)(2,1)S(1)}, u32[]{:S(2)}, u32[]{:S(2)}) collective-permute-start(bf16[128,512]{1,0:T(8,128)(2,1)S(1)} %pad_maximum_fusion.1.refs_0_), channel_id=1, source_target_pairs={{8,32},{24,48},{40,64},{56,80},{72,96},{88,112},{104,128},{120,144... | collective-permute-start | bytes 393224 | tf_op jit(solution)/shard_map/ppermute | solution.py:31
  104.6 1.3 collective-permute-start.9
  105.9 8.7 %collective-permute-start.12 = (bf16[128,512]{1,0:T(8,128)(2,1)S(1)}, bf16[128,512]{1,0:T(8,128)(2,1)S(1)}, u32[]{:S(2)}, u32[]{:S(2)}) collective-permute-start(bf16[128,512]{1,0:T(8,128)(2,1)S(1)} %collective-permute-done.10.refs_2_), channel_id=1, source_target_pairs={{0,8},{8,0},{1,9},{9,1},{2,10},{10,2},{3,11},{11,3},{4,12},{12,4},... | collective-permute-start | bytes 393224 | tf_op jit(solution)/shard_map/ppermute | solution.py:35
  116.5 8.2 %all-to-all-start.4 = ((bf16[32,16,256]{2,1,0:T(8,128)(2,1)}), bf16[32,16,256]{2,1,0:T(8,128)(2,1)S(1)}, u32[]{:S(2)}, u32[]{:S(2)}) async-start(bf16[32,16,256]{2,1,0:T(8,128)(2,1)} %broadcast_in_dim.8), calls=%async_computation.4 | async-start | bytes 524288 | tf_op jit(solution)/shard_map/all_to_all | solution.py:264
  124.7 6.4 %key_gradient.1 = (bf16[128,512]{1,0:T(8,128)(2,1)S(1)}, bf16[128,512]{1,0:T(8,128)(2,1)S(1)}, bf16[128,512]{1,0:T(8,128)(2,1)S(1)}, f32[128,512]{1,0:T(8,128)S(1)}) custom-call(s32[1]{0:T(128)} %bitcast.core_ref, bf16[4,512,1024]{2,1,0:T(8,128)(2,1)} %get-tuple-element.26.weights_ref, bf16[128,4096]{1,0:T(8,128)(2,1)} %bitcast.41, ...), custom_call_target="tpu_custom_call" | custom-call | flops 2147483648 | bytes 8388608 | tf_op jit(solution)/shard_map/key_gradient/pallas_call | solution.py:147
  131.1 2.6 %collective-permute-start.14 = (bf16[128,512]{1,0:T(8,128)(2,1)S(1)}, bf16[128,512]{1,0:T(8,128)(2,1)S(1)}, u32[]{:S(2)}, u32[]{:S(2)}) collective-permute-start(bf16[128,512]{1,0:T(8,128)(2,1)S(1)} %get-tuple-element.40), channel_id=1, source_target_pairs={{0,8},{8,0},{1,9},{9,1},{2,10},{10,2},{3,11},{11,3},{4,12},{12,4},... | collective-permute-start | bytes 393224 | tf_op jit(solution)/shard_map/ppermute | solution.py:35
  133.6 1.9 %collective-permute-start.13 = (bf16[128,512]{1,0:T(8,128)(2,1)S(1)}, bf16[128,512]{1,0:T(8,128)(2,1)S(1)}, u32[]{:S(2)}, u32[]{:S(2)}) collective-permute-start(bf16[128,512]{1,0:T(8,128)(2,1)S(1)} %get-tuple-element.39), channel_id=1, source_target_pairs={{8,0},{24,16},{40,32},{56,48},{72,64},{88,80},{104,96},{120,112},{... | collective-permute-start | bytes 393224 | tf_op jit(solution)/shard_map/ppermute | solution.py:31
  135.6 1.3 collective-permute-start.16
  136.9 1.3 collective-permute-start.15
  138.3 1.9 %collective-permute-start.17 = (bf16[512,256]{1,0:T(8,128)(2,1)S(1)}, bf16[512,256]{1,0:T(8,128)(2,1)S(1)}, u32[]{:S(2)}, u32[]{:S(2)}) collective-permute-start(bf16[512,256]{1,0:T(8,128)(2,1)S(1)} %bitcast.39), channel_id=1, source_target_pairs={{0,8},{8,0},{1,9},{9,1},{2,10},{10,2},{3,11},{11,3},{4,12},{12,4},... | collective-permute-start | bytes 786440 | tf_op jit(solution)/shard_map/ppermute | solution.py:35
  140.2 4.2 %collective-permute-done.16 = bf16[128,512]{1,0:T(8,128)(2,1)S(1)} collective-permute-done((bf16[128,512]{1,0:T(8,128)(2,1)S(1)}, bf16[128,512]{1,0:T(8,128)(2,1)S(1)}, u32[]{:S(2)}, u32[]{:S(2)}) %collective-permute-start.16) | collective-permute-done | bytes 131104 | tf_op jit(solution)/shard_map/ppermute | solution.py:31
  144.4 1.3 collective-permute-done.15
  (44 shorter events, 7.9 us)
Async XLA Ops:
  0.6 37.1 %copy-start.5 = (s32[1,128]{1,0:T(1,128)S(1)}, s32[1,128]{1,0:T(1,128)}, u32[]{:S(2)}) copy-start(s32[1,128]{1,0:T(1,128)} %position_ref.1) | copy-start | bytes 1540
  0.6 1.2 copy-start.1
  1.9 6.0 %copy-start.2 = (bf16[1,128,512]{2,1,0:T(8,128)(2,1)S(1)}, bf16[1,128,512]{2,1,0:T(8,128)(2,1)}, u32[]{:S(2)}) copy-start(bf16[1,128,512]{2,1,0:T(8,128)(2,1)} %param.7) | copy-start | bytes 393220
  3.1 21.1 %all-to-all-start = ((bf16[4,128,1024]{2,1,0:T(8,128)(2,1)}), bf16[4,128,1024]{2,1,0:T(8,128)(2,1)S(1)}, u32[]{:S(2)}, u32[]{:S(2)}) async-start(bf16[4,128,1024]{2,1,0:T(8,128)(2,1)} %bitcast.5), calls=%async_computation | async-start | bytes 2097152 | tf_op jit(solution)/shard_map/all_to_all | solution.py:216
  7.9 12.2 %collective-permute-start.1 = (bf16[128,512]{1,0:T(8,128)(2,1)S(1)}, bf16[128,512]{1,0:T(8,128)(2,1)S(1)}, u32[]{:S(2)}, u32[]{:S(2)}) collective-permute-start(bf16[128,512]{1,0:T(8,128)(2,1)S(1)} %bitcast.35), channel_id=1, source_target_pairs={{0,16},{8,24},{16,32},{24,40},{32,48},{40,56},{48,64},{56,72},{64,... | collective-permute-start | bytes 393224 | tf_op jit(solution)/shard_map/ppermute | solution.py:31
  11.9 12.2 %collective-permute-start.2 = (bf16[128,512]{1,0:T(8,128)(2,1)S(1)}, bf16[128,512]{1,0:T(8,128)(2,1)S(1)}, u32[]{:S(2)}, u32[]{:S(2)}) collective-permute-start(bf16[128,512]{1,0:T(8,128)(2,1)S(1)} %bitcast.36), channel_id=1, source_target_pairs={{8,32},{24,48},{40,64},{56,80},{72,96},{88,112},{104,128},{120,144... | collective-permute-start | bytes 393224 | tf_op jit(solution)/shard_map/ppermute | solution.py:31
  18.8 5.2 %collective-permute-start = (bf16[128,512]{1,0:T(8,128)(2,1)S(1)}, bf16[128,512]{1,0:T(8,128)(2,1)S(1)}, u32[]{:S(2)}, u32[]{:S(2)}) collective-permute-start(bf16[128,512]{1,0:T(8,128)(2,1)S(1)} %bitcast.37), channel_id=1, source_target_pairs={{0,8},{16,24},{32,40},{48,56},{64,72},{80,88},{96,104},{112,120},{... | collective-permute-start | bytes 393224 | tf_op jit(solution)/shard_map/ppermute | solution.py:31
  20.1 4.0 %collective-permute-start.3 = (bf16[128,512]{1,0:T(8,128)(2,1)S(1)}, bf16[128,512]{1,0:T(8,128)(2,1)S(1)}, u32[]{:S(2)}, u32[]{:S(2)}) collective-permute-start(bf16[128,512]{1,0:T(8,128)(2,1)S(1)} %collective-permute-done.1.refs_2_), channel_id=1, source_target_pairs={{0,8},{8,0},{1,9},{9,1},{2,10},{10,2},{3,11},{11,3},{4,12},{12,4},... | collective-permute-start | bytes 393224 | tf_op jit(solution)/shard_map/ppermute | solution.py:35
  24.2 13.5 %copy-start.3 = (bf16[128,512]{1,0:T(8,128)(2,1)}, bf16[128,512]{1,0:T(8,128)(2,1)S(1)}, u32[]{:S(2)}) copy-start(bf16[128,512]{1,0:T(8,128)(2,1)S(1)} %collective-permute-done.3.refs_4_) | copy-start | bytes 393220
  25.0 30.7 %collective-permute-start.8 = (bf16[512,1024]{1,0:T(8,128)(2,1)S(1)}, bf16[512,1024]{1,0:T(8,128)(2,1)S(1)}, u32[]{:S(2)}, u32[]{:S(2)}) collective-permute-start(bf16[512,1024]{1,0:T(8,128)(2,1)S(1)} %bitcast.26), channel_id=1, source_target_pairs={{0,8},{8,0},{1,9},{9,1},{2,10},{10,2},{3,11},{11,3},{4,12},{12,4},... | collective-permute-start | bytes 3145736 | tf_op jit(solution)/shard_map/ppermute | solution.py:35
  31.0 24.8 %all-to-all-start.1 = ((bf16[8,128,256]{2,1,0:T(8,128)(2,1)}), bf16[8,128,256]{2,1,0:T(8,128)(2,1)S(1)}, u32[]{:S(2)}, u32[]{:S(2)}) async-start(bf16[8,128,256]{2,1,0:T(8,128)(2,1)} %broadcast_in_dim.6), calls=%async_computation.1 | async-start | bytes 1048576 | tf_op jit(solution)/shard_map/all_to_all | solution.py:279
  37.7 0.9 copy-start.4
  45.5 5.6 %collective-permute-start.5 = (bf16[128,512]{1,0:T(8,128)(2,1)}, bf16[128,512]{1,0:T(8,128)(2,1)S(1)}, u32[]{:S(2)}, u32[]{:S(2)}) collective-permute-start(bf16[128,512]{1,0:T(8,128)(2,1)} %get-tuple-element.30), channel_id=1, source_target_pairs={{0,8},{8,0},{1,9},{9,1},{2,10},{10,2},{3,11},{11,3},{4,12},{12,4},... | collective-permute-start | bytes 393224 | tf_op jit(solution)/shard_map/ppermute | solution.py:35
  47.7 3.5 %collective-permute-start.4 = (bf16[128,512]{1,0:T(8,128)(2,1)}, bf16[128,512]{1,0:T(8,128)(2,1)S(1)}, u32[]{:S(2)}, u32[]{:S(2)}) collective-permute-start(bf16[128,512]{1,0:T(8,128)(2,1)} %get-tuple-element.29), channel_id=1, source_target_pairs={{8,0},{24,16},{40,32},{56,48},{72,64},{88,80},{104,96},{120,112},{... | collective-permute-start | bytes 393224 | tf_op jit(solution)/shard_map/ppermute | solution.py:31
  49.9 9.4 %collective-permute-start.7 = (bf16[128,512]{1,0:T(8,128)(2,1)}, bf16[128,512]{1,0:T(8,128)(2,1)S(1)}, u32[]{:S(2)}, u32[]{:S(2)}) collective-permute-start(bf16[128,512]{1,0:T(8,128)(2,1)} %get-tuple-element.29), channel_id=1, source_target_pairs={{32,8},{48,24},{64,40},{80,56},{96,72},{112,88},{128,104},{144,120... | collective-permute-start | bytes 393224 | tf_op jit(solution)/shard_map/ppermute | solution.py:31
  51.3 8.1 %collective-permute-start.6 = (bf16[128,512]{1,0:T(8,128)(2,1)S(1)}, bf16[128,512]{1,0:T(8,128)(2,1)S(1)}, u32[]{:S(2)}, u32[]{:S(2)}) collective-permute-start(bf16[128,512]{1,0:T(8,128)(2,1)S(1)} %add_convert_fusion.2), channel_id=1, source_target_pairs={{16,0},{24,8},{32,16},{40,24},{48,32},{56,40},{64,48},{72,56},{80,... | collective-permute-start | bytes 393224 | tf_op jit(solution)/shard_map/ppermute | solution.py:31
  84.1 0.8 copy-start
  84.9 30.7 %all-to-all-start.3 = ((bf16[64,16,256]{2,1,0:T(8,128)(2,1)}), bf16[64,16,256]{2,1,0:T(8,128)(2,1)S(1)}, u32[]{:S(2)}, u32[]{:S(2)}) async-start(bf16[64,16,256]{2,1,0:T(8,128)(2,1)} %bitcast.33), calls=%async_computation.3 | async-start | bytes 1048576 | tf_op jit(solution)/shard_map/all_to_all | solution.py:287
  95.9 10.0 %collective-permute-start.10 = (bf16[128,512]{1,0:T(8,128)(2,1)S(1)}, bf16[128,512]{1,0:T(8,128)(2,1)S(1)}, u32[]{:S(2)}, u32[]{:S(2)}) collective-permute-start(bf16[128,512]{1,0:T(8,128)(2,1)S(1)} %pad_maximum_fusion.1.refs_0_), channel_id=1, source_target_pairs={{0,16},{8,24},{16,32},{24,40},{32,48},{40,56},{48,64},{56,72},{64,... | collective-permute-start | bytes 393224 | tf_op jit(solution)/shard_map/ppermute | solution.py:31
  98.8 15.8 %collective-permute-start.11 = (bf16[128,512]{1,0:T(8,128)(2,1)S(1)}, bf16[128,512]{1,0:T(8,128)(2,1)S(1)}, u32[]{:S(2)}, u32[]{:S(2)}) collective-permute-start(bf16[128,512]{1,0:T(8,128)(2,1)S(1)} %pad_maximum_fusion.1.refs_0_), channel_id=1, source_target_pairs={{8,32},{24,48},{40,64},{56,80},{72,96},{88,112},{104,128},{120,144... | collective-permute-start | bytes 393224 | tf_op jit(solution)/shard_map/ppermute | solution.py:31
  104.6 10.1 %collective-permute-start.9 = (bf16[128,512]{1,0:T(8,128)(2,1)S(1)}, bf16[128,512]{1,0:T(8,128)(2,1)S(1)}, u32[]{:S(2)}, u32[]{:S(2)}) collective-permute-start(bf16[128,512]{1,0:T(8,128)(2,1)S(1)} %pad_maximum_fusion.1.refs_0_), channel_id=1, source_target_pairs={{0,8},{16,24},{32,40},{48,56},{64,72},{80,88},{96,104},{112,120},{... | collective-permute-start | bytes 393224 | tf_op jit(solution)/shard_map/ppermute | solution.py:31
  105.9 9.7 %collective-permute-start.12 = (bf16[128,512]{1,0:T(8,128)(2,1)S(1)}, bf16[128,512]{1,0:T(8,128)(2,1)S(1)}, u32[]{:S(2)}, u32[]{:S(2)}) collective-permute-start(bf16[128,512]{1,0:T(8,128)(2,1)S(1)} %collective-permute-done.10.refs_2_), channel_id=1, source_target_pairs={{0,8},{8,0},{1,9},{9,1},{2,10},{10,2},{3,11},{11,3},{4,12},{12,4},... | collective-permute-start | bytes 393224 | tf_op jit(solution)/shard_map/ppermute | solution.py:35
  116.5 21.8 %all-to-all-start.4 = ((bf16[32,16,256]{2,1,0:T(8,128)(2,1)}), bf16[32,16,256]{2,1,0:T(8,128)(2,1)S(1)}, u32[]{:S(2)}, u32[]{:S(2)}) async-start(bf16[32,16,256]{2,1,0:T(8,128)(2,1)} %broadcast_in_dim.8), calls=%async_computation.4 | async-start | bytes 524288 | tf_op jit(solution)/shard_map/all_to_all | solution.py:264
  131.1 5.8 %collective-permute-start.14 = (bf16[128,512]{1,0:T(8,128)(2,1)S(1)}, bf16[128,512]{1,0:T(8,128)(2,1)S(1)}, u32[]{:S(2)}, u32[]{:S(2)}) collective-permute-start(bf16[128,512]{1,0:T(8,128)(2,1)S(1)} %get-tuple-element.40), channel_id=1, source_target_pairs={{0,8},{8,0},{1,9},{9,1},{2,10},{10,2},{3,11},{11,3},{4,12},{12,4},... | collective-permute-start | bytes 393224 | tf_op jit(solution)/shard_map/ppermute | solution.py:35
  133.6 3.2 %collective-permute-start.13 = (bf16[128,512]{1,0:T(8,128)(2,1)S(1)}, bf16[128,512]{1,0:T(8,128)(2,1)S(1)}, u32[]{:S(2)}, u32[]{:S(2)}) collective-permute-start(bf16[128,512]{1,0:T(8,128)(2,1)S(1)} %get-tuple-element.39), channel_id=1, source_target_pairs={{8,0},{24,16},{40,32},{56,48},{72,64},{88,80},{104,96},{120,112},{... | collective-permute-start | bytes 393224 | tf_op jit(solution)/shard_map/ppermute | solution.py:31
  135.6 8.8 %collective-permute-start.16 = (bf16[128,512]{1,0:T(8,128)(2,1)S(1)}, bf16[128,512]{1,0:T(8,128)(2,1)S(1)}, u32[]{:S(2)}, u32[]{:S(2)}) collective-permute-start(bf16[128,512]{1,0:T(8,128)(2,1)S(1)} %get-tuple-element.39), channel_id=1, source_target_pairs={{32,8},{48,24},{64,40},{80,56},{96,72},{112,88},{128,104},{144,120... | collective-permute-start | bytes 393224 | tf_op jit(solution)/shard_map/ppermute | solution.py:31
  136.9 8.7 %collective-permute-start.15 = (bf16[128,512]{1,0:T(8,128)(2,1)S(1)}, bf16[128,512]{1,0:T(8,128)(2,1)S(1)}, u32[]{:S(2)}, u32[]{:S(2)}) collective-permute-start(bf16[128,512]{1,0:T(8,128)(2,1)S(1)} %add_convert_fusion.1), channel_id=1, source_target_pairs={{16,0},{24,8},{32,16},{40,24},{48,32},{56,40},{64,48},{72,56},{80,... | collective-permute-start | bytes 393224 | tf_op jit(solution)/shard_map/ppermute | solution.py:31
  138.3 8.1 %collective-permute-start.17 = (bf16[512,256]{1,0:T(8,128)(2,1)S(1)}, bf16[512,256]{1,0:T(8,128)(2,1)S(1)}, u32[]{:S(2)}, u32[]{:S(2)}) collective-permute-start(bf16[512,256]{1,0:T(8,128)(2,1)S(1)} %bitcast.39), channel_id=1, source_target_pairs={{0,8},{8,0},{1,9},{9,1},{2,10},{10,2},{3,11},{11,3},{4,12},{12,4},... | collective-permute-start | bytes 786440 | tf_op jit(solution)/shard_map/ppermute | solution.py:35
